TPU v7x, 32 devices: a whole 2x2x4 slice. The times are simulated.
32 devices in a mesh: section: 2 (over y), row: 4 (over z), col: 4 (over x, core).
Axes of the slice: x: 2, y: 2, z: 4, core: 2. Of those that a mesh axis runs over, the one named last changes fastest.
Arguments:
- inputs: bfloat16 [2, 2048, 1024], P(None, 'row', 'col'), may hold values from -6 to 6
- cotangent: bfloat16 [2, 2048, 1024], P(None, 'row', 'col'), may hold values from -6 to 6
- lengths: int32 [2, 8], replicated, may hold values from 0 to 512, as said below
- deal: int32 [2, 8], replicated, may hold values from 0 to 7, as said below
- query_key_value_weight: bfloat16 [2, 1024, 3, 1024], P('section', 'row', None, 'col'), may hold values from -0.1875 to 0.1875
- out_weight: bfloat16 [2, 1024, 1024], P('section', 'col', 'row'), may hold values from -0.375 to 0.375
- up_weight: bfloat16 [2, 1024, 4096], P('section', 'row', 'col'), may hold values from -0.1875 to 0.1875
- down_weight: bfloat16 [2, 4096, 1024], P('section', 'col', 'row'), may hold values from -0.09375 to 0.09375
- norm_gain: float32 [2, 2, 1024], P('section', None, 'col'), may hold values from 0.1 to 1.9
- norm_shift: float32 [2, 2, 1024], P('section', None, 'col'), may hold values from -1.75 to 1.75
- proj_bias: float32 [2, 4, 1024], P('section', None, 'col'), may hold values from -1.75 to 1.75
- up_bias: float32 [2, 4096], P('section', 'col'), may hold values from -1.75 to 1.75
Outputs:
- hidden_out: bfloat16 [2, 2, 2048, 1024], P('section', None, 'row', 'col')
- in_grad: float32 [2, 2, 2048, 1024], P('section', None, 'row', 'col')
- qkv_grad: float32 [2, 1024, 3, 1024], P('section', 'row', None, 'col')
- out_grad: float32 [2, 1024, 1024], P('section', 'col', 'row')
- up_grad: float32 [2, 1024, 4096], P('section', 'row', 'col')
- down_grad: float32 [2, 4096, 1024], P('section', 'col', 'row')
- gain_grad: float32 [2, 2, 1024], P('section', None, 'col')
- shift_grad: float32 [2, 2, 1024], P('section', None, 'col')
- bias_grad: float32 [2, 4, 1024], P('section', None, 'col')
- up_bias_grad: float32 [2, 4096], P('section', 'col')
Inputs may be any that keep to these rules, and one draw needn't show every extreme that they name: Row m holds micro-batch m's sequence lengths in given order. The two sequences with deal values 2 r and 2 r + 1 belong to row device r and together hold at most 512 tokens; in every micro-batch some device holds exactly 512. Each row is a permutation of 0 to 7; sequence i goes to row device deal // 2, first there if deal is even.
All inputs are finite; a program needn't handle non-finite values.
Results may differ from a plain program's by a relative error of at most 0.015.
Values may be sent and summed in bfloat16 or wider, within the bound.
No kernel may reach another device: no remote copies, remote signals or barrier semaphores. Data moves between devices by JAX's collectives and lax.ppermute only.
A program may use at most 192 MiB of HBM per device.

v0:
```python
import jax
import jax.numpy as jnp
from jax import lax
from jax.sharding import PartitionSpec as P

D = 1024
HEADS = 16
HEAD_DIM = 64


epsilon = 1e-05
masked_score = -1e30


def from_behind(array, axis, by):
    count = lax.axis_size(axis)
    pairs = [(i, i + by) for i in range(count) if 0 <= i + by < count]
    return lax.ppermute(array, axis, pairs)


def gelu_tanh(values):
    return jax.nn.gelu(values, approximate=True)


def owned_layout(lengths, deal, holder, rows_dev):
    amount = lengths.shape[0]
    starts = jnp.cumsum(lengths) - lengths
    ordering = jnp.arange(amount, dtype=jnp.int32)
    matches = deal[:, None] == ordering[None, :]
    own_len = jnp.sum(jnp.where(matches, lengths[:, None], 0), axis=0)
    own_start = jnp.sum(jnp.where(matches, starts[:, None], 0), axis=0)
    first_len = jnp.take(own_len, 2 * holder)
    second_len = jnp.take(own_len, 2 * holder + 1)
    first_start = jnp.take(own_start, 2 * holder)
    second_start = jnp.take(own_start, 2 * holder + 1)
    slot_ids = jnp.arange(rows_dev, dtype=jnp.int32)
    in_first = slot_ids < first_len
    in_second = jnp.logical_and(jnp.logical_not(in_first), slot_ids < first_len + second_len)
    usable = jnp.logical_or(in_first, in_second)
    position = jnp.where(in_first, slot_ids, slot_ids - first_len)
    source = jnp.where(in_first, first_start + slot_ids, second_start + position)
    source = jnp.where(usable, source, 0)
    segment = jnp.where(in_first, 0, jnp.where(in_second, 1, 2)).astype(jnp.int32)
    return (source, usable, segment, position)


def given_targets(lengths, deal, positions, rows_dev):
    amount = lengths.shape[0]
    starts = jnp.cumsum(lengths) - lengths
    ordering = jnp.arange(amount, dtype=jnp.int32)
    matches = deal[:, None] == ordering[None, :]
    own_len = jnp.sum(jnp.where(matches, lengths[:, None], 0), axis=0)
    partner_len = jnp.sum(
        jnp.where(ordering[None, :] == (deal - 1)[:, None], own_len[None, :], 0), axis=1
    )
    offset = jnp.where(deal % 2 == 1, partner_len, 0)
    base_slot = deal // 2 * rows_dev + offset - starts
    inside = jnp.logical_and(
        positions[:, None] >= starts[None, :], positions[:, None] < (starts + lengths)[None, :]
    )
    is_live = jnp.any(inside, axis=1)
    target = jnp.sum(jnp.where(inside, base_slot[None, :] + positions[:, None], 0), axis=1)
    return (is_live, target)


def spread_features(values):
    return lax.all_gather(values, "col", axis=1, tiled=True)


def sum_columns(partial_value):
    return lax.psum_scatter(partial_value, "col", scatter_dimension=1, tiled=True)


def spread_grads(values):
    return lax.all_gather(values, "col", axis=1, tiled=True)


def reduce_grads(partial_value):
    return lax.psum_scatter(partial_value, "col", scatter_dimension=1, tiled=True)


def normalize(hidden, gain, shift):
    summed, square = lax.psum((jnp.sum(hidden, axis=1), jnp.sum(hidden * hidden, axis=1)), "col")
    average = summed / D
    inverse = lax.rsqrt(square / D - average * average + epsilon)
    centered = (hidden - average[:, None]) * inverse[:, None]
    return (centered, inverse, (centered * gain + shift).astype(jnp.bfloat16))


def norm_backward(grad_norm, centered, inverse, gain):
    grad_cent = grad_norm * gain
    summed, cross = lax.psum(
        (jnp.sum(grad_cent, axis=1), jnp.sum(grad_cent * centered, axis=1)), "col"
    )
    grad_hidden = inverse[:, None] * (
        grad_cent - summed[:, None] / D - centered * (cross[:, None] / D)
    )
    return (grad_hidden, jnp.sum(grad_norm * centered, axis=0), jnp.sum(grad_norm, axis=0))


def masked_scores(query_block, key_rows, block_segment, block_position, segment, position, slopes):
    scores = jnp.einsum(
        "qhe,khe->hqk", query_block, key_rows, preferred_element_type=jnp.float32
    ) * HEAD_DIM ** (-0.5)
    distance = (block_position[:, None] - position[None, :]).astype(jnp.float32)
    allowed = jnp.logical_and(
        block_segment[:, None] == segment[None, :],
        jnp.logical_and(block_segment[:, None] < 2, distance >= 0),
    )
    scores = scores - slopes[:, None, None] * distance[None]
    return jnp.where(allowed[None], scores, masked_score)


def attend_forward(queries, key_rows, value_rows, segment, position, slopes):
    rows_dev = queries.shape[0]
    block_rows = min(512, rows_dev)

    def one_block(offset):
        scores = masked_scores(queries, key_rows, segment, position, segment, position, slopes)
        highest = jnp.max(scores, axis=2, keepdims=True)
        exp_scores = jnp.exp(scores - highest)
        summed = jnp.sum(exp_scores, axis=2, keepdims=True)
        soft_weights = (exp_scores / summed).astype(jnp.bfloat16)
        mixed_block = jnp.einsum(
            "hqk,khe->qhe", soft_weights, value_rows, preferred_element_type=jnp.float32
        )
        return (mixed_block, (highest + jnp.log(summed))[:, :, 0])

    mixed_heads, logsum = lax.map(one_block, jnp.arange(0, rows_dev, block_rows, dtype=jnp.int32))
    return (mixed_heads.reshape(rows_dev, -1), logsum)


def attend_backward(queries, key_rows, value_rows, segment, position, slopes, logsum, grad_mixed):
    rows_dev = queries.shape[0]
    block_rows = min(512, rows_dev)
    scale_factor = HEAD_DIM ** (-0.5)

    def one_block(carried, item_pair):
        offset, logsum_rows = item_pair
        scores = masked_scores(queries, key_rows, segment, position, segment, position, slopes)
        soft_weights = jnp.exp(scores - logsum_rows[:, :, None])
        grad_prob = jnp.einsum(
            "qhe,khe->hqk", grad_mixed, value_rows, preferred_element_type=jnp.float32
        )
        row_dot = jnp.sum(soft_weights * grad_prob, axis=2, keepdims=True)
        grad_score = (soft_weights * (grad_prob - row_dot)).astype(jnp.bfloat16)
        grad_query = (
            jnp.einsum("hqk,khe->qhe", grad_score, key_rows, preferred_element_type=jnp.float32)
            * scale_factor
        )
        grad_key = (
            carried[0]
            + jnp.einsum("hqk,qhe->khe", grad_score, queries, preferred_element_type=jnp.float32)
            * scale_factor
        )
        grad_value = carried[1] + jnp.einsum(
            "hqk,qhe->khe",
            soft_weights.astype(jnp.bfloat16),
            grad_mixed,
            preferred_element_type=jnp.float32,
        )
        return ((grad_key, grad_value), grad_query)

    zeros_rows = jnp.zeros(key_rows.shape, jnp.float32)
    offsets = jnp.arange(0, rows_dev, block_rows, dtype=jnp.int32)
    (grad_key, grad_value), grad_query = lax.scan(
        one_block, (zeros_rows, zeros_rows), (offsets, logsum)
    )
    return (grad_query.reshape(rows_dev, -1, HEAD_DIM), grad_key, grad_value)


def layer_forward(hidden, layout_now, weights):
    (
        complete_query_key_value,
        full_out,
        full_up,
        full_down,
        gain_rows,
        shifts,
        biases,
        up_shift,
        slopes,
    ) = weights
    usable, segment, position = layout_now
    rows_dev = hidden.shape[0]
    centered, inverse, normalized_rows = normalize(hidden, gain_rows[0], shifts[0])
    entire_rows = spread_features(normalized_rows)
    query_key_value_columns = jnp.einsum(
        "kp,pnf->knf", entire_rows, complete_query_key_value, preferred_element_type=jnp.float32
    )
    queries = (
        (query_key_value_columns[:, 0] + biases[0])
        .astype(jnp.bfloat16)
        .reshape(rows_dev, -1, HEAD_DIM)
    )
    key_rows = query_key_value_columns[:, 1].astype(jnp.bfloat16).reshape(rows_dev, -1, HEAD_DIM)
    value_rows = (
        (query_key_value_columns[:, 2] + biases[1])
        .astype(jnp.bfloat16)
        .reshape(rows_dev, -1, HEAD_DIM)
    )
    mixed_heads, logsum = attend_forward(queries, key_rows, value_rows, segment, position, slopes)
    attended = mixed_heads.astype(jnp.bfloat16)
    branch = (
        sum_columns(jnp.dot(attended, full_out, preferred_element_type=jnp.float32)) + biases[2]
    )
    middle = hidden + branch
    centered_two, inverse_two, normed_two = normalize(middle, gain_rows[1], shifts[1])
    whole_two = spread_features(normed_two)
    upper_in = jnp.dot(whole_two, full_up, preferred_element_type=jnp.float32) + up_shift
    activated = gelu_tanh(upper_in).astype(jnp.bfloat16)
    down_out = (
        sum_columns(jnp.dot(activated, full_down, preferred_element_type=jnp.float32)) + biases[3]
    )
    result = jnp.where(usable[:, None], middle + down_out, 0.0)
    stored = (
        centered,
        inverse,
        entire_rows,
        queries,
        key_rows,
        value_rows,
        logsum,
        attended,
        centered_two,
        inverse_two,
        whole_two,
        upper_in,
        activated,
    )
    return (result, stored)


def layer_backward(gradient, layout_now, weights, stored):
    (
        complete_query_key_value,
        full_out,
        full_up,
        full_down,
        gain_rows,
        shifts,
        biases,
        up_shift,
        slopes,
    ) = weights
    usable, segment, position = layout_now
    (
        centered,
        inverse,
        entire_rows,
        queries,
        key_rows,
        value_rows,
        logsum,
        attended,
        centered_two,
        inverse_two,
        whole_two,
        upper_in,
        activated,
    ) = stored
    rows_dev = gradient.shape[0]
    grad_out = jnp.where(usable[:, None], gradient, 0.0)
    grad_down = grad_out.astype(jnp.bfloat16)
    down_full = spread_grads(grad_down)
    down_term = jnp.einsum("tf,td->fd", activated, down_full, preferred_element_type=jnp.float32)
    grad_act = jnp.einsum("td,fd->tf", down_full, full_down, preferred_element_type=jnp.float32)
    grad_upper = jax.vjp(gelu_tanh, upper_in)[1](grad_act)[0].astype(jnp.bfloat16)
    up_term = jnp.einsum("td,tf->df", whole_two, grad_upper, preferred_element_type=jnp.float32)
    grad_norm_two = reduce_grads(
        jnp.einsum("tf,df->td", grad_upper, full_up, preferred_element_type=jnp.float32)
    )
    grad_mid, gain_two, shift_two = norm_backward(
        grad_norm_two, centered_two, inverse_two, gain_rows[1]
    )
    grad_mid = grad_out + grad_mid
    grad_branch = grad_mid.astype(jnp.bfloat16)
    branch_full = spread_grads(grad_branch)
    out_term = jnp.einsum("tc,td->cd", attended, branch_full, preferred_element_type=jnp.float32)
    grad_attended = (
        jnp.einsum("td,cd->tc", branch_full, full_out, preferred_element_type=jnp.float32)
        .astype(jnp.bfloat16)
        .reshape(rows_dev, -1, HEAD_DIM)
    )
    grad_query, grad_key, grad_value = attend_backward(
        queries, key_rows, value_rows, segment, position, slopes, logsum, grad_attended
    )
    query_key_value_gradient = (
        jnp.stack([grad_query, grad_key, grad_value], axis=1)
        .astype(jnp.bfloat16)
        .reshape(rows_dev, 3, -1)
    )
    query_key_value_part = jnp.einsum(
        "iy,ibv->ybv", entire_rows, query_key_value_gradient, preferred_element_type=jnp.float32
    )
    grad_norm = reduce_grads(
        jnp.einsum(
            "boz,roz->br",
            query_key_value_gradient,
            complete_query_key_value,
            preferred_element_type=jnp.float32,
        )
    )
    grad_input, gain_one, shift_one = norm_backward(grad_norm, centered, inverse, gain_rows[0])
    grad_input = grad_mid + grad_input
    qkv_sums = jnp.sum(query_key_value_gradient, axis=0, dtype=jnp.float32)
    bias_term = jnp.stack(
        [
            qkv_sums[0],
            qkv_sums[2],
            jnp.sum(grad_branch, axis=0, dtype=jnp.float32),
            jnp.sum(grad_down, axis=0, dtype=jnp.float32),
        ]
    )
    small_terms = (
        jnp.stack([gain_one, gain_two]),
        jnp.stack([shift_one, shift_two]),
        bias_term,
        jnp.sum(grad_upper, axis=0, dtype=jnp.float32),
    )
    return (grad_input, (query_key_value_part, out_term, up_term, down_term), small_terms)


def on_device(
    inputs,
    cotangent,
    lengths,
    deal,
    query_key_value_weight,
    out_weight,
    up_weight,
    down_weight,
    norm_gain,
    norm_shift,
    proj_bias,
    up_bias,
):
    section_id = lax.axis_index("section")
    holder = lax.axis_index("row")
    column = lax.axis_index("col")
    micro_count, rows_dev, width_col = inputs.shape
    per_device = width_col // HEAD_DIM
    source, usable, segment, position = jax.vmap(owned_layout, (0, 0, None, None))(
        lengths, deal, holder, rows_dev
    )
    complete_query_key_value, full_out, full_up, full_down = (
        lax.all_gather(query_key_value_weight[0], "row", axis=0, tiled=True),
        lax.all_gather(out_weight[0], "row", axis=1, tiled=True),
        lax.all_gather(up_weight[0], "row", axis=0, tiled=True),
        lax.all_gather(down_weight[0], "row", axis=1, tiled=True),
    )
    head_ids = column * per_device + jnp.arange(per_device, dtype=jnp.int32)
    slopes = jnp.exp2(-8.0 * (head_ids.astype(jnp.float32) + 1.0) / HEADS)
    weights = (
        complete_query_key_value,
        full_out,
        full_up,
        full_down,
        norm_gain[0],
        norm_shift[0],
        proj_bias[0],
        up_bias[0],
        slopes,
    )
    outgoing = jnp.where(section_id == 0, inputs, cotangent)
    portion = lax.all_gather(outgoing, "row", axis=1, tiled=True)
    length = portion.shape[1]
    picked_at = source
    inside = jnp.logical_and(usable, jnp.logical_and(picked_at >= 0, picked_at < length))
    picked = jnp.take_along_axis(portion, jnp.clip(picked_at, 0, length - 1)[:, :, None], axis=1)
    owned = jnp.where(inside[:, :, None], picked, jnp.zeros_like(inputs))
    stored_list = []
    sent_list = []
    carried = jnp.zeros((rows_dev, width_col), jnp.bfloat16)
    for moment in range(micro_count + 1):
        batch_index = jnp.clip(moment - section_id, 0, micro_count - 1)
        layout_now = (usable[batch_index], segment[batch_index], position[batch_index])
        hidden = jnp.where(section_id == 0, owned[min(moment, micro_count - 1)], carried).astype(
            jnp.float32
        )
        result, stored = layer_forward(hidden, layout_now, weights)
        rounded = result.astype(jnp.bfloat16)
        stored_list.append(stored)
        sent_list.append(rounded)
        if moment < micro_count:
            carried = from_behind(rounded, "section", 1)
    input_grads = []
    weight_totals = None
    small_totals = None
    returned_grad = jnp.zeros((rows_dev, width_col), jnp.bfloat16)
    for moment in range(micro_count + 1):
        batch_raw = moment - 1 + section_id
        batch_index = jnp.clip(batch_raw, 0, micro_count - 1)
        active = jnp.logical_and(batch_raw >= 0, batch_raw < micro_count)
        layout_now = (usable[batch_index], segment[batch_index], position[batch_index])
        earlier = stored_list[max(moment - 1, 0)]
        latter = stored_list[min(moment + 1, micro_count)]
        stored = jax.tree.map(
            lambda former, newer: jnp.where(section_id == 1, newer, former), earlier, latter
        )
        incoming = jnp.where(
            section_id == 1, owned[min(moment, micro_count - 1)], returned_grad
        ).astype(jnp.float32)
        grad_input, weight_terms, small_terms = layer_backward(
            incoming, layout_now, weights, stored
        )
        weight_terms = jax.tree.map(lambda member: jnp.where(active, member, 0.0), weight_terms)
        small_terms = jax.tree.map(lambda member: jnp.where(active, member, 0.0), small_terms)
        if weight_totals is None:
            weight_totals = weight_terms
            small_totals = small_terms
        else:
            weight_totals = jax.tree.map(
                lambda former, newer: former + newer, weight_totals, weight_terms
            )
            small_totals = jax.tree.map(
                lambda former, newer: former + newer, small_totals, small_terms
            )
        input_grads.append(grad_input)
        if moment < micro_count:
            returned_grad = from_behind(grad_input.astype(jnp.bfloat16), "section", -1)
    hidden_rows = jnp.stack(
        [
            jnp.where(section_id == 1, sent_list[batch + 1], sent_list[batch])
            for batch in range(micro_count)
        ]
    )
    grad_rows = jnp.stack(
        [
            jnp.where(section_id == 1, input_grads[batch], input_grads[batch + 1])
            for batch in range(micro_count)
        ]
    )
    values = jnp.concatenate([hidden_rows.astype(jnp.float32), grad_rows], axis=2)
    positions = jnp.arange(lax.axis_size("row") * rows_dev, dtype=jnp.int32)
    is_live, target = jax.vmap(given_targets, (0, 0, None, None))(
        lengths, deal, positions, rows_dev
    )
    picked_at = target - holder * rows_dev
    mine = jnp.logical_and(is_live, jnp.logical_and(picked_at >= 0, picked_at < rows_dev))
    picked = jnp.take_along_axis(values, jnp.clip(picked_at, 0, rows_dev - 1)[:, :, None], axis=1)
    returned_rows = jnp.transpose(
        lax.psum_scatter(
            jnp.transpose(jnp.where(mine[:, :, None], picked, 0.0), (1, 0, 2)),
            "row",
            scatter_dimension=0,
            tiled=True,
        ),
        (1, 0, 2),
    )
    hidden_out = returned_rows[:, :, :width_col].astype(jnp.bfloat16)[None]
    in_grad = returned_rows[:, :, width_col:][None]
    weight_sums = (
        lax.psum_scatter(weight_totals[0], "row", scatter_dimension=0, tiled=True),
        lax.psum_scatter(weight_totals[1], "row", scatter_dimension=1, tiled=True),
        lax.psum_scatter(weight_totals[2], "row", scatter_dimension=0, tiled=True),
        lax.psum_scatter(weight_totals[3], "row", scatter_dimension=1, tiled=True),
    )
    small_sums = lax.psum(small_totals, "row")
    return (
        hidden_out,
        in_grad,
        weight_sums[0][None],
        weight_sums[1][None],
        weight_sums[2][None],
        weight_sums[3][None],
        small_sums[0][None],
        small_sums[1][None],
        small_sums[2][None],
        small_sums[3][None],
    )


def solution(mesh):
    placed = (
        P(None, "row", "col"),
        P(None, "row", "col"),
        P(),
        P(),
        P("section", "row", None, "col"),
        P("section", "col", "row"),
        P("section", "row", "col"),
        P("section", "col", "row"),
        P("section", None, "col"),
        P("section", None, "col"),
        P("section", None, "col"),
        P("section", "col"),
    )
    return jax.shard_map(
        on_device,
        mesh=mesh,
        in_specs=placed,
        out_specs=(
            P("section", None, "row", "col"),
            P("section", None, "row", "col"),
            P("section", "row", None, "col"),
            P("section", "col", "row"),
            P("section", "row", "col"),
            P("section", "col", "row"),
            P("section", None, "col"),
            P("section", None, "col"),
            P("section", None, "col"),
            P("section", "col"),
        ),
        check_vma=False,
    )
```

profile of v0, /device:TPU:0, one launch (start us, length us, event | category | flops | bytes accessed | tf_op | source)
XLA Modules:
  0.0 1457.3 jit_solution(8329157252402859691)
XLA Ops:
  11.5 47.4 %all-gather.21.cloned.1.call-done = bf16[2,2048,256]{2,1,0:T(8,128)(2,1)} async-done(((bf16[2,512,256]{2,1,0:T(8,128)(2,1)}), bf16[2,2048,256]{2,1,0:T(8,128)(2,1)}) %all-gather.21.cloned.1.call-update) | async-done | bytes 2097168 | tf_op jit(solution)/shard_map/all_gather | solution.py:366
  58.9 19.4 %gather_fusion = bf16[1024,256]{1,0:T(8,128)(2,1)S(1)} fusion(bf16[2,2048,256]{2,1,0:T(8,128)(2,1)} %all-gather.21.cloned.1.call-done, s32[1024]{0:T(1024)S(1)} %bitcast.339), kind=kCustom, calls=%fused_computation | custom fusion | bytes 1056768 | tf_op jit(solution)/shard_map/jit(take_along_axis)/gather | solution.py:370
  78.9 6.9 all-reduce.9
  87.3 19.3 %all-gather.1 = bf16[1,256,1024]{2,1,0:T(8,128)(2,1)S(1)} all-gather(bf16[1,256,256]{2,1,0:T(8,128)(2,1)S(1)} %copy-done.104), channel_id=3, replica_groups=mesh['section'=2,'row'=4,'col'=4] {'row'}, dimensions={2}, use_global_device_ids=true | all-gather | bytes 655360 | tf_op jit(solution)/shard_map/all_gather | solution.py:348
  107.1 15.8 %all-gather.23.cloned.1.call-done = bf16[512,1024]{1,0:T(8,128)(2,1)} async-done(((bf16[512,256]{1,0:T(8,128)(2,1)}), bf16[512,1024]{1,0:T(8,128)(2,1)}) %all-gather.23.cloned.1.call-update) | async-done | bytes 1048592 | tf_op jit(solution)/shard_map/all_gather | solution.py:67
  133.5 30.9 %reduce-scatter.18.cloned.1.call-done = f32[512,256]{1,0:T(8,128)} async-done(((f32[512,1024]{1,0:T(8,128)}), f32[512,256]{1,0:T(8,128)}) %reduce-scatter.18.cloned.1.call-update) | async-done | bytes 524304 | tf_op jit(solution)/shard_map/reduce_scatter | solution.py:71
  173.7 38.1 %all-gather.49.cloned.1.call-done = bf16[1,1024,1024]{2,1,0:T(8,128)(2,1)} async-done(((bf16[1,256,1024]{2,1,0:T(8,128)(2,1)}), bf16[1,1024,1024]{2,1,0:T(8,128)(2,1)}) %all-gather.49.cloned.1.call-update) | async-done | bytes 2097168 | tf_op jit(solution)/shard_map/all_gather | solution.py:349
  211.9 17.7 %all-gather.25.cloned.1.call-done = bf16[512,1024]{1,0:T(8,128)(2,1)} async-done(((bf16[512,256]{1,0:T(8,128)(2,1)}), bf16[512,1024]{1,0:T(8,128)(2,1)}) %all-gather.25.cloned.1.call-update) | async-done | bytes 1048592 | tf_op jit(solution)/shard_map/all_gather | solution.py:67
  234.4 43.0 %all-gather.51.cloned.1.call-done = bf16[1,1024,1024]{2,1,0:T(8,128)(2,1)} async-done(((bf16[1,1024,256]{2,1,0:T(8,128)(2,1)}), bf16[1,1024,1024]{2,1,0:T(8,128)(2,1)}) %all-gather.51.cloned.1.call-update) | async-done | bytes 2097168 | tf_op jit(solution)/shard_map/all_gather | solution.py:350
  282.3 29.1 %reduce-scatter.20.cloned.1.call-done = f32[512,256]{1,0:T(8,128)} async-done(((f32[512,1024]{1,0:T(8,128)}), f32[512,256]{1,0:T(8,128)}) %reduce-scatter.20.cloned.1.call-update) | async-done | bytes 524304 | tf_op jit(solution)/shard_map/reduce_scatter | solution.py:71
  321.8 6.0 all-reduce.7
  331.0 15.7 %all-gather.27.cloned.1.call-done = bf16[512,1024]{1,0:T(8,128)(2,1)} async-done(((bf16[512,256]{1,0:T(8,128)(2,1)}), bf16[512,1024]{1,0:T(8,128)(2,1)}) %all-gather.27.cloned.1.call-update) | async-done | bytes 1048592 | tf_op jit(solution)/shard_map/all_gather | solution.py:67
  357.2 31.5 %reduce-scatter.22.cloned.1.call-done = f32[512,256]{1,0:T(8,128)} async-done(((f32[512,1024]{1,0:T(8,128)}), f32[512,256]{1,0:T(8,128)}) %reduce-scatter.22.cloned.1.call-update) | async-done | bytes 524304 | tf_op jit(solution)/shard_map/reduce_scatter | solution.py:71
  397.5 17.9 %all-gather.29.cloned.1.call-done = bf16[512,1024]{1,0:T(8,128)(2,1)} async-done(((bf16[512,256]{1,0:T(8,128)(2,1)}), bf16[512,1024]{1,0:T(8,128)(2,1)}) %all-gather.29.cloned.1.call-update) | async-done | bytes 1048592 | tf_op jit(solution)/shard_map/all_gather | solution.py:67
  424.0 31.5 %reduce-scatter.24.cloned.1.call-done = f32[512,256]{1,0:T(8,128)} async-done(((f32[512,1024]{1,0:T(8,128)}), f32[512,256]{1,0:T(8,128)}) %reduce-scatter.24.cloned.1.call-update) | async-done | bytes 524304 | tf_op jit(solution)/shard_map/reduce_scatter | solution.py:71
  468.0 18.0 %all-gather.35.cloned.1.call-done = bf16[512,1024]{1,0:T(8,128)(2,1)} async-done(((bf16[512,256]{1,0:T(8,128)(2,1)}), bf16[512,1024]{1,0:T(8,128)(2,1)}) %all-gather.35.cloned.1.call-update) | async-done | bytes 1048592 | tf_op jit(solution)/shard_map/all_gather | solution.py:75
  485.9 6.5 convert_reduce_fusion.2
  496.1 31.5 %reduce-scatter.30.cloned.1.call-done = f32[512,256]{1,0:T(8,128)} async-done(((f32[512,1024]{1,0:T(8,128)}), f32[512,256]{1,0:T(8,128)}) %reduce-scatter.30.cloned.1.call-update) | async-done | bytes 524304 | tf_op jit(solution)/shard_map/reduce_scatter | solution.py:79
  530.4 5.9 all-reduce.5
  542.7 13.4 all-gather.31.cloned.1.call-done
  569.0 6.0 all-gather.37.cloned.1.call-done
  598.9 10.2 reduce-scatter.26.cloned.1.call-done
  610.3 32.5 %reduce-scatter.32.cloned.1.call-done = f32[512,256]{1,0:T(8,128)} async-done(((f32[512,1024]{1,0:T(8,128)}), f32[512,256]{1,0:T(8,128)}) %reduce-scatter.32.cloned.1.call-update) | async-done | bytes 524304 | tf_op jit(solution)/shard_map/reduce_scatter | solution.py:79
  645.1 5.8 all-reduce.4
  654.6 8.6 collective-permute-done.2
  675.2 13.7 all-gather.39.cloned.1.call-done
  689.0 6.5 convert_reduce_fusion.1
  699.1 31.5 %reduce-scatter.34.cloned.1.call-done = f32[512,256]{1,0:T(8,128)} async-done(((f32[512,1024]{1,0:T(8,128)}), f32[512,256]{1,0:T(8,128)}) %reduce-scatter.34.cloned.1.call-update) | async-done | bytes 524304 | tf_op jit(solution)/shard_map/reduce_scatter | solution.py:79
  732.9 5.9 all-reduce.3
  743.5 15.6 %all-gather.41.cloned.1.call-done = bf16[512,1024]{1,0:T(8,128)(2,1)} async-done(((bf16[512,256]{1,0:T(8,128)(2,1)}), bf16[512,1024]{1,0:T(8,128)(2,1)}) %all-gather.41.cloned.1.call-update) | async-done | bytes 1048592 | tf_op jit(solution)/shard_map/all_gather | solution.py:75
  777.2 31.5 %reduce-scatter.36.cloned.1.call-done = f32[512,256]{1,0:T(8,128)} async-done(((f32[512,1024]{1,0:T(8,128)}), f32[512,256]{1,0:T(8,128)}) %reduce-scatter.36.cloned.1.call-update) | async-done | bytes 524304 | tf_op jit(solution)/shard_map/reduce_scatter | solution.py:79
  820.5 8.6 collective-permute-done.3
  830.0 16.0 %all-gather.43.cloned.1.call-done = bf16[512,1024]{1,0:T(8,128)(2,1)} async-done(((bf16[512,256]{1,0:T(8,128)(2,1)}), bf16[512,1024]{1,0:T(8,128)(2,1)}) %all-gather.43.cloned.1.call-update) | async-done | bytes 1048592 | tf_op jit(solution)/shard_map/all_gather | solution.py:75
  846.0 6.5 convert_reduce_fusion
  856.4 31.4 %reduce-scatter.38.cloned.1.call-done = f32[512,256]{1,0:T(8,128)} async-done(((f32[512,1024]{1,0:T(8,128)}), f32[512,256]{1,0:T(8,128)}) %reduce-scatter.38.cloned.1.call-update) | async-done | bytes 524304 | tf_op jit(solution)/shard_map/reduce_scatter | solution.py:79
  890.0 5.9 all-reduce.1
  903.9 12.5 all-gather.45.cloned.1.call-done
  939.4 10.8 reduce-scatter.28.cloned.1.call-done
  952.6 31.8 %reduce-scatter.40.cloned.1.call-done = f32[512,256]{1,0:T(8,128)} async-done(((f32[512,1024]{1,0:T(8,128)}), f32[512,256]{1,0:T(8,128)}) %reduce-scatter.40.cloned.1.call-update) | async-done | bytes 524304 | tf_op jit(solution)/shard_map/reduce_scatter | solution.py:79
  986.0 6.2 all-reduce
  994.2 49.4 %gather_fusion.1 = f32[4096,512]{1,0:T(8,128)} fusion(f32[2,512,512]{2,1,0:T(8,128)S(1)} %maximum_maximum_fusion, s32[4096]{0:T(1024)S(1)} %bitcast.338), kind=kCustom, calls=%fused_computation.1 | custom fusion | bytes 16809984 | tf_op jit(solution)/shard_map/jit(take_along_axis)/gather | solution.py:441
  1043.6 7.5 select_select_fusion
  1080.7 20.8 %all-reduce.10 = (f32[1,2,256]{2,1,0:T(2,128)}, f32[1,2,256]{2,1,0:T(2,128)}, f32[1,4,256]{2,1,0:T(4,128)}, f32[1,1024]{1,0:T(1,128)}) all-reduce(f32[1,2,256]{2,1,0:T(2,128)S(1)} %fusion.220, f32[1,2,256]{2,1,0:T(2,128)S(1)} %fusion.223, f32[1,4,256]{2,1,0:T(4,128)S(1)} %fusion.215, ...), channel_id=1, replica_groups=mesh['section'=2,'row'=4,'col'=4] {'row'}, use_global_device_ids=true, to_apply=%region_86.88 | all-reduce | flops 3072 | bytes 24576 | tf_op jit(solution)/shard_map/psum | solution.py:459
  1101.5 95.9 %reduce-scatter.42.cloned.1.call-done = f32[512,2,512]{2,0,1:T(8,128)} async-done(((f32[2048,2,512]{2,0,1:T(8,128)}), f32[512,2,512]{2,0,1:T(8,128)}) %reduce-scatter.42.cloned.1.call-update) | async-done | bytes 2097168 | tf_op jit(solution)/shard_map/reduce_scatter | solution.py:443
  1201.7 26.3 %reduce-scatter.46.cloned.1.call-done = f32[256,256]{1,0:T(8,128)} async-done(((f32[256,1024]{1,0:T(8,128)}), f32[256,256]{1,0:T(8,128)}) %reduce-scatter.46.cloned.1.call-update) | async-done | bytes 262160 | tf_op jit(solution)/shard_map/reduce_scatter | solution.py:455
  1228.0 78.4 %reduce-scatter.48.cloned.1.call-done = f32[256,1024]{1,0:T(8,128)} async-done(((f32[1024,1024]{1,0:T(8,128)}), f32[256,1024]{1,0:T(8,128)}) %reduce-scatter.48.cloned.1.call-update) | async-done | bytes 1048592 | tf_op jit(solution)/shard_map/reduce_scatter | solution.py:456
  1306.4 80.2 %reduce-scatter.50.cloned.1.call-done = f32[1024,256]{1,0:T(8,128)} async-done(((f32[1024,1024]{1,0:T(8,128)}), f32[1024,256]{1,0:T(8,128)}) %reduce-scatter.50.cloned.1.call-update) | async-done | bytes 1048592 | tf_op jit(solution)/shard_map/reduce_scatter | solution.py:457
  1386.6 63.6 %reduce-scatter.44.cloned.1.call-done = f32[256,3,256]{2,0,1:T(8,128)} async-done(((f32[1024,3,256]{2,0,1:T(8,128)}), f32[256,3,256]{2,0,1:T(8,128)}) %reduce-scatter.44.cloned.1.call-update) | async-done | bytes 786448 | tf_op jit(solution)/shard_map/reduce_scatter | solution.py:454
  (609 shorter events, 275.0 us)
Async XLA Ops:
  7.2 51.7 %all-gather.21.cloned.1.call-start = ((), (), s32[]{:S(2)}) async-start(), calls=%async_computation.17 | async-start | bytes 2621440 | tf_op jit(solution)/shard_map/all_gather | solution.py:366
  9.3 97.8 %all-gather.47.cloned.1.call-start = ((), (), s32[]{:S(2)}) async-start(), calls=%async_computation.47 | async-start | bytes 1966080 | tf_op jit(solution)/shard_map/all_gather | solution.py:347
  10.3 112.6 %all-gather.23.cloned.1.call-start = ((), (), s32[]{:S(2)}) async-start(), calls=%async_computation.18 | async-start | bytes 1310720 | tf_op jit(solution)/shard_map/all_gather | solution.py:67
  11.4 385.0 %copy-start.109 = (f32[1,1,256]{2,1,0:T(1,128)}, f32[1,1,256]{2,1,0:T(1,128)S(1)}, u32[]{:S(2)}) copy-start(f32[1,1,256]{2,1,0:T(1,128)S(1)} %get-tuple-element.365) | copy-start | bytes 3076
  86.8 77.6 %reduce-scatter.18.cloned.1.call-start = ((), (), s32[]{:S(2)}) async-start(), calls=%async_computation.19 | async-start | bytes 2621440 | tf_op jit(solution)/shard_map/reduce_scatter | solution.py:71
  86.9 301.8 %copy-start.117 = (f32[1,1,256]{2,1,0:T(1,128)}, f32[1,1,256]{2,1,0:T(1,128)S(1)}, u32[]{:S(2)}) copy-start(f32[1,1,256]{2,1,0:T(1,128)S(1)} %get-tuple-element.355) | copy-start | bytes 3076
  86.9 368.7 %copy-start.115 = (f32[1,1,256]{2,1,0:T(1,128)}, f32[1,1,256]{2,1,0:T(1,128)S(1)}, u32[]{:S(2)}) copy-start(f32[1,1,256]{2,1,0:T(1,128)S(1)} %get-tuple-element.354) | copy-start | bytes 3076
  106.5 468.5 %copy-start.14 = (bf16[1,256,1024]{2,1,0:T(8,128)(2,1)}, bf16[1,256,1024]{2,1,0:T(8,128)(2,1)S(1)}, u32[]{:S(2)}) copy-start(bf16[1,256,1024]{2,1,0:T(8,128)(2,1)S(1)} %all-gather.1) | copy-start | bytes 1572868
  132.9 96.7 %copy-start.165 = (f32[1,1024]{1,0:T(1,128)S(1)}, f32[1,1024]{1,0:T(1,128)}, u32[]{:S(2)}) copy-start(f32[1,1024]{1,0:T(1,128)} %param.25) | copy-start | bytes 12292
  132.9 79.0 %all-gather.49.cloned.1.call-start = ((), (), s32[]{:S(2)}) async-start(), calls=%async_computation.48 | async-start | bytes 2621440 | tf_op jit(solution)/shard_map/all_gather | solution.py:349
  133.5 96.1 %all-gather.25.cloned.1.call-start = ((), (), s32[]{:S(2)}) async-start(), calls=%async_computation.20 | async-start | bytes 1310720 | tf_op jit(solution)/shard_map/all_gather | solution.py:67
  165.7 362.0 %copy-start.4 = (f32[512,256]{1,0:T(8,128)}, f32[512,256]{1,0:T(8,128)S(1)}, u32[]{:S(2)}) copy-start(f32[512,256]{1,0:T(8,128)S(1)} %get-tuple-element.315) | copy-start | bytes 1572868
  171.5 224.3 %copy-start.105 = (f32[512]{0:T(512)}, f32[512]{0:T(512)S(1)}, u32[]{:S(2)}) copy-start(f32[512]{0:T(512)S(1)} %get-tuple-element.279) | copy-start | bytes 6148
  171.5 224.3 %copy-start.107 = (f32[512]{0:T(512)}, f32[512]{0:T(512)S(1)}, u32[]{:S(2)}) copy-start(f32[512]{0:T(512)S(1)} %get-tuple-element.280) | copy-start | bytes 6148
  172.4 105.0 %all-gather.51.cloned.1.call-start = ((), (), s32[]{:S(2)}) async-start(), calls=%async_computation.49 | async-start | bytes 2621440 | tf_op jit(solution)/shard_map/all_gather | solution.py:350
  173.2 138.3 %reduce-scatter.20.cloned.1.call-start = ((), (), s32[]{:S(2)}) async-start(), calls=%async_computation.21 | async-start | bytes 2621440 | tf_op jit(solution)/shard_map/reduce_scatter | solution.py:71
  281.6 65.1 %all-gather.27.cloned.1.call-start = ((), (), s32[]{:S(2)}) async-start(), calls=%async_computation.22 | async-start | bytes 1310720 | tf_op jit(solution)/shard_map/all_gather | solution.py:67
  312.6 8.9 collective-permute-start
  328.7 60.0 %reduce-scatter.22.cloned.1.call-start = ((), (), s32[]{:S(2)}) async-start(), calls=%async_computation.23 | async-start | bytes 2621440 | tf_op jit(solution)/shard_map/reduce_scatter | solution.py:71
  349.7 227.9 %copy-start.16 = (bf16[512,1,256]{0,2,1:T(8,128)(2,1)}, bf16[512,1,256]{0,2,1:T(8,128)(2,1)S(1)}, u32[]{:S(2)}) copy-start(bf16[512,1,256]{0,2,1:T(8,128)(2,1)S(1)} %slice.233) | copy-start | bytes 786436
  349.9 227.7 %copy-start.18 = (bf16[512,4,64]{0,2,1:T(8,128)(2,1)}, bf16[512,4,64]{0,2,1:T(8,128)(2,1)S(1)}, u32[]{:S(2)}) copy-start(bf16[512,4,64]{0,2,1:T(8,128)(2,1)S(1)} %add_convert_fusion.4) | copy-start | bytes 786436
  357.1 58.2 %all-gather.29.cloned.1.call-start = ((), (), s32[]{:S(2)}) async-start(), calls=%async_computation.24 | async-start | bytes 1310720 | tf_op jit(solution)/shard_map/all_gather | solution.py:67
  397.3 58.3 %reduce-scatter.24.cloned.1.call-start = ((), (), s32[]{:S(2)}) async-start(), calls=%async_computation.25 | async-start | bytes 2621440 | tf_op jit(solution)/shard_map/reduce_scatter | solution.py:71
  424.0 61.9 %all-gather.35.cloned.1.call-start = ((), (), s32[]{:S(2)}) async-start(), calls=%async_computation.30 | async-start | bytes 1310720 | tf_op jit(solution)/shard_map/all_gather | solution.py:75
  457.5 8.9 collective-permute-start.1
  467.9 59.8 %reduce-scatter.30.cloned.1.call-start = ((), (), s32[]{:S(2)}) async-start(), calls=%async_computation.31 | async-start | bytes 2621440 | tf_op jit(solution)/shard_map/reduce_scatter | solution.py:79
  496.1 60.0 %all-gather.31.cloned.1.call-start = ((), (), s32[]{:S(2)}) async-start(), calls=%async_computation.26 | async-start | bytes 1310720 | tf_op jit(solution)/shard_map/all_gather | solution.py:67
  538.0 37.1 %all-gather.37.cloned.1.call-start = ((), (), s32[]{:S(2)}) async-start(), calls=%async_computation.32 | async-start | bytes 1310720 | tf_op jit(solution)/shard_map/all_gather | solution.py:75
  542.4 66.6 %reduce-scatter.26.cloned.1.call-start = ((), (), s32[]{:S(2)}) async-start(), calls=%async_computation.27 | async-start | bytes 2621440 | tf_op jit(solution)/shard_map/reduce_scatter | solution.py:71
  566.5 76.4 %reduce-scatter.32.cloned.1.call-start = ((), (), s32[]{:S(2)}) async-start(), calls=%async_computation.33 | async-start | bytes 2621440 | tf_op jit(solution)/shard_map/reduce_scatter | solution.py:79
  598.8 71.2 %all-gather.33.cloned.1.call-start = ((), (), s32[]{:S(2)}) async-start(), calls=%async_computation.28 | async-start | bytes 1310720 | tf_op jit(solution)/shard_map/all_gather | solution.py:67
  610.3 277.5 %copy-start.6 = (f32[512,256]{1,0:T(8,128)}, f32[512,256]{1,0:T(8,128)S(1)}, u32[]{:S(2)}) copy-start(f32[512,256]{1,0:T(8,128)S(1)} %get-tuple-element.310) | copy-start | bytes 1572868
  651.9 37.0 %all-gather.39.cloned.1.call-start = ((), (), s32[]{:S(2)}) async-start(), calls=%async_computation.34 | async-start | bytes 1310720 | tf_op jit(solution)/shard_map/all_gather | solution.py:75
  653.4 9.9 collective-permute-start.2
  664.1 66.5 %reduce-scatter.34.cloned.1.call-start = ((), (), s32[]{:S(2)}) async-start(), calls=%async_computation.35 | async-start | bytes 2621440 | tf_op jit(solution)/shard_map/reduce_scatter | solution.py:79
  699.0 60.1 %all-gather.41.cloned.1.call-start = ((), (), s32[]{:S(2)}) async-start(), calls=%async_computation.36 | async-start | bytes 1310720 | tf_op jit(solution)/shard_map/all_gather | solution.py:75
  741.1 67.7 %reduce-scatter.36.cloned.1.call-start = ((), (), s32[]{:S(2)}) async-start(), calls=%async_computation.37 | async-start | bytes 2621440 | tf_op jit(solution)/shard_map/reduce_scatter | solution.py:79
  777.1 68.9 %all-gather.43.cloned.1.call-start = ((), (), s32[]{:S(2)}) async-start(), calls=%async_computation.38 | async-start | bytes 1310720 | tf_op jit(solution)/shard_map/all_gather | solution.py:75
  819.2 9.9 collective-permute-start.3
  829.9 57.8 %reduce-scatter.38.cloned.1.call-start = ((), (), s32[]{:S(2)}) async-start(), calls=%async_computation.39 | async-start | bytes 2621440 | tf_op jit(solution)/shard_map/reduce_scatter | solution.py:79
  856.1 60.3 %all-gather.45.cloned.1.call-start = ((), (), s32[]{:S(2)}) async-start(), calls=%async_computation.40 | async-start | bytes 1310720 | tf_op jit(solution)/shard_map/all_gather | solution.py:75
  898.3 51.9 %reduce-scatter.28.cloned.1.call-start = ((), (), s32[]{:S(2)}) async-start(), calls=%async_computation.29 | async-start | bytes 2621440 | tf_op jit(solution)/shard_map/reduce_scatter | solution.py:71
  902.6 81.8 %reduce-scatter.40.cloned.1.call-start = ((), (), s32[]{:S(2)}) async-start(), calls=%async_computation.41 | async-start | bytes 2621440 | tf_op jit(solution)/shard_map/reduce_scatter | solution.py:79
  938.2 259.2 %reduce-scatter.42.cloned.1.call-start = ((), (), s32[]{:S(2)}) async-start(), calls=%async_computation.42 | async-start | bytes 10485760 | tf_op jit(solution)/shard_map/reduce_scatter | solution.py:443
  1051.1 176.9 %reduce-scatter.46.cloned.1.call-start = ((), (), s32[]{:S(2)}) async-start(), calls=%async_computation.44 | async-start | bytes 1310720 | tf_op jit(solution)/shard_map/reduce_scatter | solution.py:455
  1055.4 251.0 %reduce-scatter.48.cloned.1.call-start = ((), (), s32[]{:S(2)}) async-start(), calls=%async_computation.45 | async-start | bytes 5242880 | tf_op jit(solution)/shard_map/reduce_scatter | solution.py:456
  1063.4 323.2 %reduce-scatter.50.cloned.1.call-start = ((), (), s32[]{:S(2)}) async-start(), calls=%async_computation.46 | async-start | bytes 5242880 | tf_op jit(solution)/shard_map/reduce_scatter | solution.py:457
  1072.6 377.7 %reduce-scatter.44.cloned.1.call-start = ((), (), s32[]{:S(2)}) async-start(), calls=%async_computation.43 | async-start | bytes 3932160 | tf_op jit(solution)/shard_map/reduce_scatter | solution.py:454
  (157 other events, 1931.9 us)
Sparse Core Ops, SparseCore 0:
  10.2 48.6 all-gather.20
  61.0 44.6 all-gather.46
  107.9 15.0 all-gather.22
  133.0 31.4 reduce-scatter.17
  165.9 45.9 all-gather.48
  213.9 15.5 all-gather.24
  231.2 46.2 all-gather.50
  281.8 29.6 reduce-scatter.19
  328.9 17.8 all-gather.26
  357.2 31.4 reduce-scatter.21
  397.4 17.9 all-gather.28
  424.1 31.4 reduce-scatter.23
  468.0 17.8 all-gather.34
  496.2 31.4 reduce-scatter.29
  538.1 17.9 all-gather.30
  558.1 16.8 all-gather.36
  577.6 31.4 reduce-scatter.25
  611.4 31.4 reduce-scatter.31
  652.0 17.9 all-gather.32
  672.1 16.8 all-gather.38
  699.2 31.4 reduce-scatter.33
  741.2 17.9 all-gather.40
  777.3 31.4 reduce-scatter.35
  830.0 15.9 all-gather.42
  856.3 31.4 reduce-scatter.37
  898.4 17.9 all-gather.44
  918.8 31.4 reduce-scatter.27
  952.9 31.4 reduce-scatter.39
  1051.3 146.0 reduce-scatter.41
  1200.1 27.8 reduce-scatter.45
  1231.0 75.4 reduce-scatter.47
  1309.3 77.2 reduce-scatter.49
  1389.4 60.7 reduce-scatter.43
where the time goes:
time: 1470 us; the launch traced here: 1460 us
  waiting for transfers between devices  1010 us (69%)
  matrix products  136 us (9%)
  local copies, waits for them, and re-layouts  103 us (7%)
  blocking collectives  99.9 us (7%)
  other arithmetic  83.7 us (6%)
  between operations  16.9 us (1%)
    reduce_scatter x6, waiting for transfers between devices, reduce_grads(): lax.psum_scatter(partial_value, 'col', scatter_dimension=1, tiled=True)  190 us
    reduce_scatter x6, waiting for transfers between devices, sum_columns(): lax.psum_scatter(partial_value, 'col', scatter_dimension=1, tiled=True)  144 us
    reduce_scatter x1, waiting for transfers between devices, on_device(): lax.psum_scatter(jnp.transpose(jnp.where(mine[:, :, None], picked, 0.0),...  95.9 us
    all_gather x6, waiting for transfers between devices, spread_features(): return lax.all_gather(values, 'col', axis=1, tiled=True)  85.9 us
    all_gather x6, waiting for transfers between devices, spread_grads(): return lax.all_gather(values, 'col', axis=1, tiled=True)  81.9 us
    reduce_scatter x1, waiting for transfers between devices, on_device(): lax.psum_scatter(weight_totals[3], 'row', scatter_dimension=1, tiled=True)  80.2 us
    reduce_scatter x1, waiting for transfers between devices, on_device(): lax.psum_scatter(weight_totals[2], 'row', scatter_dimension=0, tiled=True)  78.4 us
    reduce_scatter x1, waiting for transfers between devices, on_device(): lax.psum_scatter(weight_totals[0], 'row', scatter_dimension=0, tiled=True)  63.6 us
  transfers between devices with their start and end apart: 37, of which 36 were waited for; matrix products, arithmetic and copies ran while one was open for 9% of the time, Pallas kernels for 0%

commit v1 on v0

v1 whole, which is shorter than its diff:
```python
import jax
import jax.numpy as jnp
from jax import lax
from jax.sharding import PartitionSpec as P

HEAD_DIM = 64
epsilon = 1e-05
masked_score = -1e30
F32 = jnp.float32
BF16 = jnp.bfloat16


def mm(a, b, dims):
    return lax.dot_general(a, b, ((dims[0], dims[1]), ((), ())), preferred_element_type=F32)


def nn(a, b):
    return mm(a, b, ((1,), (0,)))


def nt(a, b):
    return mm(a, b, ((1,), (1,)))


def tn(a, b):
    return mm(a, b, ((0,), (0,)))


def swap_bit(array, axis, bit):
    count = lax.axis_size(axis)
    return lax.ppermute(array, axis, [(i, i ^ bit) for i in range(count)])


def spread_tokens(own):
    count = lax.axis_size("col")
    blocks = {0: own}
    bit = count // 2
    while bit >= 1:
        held = sorted(blocks)
        sent = swap_bit(jnp.concatenate([blocks[b] for b in held], axis=0), "col", bit)
        size = own.shape[0]
        for place, b in enumerate(held):
            blocks[b ^ bit] = sent[place * size : (place + 1) * size]
        bit //= 2
    return jnp.concatenate([blocks[b] for b in range(count)], axis=0)


def sum_tokens(partial):
    count = lax.axis_size("col")
    size = partial.shape[0] // count
    blocks = {b: partial[b * size : (b + 1) * size] for b in range(count)}
    bit = 1
    while bit < count:
        far = [b for b in sorted(blocks) if b & bit]
        sent = swap_bit(
            jnp.concatenate([blocks[b].astype(BF16) for b in far], axis=0), "col", bit
        )
        for place, b in enumerate(far):
            blocks[b ^ bit] = blocks[b ^ bit] + sent[place * size : (place + 1) * size].astype(F32)
            del blocks[b]
        bit *= 2
    return blocks[0]


def owned_layout(lengths, deal, holder, rows_dev):
    starts = jnp.cumsum(lengths) - lengths
    first = deal == 2 * holder
    second = deal == 2 * holder + 1
    first_len = jnp.sum(jnp.where(first, lengths, 0))
    second_len = jnp.sum(jnp.where(second, lengths, 0))
    first_start = jnp.sum(jnp.where(first, starts, 0))
    second_start = jnp.sum(jnp.where(second, starts, 0))
    slots = jnp.arange(rows_dev, dtype=jnp.int32)
    in_first = slots < first_len
    in_second = jnp.logical_and(jnp.logical_not(in_first), slots < first_len + second_len)
    usable = jnp.logical_or(in_first, in_second)
    position = jnp.where(in_first, slots, slots - first_len)
    source = jnp.where(in_first, first_start + slots, second_start + position)
    source = jnp.where(usable, source, -1)
    segment = jnp.where(in_first, 0, jnp.where(in_second, 1, 2)).astype(jnp.int32)
    return source, usable, segment, position


def given_targets(lengths, deal, positions, rows_dev):
    starts = jnp.cumsum(lengths) - lengths
    before = deal[None, :] == (deal - 1)[:, None]
    partner_len = jnp.sum(jnp.where(before, lengths[None, :], 0), axis=1)
    offset = jnp.where(deal % 2 == 1, partner_len, 0)
    base = deal // 2 * rows_dev + offset - starts
    inside = jnp.logical_and(
        positions[:, None] >= starts[None, :], positions[:, None] < (starts + lengths)[None, :]
    )
    target = jnp.sum(jnp.where(inside, base[None, :] + positions[:, None], 0), axis=1)
    return jnp.where(jnp.any(inside, axis=1), target, -1)


def pick_rows(rows, wanted):
    onehot = (wanted[:, None] == jnp.arange(rows.shape[0], dtype=jnp.int32)[None, :]).astype(BF16)
    return nn(onehot, rows)


def normalize(hidden, gain, shift):
    average = jnp.mean(hidden, axis=1, keepdims=True)
    square = jnp.mean(hidden * hidden, axis=1, keepdims=True)
    inverse = lax.rsqrt(square - average * average + epsilon)
    centered = (hidden - average) * inverse
    return centered, inverse, (centered * gain + shift).astype(BF16)


def norm_backward(grad_norm, centered, inverse, gain):
    grad_cent = grad_norm * gain
    summed = jnp.mean(grad_cent, axis=1, keepdims=True)
    cross = jnp.mean(grad_cent * centered, axis=1, keepdims=True)
    grad_hidden = inverse * (grad_cent - summed - centered * cross)
    return grad_hidden, jnp.sum(grad_norm * centered, axis=0), jnp.sum(grad_norm, axis=0)


def gelu_tanh(values):
    return jax.nn.gelu(values, approximate=True)


def masked_scores(queries, key_rows, segment, position, slopes):
    scores = jnp.einsum(
        "qhe,khe->hqk", queries, key_rows, preferred_element_type=F32
    ) * HEAD_DIM ** (-0.5)
    distance = (position[:, None] - position[None, :]).astype(F32)
    allowed = jnp.logical_and(
        segment[:, None] == segment[None, :],
        jnp.logical_and(segment[:, None] < 2, distance >= 0),
    )
    scores = scores - slopes[:, None, None] * distance[None]
    return jnp.where(allowed[None], scores, masked_score)


def attend_forward(queries, key_rows, value_rows, segment, position, slopes):
    rows = queries.shape[0]
    scores = masked_scores(queries, key_rows, segment, position, slopes)
    highest = jnp.max(scores, axis=2, keepdims=True)
    exp_scores = jnp.exp(scores - highest)
    summed = jnp.sum(exp_scores, axis=2, keepdims=True)
    soft = (exp_scores / summed).astype(BF16)
    mixed = jnp.einsum("hqk,khe->qhe", soft, value_rows, preferred_element_type=F32)
    return mixed.reshape(rows, -1).astype(BF16), highest + jnp.log(summed)


def attend_backward(queries, key_rows, value_rows, segment, position, slopes, logsum, grad_mixed):
    scale = HEAD_DIM ** (-0.5)
    rows = queries.shape[0]
    scores = masked_scores(queries, key_rows, segment, position, slopes)
    soft = jnp.exp(scores - logsum)
    grad_prob = jnp.einsum("qhe,khe->hqk", grad_mixed, value_rows, preferred_element_type=F32)
    row_dot = jnp.sum(soft * grad_prob, axis=2, keepdims=True)
    grad_score = (soft * (grad_prob - row_dot)).astype(BF16)
    grad_query = (
        jnp.einsum("hqk,khe->qhe", grad_score, key_rows, preferred_element_type=F32) * scale
    )
    grad_key = jnp.einsum("hqk,qhe->khe", grad_score, queries, preferred_element_type=F32) * scale
    grad_value = jnp.einsum(
        "hqk,qhe->khe", soft.astype(BF16), grad_mixed, preferred_element_type=F32
    )
    return jnp.concatenate(
        [g.astype(BF16).reshape(rows, -1) for g in (grad_query, grad_key, grad_value)], axis=1
    )


def times_rows(left, weight):
    half = weight[0].shape[0]
    return nn(left[:, :half], weight[0]) + nn(left[:, half:], weight[1])


def times_rows_back(left, weight):
    return jnp.concatenate([nt(left, weight[0]), nt(left, weight[1])], axis=1)


def layer_forward(hidden, layout, weights, small):
    usable, segment, position, slopes = layout
    attn_w, up_w, down_w = weights
    width = attn_w[0].shape[1] // 4
    gain, shift, bias_q, bias_v, bias_out, bias_down, up_bias = small
    centered, inverse, normed = normalize(hidden, gain[0], shift[0])
    rows_all = spread_tokens(normed)
    rows = rows_all.shape[0]
    qkv_w = [w[:, : 3 * width] for w in attn_w]
    out_w = [w[:, 3 * width :] for w in attn_w]
    qkv = times_rows(rows_all, qkv_w)
    queries = (qkv[:, :width] + bias_q).astype(BF16).reshape(rows, -1, HEAD_DIM)
    key_rows = qkv[:, width : 2 * width].astype(BF16).reshape(rows, -1, HEAD_DIM)
    value_rows = (qkv[:, 2 * width :] + bias_v).astype(BF16).reshape(rows, -1, HEAD_DIM)
    attended, logsum = attend_forward(queries, key_rows, value_rows, segment, position, slopes)
    branch = sum_tokens(times_rows_back(attended, out_w)) + bias_out
    middle = hidden + branch
    centered_two, inverse_two, normed_two = normalize(middle, gain[1], shift[1])
    rows_two = spread_tokens(normed_two)
    upper_in = times_rows(rows_two, up_w) + up_bias
    activated = gelu_tanh(upper_in).astype(BF16)
    down_out = sum_tokens(times_rows_back(activated, down_w)) + bias_down
    result = jnp.where(usable[:, None], middle + down_out, 0.0)
    stored = (
        centered,
        inverse,
        rows_all,
        queries,
        key_rows,
        value_rows,
        logsum,
        attended,
        centered_two,
        inverse_two,
        rows_two,
        upper_in,
        activated,
    )
    return result, stored


def layer_backward(grad_out, layout, weights, small, stored):
    usable, segment, position, slopes = layout
    attn_w, up_w, down_w = weights
    width = attn_w[0].shape[1] // 4
    gain = small[0]
    (
        centered,
        inverse,
        rows_all,
        queries,
        key_rows,
        value_rows,
        logsum,
        attended,
        centered_two,
        inverse_two,
        rows_two,
        upper_in,
        activated,
    ) = stored
    qkv_w = [w[:, : 3 * width] for w in attn_w]
    out_w = [w[:, 3 * width :] for w in attn_w]
    grad_down = grad_out.astype(BF16)
    down_all = spread_tokens(grad_down)
    grad_act = times_rows(down_all, down_w)
    grad_upper = jax.vjp(gelu_tanh, upper_in)[1](grad_act)[0].astype(BF16)
    grad_norm_two = sum_tokens(times_rows_back(grad_upper, up_w))
    down_term = tn(down_all, activated).astype(BF16)
    up_term = tn(rows_two, grad_upper).astype(BF16)
    grad_mid, gain_two, shift_two = norm_backward(
        grad_norm_two, centered_two, inverse_two, gain[1]
    )
    grad_mid = grad_out + grad_mid
    grad_branch = grad_mid.astype(BF16)
    branch_all = spread_tokens(grad_branch)
    grad_attended = times_rows(branch_all, out_w).astype(BF16).reshape(queries.shape)
    grad_qkv = attend_backward(
        queries, key_rows, value_rows, segment, position, slopes, logsum, grad_attended
    )
    grad_norm = sum_tokens(times_rows_back(grad_qkv, qkv_w))
    attn_term = jnp.concatenate(
        [tn(rows_all, grad_qkv).astype(BF16), tn(branch_all, attended).astype(BF16)], axis=1
    )
    grad_in, gain_one, shift_one = norm_backward(grad_norm, centered, inverse, gain[0])
    grad_input = grad_mid + grad_in
    token_sums = jnp.stack(
        [
            gain_one,
            gain_two,
            shift_one,
            shift_two,
            jnp.sum(grad_branch, axis=0, dtype=F32),
            jnp.sum(grad_down, axis=0, dtype=F32),
        ]
    )
    qkv_sums = jnp.sum(grad_qkv, axis=0, dtype=F32)
    column_sums = jnp.concatenate(
        [qkv_sums[:width], qkv_sums[2 * width :], jnp.sum(grad_upper, axis=0, dtype=F32)]
    )
    return grad_input, (attn_term, up_term, down_term), token_sums, column_sums


def on_device(
    inputs,
    cotangent,
    lengths,
    deal,
    query_key_value_weight,
    out_weight,
    up_weight,
    down_weight,
    norm_gain,
    norm_shift,
    proj_bias,
    up_bias,
):
    section = lax.axis_index("section")
    holder = lax.axis_index("row")
    column = lax.axis_index("col")
    rows_count, cols_count = lax.axis_size("row"), lax.axis_size("col")
    micro_count, rows_dev, width = inputs.shape
    model = width * cols_count
    heads_dev = width // HEAD_DIM
    heads = heads_dev * cols_count
    tokens = rows_dev // cols_count
    block = model // rows_count
    half = block // 2
    is_zero = section == 0

    def pick(zero, one):
        return jnp.where(is_zero, zero, one)

    def own_first(array, axis):
        shape = array.shape
        split = array.reshape(shape[:axis] + (rows_count, 2, half) + shape[axis + 1 :])
        parts = [lax.index_in_dim(split, i, axis + 1, keepdims=False) for i in (0, 1)]
        flat = [p.reshape(shape[:axis] + (model // 2,) + shape[axis + 1 :]) for p in parts]
        return jnp.concatenate([pick(flat[0], flat[1]), pick(flat[1], flat[0])], axis=axis)

    def true_order(array, axis):
        shape = array.shape
        mine = lax.slice_in_dim(array, 0, model // 2, axis=axis)
        other = lax.slice_in_dim(array, model // 2, model, axis=axis)
        parts = [
            p.reshape(shape[:axis] + (rows_count, 1, half) + shape[axis + 1 :])
            for p in (pick(mine, other), pick(other, mine))
        ]
        return jnp.concatenate(parts, axis=axis + 1).reshape(shape)

    packed = (
        jnp.concatenate(
            [query_key_value_weight[0].reshape(block, 3 * width), out_weight[0].T], axis=1
        ),
        up_weight[0],
        down_weight[0].T,
    )
    kept = [pick(w[:half], w[half:]) for w in packed]
    given = [swap_bit(pick(w[half:], w[:half]), "section", 1) for w in packed]
    halves = (
        [pick(k, g) for k, g in zip(kept, given)],
        [pick(g, k) for k, g in zip(kept, given)],
    )

    def gather_weight(piece):
        mine = lax.all_gather(piece, "row", axis=0, tiled=True)
        return (mine, swap_bit(mine, "section", 1))

    mine_small = jnp.concatenate(
        [norm_gain[0], norm_shift[0], proj_bias[0], up_bias[0].reshape(-1, width)], axis=0
    )
    all_small = lax.all_gather(mine_small, ("section", "col"), axis=0, tiled=False)
    all_small = all_small.reshape((2, cols_count) + mine_small.shape)

    def layer_small(layer):
        table = all_small[layer]
        whole = own_first(jnp.transpose(table[:, :8], (1, 0, 2)).reshape(8, model), 1)
        own = jnp.take(table, column, axis=0)
        return (
            whole[0:2],
            whole[2:4],
            own[4],
            own[5],
            whole[6],
            whole[7],
            own[8:].reshape(-1),
        )

    source, usable, segment, position = owned_layout(
        lengths[section], deal[section], holder, rows_dev
    )
    order = jnp.bitwise_xor(column, jnp.arange(cols_count, dtype=jnp.int32))

    def xor_order(values):
        return values.reshape(cols_count, tokens)[order].reshape(rows_dev)

    own_usable = usable.reshape(cols_count, tokens)[column]
    head_ids = column * heads_dev + jnp.arange(heads_dev, dtype=jnp.int32)
    slopes = jnp.exp2(-8.0 * (head_ids.astype(F32) + 1.0) / heads)
    layout = (own_usable, xor_order(segment), xor_order(position), slopes)

    def deal_rows(array):
        portion = lax.all_gather(pick(array[0], array[1]), "row", axis=0, tiled=True)
        owned = pick_rows(portion, source).astype(BF16)
        own = lax.all_to_all(
            owned.reshape(cols_count, tokens, width), "col", split_axis=0, concat_axis=0
        )
        return own_first(jnp.transpose(own, (1, 0, 2)).reshape(tokens, model), 1)

    weights = [[None] * 3, [None] * 3]
    first_rows = deal_rows(inputs)
    for layer in range(2):
        for kind in range(3):
            weights[layer][kind] = gather_weight(halves[layer][kind])
    smalls = [layer_small(0), layer_small(1)]

    hidden_zero, stored_zero = layer_forward(first_rows.astype(F32), layout, weights[0], smalls[0])
    middle_in = hidden_zero.astype(BF16)
    hidden_one, stored_one = layer_forward(
        middle_in.astype(F32), layout, weights[1], smalls[1]
    )
    last_out = hidden_one.astype(BF16)

    positions = holder * rows_dev + jnp.arange(rows_dev, dtype=jnp.int32)
    targets = jax.vmap(given_targets, (0, 0, None, None))(lengths, deal, positions, rows_dev)

    def give_back(zero, one):
        def by_features(own):
            parts = true_order(own, 1).reshape(tokens, cols_count, width)
            got = lax.all_to_all(
                jnp.transpose(parts, (1, 0, 2)), "col", split_axis=0, concat_axis=0
            )
            return got.reshape(rows_dev, width)

        stays = by_features(pick(zero, one))
        comes = swap_bit(by_features(pick(one, zero)), "section", 1)
        both = jnp.stack([pick(stays, comes), pick(comes, stays)])
        whole = lax.all_gather(both, "row", axis=1, tiled=True)
        return jnp.stack([pick_rows(whole[m], targets[m]) for m in range(micro_count)])

    hidden_out = give_back(middle_in, last_out).astype(BF16)

    grad_one = deal_rows(cotangent).astype(F32)
    grad_one_in, terms_one, token_one, column_one = layer_backward(
        grad_one, layout, weights[1], smalls[1], stored_one
    )
    grad_zero = grad_one_in.astype(BF16)
    grad_zero = jnp.where(own_usable[:, None], grad_zero, jnp.zeros_like(grad_zero)).astype(F32)
    grad_zero_in, terms_zero, token_zero, column_zero = layer_backward(
        grad_zero, layout, weights[0], smalls[0], stored_zero
    )

    def reduce_weight(term):
        mine, other = term[: model // 2], term[model // 2 :]
        total = (mine.astype(F32) + swap_bit(other, "section", 1).astype(F32)).astype(BF16)
        return lax.psum_scatter(total, "row", scatter_dimension=0, tiled=True)

    sums_one = [reduce_weight(t) for t in terms_one]
    sums_zero = [reduce_weight(t) for t in terms_zero]
    finals = []
    for zero, one in zip(sums_zero, sums_one):
        mine = pick(zero, one)
        other = swap_bit(pick(one, zero), "section", 1)
        finals.append(
            jnp.concatenate([pick(mine, other), pick(other, mine)], axis=0).astype(F32)
        )
    qkv_grad = finals[0][:, : 3 * width].reshape(block, 3, width)
    out_grad = finals[0][:, 3 * width :].T
    up_grad = finals[1]
    down_grad = finals[2].T

    in_grad = give_back(grad_zero_in.astype(BF16), grad_one_in.astype(BF16))

    token_sums = jnp.stack([true_order(token_zero, 1), true_order(token_one, 1)])
    token_sums = lax.psum(token_sums, ("section", "row", "col"))
    column_sums = lax.psum(jnp.stack([column_zero, column_one]), ("section", "row"))
    token_sums = lax.dynamic_slice_in_dim(
        pick(token_sums[0], token_sums[1]), column * width, width, axis=1
    )
    column_sums = pick(column_sums[0], column_sums[1])
    bias_grad = jnp.concatenate(
        [column_sums[: 2 * width].reshape(2, width), token_sums[4:6]], axis=0
    )
    return (
        hidden_out[None],
        in_grad[None],
        qkv_grad[None],
        out_grad[None],
        up_grad[None],
        down_grad[None],
        token_sums[0:2][None],
        token_sums[2:4][None],
        bias_grad[None],
        column_sums[2 * width :][None],
    )


def solution(mesh):
    placed = (
        P(None, "row", "col"),
        P(None, "row", "col"),
        P(),
        P(),
        P("section", "row", None, "col"),
        P("section", "col", "row"),
        P("section", "row", "col"),
        P("section", "col", "row"),
        P("section", None, "col"),
        P("section", None, "col"),
        P("section", None, "col"),
        P("section", "col"),
    )
    return jax.shard_map(
        on_device,
        mesh=mesh,
        in_specs=placed,
        out_specs=(
            P("section", None, "row", "col"),
            P("section", None, "row", "col"),
            P("section", "row", None, "col"),
            P("section", "col", "row"),
            P("section", "row", "col"),
            P("section", "col", "row"),
            P("section", None, "col"),
            P("section", None, "col"),
            P("section", None, "col"),
            P("section", "col"),
        ),
        check_vma=False,
    )
```

time: 1470 us -> 683 us (0.46)
  waiting for transfers between devices: 1010 us -> 273 us
  matrix products: 136 us -> 68.9 us
  starting transfers between devices: 12.9 us -> 74.6 us
  local copies, waits for them, and re-layouts: 103 us -> 53.2 us
    reduce_scatter x17 -> x0, waiting for transfers between devices: 679 us -> none  [the longest x6 190 us: reduce_grads(): lax.psum_scatter(partial_value, 'col', scatter_dimension=1, tiled=True)]
    all_gather x16 -> x10, waiting for transfers between devices: 296 us -> 69.4 us  [the longest x6 53.1 us: gather_weight(): mine = lax.all_gather(piece, 'row', axis=0, tiled=True)]
    ppermute x4 -> x52, waiting for transfers between devices: 28.2 us -> 187 us  [swap_bit(): return lax.ppermute(array, axis, [(i, i ^ bit) for i in range(count)])]
    gather x2, local copies, waits for them, and re-layouts: 68.8 us -> 1.12 us  [xor_order(): return values.reshape(cols_count, tokens)[order].reshape(rows_dev)]
    dot_general x57 -> x58, matrix products: 136 us -> 68.9 us  [the longest x46 57.7 us: mm(): lax.dot_general(a, b, ((dims[0], dims[1]), ((), ())), preferred_element_t...]
    ppermute x4 -> x52, starting transfers between devices: 9.36 us -> 50.7 us  [swap_bit(): return lax.ppermute(array, axis, [(i, i ^ bit) for i in range(count)])]
    all_to_all x0 -> x6, starting transfers between devices: none -> 21.7 us  [the longest x4 14.3 us: by_features(): lax.all_to_all(jnp.transpose(parts, (1, 0, 2)), 'col', split_axis=0, conc...]
    unnamed x339 -> x456, local copies, waits for them, and re-layouts: 17.9 us -> 35.1 us
  transfers between devices with their start and end apart: 37 -> 74, of which waited for: 36 -> 35; matrix products, arithmetic and copies ran while one was open for 9% -> 28% of each run, Pallas kernels for 0% -> 0%
where the time goes in v1:
time: 683 us; the launch traced here: 672 us
  waiting for transfers between devices  273 us (40%)
  other arithmetic  94.3 us (14%)
  blocking collectives  88.7 us (13%)
  starting transfers between devices  74.6 us (11%)
  matrix products  68.9 us (10%)
  local copies, waits for them, and re-layouts  53.2 us (8%)
  between operations  19.2 us (3%)
    ppermute x52, waiting for transfers between devices, swap_bit(): return lax.ppermute(array, axis, [(i, i ^ bit) for i in range(count)])  187 us
    dot_general x46, matrix products, mm(): lax.dot_general(a, b, ((dims[0], dims[1]), ((), ())), preferred_element_t...  57.7 us
    all_gather x6, waiting for transfers between devices, gather_weight(): mine = lax.all_gather(piece, 'row', axis=0, tiled=True)  53.1 us
    ppermute x52, starting transfers between devices, swap_bit(): return lax.ppermute(array, axis, [(i, i ^ bit) for i in range(count)])  50.7 us
    psum x1, blocking collectives, on_device(): token_sums = lax.psum(token_sums, ('section', 'row', 'col'))  41.7 us
    unnamed x456, local copies, waits for them, and re-layouts  35.1 us
    psum x1, blocking collectives, on_device(): lax.psum(jnp.stack([column_zero, column_one]), ('section', 'row'))  34.6 us
    all_gather x2, waiting for transfers between devices, deal_rows(): lax.all_gather(pick(array[0], array[1]), 'row', axis=0, tiled=True)  16.3 us
  transfers between devices with their start and end apart: 74, of which 35 were waited for; matrix products, arithmetic and copies ran while one was open for 28% of the time, Pallas kernels for 0%

profile of v1, /device:TPU:0, one launch (start us, length us, event | category | flops | bytes accessed | tf_op | source)
XLA Modules:
  0.0 671.7 jit_solution(1293539286095416655)
XLA Ops:
  9.5 3.0 collective-permute-start.2
  16.8 12.3 %all-gather.3 = f32[8,12,256]{2,1,0:T(8,128)S(1)} all-gather(f32[1,12,256]{2,1,0:T(8,128)S(1)} %maximum_bitcast_fusion.1), channel_id=3, replica_groups=mesh['section'=2,'row'=4,'col'=4] {'section','col'}, dimensions={0}, use_global_device_ids=true | all-gather | bytes 110592 | tf_op jit(solution)/shard_map/all_gather | solution.py:346
  37.3 5.3 all-gather.31.cloned.1.call-done
  42.7 2.8 fusion.51
  45.5 3.4 all-to-all-start
  49.0 5.9 all-to-all-done
  57.8 16.8 %all-gather.15.cloned.1.call-done = bf16[512,1024]{0,1:T(8,128)(2,1)} async-done(((bf16[128,1024]{0,1:T(8,128)(2,1)}), bf16[512,1024]{0,1:T(8,128)(2,1)}) %all-gather.15.cloned.1.call-update) | async-done | bytes 1048592 | tf_op jit(solution)/shard_map/all_gather | solution.py:340
  78.4 20.1 %collective-permute-done.3 = bf16[512,1024]{0,1:T(8,128)(2,1)S(1)} collective-permute-done((bf16[512,1024]{0,1:T(8,128)(2,1)}, bf16[512,1024]{0,1:T(8,128)(2,1)S(1)}, u32[]{:S(2)}, u32[]{:S(2)}) %collective-permute-start.3) | collective-permute-done | bytes 1048608 | tf_op jit(solution)/shard_map/ppermute | solution.py:31
  112.5 4.7 collective-permute-done.10
  124.4 3.9 collective-permute-done.6
  128.7 18.9 %all-gather.19.cloned.1.call-done = bf16[512,1024]{0,1:T(8,128)(2,1)} async-done(((bf16[128,1024]{0,1:T(8,128)(2,1)}), bf16[512,1024]{0,1:T(8,128)(2,1)}) %all-gather.19.cloned.1.call-update) | async-done | bytes 1048592 | tf_op jit(solution)/shard_map/all_gather | solution.py:340
  149.9 2.7 multiply_convert_fusion.3
  153.3 18.3 %collective-permute-done.11 = bf16[512,1024]{0,1:T(8,128)(2,1)S(1)} collective-permute-done((bf16[512,1024]{0,1:T(8,128)(2,1)}, bf16[512,1024]{0,1:T(8,128)(2,1)S(1)}, u32[]{:S(2)}, u32[]{:S(2)}) %collective-permute-start.11) | collective-permute-done | bytes 1048608 | tf_op jit(solution)/shard_map/ppermute | solution.py:31
  180.8 4.4 collective-permute-done.13
  189.6 4.3 collective-permute-done.14
  195.4 11.0 %all-gather.33.cloned.1.call-done = bf16[1,2048,256]{2,1,0:T(8,128)(2,1)} async-done(((bf16[1,512,256]{2,1,0:T(8,128)(2,1)}), bf16[1,2048,256]{2,1,0:T(8,128)(2,1)}) %all-gather.33.cloned.1.call-update) | async-done | bytes 1048592 | tf_op jit(solution)/shard_map/all_gather | solution.py:377
  209.4 4.0 all-to-all-start.3
  240.3 4.2 collective-permute-done.18
  250.8 17.0 %all-gather.23.cloned.1.call-done = bf16[512,1024]{0,1:T(8,128)(2,1)} async-done(((bf16[128,1024]{0,1:T(8,128)(2,1)}), bf16[512,1024]{0,1:T(8,128)(2,1)}) %all-gather.23.cloned.1.call-update) | async-done | bytes 1048592 | tf_op jit(solution)/shard_map/all_gather | solution.py:340
  271.9 19.9 %collective-permute-done.21 = bf16[512,1024]{0,1:T(8,128)(2,1)S(1)} collective-permute-done((bf16[512,1024]{0,1:T(8,128)(2,1)}, bf16[512,1024]{0,1:T(8,128)(2,1)S(1)}, u32[]{:S(2)}, u32[]{:S(2)}) %collective-permute-start.21) | collective-permute-done | bytes 1048608 | tf_op jit(solution)/shard_map/ppermute | solution.py:31
  297.2 2.6 convert_reduce_fusion
  306.5 19.0 %collective-permute-done.47 = bf16[512,1024]{1,0:T(8,128)(2,1)S(1)} collective-permute-done((bf16[512,1024]{1,0:T(8,128)(2,1)S(1)}, bf16[512,1024]{1,0:T(8,128)(2,1)S(1)}, u32[]{:S(2)}, u32[]{:S(2)}) %collective-permute-start.47) | collective-permute-done | bytes 1048608 | tf_op jit(solution)/shard_map/ppermute | solution.py:31
  328.4 2.8 convolution_convert_fusion
  337.8 5.6 collective-permute-done.24
  346.1 10.9 %collective-permute-done.50 = bf16[512,1024]{1,0:T(8,128)(2,1)S(1)} collective-permute-done((bf16[512,1024]{1,0:T(8,128)(2,1)S(1)}, bf16[512,1024]{1,0:T(8,128)(2,1)S(1)}, u32[]{:S(2)}, u32[]{:S(2)}) %collective-permute-start.50) | collective-permute-done | bytes 1048608 | tf_op jit(solution)/shard_map/ppermute | solution.py:31
  360.1 4.1 all-to-all-start.2
  370.2 3.4 all-to-all-start.1
  379.8 3.8 collective-permute-done.25
  406.5 2.8 collective-permute-done.33
  415.2 6.2 collective-permute-done.34
  424.2 6.1 collective-permute-done.44
  430.4 2.6 add_convert_fusion.4
  438.7 2.6 convert_reduce_fusion.1
  447.1 20.2 %collective-permute-done.46 = bf16[512,1024]{1,0:T(8,128)(2,1)S(1)} collective-permute-done((bf16[512,1024]{1,0:T(8,128)(2,1)S(1)}, bf16[512,1024]{1,0:T(8,128)(2,1)S(1)}, u32[]{:S(2)}, u32[]{:S(2)}) %collective-permute-start.46) | collective-permute-done | bytes 1048608 | tf_op jit(solution)/shard_map/ppermute | solution.py:31
  485.2 2.3 multiply_reduce_fusion.3
  489.9 13.2 %collective-permute-done.49 = bf16[512,1024]{1,0:T(8,128)(2,1)} collective-permute-done((bf16[512,1024]{1,0:T(8,128)(2,1)}, bf16[512,1024]{1,0:T(8,128)(2,1)}, u32[]{:S(2)}, u32[]{:S(2)}) %collective-permute-start.49) | collective-permute-done | bytes 1048608 | tf_op jit(solution)/shard_map/ppermute | solution.py:31
  503.1 2.7 add_convert_fusion.1
  529.0 34.6 %psum.15 = f32[2,1536]{1,0:T(2,128)S(1)} all-reduce(f32[2,1536]{1,0:T(2,128)S(1)} %pad_maximum_fusion.49), channel_id=1, replica_groups=mesh['section'=2,'row'=4,'col'=4] {'section','row'}, use_global_device_ids=true, to_apply=%region_54.56 | all-reduce | flops 3072 | bytes 24576 | tf_op jit(solution)/shard_map/psum | solution.py:450
  570.3 3.4 all-to-all-start.5
  574.5 5.2 all-to-all-done.5
  579.7 3.4 all-to-all-start.4
  586.0 3.1 all-to-all-done.4
  589.3 2.9 collective-permute-done.42
  593.3 41.7 %psum.14 = f32[2,6,1024]{2,1,0:T(8,128)S(1)} all-reduce(f32[2,6,1024]{2,1,0:T(8,128)S(1)} %pad_maximum_fusion.46), channel_id=1, replica_groups=mesh['section'=2,'row'=4,'col'=4] {'section','row','col'}, use_global_device_ids=true, to_apply=%region_49.51 | all-reduce | flops 12288 | bytes 98304 | tf_op jit(solution)/shard_map/psum | solution.py:449
  636.8 2.3 collective-permute-start.48
  641.0 5.3 collective-permute-done.48
  646.4 4.1 collective-permute-done.51
  654.6 4.1 collective-permute-done.45
  (856 shorter events, 248.3 us)
Async XLA Ops:
  7.2 35.5 %all-gather.31.cloned.1.call-start = ((), (), s32[]{:S(2)}) async-start(), calls=%async_computation.20 | async-start | bytes 1310720 | tf_op jit(solution)/shard_map/all_gather | solution.py:377
  9.5 26.9 %collective-permute-start.2 = (bf16[128,1024]{0,1:T(8,128)(2,1)S(1)}, bf16[128,1024]{0,1:T(8,128)(2,1)S(1)}, u32[]{:S(2)}, u32[]{:S(2)}) collective-permute-start(bf16[128,1024]{0,1:T(8,128)(2,1)S(1)} %broadcast_select_fusion.22), channel_id=1, source_target_pairs={{0,16},{16,0},{1,17},{17,1},{2,18},{18,2},{3,19},{19,3},{4,20},{20... | collective-permute-start | bytes 786440 | tf_op jit(solution)/shard_map/ppermute | solution.py:31
  14.3 60.2 %all-gather.15.cloned.1.call-start = ((), (), s32[]{:S(2)}) async-start(), calls=%async_computation.12 | async-start | bytes 1310720 | tf_op jit(solution)/shard_map/all_gather | solution.py:340
  15.5 60.8 %collective-permute-start.8 = (bf16[128,1024]{0,1:T(8,128)(2,1)}, bf16[128,1024]{0,1:T(8,128)(2,1)}, u32[]{:S(2)}, u32[]{:S(2)}) collective-permute-start(bf16[128,1024]{0,1:T(8,128)(2,1)} %select_bitcast_fusion.2), channel_id=1, source_target_pairs={{0,16},{16,0},{1,17},{17,1},{2,18},{18,2},{3,19},{19,3},{4,20},{20... | collective-permute-start | bytes 786440 | tf_op jit(solution)/shard_map/ppermute | solution.py:31
  48.9 74.1 %all-gather.17.cloned.1.call-start = ((), (), s32[]{:S(2)}) async-start(), calls=%async_computation.13 | async-start | bytes 1310720 | tf_op jit(solution)/shard_map/all_gather | solution.py:340
  55.7 19.3 %collective-permute-start = (bf16[128,1024]{0,1:T(8,128)(2,1)S(1)}, bf16[128,1024]{0,1:T(8,128)(2,1)S(1)}, u32[]{:S(2)}, u32[]{:S(2)}) collective-permute-start(bf16[128,1024]{0,1:T(8,128)(2,1)S(1)} %fusion.94), channel_id=1, source_target_pairs={{0,2},{1,3},{2,0},{3,1},{4,6},{5,7},{6,4},{7,5},{8,10},{9,11},{10,... | collective-permute-start | bytes 786440 | tf_op jit(solution)/shard_map/ppermute | solution.py:31
  74.5 24.0 %collective-permute-start.3 = (bf16[512,1024]{0,1:T(8,128)(2,1)}, bf16[512,1024]{0,1:T(8,128)(2,1)S(1)}, u32[]{:S(2)}, u32[]{:S(2)}) collective-permute-start(bf16[512,1024]{0,1:T(8,128)(2,1)} %all-gather.15.cloned.1.call-done), channel_id=1, source_target_pairs={{0,16},{16,0},{1,17},{17,1},{2,18},{18,2},{3,19},{19,3},{4,20},{20... | collective-permute-start | bytes 3145736 | tf_op jit(solution)/shard_map/ppermute | solution.py:31
  78.2 69.4 %all-gather.19.cloned.1.call-start = ((), (), s32[]{:S(2)}) async-start(), calls=%async_computation.14 | async-start | bytes 1310720 | tf_op jit(solution)/shard_map/all_gather | solution.py:340
  118.1 70.0 %all-gather.21.cloned.1.call-start = ((), (), s32[]{:S(2)}) async-start(), calls=%async_computation.15 | async-start | bytes 1310720 | tf_op jit(solution)/shard_map/all_gather | solution.py:340
  122.9 25.3 %collective-permute-start.9 = (bf16[512,1024]{0,1:T(8,128)(2,1)}, bf16[512,1024]{0,1:T(8,128)(2,1)S(1)}, u32[]{:S(2)}, u32[]{:S(2)}) collective-permute-start(bf16[512,1024]{0,1:T(8,128)(2,1)} %all-gather.17.cloned.1.call-done), channel_id=1, source_target_pairs={{0,16},{16,0},{1,17},{17,1},{2,18},{18,2},{3,19},{19,3},{4,20},{20... | collective-permute-start | bytes 3145736 | tf_op jit(solution)/shard_map/ppermute | solution.py:31
  128.4 19.7 %collective-permute-start.7 = (bf16[256,1024]{0,1:T(8,128)(2,1)S(1)}, bf16[256,1024]{0,1:T(8,128)(2,1)S(1)}, u32[]{:S(2)}, u32[]{:S(2)}) collective-permute-start(bf16[256,1024]{0,1:T(8,128)(2,1)S(1)} %pad_maximum_fusion.22), channel_id=1, source_target_pairs={{0,1},{1,0},{2,3},{3,2},{4,5},{5,4},{6,7},{7,6},{8,9},{9,8},{10,11... | collective-permute-start | bytes 1572872 | tf_op jit(solution)/shard_map/ppermute | solution.py:31
  128.5 77.9 %all-gather.33.cloned.1.call-start = ((), (), s32[]{:S(2)}) async-start(), calls=%async_computation.21 | async-start | bytes 1310720 | tf_op jit(solution)/shard_map/all_gather | solution.py:377
  147.6 24.0 %collective-permute-start.11 = (bf16[512,1024]{0,1:T(8,128)(2,1)}, bf16[512,1024]{0,1:T(8,128)(2,1)S(1)}, u32[]{:S(2)}, u32[]{:S(2)}) collective-permute-start(bf16[512,1024]{0,1:T(8,128)(2,1)} %all-gather.19.cloned.1.call-done), channel_id=1, source_target_pairs={{0,16},{16,0},{1,17},{17,1},{2,18},{18,2},{3,19},{19,3},{4,20},{20... | collective-permute-start | bytes 3145736 | tf_op jit(solution)/shard_map/ppermute | solution.py:31
  175.2 62.5 %all-gather.25.cloned.1.call-start = ((), (), s32[]{:S(2)}) async-start(), calls=%async_computation.17 | async-start | bytes 1310720 | tf_op jit(solution)/shard_map/all_gather | solution.py:340
  188.1 26.2 %collective-permute-start.16 = (bf16[512,1024]{0,1:T(8,128)(2,1)}, bf16[512,1024]{0,1:T(8,128)(2,1)}, u32[]{:S(2)}, u32[]{:S(2)}) collective-permute-start(bf16[512,1024]{0,1:T(8,128)(2,1)} %all-gather.21.cloned.1.call-done), channel_id=1, source_target_pairs={{0,16},{16,0},{1,17},{17,1},{2,18},{18,2},{3,19},{19,3},{4,20},{20... | collective-permute-start | bytes 3145736 | tf_op jit(solution)/shard_map/ppermute | solution.py:31
  194.0 19.5 %collective-permute-start.15 = (bf16[256,1024]{0,1:T(8,128)(2,1)S(1)}, bf16[256,1024]{0,1:T(8,128)(2,1)S(1)}, u32[]{:S(2)}, u32[]{:S(2)}) collective-permute-start(bf16[256,1024]{0,1:T(8,128)(2,1)S(1)} %pad_maximum_fusion.24), channel_id=1, source_target_pairs={{0,1},{1,0},{2,3},{3,2},{4,5},{5,4},{6,7},{7,6},{8,9},{9,8},{10,11... | collective-permute-start | bytes 1572872 | tf_op jit(solution)/shard_map/ppermute | solution.py:31
  209.4 18.9 %all-to-all-start.3 = ((bf16[4,128,256]{1,2,0:T(8,128)(2,1)}), bf16[4,128,256]{1,2,0:T(8,128)(2,1)}, u32[]{:S(2)}, u32[]{:S(2)}) async-start(bf16[4,128,256]{1,2,0:T(8,128)(2,1)} %copy.178), calls=%async_computation.3 | async-start | bytes 524288 | tf_op jit(solution)/shard_map/all_to_all | solution.py:379
  213.4 54.4 %all-gather.23.cloned.1.call-start = ((), (), s32[]{:S(2)}) async-start(), calls=%async_computation.16 | async-start | bytes 1310720 | tf_op jit(solution)/shard_map/all_gather | solution.py:340
  227.8 253.8 %reduce-scatter.25.cloned.1.call-start = ((), (), s32[]{:S(2)}) async-start(), calls=%async_computation.25 | async-start | bytes 1310720
  233.5 11.0 %collective-permute-start.18 = (bf16[128,1024]{0,1:T(8,128)(2,1)}, bf16[128,1024]{0,1:T(8,128)(2,1)}, u32[]{:S(2)}, u32[]{:S(2)}) collective-permute-start(bf16[128,1024]{0,1:T(8,128)(2,1)} %fusion.156), channel_id=1, source_target_pairs={{0,2},{1,3},{2,0},{3,1},{4,6},{5,7},{6,4},{7,5},{8,10},{9,11},{10,... | collective-permute-start | bytes 786440 | tf_op jit(solution)/shard_map/ppermute | solution.py:31
  237.7 32.0 %collective-permute-start.22 = (bf16[512,1024]{0,1:T(8,128)(2,1)}, bf16[512,1024]{0,1:T(8,128)(2,1)}, u32[]{:S(2)}, u32[]{:S(2)}) collective-permute-start(bf16[512,1024]{0,1:T(8,128)(2,1)} %all-gather.25.cloned.1.call-done), channel_id=1, source_target_pairs={{0,16},{16,0},{1,17},{17,1},{2,18},{18,2},{3,19},{19,3},{4,20},{20... | collective-permute-start | bytes 3145736 | tf_op jit(solution)/shard_map/ppermute | solution.py:31
  240.3 28.2 %collective-permute-start.27 = (bf16[256,1024]{0,1:T(8,128)(2,1)}, bf16[256,1024]{0,1:T(8,128)(2,1)}, u32[]{:S(2)}, u32[]{:S(2)}) collective-permute-start(bf16[256,1024]{0,1:T(8,128)(2,1)} %pad_maximum_fusion.30), channel_id=1, source_target_pairs={{0,1},{1,0},{2,3},{3,2},{4,5},{5,4},{6,7},{7,6},{8,9},{9,8},{10,11... | collective-permute-start | bytes 1572872 | tf_op jit(solution)/shard_map/ppermute | solution.py:31
  246.3 22.0 %collective-permute-start.19 = (bf16[128,1024]{0,1:T(8,128)(2,1)S(1)}, bf16[128,1024]{0,1:T(8,128)(2,1)S(1)}, u32[]{:S(2)}, u32[]{:S(2)}) collective-permute-start(bf16[128,1024]{0,1:T(8,128)(2,1)S(1)} %add_convert_fusion.6), channel_id=1, source_target_pairs={{0,2},{1,3},{2,0},{3,1},{4,6},{5,7},{6,4},{7,5},{8,10},{9,11},{10,... | collective-permute-start | bytes 786440 | tf_op jit(solution)/shard_map/ppermute | solution.py:31
  267.8 24.0 %collective-permute-start.21 = (bf16[512,1024]{0,1:T(8,128)(2,1)}, bf16[512,1024]{0,1:T(8,128)(2,1)S(1)}, u32[]{:S(2)}, u32[]{:S(2)}) collective-permute-start(bf16[512,1024]{0,1:T(8,128)(2,1)} %all-gather.23.cloned.1.call-done), channel_id=1, source_target_pairs={{0,16},{16,0},{1,17},{17,1},{2,18},{18,2},{3,19},{19,3},{4,20},{20... | collective-permute-start | bytes 3145736 | tf_op jit(solution)/shard_map/ppermute | solution.py:31
  301.2 24.3 %collective-permute-start.47 = (bf16[512,1024]{1,0:T(8,128)(2,1)S(1)}, bf16[512,1024]{1,0:T(8,128)(2,1)S(1)}, u32[]{:S(2)}, u32[]{:S(2)}) collective-permute-start(bf16[512,1024]{1,0:T(8,128)(2,1)S(1)} %slice.955), channel_id=1, source_target_pairs={{0,16},{16,0},{1,17},{17,1},{2,18},{18,2},{3,19},{19,3},{4,20},{20... | collective-permute-start | bytes 3145736 | tf_op jit(solution)/shard_map/ppermute | solution.py:31
  303.8 29.3 %collective-permute-start.23 = (bf16[256,1024]{0,1:T(8,128)(2,1)}, bf16[256,1024]{0,1:T(8,128)(2,1)}, u32[]{:S(2)}, u32[]{:S(2)}) collective-permute-start(bf16[256,1024]{0,1:T(8,128)(2,1)} %pad_maximum_fusion.27), channel_id=1, source_target_pairs={{0,1},{1,0},{2,3},{3,2},{4,5},{5,4},{6,7},{7,6},{8,9},{9,8},{10,11... | collective-permute-start | bytes 1572872 | tf_op jit(solution)/shard_map/ppermute | solution.py:31
  327.0 156.4 %reduce-scatter.29.cloned.1.call-start = ((), (), s32[]{:S(2)}) async-start(), calls=%async_computation.27 | async-start | bytes 1310720
  331.3 25.6 %collective-permute-start.50 = (bf16[512,1024]{1,0:T(8,128)(2,1)S(1)}, bf16[512,1024]{1,0:T(8,128)(2,1)S(1)}, u32[]{:S(2)}, u32[]{:S(2)}) collective-permute-start(bf16[512,1024]{1,0:T(8,128)(2,1)S(1)} %slice.959), channel_id=1, source_target_pairs={{0,16},{16,0},{1,17},{17,1},{2,18},{18,2},{3,19},{19,3},{4,20},{20... | collective-permute-start | bytes 3145736 | tf_op jit(solution)/shard_map/ppermute | solution.py:31
  337.3 26.9 %collective-permute-start.29 = (bf16[128,1024]{0,1:T(8,128)(2,1)}, bf16[128,1024]{0,1:T(8,128)(2,1)}, u32[]{:S(2)}, u32[]{:S(2)}) collective-permute-start(bf16[128,1024]{0,1:T(8,128)(2,1)} %fusion.139), channel_id=1, source_target_pairs={{0,2},{1,3},{2,0},{3,1},{4,6},{5,7},{6,4},{7,5},{8,10},{9,11},{10,... | collective-permute-start | bytes 786440 | tf_op jit(solution)/shard_map/ppermute | solution.py:31
  360.1 10.2 %all-to-all-start.2 = ((bf16[4,128,256]{1,2,0:T(8,128)(2,1)}), bf16[4,128,256]{1,2,0:T(8,128)(2,1)}, u32[]{:S(2)}, u32[]{:S(2)}) async-start(bf16[4,128,256]{1,2,0:T(8,128)(2,1)} %bitcast.374), calls=%async_computation.2 | async-start | bytes 524288 | tf_op jit(solution)/shard_map/all_to_all | solution.py:404
  373.6 132.8 %all-gather.27.cloned.1.call-start = ((), (), s32[]{:S(2)}) async-start(), calls=%async_computation.18 | async-start | bytes 2621440 | tf_op jit(solution)/shard_map/all_gather | solution.py:412
  385.5 124.9 %reduce-scatter.21.cloned.1.call-start = ((), (), s32[]{:S(2)}) async-start(), calls=%async_computation.23 | async-start | bytes 1310720
  404.7 25.7 %collective-permute-start.44 = (bf16[512,1024]{0,1:T(8,128)(2,1)}, bf16[512,1024]{0,1:T(8,128)(2,1)}, u32[]{:S(2)}, u32[]{:S(2)}) collective-permute-start(bf16[512,1024]{0,1:T(8,128)(2,1)} %pad_maximum_fusion.8), channel_id=1, source_target_pairs={{0,16},{16,0},{1,17},{17,1},{2,18},{18,2},{3,19},{19,3},{4,20},{20... | collective-permute-start | bytes 3145736 | tf_op jit(solution)/shard_map/ppermute | solution.py:31
  422.2 13.3 %collective-permute-start.35 = (bf16[256,1024]{0,1:T(8,128)(2,1)}, bf16[256,1024]{0,1:T(8,128)(2,1)}, u32[]{:S(2)}, u32[]{:S(2)}) collective-permute-start(bf16[256,1024]{0,1:T(8,128)(2,1)} %pad_maximum_fusion.34), channel_id=1, source_target_pairs={{0,1},{1,0},{2,3},{3,2},{4,5},{5,4},{6,7},{7,6},{8,9},{9,8},{10,11... | collective-permute-start | bytes 1572872 | tf_op jit(solution)/shard_map/ppermute | solution.py:31
  435.3 200.4 %reduce-scatter.23.cloned.1.call-start = ((), (), s32[]{:S(2)}) async-start(), calls=%async_computation.24 | async-start | bytes 1310720
  442.8 24.5 %collective-permute-start.46 = (bf16[512,1024]{1,0:T(8,128)(2,1)S(1)}, bf16[512,1024]{1,0:T(8,128)(2,1)S(1)}, u32[]{:S(2)}, u32[]{:S(2)}) collective-permute-start(bf16[512,1024]{1,0:T(8,128)(2,1)S(1)} %slice.953), channel_id=1, source_target_pairs={{0,16},{16,0},{1,17},{17,1},{2,18},{18,2},{3,19},{19,3},{4,20},{20... | collective-permute-start | bytes 3145736 | tf_op jit(solution)/shard_map/ppermute | solution.py:31
  447.1 25.7 %collective-permute-start.36 = (bf16[256,1024]{0,1:T(8,128)(2,1)}, bf16[256,1024]{0,1:T(8,128)(2,1)}, u32[]{:S(2)}, u32[]{:S(2)}) collective-permute-start(bf16[256,1024]{0,1:T(8,128)(2,1)} %pad_maximum_fusion.35), channel_id=1, source_target_pairs={{0,1},{1,0},{2,3},{3,2},{4,5},{5,4},{6,7},{7,6},{8,9},{9,8},{10,11... | collective-permute-start | bytes 1572872 | tf_op jit(solution)/shard_map/ppermute | solution.py:31
  468.7 170.4 %reduce-scatter.27.cloned.1.call-start = ((), (), s32[]{:S(2)}) async-start(), calls=%async_computation.26 | async-start | bytes 1310720
  474.7 10.5 %collective-permute-start.37 = (bf16[128,1024]{0,1:T(8,128)(2,1)}, bf16[128,1024]{0,1:T(8,128)(2,1)}, u32[]{:S(2)}, u32[]{:S(2)}) collective-permute-start(bf16[128,1024]{0,1:T(8,128)(2,1)} %fusion.127), channel_id=1, source_target_pairs={{0,2},{1,3},{2,0},{3,1},{4,6},{5,7},{6,4},{7,5},{8,10},{9,11},{10,... | collective-permute-start | bytes 786440 | tf_op jit(solution)/shard_map/ppermute | solution.py:31
  479.2 23.9 %collective-permute-start.49 = (bf16[512,1024]{1,0:T(8,128)(2,1)}, bf16[512,1024]{1,0:T(8,128)(2,1)}, u32[]{:S(2)}, u32[]{:S(2)}) collective-permute-start(bf16[512,1024]{1,0:T(8,128)(2,1)} %slice.957), channel_id=1, source_target_pairs={{0,16},{16,0},{1,17},{17,1},{2,18},{18,2},{3,19},{19,3},{4,20},{20... | collective-permute-start | bytes 3145736 | tf_op jit(solution)/shard_map/ppermute | solution.py:31
  488.6 17.6 %collective-permute-start.38 = (bf16[128,1024]{0,1:T(8,128)(2,1)S(1)}, bf16[128,1024]{0,1:T(8,128)(2,1)S(1)}, u32[]{:S(2)}, u32[]{:S(2)}) collective-permute-start(bf16[128,1024]{0,1:T(8,128)(2,1)S(1)} %get-tuple-element.104), channel_id=1, source_target_pairs={{0,2},{1,3},{2,0},{3,1},{4,6},{5,7},{6,4},{7,5},{8,10},{9,11},{10,... | collective-permute-start | bytes 786440 | tf_op jit(solution)/shard_map/ppermute | solution.py:31
  505.8 144.8 %reduce-scatter.19.cloned.1.call-start = ((), (), s32[]{:S(2)}) async-start(), calls=%async_computation.22 | async-start | bytes 1310720
  525.1 40.7 %collective-permute-start.43 = (bf16[512,1024]{0,1:T(8,128)(2,1)}, bf16[512,1024]{0,1:T(8,128)(2,1)}, u32[]{:S(2)}, u32[]{:S(2)}) collective-permute-start(bf16[512,1024]{0,1:T(8,128)(2,1)} %pad_maximum_fusion.9), channel_id=1, source_target_pairs={{0,16},{16,0},{1,17},{17,1},{2,18},{18,2},{3,19},{19,3},{4,20},{20... | collective-permute-start | bytes 3145736 | tf_op jit(solution)/shard_map/ppermute | solution.py:31
  528.0 35.7 %collective-permute-start.41 = (bf16[128,1024]{0,1:T(8,128)(2,1)}, bf16[128,1024]{0,1:T(8,128)(2,1)S(1)}, u32[]{:S(2)}, u32[]{:S(2)}) collective-permute-start(bf16[128,1024]{0,1:T(8,128)(2,1)} %fusion.121), channel_id=1, source_target_pairs={{0,2},{1,3},{2,0},{3,1},{4,6},{5,7},{6,4},{7,5},{8,10},{9,11},{10,... | collective-permute-start | bytes 786440 | tf_op jit(solution)/shard_map/ppermute | solution.py:31
  570.3 9.4 %all-to-all-start.5 = ((bf16[4,128,256]{1,2,0:T(8,128)(2,1)}), bf16[4,128,256]{1,2,0:T(8,128)(2,1)S(1)}, u32[]{:S(2)}, u32[]{:S(2)}) async-start(bf16[4,128,256]{1,2,0:T(8,128)(2,1)} %bitcast.122), calls=%async_computation.5 | async-start | bytes 524288 | tf_op jit(solution)/shard_map/all_to_all | solution.py:404
  583.1 77.7 %all-gather.29.cloned.1.call-start = ((), (), s32[]{:S(2)}) async-start(), calls=%async_computation.19 | async-start | bytes 2621440 | tf_op jit(solution)/shard_map/all_gather | solution.py:412
  636.8 9.5 %collective-permute-start.48 = (bf16[128,1024]{0,1:T(8,128)(2,1)S(1)}, bf16[128,1024]{0,1:T(8,128)(2,1)S(1)}, u32[]{:S(2)}, u32[]{:S(2)}) collective-permute-start(bf16[128,1024]{0,1:T(8,128)(2,1)S(1)} %broadcast_select_fusion.6), channel_id=1, source_target_pairs={{0,16},{16,0},{1,17},{17,1},{2,18},{18,2},{3,19},{19,3},{4,20},{20... | collective-permute-start | bytes 786440 | tf_op jit(solution)/shard_map/ppermute | solution.py:31
  640.3 10.2 %collective-permute-start.51 = (bf16[128,1024]{0,1:T(8,128)(2,1)S(1)}, bf16[128,1024]{0,1:T(8,128)(2,1)S(1)}, u32[]{:S(2)}, u32[]{:S(2)}) collective-permute-start(bf16[128,1024]{0,1:T(8,128)(2,1)S(1)} %broadcast_select_fusion.4), channel_id=1, source_target_pairs={{0,16},{16,0},{1,17},{17,1},{2,18},{18,2},{3,19},{19,3},{4,20},{20... | collective-permute-start | bytes 786440 | tf_op jit(solution)/shard_map/ppermute | solution.py:31
  (245 other events, 1993.8 us)
Sparse Core Ops, SparseCore 0:
  14.4 28.2 all-gather.30
  44.8 29.6 all-gather.14
  78.3 29.6 all-gather.16
  118.2 29.3 all-gather.18
  149.6 28.4 all-gather.20
  180.1 26.2 all-gather.32
  208.0 29.6 all-gather.24
  239.3 28.4 all-gather.22
  327.1 26.3 reduce-scatter.24
  358.5 26.3 reduce-scatter.28
  387.0 44.5 all-gather.26
  435.4 25.3 reduce-scatter.20
  468.9 25.4 reduce-scatter.22
  505.9 25.7 reduce-scatter.26
  569.0 24.8 reduce-scatter.18
  595.9 45.5 all-gather.28

commit v2 on v1

--- a/solution.py
+++ b/solution.py
@@ -31,35 +31,41 @@
     return lax.ppermute(array, axis, [(i, i ^ bit) for i in range(count)])
 
 
+def column_bits():
+    count = lax.axis_size("col")
+    return [1 << i for i in reversed(range(count.bit_length() - 1))]
+
+
+def spread_order():
+    order = [0]
+    for bit in column_bits():
+        order = order + [o ^ bit for o in order]
+    return order
+
+
 def spread_tokens(own):
-    count = lax.axis_size("col")
-    blocks = {0: own}
-    bit = count // 2
-    while bit >= 1:
-        held = sorted(blocks)
-        sent = swap_bit(jnp.concatenate([blocks[b] for b in held], axis=0), "col", bit)
-        size = own.shape[0]
-        for place, b in enumerate(held):
-            blocks[b ^ bit] = sent[place * size : (place + 1) * size]
-        bit //= 2
-    return jnp.concatenate([blocks[b] for b in range(count)], axis=0)
+    held = own
+    for bit in column_bits():
+        held = jnp.concatenate([held, swap_bit(held, "col", bit)], axis=0)
+    return held
 
 
 def sum_tokens(partial):
-    count = lax.axis_size("col")
-    size = partial.shape[0] // count
-    blocks = {b: partial[b * size : (b + 1) * size] for b in range(count)}
-    bit = 1
-    while bit < count:
-        far = [b for b in sorted(blocks) if b & bit]
-        sent = swap_bit(
-            jnp.concatenate([blocks[b].astype(BF16) for b in far], axis=0), "col", bit
-        )
-        for place, b in enumerate(far):
-            blocks[b ^ bit] = blocks[b ^ bit] + sent[place * size : (place + 1) * size].astype(F32)
-            del blocks[b]
-        bit *= 2
-    return blocks[0]
+    held = partial
+    for bit in reversed(column_bits()):
+        half = held.shape[0] // 2
+        held = held[:half] + swap_bit(held[half:].astype(BF16), "col", bit).astype(F32)
+    return held
+
+
+def gather_direct(array):
+    count = lax.axis_size("row")
+    copies = jnp.broadcast_to(array[None], (count,) + array.shape)
+    return lax.all_to_all(copies, "row", split_axis=0, concat_axis=0)
+
+
+def together(*values):
+    return lax.optimization_barrier(values)
 
 
 def owned_layout(lengths, deal, holder, rows_dev):
@@ -213,66 +219,61 @@
     return result, stored
 
 
-def layer_backward(grad_out, layout, weights, small, stored):
+def ffn_backward(grad_out, weights, small, stored, meanwhile):
+    _, up_w, down_w = weights
+    gain = small[0]
+    centered_two, inverse_two, rows_two, upper_in, activated = stored[8:]
+    half = up_w[0].shape[0]
+    grad_down = grad_out.astype(BF16)
+    down_all = spread_tokens(grad_down)
+    if meanwhile:
+        down_all, *meanwhile = together(down_all, *meanwhile)
+    grad_act = times_rows(down_all, down_w)
+    grad_upper = jax.vjp(gelu_tanh, upper_in)[1](grad_act)[0].astype(BF16)
+    grad_norm = sum_tokens(times_rows_back(grad_upper, up_w))
+    terms = [
+        [tn(rows_two[:, part], grad_upper).astype(BF16), tn(down_all[:, part], activated).astype(BF16)]
+        for part in (slice(0, half), slice(half, None))
+    ]
+    grad_mid, gain_two, shift_two = norm_backward(grad_norm, centered_two, inverse_two, gain[1])
+    grad_mid = grad_out + grad_mid
+    token_sums = [gain_two, shift_two, jnp.sum(grad_down, axis=0, dtype=F32)]
+    return grad_mid, terms, token_sums, jnp.sum(grad_upper, axis=0, dtype=F32), meanwhile
+
+
+def attn_backward(grad_mid, layout, weights, small, stored, meanwhile):
     usable, segment, position, slopes = layout
-    attn_w, up_w, down_w = weights
+    attn_w = weights[0]
     width = attn_w[0].shape[1] // 4
+    half = attn_w[0].shape[0]
     gain = small[0]
-    (
-        centered,
-        inverse,
-        rows_all,
-        queries,
-        key_rows,
-        value_rows,
-        logsum,
-        attended,
-        centered_two,
-        inverse_two,
-        rows_two,
-        upper_in,
-        activated,
-    ) = stored
+    centered, inverse, rows_all, queries, key_rows, value_rows, logsum, attended = stored[:8]
     qkv_w = [w[:, : 3 * width] for w in attn_w]
     out_w = [w[:, 3 * width :] for w in attn_w]
-    grad_down = grad_out.astype(BF16)
-    down_all = spread_tokens(grad_down)
-    grad_act = times_rows(down_all, down_w)
-    grad_upper = jax.vjp(gelu_tanh, upper_in)[1](grad_act)[0].astype(BF16)
-    grad_norm_two = sum_tokens(times_rows_back(grad_upper, up_w))
-    down_term = tn(down_all, activated).astype(BF16)
-    up_term = tn(rows_two, grad_upper).astype(BF16)
-    grad_mid, gain_two, shift_two = norm_backward(
-        grad_norm_two, centered_two, inverse_two, gain[1]
-    )
-    grad_mid = grad_out + grad_mid
     grad_branch = grad_mid.astype(BF16)
     branch_all = spread_tokens(grad_branch)
+    if meanwhile:
+        branch_all, *meanwhile = together(branch_all, *meanwhile)
     grad_attended = times_rows(branch_all, out_w).astype(BF16).reshape(queries.shape)
     grad_qkv = attend_backward(
         queries, key_rows, value_rows, segment, position, slopes, logsum, grad_attended
     )
     grad_norm = sum_tokens(times_rows_back(grad_qkv, qkv_w))
-    attn_term = jnp.concatenate(
-        [tn(rows_all, grad_qkv).astype(BF16), tn(branch_all, attended).astype(BF16)], axis=1
-    )
+    terms = [
+        jnp.concatenate(
+            [
+                tn(rows_all[:, part], grad_qkv).astype(BF16),
+                tn(branch_all[:, part], attended).astype(BF16),
+            ],
+            axis=1,
+        )
+        for part in (slice(0, half), slice(half, None))
+    ]
     grad_in, gain_one, shift_one = norm_backward(grad_norm, centered, inverse, gain[0])
-    grad_input = grad_mid + grad_in
-    token_sums = jnp.stack(
-        [
-            gain_one,
-            gain_two,
-            shift_one,
-            shift_two,
-            jnp.sum(grad_branch, axis=0, dtype=F32),
-            jnp.sum(grad_down, axis=0, dtype=F32),
-        ]
-    )
+    token_sums = [gain_one, shift_one, jnp.sum(grad_branch, axis=0, dtype=F32)]
     qkv_sums = jnp.sum(grad_qkv, axis=0, dtype=F32)
-    column_sums = jnp.concatenate(
-        [qkv_sums[:width], qkv_sums[2 * width :], jnp.sum(grad_upper, axis=0, dtype=F32)]
-    )
-    return grad_input, (attn_term, up_term, down_term), token_sums, column_sums
+    column_sums = jnp.concatenate([qkv_sums[:width], qkv_sums[2 * width :]])
+    return grad_mid + grad_in, terms, token_sums, column_sums, meanwhile
 
 
 def on_device(
@@ -329,6 +330,7 @@
         up_weight[0],
         down_weight[0].T,
     )
+    packed = (packed[0], jnp.concatenate(packed[1:], axis=1))
     kept = [pick(w[:half], w[half:]) for w in packed]
     given = [swap_bit(pick(w[half:], w[:half]), "section", 1) for w in packed]
     halves = (
@@ -336,9 +338,11 @@
         [pick(g, k) for k, g in zip(kept, given)],
     )
 
-    def gather_weight(piece):
-        mine = lax.all_gather(piece, "row", axis=0, tiled=True)
-        return (mine, swap_bit(mine, "section", 1))
+    def gather_weights(pieces):
+        attn = lax.all_gather(pieces[0], "row", axis=0, tiled=True)
+        ffn = lax.all_gather(pieces[1], "row", axis=0, tiled=True)
+        up, down = ffn[:, : ffn.shape[1] // 2], ffn[:, ffn.shape[1] // 2 :]
+        return [(mine, swap_bit(mine, "section", 1)) for mine in (attn, up, down)]
 
     mine_small = jnp.concatenate(
         [norm_gain[0], norm_shift[0], proj_bias[0], up_bias[0].reshape(-1, width)], axis=0
@@ -363,7 +367,7 @@
     source, usable, segment, position = owned_layout(
         lengths[section], deal[section], holder, rows_dev
     )
-    order = jnp.bitwise_xor(column, jnp.arange(cols_count, dtype=jnp.int32))
+    order = jnp.bitwise_xor(column, jnp.array(spread_order(), jnp.int32))
 
     def xor_order(values):
         return values.reshape(cols_count, tokens)[order].reshape(rows_dev)
@@ -374,18 +378,15 @@
     layout = (own_usable, xor_order(segment), xor_order(position), slopes)
 
     def deal_rows(array):
-        portion = lax.all_gather(pick(array[0], array[1]), "row", axis=0, tiled=True)
+        portion = gather_direct(pick(array[0], array[1])).reshape(-1, width)
         owned = pick_rows(portion, source).astype(BF16)
         own = lax.all_to_all(
             owned.reshape(cols_count, tokens, width), "col", split_axis=0, concat_axis=0
         )
         return own_first(jnp.transpose(own, (1, 0, 2)).reshape(tokens, model), 1)
 
-    weights = [[None] * 3, [None] * 3]
     first_rows = deal_rows(inputs)
-    for layer in range(2):
-        for kind in range(3):
-            weights[layer][kind] = gather_weight(halves[layer][kind])
+    weights = [gather_weights(halves[0]), gather_weights(halves[1])]
     smalls = [layer_small(0), layer_small(1)]
 
     hidden_zero, stored_zero = layer_forward(first_rows.astype(F32), layout, weights[0], smalls[0])
@@ -396,65 +397,101 @@
     last_out = hidden_one.astype(BF16)
 
     positions = holder * rows_dev + jnp.arange(rows_dev, dtype=jnp.int32)
-    targets = jax.vmap(given_targets, (0, 0, None, None))(lengths, deal, positions, rows_dev)
-
-    def give_back(zero, one):
-        def by_features(own):
-            parts = true_order(own, 1).reshape(tokens, cols_count, width)
-            got = lax.all_to_all(
-                jnp.transpose(parts, (1, 0, 2)), "col", split_axis=0, concat_axis=0
-            )
-            return got.reshape(rows_dev, width)
-
-        stays = by_features(pick(zero, one))
-        comes = swap_bit(by_features(pick(one, zero)), "section", 1)
-        both = jnp.stack([pick(stays, comes), pick(comes, stays)])
-        whole = lax.all_gather(both, "row", axis=1, tiled=True)
-        return jnp.stack([pick_rows(whole[m], targets[m]) for m in range(micro_count)])
-
-    hidden_out = give_back(middle_in, last_out).astype(BF16)
+    targets = given_targets(lengths[section], deal[section], positions, rows_dev)
+
+    def by_features(own, lanes):
+        parts = true_order(own.reshape(-1, model), 1).reshape(tokens, lanes, cols_count, width)
+        return jnp.transpose(parts, (2, 1, 0, 3))
+
+    both = jnp.concatenate([middle_in[:, None], last_out[:, None]], axis=1)
+    both = lax.all_to_all(by_features(both, 2), "col", split_axis=0, concat_axis=0)
+    both = jnp.transpose(both, (0, 2, 1, 3)).reshape(rows_dev, 2 * width)
+    both = lax.all_gather(both, "row", axis=0, tiled=True)
+    both = pick_rows(both, targets).astype(BF16)
+    stays = pick(both[:, :width], both[:, width:])
+    comes = swap_bit(pick(both[:, width:], both[:, :width]), "section", 1)
+    hidden_out = jnp.stack([pick(stays, comes), pick(comes, stays)])
+
+    extra = 16
+
+    def rows_and_sums(grad_in, token_sums, column_sums):
+        sums = true_order(jnp.stack(token_sums), 1).reshape(-1, cols_count, width)
+        count = sums.shape[0]
+        sums = jnp.pad(jnp.transpose(sums, (1, 0, 2)), ((0, 0), (0, extra - count), (0, 0)))
+        rows = by_features(grad_in, 1)[:, 0]
+        got = lax.all_to_all(
+            jnp.concatenate([rows, sums.astype(BF16)], axis=1), "col", split_axis=0, concat_axis=0
+        )
+        sums = jnp.sum(got[:, tokens : tokens + count].astype(F32), axis=0)
+        sums = jnp.concatenate([sums, jnp.concatenate(column_sums).reshape(-1, width)], axis=0)
+        sums = jnp.pad(sums, ((0, extra - sums.shape[0]), (0, 0)))
+        rows = jnp.concatenate([got[:, :tokens].reshape(rows_dev, width), sums.astype(BF16)], axis=0)
+        all_rows = gather_direct(rows)
+        picked = pick_rows(all_rows[:, :rows_dev].reshape(-1, width), targets)
+        return jnp.concatenate([picked, jnp.sum(all_rows[:, rows_dev:].astype(F32), axis=0)], axis=0)
+
+    def send_term(terms):
+        return [swap_bit(t, "section", 1) for t in terms[1]]
+
+    def add_term(terms, come):
+        parts = [(m.astype(F32) + c.astype(F32)).astype(BF16) for m, c in zip(terms[0], come)]
+        return jnp.concatenate(parts, axis=1) if len(parts) > 1 else parts[0]
+
+    def reduce_rows(total):
+        return lax.psum_scatter(total, "row", scatter_dimension=0, tiled=True)
 
     grad_one = deal_rows(cotangent).astype(F32)
-    grad_one_in, terms_one, token_one, column_one = layer_backward(
-        grad_one, layout, weights[1], smalls[1], stored_one
-    )
-    grad_zero = grad_one_in.astype(BF16)
-    grad_zero = jnp.where(own_usable[:, None], grad_zero, jnp.zeros_like(grad_zero)).astype(F32)
-    grad_zero_in, terms_zero, token_zero, column_zero = layer_backward(
-        grad_zero, layout, weights[0], smalls[0], stored_zero
-    )
-
-    def reduce_weight(term):
-        mine, other = term[: model // 2], term[model // 2 :]
-        total = (mine.astype(F32) + swap_bit(other, "section", 1).astype(F32)).astype(BF16)
-        return lax.psum_scatter(total, "row", scatter_dimension=0, tiled=True)
-
-    sums_one = [reduce_weight(t) for t in terms_one]
-    sums_zero = [reduce_weight(t) for t in terms_zero]
-    finals = []
-    for zero, one in zip(sums_zero, sums_one):
+    grad_mid, ffn_one, sums_a, up_sum, _ = ffn_backward(
+        grad_one, weights[1], smalls[1], stored_one, []
+    )
+    come_ffn_one = send_term(ffn_one)
+    grad_one_in, attn_one, sums_b, qv_sum, _ = attn_backward(
+        grad_mid, layout, weights[1], smalls[1], stored_one, []
+    )
+    come_attn_one = send_term([[attn_one[0]], [attn_one[1]]])
+    back_one = rows_and_sums(
+        grad_one_in.astype(BF16),
+        [sums_b[0], sums_a[0], sums_b[1], sums_a[1], sums_b[2], sums_a[2]],
+        [qv_sum, up_sum],
+    )
+    grad_zero = jnp.where(own_usable[:, None], grad_one_in.astype(BF16), 0.0).astype(F32)
+    grad_mid, ffn_zero, sums_a, up_sum, come_ffn_one = ffn_backward(
+        grad_zero, weights[0], smalls[0], stored_zero, come_ffn_one
+    )
+    ffn_one = reduce_rows(add_term(ffn_one, come_ffn_one))
+    come_ffn_zero = send_term(ffn_zero)
+    grad_zero_in, attn_zero, sums_b, qv_sum, come_attn_one = attn_backward(
+        grad_mid, layout, weights[0], smalls[0], stored_zero, come_attn_one
+    )
+    attn_one = reduce_rows(add_term([[attn_one[0]]], come_attn_one))
+    come_attn_zero = send_term([[attn_zero[0]], [attn_zero[1]]])
+    back_zero = rows_and_sums(
+        grad_zero_in.astype(BF16),
+        [sums_b[0], sums_a[0], sums_b[1], sums_a[1], sums_b[2], sums_a[2]],
+        [qv_sum, up_sum],
+    )
+    ffn_zero = reduce_rows(add_term(ffn_zero, come_ffn_zero))
+    attn_zero = reduce_rows(add_term([[attn_zero[0]]], come_attn_zero))
+
+    def both_halves(zero, one):
         mine = pick(zero, one)
         other = swap_bit(pick(one, zero), "section", 1)
-        finals.append(
-            jnp.concatenate([pick(mine, other), pick(other, mine)], axis=0).astype(F32)
-        )
-    qkv_grad = finals[0][:, : 3 * width].reshape(block, 3, width)
-    out_grad = finals[0][:, 3 * width :].T
-    up_grad = finals[1]
-    down_grad = finals[2].T
-
-    in_grad = give_back(grad_zero_in.astype(BF16), grad_one_in.astype(BF16))
-
-    token_sums = jnp.stack([true_order(token_zero, 1), true_order(token_one, 1)])
-    token_sums = lax.psum(token_sums, ("section", "row", "col"))
-    column_sums = lax.psum(jnp.stack([column_zero, column_one]), ("section", "row"))
-    token_sums = lax.dynamic_slice_in_dim(
-        pick(token_sums[0], token_sums[1]), column * width, width, axis=1
-    )
-    column_sums = pick(column_sums[0], column_sums[1])
-    bias_grad = jnp.concatenate(
-        [column_sums[: 2 * width].reshape(2, width), token_sums[4:6]], axis=0
-    )
+        return jnp.concatenate([pick(mine, other), pick(other, mine)], axis=0).astype(F32)
+
+    ffn_grad = both_halves(ffn_zero, ffn_one)
+    attn_grad = both_halves(attn_zero, attn_one)
+    qkv_grad = attn_grad[:, : 3 * width].reshape(block, 3, width)
+    out_grad = attn_grad[:, 3 * width :].T
+    up_grad = ffn_grad[:, : ffn_grad.shape[1] // 2]
+    down_grad = ffn_grad[:, ffn_grad.shape[1] // 2 :].T
+
+    stays = pick(back_zero, back_one)
+    comes = swap_bit(pick(back_one, back_zero).astype(BF16), "section", 1).astype(F32)
+    kept, came = stays[:rows_dev], comes[:rows_dev]
+    in_grad = jnp.stack([pick(kept, came), pick(came, kept)])
+    sums = stays[rows_dev:] + comes[rows_dev:]
+    bias_grad = jnp.concatenate([sums[6:8], sums[4:6]], axis=0)
+    hidden_units = up_bias.shape[1]
     return (
         hidden_out[None],
         in_grad[None],
@@ -462,10 +499,10 @@
         out_grad[None],
         up_grad[None],
         down_grad[None],
-        token_sums[0:2][None],
-        token_sums[2:4][None],
+        sums[0:2][None],
+        sums[2:4][None],
         bias_grad[None],
-        column_sums[2 * width :][None],
+        sums[8 : 8 + hidden_units // width].reshape(1, hidden_units),
     )
 
 

time: 683 us -> 718 us (1.051)
  waiting for transfers between devices: 273 us -> 393 us
  blocking collectives: 88.7 us -> 10.9 us
  other arithmetic: 94.3 us -> 72.9 us
  matrix products: 68.9 us -> 80.4 us
  starting transfers between devices: 74.6 us -> 83.4 us
    psum x2 -> x0, blocking collectives: 76.4 us -> none  [the longest x1 41.7 us: on_device(): token_sums = lax.psum(token_sums, ('section', 'row', 'col'))]
    ppermute x52 -> x50, waiting for transfers between devices: 187 us -> 253 us  [swap_bit(): return lax.ppermute(array, axis, [(i, i ^ bit) for i in range(count)])]
    all_to_all x4 -> x7, waiting for transfers between devices: 10.5 us -> 61.7 us  [the longest x4 50.5 us: gather_direct(): return lax.all_to_all(copies, 'row', split_axis=0, concat_axis=0)]
    reduce_scatter x0 -> x4, waiting for transfers between devices: none -> 24 us  [reduce_rows(): return lax.psum_scatter(total, 'row', scatter_dimension=0, tiled=True)]
    all_gather x10 -> x5, waiting for transfers between devices: 69.4 us -> 47.9 us  [the longest x2 41.2 us: gather_weights(): attn = lax.all_gather(pieces[0], 'row', axis=0, tiled=True)]
    all_to_all x4 -> x7, starting transfers between devices: 14.3 us -> 28 us  [the longest x4 16.8 us: gather_direct(): return lax.all_to_all(copies, 'row', split_axis=0, concat_axis=0)]
    unnamed x456 -> x282, local copies, waits for them, and re-layouts: 35.1 us -> 24.5 us
    convert_element_type x16 -> x10, other arithmetic: 19.1 us -> 10.4 us  [the longest x5 9.56 us: add_term(): (m.astype(F32) + c.astype(F32)).astype(BF16)]
  transfers between devices with their start and end apart: 74 -> 68, of which waited for: 35 -> 40; matrix products, arithmetic and copies ran while one was open for 28% -> 23% of each run, Pallas kernels for 0% -> 0%
where the time goes in v2:
time: 718 us; the launch traced here: 711 us
  waiting for transfers between devices  393 us (55%)
  starting transfers between devices  83.4 us (12%)
  matrix products  80.4 us (11%)
  other arithmetic  72.9 us (10%)
  local copies, waits for them, and re-layouts  53.1 us (7%)
  between operations  18 us (3%)
  blocking collectives  10.9 us (2%)
    ppermute x50, waiting for transfers between devices, swap_bit(): return lax.ppermute(array, axis, [(i, i ^ bit) for i in range(count)])  253 us
    dot_general x53, matrix products, mm(): lax.dot_general(a, b, ((dims[0], dims[1]), ((), ())), preferred_element_t...  60.5 us
    all_to_all x4, waiting for transfers between devices, gather_direct(): return lax.all_to_all(copies, 'row', split_axis=0, concat_axis=0)  50.5 us
    ppermute x50, starting transfers between devices, swap_bit(): return lax.ppermute(array, axis, [(i, i ^ bit) for i in range(count)])  46.5 us
    all_gather x2, waiting for transfers between devices, gather_weights(): attn = lax.all_gather(pieces[0], 'row', axis=0, tiled=True)  41.2 us
    unnamed x282, local copies, waits for them, and re-layouts  24.5 us
    reduce_scatter x4, waiting for transfers between devices, reduce_rows(): return lax.psum_scatter(total, 'row', scatter_dimension=0, tiled=True)  24 us
    all_to_all x4, starting transfers between devices, gather_direct(): return lax.all_to_all(copies, 'row', split_axis=0, concat_axis=0)  16.8 us
  transfers between devices with their start and end apart: 68, of which 40 were waited for; matrix products, arithmetic and copies ran while one was open for 23% of the time, Pallas kernels for 0%

profile of v2, /device:TPU:0, one launch (start us, length us, event | category | flops | bytes accessed | tf_op | source)
XLA Modules:
  0.0 711.3 jit_solution(14606221297379693652)
XLA Ops:
  10.4 3.0 collective-permute-start.2
  15.0 5.3 all-to-all-start
  24.9 10.9 %all-gather.1 = f32[8,12,256]{2,1,0:T(8,128)S(1)} all-gather(f32[1,12,256]{2,1,0:T(8,128)S(1)} %maximum_bitcast_fusion.2), channel_id=2, replica_groups=mesh['section'=2,'row'=4,'col'=4] {'section','col'}, dimensions={0}, use_global_device_ids=true | all-gather | bytes 110592 | tf_op jit(solution)/shard_map/all_gather | solution.py:350
  47.1 3.4 all-to-all-start.1
  50.6 5.9 all-to-all-done.1
  58.3 11.3 %all-gather.8.cloned.1.call-done = bf16[512,1024]{1,0:T(8,128)(2,1)} async-done(((bf16[128,1024]{1,0:T(8,128)(2,1)}), bf16[512,1024]{1,0:T(8,128)(2,1)}) %all-gather.8.cloned.1.call-update) | async-done | bytes 1048592 | tf_op jit(solution)/shard_map/all_gather | solution.py:342
  77.6 17.0 %collective-permute-done.3 = bf16[512,1024]{1,0:T(8,128)(2,1)S(1)} collective-permute-done((bf16[512,1024]{1,0:T(8,128)(2,1)}, bf16[512,1024]{1,0:T(8,128)(2,1)S(1)}, u32[]{:S(2)}, u32[]{:S(2)}) %collective-permute-start.3) | collective-permute-done | bytes 1048608 | tf_op jit(solution)/shard_map/ppermute | solution.py:31
  101.6 3.2 fusion.54
  110.2 6.9 collective-permute-done.5
  127.8 21.0 %collective-permute-done.9 = bf16[512,1024]{1,0:T(8,128)(2,1)S(1)} collective-permute-done((bf16[512,1024]{1,0:T(8,128)(2,1)S(1)}, bf16[512,1024]{1,0:T(8,128)(2,1)S(1)}, u32[]{:S(2)}, u32[]{:S(2)}) %collective-permute-start.9) | collective-permute-done | bytes 1048608 | tf_op jit(solution)/shard_map/ppermute | solution.py:31
  153.9 16.2 %collective-permute-done.10 = bf16[512,1024]{1,0:T(8,128)(2,1)S(1)} collective-permute-done((bf16[512,1024]{1,0:T(8,128)(2,1)S(1)}, bf16[512,1024]{1,0:T(8,128)(2,1)S(1)}, u32[]{:S(2)}, u32[]{:S(2)}) %collective-permute-start.10) | collective-permute-done | bytes 1048608 | tf_op jit(solution)/shard_map/ppermute | solution.py:31
  173.9 4.2 all-to-all-start.3
  180.6 6.6 collective-permute-done.12
  189.3 29.9 %all-gather.12.cloned.1.call-done = bf16[512,1024]{1,0:T(8,128)(2,1)} async-done(((bf16[128,1024]{1,0:T(8,128)(2,1)}), bf16[512,1024]{1,0:T(8,128)(2,1)}) %all-gather.12.cloned.1.call-update) | async-done | bytes 1048592 | tf_op jit(solution)/shard_map/all_gather | solution.py:342
  225.4 4.5 all-to-all-start.4
  231.1 13.3 %collective-permute-done.15 = bf16[512,1024]{1,0:T(8,128)(2,1)S(1)} collective-permute-done((bf16[512,1024]{1,0:T(8,128)(2,1)}, bf16[512,1024]{1,0:T(8,128)(2,1)S(1)}, u32[]{:S(2)}, u32[]{:S(2)}) %collective-permute-start.15) | collective-permute-done | bytes 1048608 | tf_op jit(solution)/shard_map/ppermute | solution.py:31
  261.7 4.9 all-gather.14.cloned.1.call-done
  276.7 3.8 collective-permute-done.18
  282.4 12.1 %collective-permute-done.21 = bf16[512,1024]{1,0:T(8,128)(2,1)S(1)} collective-permute-done((bf16[512,1024]{1,0:T(8,128)(2,1)S(1)}, bf16[512,1024]{1,0:T(8,128)(2,1)S(1)}, u32[]{:S(2)}, u32[]{:S(2)}) %collective-permute-start.21) | collective-permute-done | bytes 1048608 | tf_op jit(solution)/shard_map/ppermute | solution.py:31
  295.4 20.5 %collective-permute-done.20 = bf16[512,1024]{1,0:T(8,128)(2,1)S(1)} collective-permute-done((bf16[512,1024]{1,0:T(8,128)(2,1)S(1)}, bf16[512,1024]{1,0:T(8,128)(2,1)S(1)}, u32[]{:S(2)}, u32[]{:S(2)}) %collective-permute-start.20) | collective-permute-done | bytes 1048608 | tf_op jit(solution)/shard_map/ppermute | solution.py:31
  327.1 6.2 collective-permute-done.28
  333.8 4.2 collective-permute-done.23
  340.2 5.9 collective-permute-done.29
  359.9 6.2 collective-permute-done.32
  371.9 3.2 collective-permute-done.33
  377.3 18.7 %collective-permute-done.36 = bf16[512,1024]{1,0:T(8,128)(2,1)S(1)} collective-permute-done((bf16[512,1024]{1,0:T(8,128)(2,1)S(1)}, bf16[512,1024]{1,0:T(8,128)(2,1)S(1)}, u32[]{:S(2)}, u32[]{:S(2)}) %collective-permute-start.36) | collective-permute-done | bytes 1048608 | tf_op jit(solution)/shard_map/ppermute | solution.py:31
  397.0 19.5 %collective-permute-done.35 = bf16[512,1024]{1,0:T(8,128)(2,1)} collective-permute-done((bf16[512,1024]{1,0:T(8,128)(2,1)S(1)}, bf16[512,1024]{1,0:T(8,128)(2,1)}, u32[]{:S(2)}, u32[]{:S(2)}) %collective-permute-start.35) | collective-permute-done | bytes 1048608 | tf_op jit(solution)/shard_map/ppermute | solution.py:31
  436.0 7.2 %collective-permute-done.38 = bf16[128,1024]{0,1:T(8,128)(2,1)S(1)} collective-permute-done((bf16[128,1024]{0,1:T(8,128)(2,1)S(1)}, bf16[128,1024]{0,1:T(8,128)(2,1)S(1)}, u32[]{:S(2)}, u32[]{:S(2)}) %collective-permute-start.38) | collective-permute-done | bytes 262176 | tf_op jit(solution)/shard_map/ppermute | solution.py:31
  450.9 4.3 all-to-all-start.2
  457.5 6.5 all-to-all-done.2
  477.7 3.3 multiply_reduce_fusion
  490.9 3.1 convolution_convert_fusion.1
  494.9 18.6 %collective-permute-done.45 = bf16[512,1024]{1,0:T(8,128)(2,1)} collective-permute-done((bf16[512,1024]{1,0:T(8,128)(2,1)}, bf16[512,1024]{1,0:T(8,128)(2,1)}, u32[]{:S(2)}, u32[]{:S(2)}) %collective-permute-start.45) | collective-permute-done | bytes 1048608 | tf_op jit(solution)/shard_map/ppermute | solution.py:31
  516.1 3.0 convolution_convert_fusion
  520.9 3.5 all-to-all-start.7
  534.5 3.2 convolution_convert_fusion.4
  544.4 3.8 collective-permute-done.43
  551.8 3.5 all-to-all-start.5
  557.0 4.6 all-to-all-done.5
  562.7 3.5 all-to-all-start.8
  568.4 17.3 %collective-permute-done.48 = bf16[512,1024]{1,0:T(8,128)(2,1)} collective-permute-done((bf16[512,1024]{1,0:T(8,128)(2,1)}, bf16[512,1024]{1,0:T(8,128)(2,1)}, u32[]{:S(2)}, u32[]{:S(2)}) %collective-permute-start.48) | collective-permute-done | bytes 1048608 | tf_op jit(solution)/shard_map/ppermute | solution.py:31
  590.6 30.4 %all-to-all-done.8 = bf16[4,528,256]{2,1,0:T(8,128)(2,1)S(1)} async-done(((bf16[4,528,256]{2,1,0:T(8,128)(2,1)}), bf16[4,528,256]{2,1,0:T(8,128)(2,1)S(1)}, u32[]{:S(2)}, u32[]{:S(2)}) %all-to-all-start.8) | async-done | bytes 1081376 | tf_op jit(solution)/shard_map/all_to_all | solution.py:64
  622.1 3.7 all-to-all-start.6
  627.0 2.9 fusion.38
  630.9 18.8 %all-to-all-done.6 = bf16[4,528,256]{2,1,0:T(8,128)(2,1)S(1)} async-done(((bf16[4,528,256]{2,1,0:T(8,128)(2,1)}), bf16[4,528,256]{2,1,0:T(8,128)(2,1)S(1)}, u32[]{:S(2)}, u32[]{:S(2)}) %all-to-all-start.6) | async-done | bytes 1081376 | tf_op jit(solution)/shard_map/all_to_all | solution.py:64
  652.8 5.2 collective-permute-done.44
  661.9 24.0 %reduce-scatter.9.cloned.1.call-done = bf16[128,2048]{1,0:T(8,128)(2,1)} async-done(((bf16[512,2048]{1,0:T(8,128)(2,1)}), bf16[128,2048]{1,0:T(8,128)(2,1)}) %reduce-scatter.9.cloned.1.call-update) | async-done | bytes 524304 | tf_op jit(solution)/shard_map/reduce_scatter | solution.py:441
  692.3 8.4 %collective-permute-done.49 = bf16[128,2048]{1,0:T(8,128)(2,1)} collective-permute-done((bf16[128,2048]{1,0:T(8,128)(2,1)S(1)}, bf16[128,2048]{1,0:T(8,128)(2,1)}, u32[]{:S(2)}, u32[]{:S(2)}) %collective-permute-start.49) | collective-permute-done | bytes 524320 | tf_op jit(solution)/shard_map/ppermute | solution.py:31
  (660 shorter events, 247.0 us)
Async XLA Ops:
  10.4 28.9 %collective-permute-start.2 = (bf16[128,1024]{1,0:T(8,128)(2,1)}, bf16[128,1024]{1,0:T(8,128)(2,1)}, u32[]{:S(2)}, u32[]{:S(2)}) collective-permute-start(bf16[128,1024]{1,0:T(8,128)(2,1)} %broadcast_select_fusion.14), channel_id=1, source_target_pairs={{0,16},{16,0},{1,17},{17,1},{2,18},{18,2},{3,19},{19,3},{4,20},{20... | collective-permute-start | bytes 786440 | tf_op jit(solution)/shard_map/ppermute | solution.py:31
  13.8 60.0 %collective-permute-start.8 = (bf16[128,2048]{1,0:T(8,128)(2,1)S(1)}, bf16[128,2048]{1,0:T(8,128)(2,1)}, u32[]{:S(2)}, u32[]{:S(2)}) collective-permute-start(bf16[128,2048]{1,0:T(8,128)(2,1)S(1)} %broadcast_select_fusion.6), channel_id=1, source_target_pairs={{0,16},{16,0},{1,17},{17,1},{2,18},{18,2},{3,19},{19,3},{4,20},{20... | collective-permute-start | bytes 1572872 | tf_op jit(solution)/shard_map/ppermute | solution.py:31
  15.0 30.5 %all-to-all-start = ((bf16[4,512,256]{2,1,0:T(8,128)(2,1)}), bf16[4,512,256]{2,1,0:T(8,128)(2,1)S(1)}, u32[]{:S(2)}, u32[]{:S(2)}) async-start(bf16[4,512,256]{2,1,0:T(8,128)(2,1)} %broadcast_in_dim.223), calls=%async_computation | async-start | bytes 2097152 | tf_op jit(solution)/shard_map/all_to_all | solution.py:64
  20.4 49.3 %all-gather.8.cloned.1.call-start = ((), (), s32[]{:S(2)}) async-start(), calls=%async_computation.13 | async-start | bytes 1310720 | tf_op jit(solution)/shard_map/all_gather | solution.py:342
  47.1 9.4 %all-to-all-start.1 = ((bf16[4,128,256]{2,1,0:T(8,128)(2,1)}), bf16[4,128,256]{2,1,0:T(8,128)(2,1)S(1)}, u32[]{:S(2)}, u32[]{:S(2)}) async-start(bf16[4,128,256]{2,1,0:T(8,128)(2,1)} %bitcast.11), calls=%async_computation.1 | async-start | bytes 524288 | tf_op jit(solution)/shard_map/all_to_all | solution.py:383
  50.5 70.5 %all-gather.10.cloned.1.call-start = ((), (), s32[]{:S(2)}) async-start(), calls=%async_computation.14 | async-start | bytes 2621440 | tf_op jit(solution)/shard_map/all_gather | solution.py:343
  57.3 15.2 %collective-permute-start = (bf16[128,1024]{0,1:T(8,128)(2,1)S(1)}, bf16[128,1024]{0,1:T(8,128)(2,1)S(1)}, u32[]{:S(2)}, u32[]{:S(2)}) collective-permute-start(bf16[128,1024]{0,1:T(8,128)(2,1)S(1)} %fusion.101), channel_id=1, source_target_pairs={{0,2},{1,3},{2,0},{3,1},{4,6},{5,7},{6,4},{7,5},{8,10},{9,11},{10,... | collective-permute-start | bytes 786440 | tf_op jit(solution)/shard_map/ppermute | solution.py:31
  69.6 25.0 %collective-permute-start.3 = (bf16[512,1024]{1,0:T(8,128)(2,1)}, bf16[512,1024]{1,0:T(8,128)(2,1)S(1)}, u32[]{:S(2)}, u32[]{:S(2)}) collective-permute-start(bf16[512,1024]{1,0:T(8,128)(2,1)} %all-gather.8.cloned.1.call-done), channel_id=1, source_target_pairs={{0,16},{16,0},{1,17},{17,1},{2,18},{18,2},{3,19},{19,3},{4,20},{20... | collective-permute-start | bytes 3145736 | tf_op jit(solution)/shard_map/ppermute | solution.py:31
  76.2 143.0 %all-gather.12.cloned.1.call-start = ((), (), s32[]{:S(2)}) async-start(), calls=%async_computation.15 | async-start | bytes 1310720 | tf_op jit(solution)/shard_map/all_gather | solution.py:342
  122.7 26.1 %collective-permute-start.9 = (bf16[512,1024]{1,0:T(8,128)(2,1)S(1)}, bf16[512,1024]{1,0:T(8,128)(2,1)S(1)}, u32[]{:S(2)}, u32[]{:S(2)}) collective-permute-start(bf16[512,1024]{1,0:T(8,128)(2,1)S(1)} %get-tuple-element.149), channel_id=1, source_target_pairs={{0,16},{16,0},{1,17},{17,1},{2,18},{18,2},{3,19},{19,3},{4,20},{20... | collective-permute-start | bytes 3145736 | tf_op jit(solution)/shard_map/ppermute | solution.py:31
  126.2 43.9 %collective-permute-start.10 = (bf16[512,1024]{1,0:T(8,128)(2,1)S(1)}, bf16[512,1024]{1,0:T(8,128)(2,1)S(1)}, u32[]{:S(2)}, u32[]{:S(2)}) collective-permute-start(bf16[512,1024]{1,0:T(8,128)(2,1)S(1)} %get-tuple-element.148), channel_id=1, source_target_pairs={{0,16},{16,0},{1,17},{17,1},{2,18},{18,2},{3,19},{19,3},{4,20},{20... | collective-permute-start | bytes 3145736 | tf_op jit(solution)/shard_map/ppermute | solution.py:31
  173.9 48.5 %all-to-all-start.3 = ((bf16[4,512,256]{2,1,0:T(8,128)(2,1)}), bf16[4,512,256]{2,1,0:T(8,128)(2,1)}, u32[]{:S(2)}, u32[]{:S(2)}) async-start(bf16[4,512,256]{2,1,0:T(8,128)(2,1)} %broadcast_in_dim.235), calls=%async_computation.3 | async-start | bytes 2097152 | tf_op jit(solution)/shard_map/all_to_all | solution.py:64
  178.2 88.5 %all-gather.14.cloned.1.call-start = ((), (), s32[]{:S(2)}) async-start(), calls=%async_computation.16 | async-start | bytes 2621440 | tf_op jit(solution)/shard_map/all_gather | solution.py:343
  178.4 8.8 %collective-permute-start.12 = (bf16[128,1024]{0,1:T(8,128)(2,1)S(1)}, bf16[128,1024]{0,1:T(8,128)(2,1)S(1)}, u32[]{:S(2)}, u32[]{:S(2)}) collective-permute-start(bf16[128,1024]{0,1:T(8,128)(2,1)S(1)} %slice.1145), channel_id=1, source_target_pairs={{0,2},{1,3},{2,0},{3,1},{4,6},{5,7},{6,4},{7,5},{8,10},{9,11},{10,... | collective-permute-start | bytes 786440 | tf_op jit(solution)/shard_map/ppermute | solution.py:31
  187.8 32.9 %collective-permute-start.13 = (bf16[128,1024]{0,1:T(8,128)(2,1)S(1)}, bf16[128,1024]{0,1:T(8,128)(2,1)S(1)}, u32[]{:S(2)}, u32[]{:S(2)}) collective-permute-start(bf16[128,1024]{0,1:T(8,128)(2,1)S(1)} %fusion.115), channel_id=1, source_target_pairs={{0,2},{1,3},{2,0},{3,1},{4,6},{5,7},{6,4},{7,5},{8,10},{9,11},{10,... | collective-permute-start | bytes 786440 | tf_op jit(solution)/shard_map/ppermute | solution.py:31
  219.2 25.2 %collective-permute-start.15 = (bf16[512,1024]{1,0:T(8,128)(2,1)}, bf16[512,1024]{1,0:T(8,128)(2,1)S(1)}, u32[]{:S(2)}, u32[]{:S(2)}) collective-permute-start(bf16[512,1024]{1,0:T(8,128)(2,1)} %all-gather.12.cloned.1.call-done), channel_id=1, source_target_pairs={{0,16},{16,0},{1,17},{17,1},{2,18},{18,2},{3,19},{19,3},{4,20},{20... | collective-permute-start | bytes 3145736 | tf_op jit(solution)/shard_map/ppermute | solution.py:31
  225.4 30.3 %all-to-all-start.4 = ((bf16[4,128,256]{1,2,0:T(8,128)(2,1)}), bf16[4,128,256]{1,2,0:T(8,128)(2,1)}, u32[]{:S(2)}, u32[]{:S(2)}) async-start(bf16[4,128,256]{1,2,0:T(8,128)(2,1)} %copy.290), calls=%async_computation.4 | async-start | bytes 524288 | tf_op jit(solution)/shard_map/all_to_all | solution.py:383
  257.4 16.7 %collective-permute-start.25 = (bf16[128,1024]{0,1:T(8,128)(2,1)}, bf16[128,1024]{0,1:T(8,128)(2,1)}, u32[]{:S(2)}, u32[]{:S(2)}) collective-permute-start(bf16[128,1024]{0,1:T(8,128)(2,1)} %pad_maximum_fusion.39), channel_id=1, source_target_pairs={{0,2},{1,3},{2,0},{3,1},{4,6},{5,7},{6,4},{7,5},{8,10},{9,11},{10,... | collective-permute-start | bytes 786440 | tf_op jit(solution)/shard_map/ppermute | solution.py:31
  261.1 10.8 %collective-permute-start.17 = (bf16[128,1024]{0,1:T(8,128)(2,1)S(1)}, bf16[128,1024]{0,1:T(8,128)(2,1)S(1)}, u32[]{:S(2)}, u32[]{:S(2)}) collective-permute-start(bf16[128,1024]{0,1:T(8,128)(2,1)S(1)} %slice.1143), channel_id=1, source_target_pairs={{0,2},{1,3},{2,0},{3,1},{4,6},{5,7},{6,4},{7,5},{8,10},{9,11},{10,... | collective-permute-start | bytes 786440 | tf_op jit(solution)/shard_map/ppermute | solution.py:31
  268.4 26.1 %collective-permute-start.21 = (bf16[512,1024]{1,0:T(8,128)(2,1)S(1)}, bf16[512,1024]{1,0:T(8,128)(2,1)S(1)}, u32[]{:S(2)}, u32[]{:S(2)}) collective-permute-start(bf16[512,1024]{1,0:T(8,128)(2,1)S(1)} %get-tuple-element.146), channel_id=1, source_target_pairs={{0,16},{16,0},{1,17},{17,1},{2,18},{18,2},{3,19},{19,3},{4,20},{20... | collective-permute-start | bytes 3145736 | tf_op jit(solution)/shard_map/ppermute | solution.py:31
  275.2 40.6 %collective-permute-start.20 = (bf16[512,1024]{1,0:T(8,128)(2,1)S(1)}, bf16[512,1024]{1,0:T(8,128)(2,1)S(1)}, u32[]{:S(2)}, u32[]{:S(2)}) collective-permute-start(bf16[512,1024]{1,0:T(8,128)(2,1)S(1)} %get-tuple-element.147), channel_id=1, source_target_pairs={{0,16},{16,0},{1,17},{17,1},{2,18},{18,2},{3,19},{19,3},{4,20},{20... | collective-permute-start | bytes 3145736 | tf_op jit(solution)/shard_map/ppermute | solution.py:31
  280.6 14.6 %collective-permute-start.19 = (bf16[256,1024]{0,1:T(8,128)(2,1)S(1)}, bf16[256,1024]{0,1:T(8,128)(2,1)S(1)}, u32[]{:S(2)}, u32[]{:S(2)}) collective-permute-start(bf16[256,1024]{0,1:T(8,128)(2,1)S(1)} %pad_maximum_fusion.28), channel_id=1, source_target_pairs={{0,1},{1,0},{2,3},{3,2},{4,5},{5,4},{6,7},{7,6},{8,9},{9,8},{10,11... | collective-permute-start | bytes 1572872 | tf_op jit(solution)/shard_map/ppermute | solution.py:31
  324.0 9.2 %collective-permute-start.28 = (bf16[128,1024]{0,1:T(8,128)(2,1)S(1)}, bf16[128,1024]{0,1:T(8,128)(2,1)S(1)}, u32[]{:S(2)}, u32[]{:S(2)}) collective-permute-start(bf16[128,1024]{0,1:T(8,128)(2,1)S(1)} %slice.1141), channel_id=1, source_target_pairs={{0,2},{1,3},{2,0},{3,1},{4,6},{5,7},{6,4},{7,5},{8,10},{9,11},{10,... | collective-permute-start | bytes 786440 | tf_op jit(solution)/shard_map/ppermute | solution.py:31
  325.8 12.2 %collective-permute-start.23 = (bf16[128,1024]{0,1:T(8,128)(2,1)S(1)}, bf16[128,1024]{0,1:T(8,128)(2,1)S(1)}, u32[]{:S(2)}, u32[]{:S(2)}) collective-permute-start(bf16[128,1024]{0,1:T(8,128)(2,1)S(1)} %slice.1142), channel_id=1, source_target_pairs={{0,2},{1,3},{2,0},{3,1},{4,6},{5,7},{6,4},{7,5},{8,10},{9,11},{10,... | collective-permute-start | bytes 786440 | tf_op jit(solution)/shard_map/ppermute | solution.py:31
  357.6 8.4 %collective-permute-start.32 = (bf16[128,1024]{0,1:T(8,128)(2,1)S(1)}, bf16[128,1024]{0,1:T(8,128)(2,1)S(1)}, u32[]{:S(2)}, u32[]{:S(2)}) collective-permute-start(bf16[128,1024]{0,1:T(8,128)(2,1)S(1)} %slice.1140), channel_id=1, source_target_pairs={{0,2},{1,3},{2,0},{3,1},{4,6},{5,7},{6,4},{7,5},{8,10},{9,11},{10,... | collective-permute-start | bytes 786440 | tf_op jit(solution)/shard_map/ppermute | solution.py:31
  369.8 26.2 %collective-permute-start.36 = (bf16[512,1024]{1,0:T(8,128)(2,1)S(1)}, bf16[512,1024]{1,0:T(8,128)(2,1)S(1)}, u32[]{:S(2)}, u32[]{:S(2)}) collective-permute-start(bf16[512,1024]{1,0:T(8,128)(2,1)S(1)} %convolution_convert_fusion.6), channel_id=1, source_target_pairs={{0,16},{16,0},{1,17},{17,1},{2,18},{18,2},{3,19},{19,3},{4,20},{20... | collective-permute-start | bytes 3145736 | tf_op jit(solution)/shard_map/ppermute | solution.py:31
  371.3 45.2 %collective-permute-start.35 = (bf16[512,1024]{1,0:T(8,128)(2,1)S(1)}, bf16[512,1024]{1,0:T(8,128)(2,1)}, u32[]{:S(2)}, u32[]{:S(2)}) collective-permute-start(bf16[512,1024]{1,0:T(8,128)(2,1)S(1)} %convolution_convert_fusion.7), channel_id=1, source_target_pairs={{0,16},{16,0},{1,17},{17,1},{2,18},{18,2},{3,19},{19,3},{4,20},{20... | collective-permute-start | bytes 3145736 | tf_op jit(solution)/shard_map/ppermute | solution.py:31
  422.8 10.2 %collective-permute-start.37 = (bf16[256,1024]{0,1:T(8,128)(2,1)}, bf16[256,1024]{0,1:T(8,128)(2,1)}, u32[]{:S(2)}, u32[]{:S(2)}) collective-permute-start(bf16[256,1024]{0,1:T(8,128)(2,1)} %fusion.74), channel_id=1, source_target_pairs={{0,1},{1,0},{2,3},{3,2},{4,5},{5,4},{6,7},{7,6},{8,9},{9,8},{10,11... | collective-permute-start | bytes 1572872 | tf_op jit(solution)/shard_map/ppermute | solution.py:31
  434.4 8.8 %collective-permute-start.38 = (bf16[128,1024]{0,1:T(8,128)(2,1)S(1)}, bf16[128,1024]{0,1:T(8,128)(2,1)S(1)}, u32[]{:S(2)}, u32[]{:S(2)}) collective-permute-start(bf16[128,1024]{0,1:T(8,128)(2,1)S(1)} %slice.1139), channel_id=1, source_target_pairs={{0,2},{1,3},{2,0},{3,1},{4,6},{5,7},{6,4},{7,5},{8,10},{9,11},{10,... | collective-permute-start | bytes 786440 | tf_op jit(solution)/shard_map/ppermute | solution.py:31
  444.9 10.3 %collective-permute-start.39 = (bf16[128,1024]{0,1:T(8,128)(2,1)S(1)}, bf16[128,1024]{0,1:T(8,128)(2,1)}, u32[]{:S(2)}, u32[]{:S(2)}) collective-permute-start(bf16[128,1024]{0,1:T(8,128)(2,1)S(1)} %get-tuple-element.134), channel_id=1, source_target_pairs={{0,2},{1,3},{2,0},{3,1},{4,6},{5,7},{6,4},{7,5},{8,10},{9,11},{10,... | collective-permute-start | bytes 786440 | tf_op jit(solution)/shard_map/ppermute | solution.py:31
  446.6 24.8 %collective-permute-start.41 = (bf16[512,1024]{1,0:T(8,128)(2,1)}, bf16[512,1024]{1,0:T(8,128)(2,1)}, u32[]{:S(2)}, u32[]{:S(2)}) collective-permute-start(bf16[512,1024]{1,0:T(8,128)(2,1)} %pad_maximum_fusion.18), channel_id=1, source_target_pairs={{0,16},{16,0},{1,17},{17,1},{2,18},{18,2},{3,19},{19,3},{4,20},{20... | collective-permute-start | bytes 3145736 | tf_op jit(solution)/shard_map/ppermute | solution.py:31
  450.9 13.2 %all-to-all-start.2 = ((bf16[4,2,128,256]{3,1,2,0:T(2,128)(2,1)}), bf16[4,2,128,256]{3,1,2,0:T(2,128)(2,1)}, u32[]{:S(2)}, u32[]{:S(2)}) async-start(bf16[4,2,128,256]{3,1,2,0:T(2,128)(2,1)} %copy.289), calls=%async_computation.2 | async-start | bytes 1048576 | tf_op jit(solution)/shard_map/all_to_all | solution.py:407
  455.1 171.9 %all-gather.16.cloned.1.call-start = ((), (), s32[]{:S(2)}) async-start(), calls=%async_computation.17 | async-start | bytes 2621440 | tf_op jit(solution)/shard_map/all_gather | solution.py:409
  457.1 12.4 %collective-permute-start.40 = (bf16[256,1024]{0,1:T(8,128)(2,1)}, bf16[256,1024]{0,1:T(8,128)(2,1)}, u32[]{:S(2)}, u32[]{:S(2)}) collective-permute-start(bf16[256,1024]{0,1:T(8,128)(2,1)} %pad_maximum_fusion.34), channel_id=1, source_target_pairs={{0,1},{1,0},{2,3},{3,2},{4,5},{5,4},{6,7},{7,6},{8,9},{9,8},{10,11... | collective-permute-start | bytes 1572872 | tf_op jit(solution)/shard_map/ppermute | solution.py:31
  466.0 193.8 %reduce-scatter.7.cloned.1.call-start = ((), (), s32[]{:S(2)}) async-start(), calls=%async_computation.19 | async-start | bytes 1310720 | tf_op jit(solution)/shard_map/reduce_scatter | solution.py:441
  485.4 174.4 %reduce-scatter.5.cloned.1.call-start = ((), (), s32[]{:S(2)}) async-start(), calls=%async_computation.18 | async-start | bytes 1310720 | tf_op jit(solution)/shard_map/reduce_scatter | solution.py:441
  489.2 24.4 %collective-permute-start.45 = (bf16[512,1024]{1,0:T(8,128)(2,1)}, bf16[512,1024]{1,0:T(8,128)(2,1)}, u32[]{:S(2)}, u32[]{:S(2)}) collective-permute-start(bf16[512,1024]{1,0:T(8,128)(2,1)} %pad_maximum_fusion.19), channel_id=1, source_target_pairs={{0,16},{16,0},{1,17},{17,1},{2,18},{18,2},{3,19},{19,3},{4,20},{20... | collective-permute-start | bytes 3145736 | tf_op jit(solution)/shard_map/ppermute | solution.py:31
  520.9 13.6 %all-to-all-start.7 = ((bf16[4,144,256]{2,1,0:T(8,128)(2,1)}), bf16[4,144,256]{2,1,0:T(8,128)(2,1)S(1)}, u32[]{:S(2)}, u32[]{:S(2)}) async-start(bf16[4,144,256]{2,1,0:T(8,128)(2,1)} %copy.308), calls=%async_computation.7 | async-start | bytes 589824 | tf_op jit(solution)/shard_map/all_to_all | solution.py:422
  524.3 137.6 %reduce-scatter.11.cloned.1.call-start = ((), (), s32[]{:S(2)}) async-start(), calls=%async_computation.21 | async-start | bytes 2621440 | tf_op jit(solution)/shard_map/reduce_scatter | solution.py:441
  537.7 28.6 %collective-permute-start.47 = (bf16[512,1024]{1,0:T(8,128)(2,1)}, bf16[512,1024]{1,0:T(8,128)(2,1)}, u32[]{:S(2)}, u32[]{:S(2)}) collective-permute-start(bf16[512,1024]{1,0:T(8,128)(2,1)} %convolution_convert_fusion.4), channel_id=1, source_target_pairs={{0,16},{16,0},{1,17},{17,1},{2,18},{18,2},{3,19},{19,3},{4,20},{20... | collective-permute-start | bytes 3145736 | tf_op jit(solution)/shard_map/ppermute | solution.py:31
  543.4 42.2 %collective-permute-start.48 = (bf16[512,1024]{1,0:T(8,128)(2,1)}, bf16[512,1024]{1,0:T(8,128)(2,1)}, u32[]{:S(2)}, u32[]{:S(2)}) collective-permute-start(bf16[512,1024]{1,0:T(8,128)(2,1)} %convolution_convert_fusion.2), channel_id=1, source_target_pairs={{0,16},{16,0},{1,17},{17,1},{2,18},{18,2},{3,19},{19,3},{4,20},{20... | collective-permute-start | bytes 3145736 | tf_op jit(solution)/shard_map/ppermute | solution.py:31
  551.8 9.8 %all-to-all-start.5 = ((bf16[4,144,256]{2,1,0:T(8,128)(2,1)}), bf16[4,144,256]{2,1,0:T(8,128)(2,1)S(1)}, u32[]{:S(2)}, u32[]{:S(2)}) async-start(bf16[4,144,256]{2,1,0:T(8,128)(2,1)} %copy.301), calls=%async_computation.5 | async-start | bytes 589824 | tf_op jit(solution)/shard_map/all_to_all | solution.py:422
  562.7 58.3 %all-to-all-start.8 = ((bf16[4,528,256]{2,1,0:T(8,128)(2,1)}), bf16[4,528,256]{2,1,0:T(8,128)(2,1)S(1)}, u32[]{:S(2)}, u32[]{:S(2)}) async-start(bf16[4,528,256]{2,1,0:T(8,128)(2,1)} %broadcast_in_dim.238), calls=%async_computation.8 | async-start | bytes 2162688 | tf_op jit(solution)/shard_map/all_to_all | solution.py:64
  566.2 119.7 %reduce-scatter.9.cloned.1.call-start = ((), (), s32[]{:S(2)}) async-start(), calls=%async_computation.20 | async-start | bytes 2621440 | tf_op jit(solution)/shard_map/reduce_scatter | solution.py:441
  622.1 27.6 %all-to-all-start.6 = ((bf16[4,528,256]{2,1,0:T(8,128)(2,1)}), bf16[4,528,256]{2,1,0:T(8,128)(2,1)S(1)}, u32[]{:S(2)}, u32[]{:S(2)}) async-start(bf16[4,528,256]{2,1,0:T(8,128)(2,1)} %broadcast_in_dim.237), calls=%async_computation.6 | async-start | bytes 2162688 | tf_op jit(solution)/shard_map/all_to_all | solution.py:64
  630.0 21.9 %collective-permute-start.24 = (bf16[512,256]{1,0:T(8,128)(2,1)S(1)}, bf16[512,256]{1,0:T(8,128)(2,1)S(1)}, u32[]{:S(2)}, u32[]{:S(2)}) collective-permute-start(bf16[512,256]{1,0:T(8,128)(2,1)S(1)} %broadcast_select_fusion.19), channel_id=1, source_target_pairs={{0,16},{16,0},{1,17},{17,1},{2,18},{18,2},{3,19},{19,3},{4,20},{20... | collective-permute-start | bytes 786440 | tf_op jit(solution)/shard_map/ppermute | solution.py:31
  660.8 28.9 %collective-permute-start.46 = (bf16[128,1024]{1,0:T(8,128)(2,1)S(1)}, bf16[128,1024]{1,0:T(8,128)(2,1)S(1)}, u32[]{:S(2)}, u32[]{:S(2)}) collective-permute-start(bf16[128,1024]{1,0:T(8,128)(2,1)S(1)} %broadcast_select_fusion.10), channel_id=1, source_target_pairs={{0,16},{16,0},{1,17},{17,1},{2,18},{18,2},{3,19},{19,3},{4,20},{20... | collective-permute-start | bytes 786440 | tf_op jit(solution)/shard_map/ppermute | solution.py:31
  687.0 13.7 %collective-permute-start.49 = (bf16[128,2048]{1,0:T(8,128)(2,1)S(1)}, bf16[128,2048]{1,0:T(8,128)(2,1)}, u32[]{:S(2)}, u32[]{:S(2)}) collective-permute-start(bf16[128,2048]{1,0:T(8,128)(2,1)S(1)} %broadcast_select_fusion.2), channel_id=1, source_target_pairs={{0,16},{16,0},{1,17},{17,1},{2,18},{18,2},{3,19},{19,3},{4,20},{20... | collective-permute-start | bytes 1572872 | tf_op jit(solution)/shard_map/ppermute | solution.py:31
  (154 other events, 1337.7 us)
Sparse Core Ops, SparseCore 0:
  41.3 28.2 all-gather.7
  76.3 44.6 all-gather.9
  171.9 47.2 all-gather.11
  222.5 44.1 all-gather.13
  466.1 43.0 all-gather.15
  511.9 25.8 reduce-scatter.6
  540.2 25.7 reduce-scatter.4
  568.3 60.5 reduce-scatter.10
  631.3 54.5 reduce-scatter.8

commit v3 on v2

v3 whole, which is shorter than its diff:
```python
import jax
import jax.numpy as jnp
from jax import lax
from jax.sharding import PartitionSpec as P

HEAD_DIM = 64
epsilon = 1e-05
masked_score = -1e30
F32 = jnp.float32
BF16 = jnp.bfloat16
PLANE = ("section", "col")


def mm(a, b, dims):
    return lax.dot_general(a, b, ((dims[0], dims[1]), ((), ())), preferred_element_type=F32)


def nn(a, b):
    return mm(a, b, ((1,), (0,)))


def nt(a, b):
    return mm(a, b, ((1,), (1,)))


def tn(a, b):
    return mm(a, b, ((0,), (0,)))


def plane_size():
    return lax.axis_size("section") * lax.axis_size("col")


def send(array, mask):
    return lax.ppermute(array, PLANE, [(i, i ^ mask) for i in range(plane_size())])


def far_masks():
    return list(range(2, plane_size(), 2))


def spread_order():
    near = [0] + far_masks()
    return near + [m ^ 1 for m in near]


def spread(own):
    near = jnp.concatenate([own] + [send(own, m) for m in far_masks()], axis=1)
    return jnp.concatenate([near, send(near, 1)], axis=1)


def sum_up(partial):
    half = partial.shape[1] // 2
    masks = far_masks()
    size = half // (len(masks) + 1)
    near = partial[:, :half] + send(partial[:, half:].astype(BF16), 1).astype(F32)
    total = near[:, :size]
    for i, m in enumerate(masks):
        total = total + send(near[:, (i + 1) * size : (i + 2) * size].astype(BF16), m).astype(F32)
    return total


def gather_direct(array):
    count = lax.axis_size("row")
    copies = jnp.broadcast_to(array[None], (count,) + array.shape)
    return lax.all_to_all(copies, "row", split_axis=0, concat_axis=0)


def owned_layout(lengths, deal, holder, rows_dev):
    starts = jnp.cumsum(lengths) - lengths
    first = deal == 2 * holder
    second = deal == 2 * holder + 1
    first_len = jnp.sum(jnp.where(first, lengths, 0))
    second_len = jnp.sum(jnp.where(second, lengths, 0))
    first_start = jnp.sum(jnp.where(first, starts, 0))
    second_start = jnp.sum(jnp.where(second, starts, 0))
    slots = jnp.arange(rows_dev, dtype=jnp.int32)
    in_first = slots < first_len
    in_second = jnp.logical_and(jnp.logical_not(in_first), slots < first_len + second_len)
    usable = jnp.logical_or(in_first, in_second)
    position = jnp.where(in_first, slots, slots - first_len)
    source = jnp.where(in_first, first_start + slots, second_start + position)
    source = jnp.where(usable, source, -1)
    segment = jnp.where(in_first, 0, jnp.where(in_second, 1, 2)).astype(jnp.int32)
    return source, usable, segment, position


def given_targets(lengths, deal, positions, rows_dev):
    starts = jnp.cumsum(lengths) - lengths
    before = deal[None, :] == (deal - 1)[:, None]
    partner_len = jnp.sum(jnp.where(before, lengths[None, :], 0), axis=1)
    offset = jnp.where(deal % 2 == 1, partner_len, 0)
    base = deal // 2 * rows_dev + offset - starts
    inside = jnp.logical_and(
        positions[:, None] >= starts[None, :], positions[:, None] < (starts + lengths)[None, :]
    )
    target = jnp.sum(jnp.where(inside, base[None, :] + positions[:, None], 0), axis=1)
    return jnp.where(jnp.any(inside, axis=1), target, -1)


def pick_rows(rows, wanted):
    onehot = (wanted[:, None] == jnp.arange(rows.shape[0], dtype=jnp.int32)[None, :]).astype(BF16)
    return nn(onehot, rows)


def normalize(hidden, gain, shift):
    average = jnp.mean(hidden, axis=-1, keepdims=True)
    square = jnp.mean(hidden * hidden, axis=-1, keepdims=True)
    inverse = lax.rsqrt(square - average * average + epsilon)
    centered = (hidden - average) * inverse
    return centered, inverse, (centered * gain + shift).astype(BF16)


def norm_backward(grad_norm, centered, inverse, gain):
    grad_cent = grad_norm * gain
    summed = jnp.mean(grad_cent, axis=-1, keepdims=True)
    cross = jnp.mean(grad_cent * centered, axis=-1, keepdims=True)
    grad_hidden = inverse * (grad_cent - summed - centered * cross)
    return grad_hidden, jnp.sum(grad_norm * centered, axis=(0, 1)), jnp.sum(grad_norm, axis=(0, 1))


def gelu_tanh(values):
    return jax.nn.gelu(values, approximate=True)


def masked_scores(queries, key_rows, segment, position, slopes):
    scores = jnp.einsum(
        "mqhe,mkhe->mhqk", queries, key_rows, preferred_element_type=F32
    ) * HEAD_DIM ** (-0.5)
    distance = (position[:, :, None] - position[:, None, :]).astype(F32)
    allowed = jnp.logical_and(
        segment[:, :, None] == segment[:, None, :],
        jnp.logical_and(segment[:, :, None] < 2, distance >= 0),
    )
    scores = scores - slopes[:, None, None] * distance[:, None]
    return jnp.where(allowed[:, None], scores, masked_score)


def attend_forward(queries, key_rows, value_rows, segment, position, slopes):
    scores = masked_scores(queries, key_rows, segment, position, slopes)
    highest = jnp.max(scores, axis=3, keepdims=True)
    exp_scores = jnp.exp(scores - highest)
    summed = jnp.sum(exp_scores, axis=3, keepdims=True)
    soft = (exp_scores / summed).astype(BF16)
    mixed = jnp.einsum("mhqk,mkhe->mqhe", soft, value_rows, preferred_element_type=F32)
    return mixed.reshape(mixed.shape[:2] + (-1,)).astype(BF16), highest + jnp.log(summed)


def attend_backward(queries, key_rows, value_rows, segment, position, slopes, logsum, grad_mixed):
    scale = HEAD_DIM ** (-0.5)
    flat = queries.shape[:2] + (-1,)
    scores = masked_scores(queries, key_rows, segment, position, slopes)
    soft = jnp.exp(scores - logsum)
    grad_prob = jnp.einsum("mqhe,mkhe->mhqk", grad_mixed, value_rows, preferred_element_type=F32)
    row_dot = jnp.sum(soft * grad_prob, axis=3, keepdims=True)
    grad_score = (soft * (grad_prob - row_dot)).astype(BF16)
    grad_query = (
        jnp.einsum("mhqk,mkhe->mqhe", grad_score, key_rows, preferred_element_type=F32) * scale
    )
    grad_key = (
        jnp.einsum("mhqk,mqhe->mkhe", grad_score, queries, preferred_element_type=F32) * scale
    )
    grad_value = jnp.einsum(
        "mhqk,mqhe->mkhe", soft.astype(BF16), grad_mixed, preferred_element_type=F32
    )
    return jnp.concatenate(
        [g.astype(BF16).reshape(flat) for g in (grad_query, grad_key, grad_value)], axis=2
    )


def rows_of(array):
    return array.reshape(-1, array.shape[-1])


def layer_forward(hidden, layout, weights, small):
    usable, segment, position, slopes = layout
    attn_w, up_w, down_w = weights
    width = attn_w.shape[1] // 4
    gain, shift, bias_q, bias_v, bias_out, bias_down, up_bias = small
    centered, inverse, normed = normalize(hidden, gain[0], shift[0])
    rows_all = spread(normed)
    micro, tokens, model = rows_all.shape
    heads = (micro, tokens, -1, HEAD_DIM)
    qkv = nn(rows_of(rows_all), attn_w[:, : 3 * width]).reshape(micro, tokens, -1)
    queries = (qkv[:, :, :width] + bias_q).astype(BF16).reshape(heads)
    key_rows = qkv[:, :, width : 2 * width].astype(BF16).reshape(heads)
    value_rows = (qkv[:, :, 2 * width :] + bias_v).astype(BF16).reshape(heads)
    attended, logsum = attend_forward(queries, key_rows, value_rows, segment, position, slopes)
    branch = sum_up(nt(rows_of(attended), attn_w[:, 3 * width :]).reshape(micro, tokens, model))
    middle = hidden + branch + bias_out
    centered_two, inverse_two, normed_two = normalize(middle, gain[1], shift[1])
    rows_two = spread(normed_two)
    upper_in = nn(rows_of(rows_two), up_w) + up_bias
    activated = gelu_tanh(upper_in).astype(BF16)
    down_out = sum_up(nt(activated, down_w).reshape(micro, tokens, model)) + bias_down
    result = jnp.where(usable[:, :, None], middle + down_out, 0.0)
    attn_stored = (centered, inverse, rows_all, queries, key_rows, value_rows, logsum, attended)
    ffn_stored = (centered_two, inverse_two, rows_two, upper_in, activated)
    return result, attn_stored, ffn_stored


def ffn_backward(grad_out, weights, small, stored):
    _, up_w, down_w = weights
    gain = small[0]
    centered, inverse, rows_two, upper_in, activated = stored
    grad_down = grad_out.astype(BF16)
    down_all = spread(grad_down)
    grad_act = nn(rows_of(down_all), down_w)
    grad_upper = jax.vjp(gelu_tanh, upper_in)[1](grad_act)[0].astype(BF16)
    grad_norm = sum_up(nt(grad_upper, up_w).reshape(down_all.shape))
    term = jnp.concatenate(
        [
            tn(rows_of(rows_two), grad_upper).astype(BF16),
            tn(rows_of(down_all), activated).astype(BF16),
        ],
        axis=1,
    )
    grad_mid, gain_sum, shift_sum = norm_backward(grad_norm, centered, inverse, gain[1])
    token_sums = [gain_sum, shift_sum, jnp.sum(grad_down, axis=(0, 1), dtype=F32)]
    return grad_out + grad_mid, term, token_sums, jnp.sum(grad_upper, axis=0, dtype=F32)


def attn_backward(grad_mid, layout, weights, small, stored):
    usable, segment, position, slopes = layout
    attn_w = weights[0]
    width = attn_w.shape[1] // 4
    gain = small[0]
    centered, inverse, rows_all, queries, key_rows, value_rows, logsum, attended = stored
    grad_branch = grad_mid.astype(BF16)
    branch_all = spread(grad_branch)
    grad_attended = nn(rows_of(branch_all), attn_w[:, 3 * width :]).astype(BF16)
    grad_qkv = attend_backward(
        queries,
        key_rows,
        value_rows,
        segment,
        position,
        slopes,
        logsum,
        grad_attended.reshape(queries.shape),
    )
    grad_qkv = rows_of(grad_qkv)
    grad_norm = sum_up(nt(grad_qkv, attn_w[:, : 3 * width]).reshape(branch_all.shape))
    term = jnp.concatenate(
        [
            tn(rows_of(rows_all), grad_qkv).astype(BF16),
            tn(rows_of(branch_all), rows_of(attended)).astype(BF16),
        ],
        axis=1,
    )
    grad_in, gain_sum, shift_sum = norm_backward(grad_norm, centered, inverse, gain[0])
    token_sums = [gain_sum, shift_sum, jnp.sum(grad_branch, axis=(0, 1), dtype=F32)]
    qkv_sums = jnp.sum(grad_qkv, axis=0, dtype=F32)
    column_sums = jnp.concatenate([qkv_sums[:width], qkv_sums[2 * width :]])
    return grad_mid + grad_in, term, token_sums, column_sums


def on_device(
    inputs,
    cotangent,
    lengths,
    deal,
    query_key_value_weight,
    out_weight,
    up_weight,
    down_weight,
    norm_gain,
    norm_shift,
    proj_bias,
    up_bias,
):
    section = lax.axis_index("section")
    holder = lax.axis_index("row")
    column = lax.axis_index("col")
    cols_count = lax.axis_size("col")
    micro_count, rows_dev, width = inputs.shape
    model = width * cols_count
    count = plane_size()
    place = section * cols_count + column
    tokens = rows_dev // count
    block = query_key_value_weight.shape[1]
    half = width // 2
    heads_dev = half // HEAD_DIM
    hidden_half = up_weight.shape[2] // 2
    is_zero = section == 0

    def pick(zero, one):
        return jnp.where(is_zero, zero, one)

    def halves(array, axis):
        size = array.shape[axis] // 2
        return (
            lax.slice_in_dim(array, 0, size, axis=axis),
            lax.slice_in_dim(array, size, 2 * size, axis=axis),
        )

    attn_parts = [
        jnp.concatenate([q.reshape(block, 3 * half), o.T], axis=1)
        for q, o in zip(halves(query_key_value_weight[0], 2), halves(out_weight[0], 0))
    ]
    ffn_parts = [
        jnp.concatenate([u, d.T], axis=1)
        for u, d in zip(halves(up_weight[0], 1), halves(down_weight[0], 0))
    ]

    def both_layers(parts):
        kept, given = pick(parts[0], parts[1]), pick(parts[1], parts[0])
        came = send(given, cols_count)
        return pick(kept, came), pick(came, kept)

    attn_pieces = both_layers(attn_parts)
    ffn_pieces = both_layers(ffn_parts)

    def gather_weights(layer):
        attn = lax.all_gather(attn_pieces[layer], "row", axis=0, tiled=True)
        ffn = lax.all_gather(ffn_pieces[layer], "row", axis=0, tiled=True)
        return attn, ffn[:, :hidden_half], ffn[:, hidden_half:]

    mine_small = jnp.concatenate(
        [norm_gain[0], norm_shift[0], proj_bias[0], up_bias[0].reshape(-1, width)], axis=0
    )
    all_small = lax.all_gather(mine_small, PLANE, axis=0, tiled=False)
    all_small = all_small.reshape((2, cols_count) + mine_small.shape)

    def layer_small(layer):
        table = all_small[layer]
        whole = jnp.transpose(table[:, :8], (1, 0, 2)).reshape(8, model)
        own = lax.dynamic_index_in_dim(table, column, axis=0, keepdims=False)
        own_half = pick(own[:, :half], own[:, half:])
        hidden = own[8:].reshape(2, hidden_half)
        return (
            whole[0:2],
            whole[2:4],
            own_half[4],
            own_half[5],
            whole[6],
            whole[7],
            pick(hidden[0], hidden[1]),
        )

    source, usable, segment, position = jax.vmap(owned_layout, (0, 0, None, None))(
        lengths, deal, holder, rows_dev
    )
    source = pick(source[0], source[1])
    order = jnp.bitwise_xor(place, jnp.array(spread_order(), jnp.int32))

    def in_spread_order(values):
        values = values.reshape(micro_count, count, tokens)
        return jnp.take(values, order, axis=1).reshape(micro_count, rows_dev)

    own_usable = lax.dynamic_index_in_dim(
        usable.reshape(micro_count, count, tokens), place, axis=1, keepdims=False
    )
    head_ids = (
        column * (2 * heads_dev) + section * heads_dev + jnp.arange(heads_dev, dtype=jnp.int32)
    )
    slopes = jnp.exp2(-8.0 * (head_ids.astype(F32) + 1.0) / (model // HEAD_DIM))
    layout = (own_usable, in_spread_order(segment), in_spread_order(position), slopes)

    def deal_rows(array):
        portion = gather_direct(pick(array[0], array[1])).reshape(-1, width)
        owned = pick_rows(portion, source).astype(BF16)
        own = lax.all_to_all(
            owned.reshape(count, tokens, width), PLANE, split_axis=0, concat_axis=0
        )
        own = own.reshape(micro_count, cols_count, tokens, width)
        return jnp.transpose(own, (0, 2, 1, 3)).reshape(micro_count, tokens, model)

    first_rows = deal_rows(inputs)
    weights = [gather_weights(0), gather_weights(1)]
    smalls = [layer_small(0), layer_small(1)]

    hidden_zero, attn_zero, ffn_zero = layer_forward(
        first_rows.astype(F32), layout, weights[0], smalls[0]
    )
    middle_in = hidden_zero.astype(BF16)
    hidden_one, attn_one, ffn_one = layer_forward(
        middle_in.astype(F32), layout, weights[1], smalls[1]
    )
    last_out = hidden_one.astype(BF16)

    positions = holder * rows_dev + jnp.arange(rows_dev, dtype=jnp.int32)
    targets = given_targets(lengths[section], deal[section], positions, rows_dev)

    def to_columns(own):
        parts = own.reshape(micro_count, tokens, cols_count, width)
        return jnp.transpose(parts, (0, 2, 1, 3)).reshape(count, tokens, width)

    both = jnp.concatenate([to_columns(middle_in), to_columns(last_out)], axis=2)
    both = lax.all_to_all(both, PLANE, split_axis=0, concat_axis=0).reshape(rows_dev, 2 * width)
    both = lax.all_gather(both, "row", axis=0, tiled=True)
    both = pick_rows(both, targets).astype(BF16)
    stays = pick(both[:, :width], both[:, width:])
    comes = send(pick(both[:, width:], both[:, :width]), cols_count)
    hidden_out = jnp.stack([pick(stays, comes), pick(comes, stays)])

    extra = 16

    def rows_and_sums(grad_in, token_sums, column_sums):
        sums = jnp.stack(token_sums).reshape(-1, cols_count, width)
        lanes = sums.shape[0]
        sums = jnp.pad(jnp.transpose(sums, (1, 0, 2)), ((0, 0), (0, extra - lanes), (0, 0)))
        sums = jnp.concatenate([sums.astype(BF16)] * micro_count, axis=0)
        got = lax.all_to_all(
            jnp.concatenate([to_columns(grad_in), sums], axis=1),
            PLANE,
            split_axis=0,
            concat_axis=0,
        )
        sums = jnp.sum(got[:, tokens : tokens + lanes].astype(F32), axis=0)
        sums = jnp.concatenate([sums, jnp.concatenate(column_sums).reshape(-1, width)], axis=0)
        sums = jnp.pad(sums, ((0, extra - sums.shape[0]), (0, 0)))
        rows = jnp.concatenate([got[:, :tokens].reshape(rows_dev, width), sums.astype(BF16)], axis=0)
        all_rows = gather_direct(rows)
        picked = pick_rows(all_rows[:, :rows_dev].reshape(-1, width), targets)
        return jnp.concatenate([picked, jnp.sum(all_rows[:, rows_dev:].astype(F32), axis=0)], axis=0)

    def reduce_rows(total):
        return lax.psum_scatter(total, "row", scatter_dimension=0, tiled=True)

    grad_one = deal_rows(cotangent).astype(F32)
    grad_mid, term, sums_a, up_sum = ffn_backward(grad_one, weights[1], smalls[1], ffn_one)
    ffn_term_one = reduce_rows(term)
    grad_one_in, term, sums_b, qv_sum = attn_backward(
        grad_mid, layout, weights[1], smalls[1], attn_one
    )
    attn_term_one = reduce_rows(term)
    grad_one_in = grad_one_in.astype(BF16)
    back_one = rows_and_sums(
        grad_one_in,
        [sums_b[0], sums_a[0], sums_b[1], sums_a[1], sums_b[2], sums_a[2]],
        [qv_sum, up_sum],
    )
    grad_zero = jnp.where(own_usable[:, :, None], grad_one_in, jnp.zeros_like(grad_one_in))
    grad_mid, term, sums_a, up_sum = ffn_backward(
        grad_zero.astype(F32), weights[0], smalls[0], ffn_zero
    )
    ffn_term_zero = reduce_rows(term)
    grad_zero_in, term, sums_b, qv_sum = attn_backward(
        grad_mid, layout, weights[0], smalls[0], attn_zero
    )
    attn_term_zero = reduce_rows(term)
    back_zero = rows_and_sums(
        grad_zero_in.astype(BF16),
        [sums_b[0], sums_a[0], sums_b[1], sums_a[1], sums_b[2], sums_a[2]],
        [qv_sum, up_sum],
    )

    def both_halves(zero, one):
        mine = pick(zero, one)
        other = send(pick(one, zero), cols_count)
        return pick(mine, other).astype(F32), pick(other, mine).astype(F32)

    attn_grad = jnp.stack(
        [g.reshape(block, 4, half) for g in both_halves(attn_term_zero, attn_term_one)], axis=2
    ).reshape(block, 4, width)
    ffn_grad = both_halves(ffn_term_zero, ffn_term_one)
    up_grad = jnp.concatenate([g[:, :hidden_half] for g in ffn_grad], axis=1)
    down_grad = jnp.concatenate([g[:, hidden_half:].T for g in ffn_grad], axis=0)

    stays = pick(back_zero, back_one)
    comes = send(pick(back_one, back_zero).astype(BF16), cols_count).astype(F32)
    kept, came = stays[:rows_dev], comes[:rows_dev]
    in_grad = jnp.stack([pick(kept, came), pick(came, kept)])
    sums = stays[rows_dev:]
    kept, came = sums[6:].reshape(-1), comes[rows_dev + 6 :].reshape(-1)
    first, second = pick(kept, came), pick(came, kept)
    bias_grad = jnp.stack(
        [
            jnp.concatenate([first[:half], second[:half]]),
            jnp.concatenate([first[half:width], second[half:width]]),
            sums[4],
            sums[5],
        ]
    )
    up_sums = jnp.concatenate(
        [first[width : width + hidden_half], second[width : width + hidden_half]]
    )
    return (
        hidden_out[None],
        in_grad[None],
        attn_grad[:, :3][None],
        attn_grad[:, 3].T[None],
        up_grad[None],
        down_grad[None],
        sums[0:2][None],
        sums[2:4][None],
        bias_grad[None],
        up_sums[None],
    )


def solution(mesh):
    placed = (
        P(None, "row", "col"),
        P(None, "row", "col"),
        P(),
        P(),
        P("section", "row", None, "col"),
        P("section", "col", "row"),
        P("section", "row", "col"),
        P("section", "col", "row"),
        P("section", None, "col"),
        P("section", None, "col"),
        P("section", None, "col"),
        P("section", "col"),
    )
    return jax.shard_map(
        on_device,
        mesh=mesh,
        in_specs=placed,
        out_specs=(
            P("section", None, "row", "col"),
            P("section", None, "row", "col"),
            P("section", "row", None, "col"),
            P("section", "col", "row"),
            P("section", "row", "col"),
            P("section", "col", "row"),
            P("section", None, "col"),
            P("section", None, "col"),
            P("section", None, "col"),
            P("section", "col"),
        ),
        check_vma=False,
    )
```

time: 718 us -> 658 us (0.916)
  waiting for transfers between devices: 393 us -> 270 us
  local copies, waits for them, and re-layouts: 53.1 us -> 97.8 us
  starting transfers between devices: 83.4 us -> 101 us
    ppermute x50 -> x70, waiting for transfers between devices: 253 us -> 180 us  [send(): lax.ppermute(array, PLANE, [(i, i ^ mask) for i in range(plane_size())])]
    reduce_scatter x4, waiting for transfers between devices: 24 us -> 0.07 us  [reduce_rows(): return lax.psum_scatter(total, 'row', scatter_dimension=0, tiled=True)]
    ppermute x50 -> x70, starting transfers between devices: 46.5 us -> 64.7 us  [send(): lax.ppermute(array, PLANE, [(i, i ^ mask) for i in range(plane_size())])]
    unnamed x282 -> x336, local copies, waits for them, and re-layouts: 24.5 us -> 42.6 us
    all_gather x4, waiting for transfers between devices: 47.9 us -> 32.1 us  [the longest x2 24.2 us: gather_weights(): attn = lax.all_gather(attn_pieces[layer], 'row', axis=0, tiled=True)]
    all_to_all x4, waiting for transfers between devices: 50.5 us -> 34.8 us  [gather_direct(): return lax.all_to_all(copies, 'row', split_axis=0, concat_axis=0)]
    concatenate x4 -> x16, local copies, waits for them, and re-layouts: 4.74 us -> 19.1 us  [the longest x8 10.7 us: spread(): return jnp.concatenate([near, send(near, 1)], axis=1)]
    convert_element_type x16 -> x7, other arithmetic: 12.7 us -> 0.74 us  [the longest x2 0.25 us: layer_forward(): queries = (qkv[:, :, :width] + bias_q).astype(BF16).reshape(heads)]
  transfers between devices with their start and end apart: 68 -> 88, of which waited for: 40 -> 59; matrix products, arithmetic and copies ran while one was open for 23% -> 30% of each run, Pallas kernels for 0% -> 0%
where the time goes in v3:
time: 658 us; the launch traced here: 648 us
  waiting for transfers between devices  270 us (41%)
  starting transfers between devices  101 us (15%)
  local copies, waits for them, and re-layouts  97.8 us (15%)
  matrix products  83.4 us (13%)
  other arithmetic  69.3 us (11%)
  between operations  17 us (3%)
  blocking collectives  9.2 us (1%)
    ppermute x70, waiting for transfers between devices, send(): lax.ppermute(array, PLANE, [(i, i ^ mask) for i in range(plane_size())])  180 us
    ppermute x70, starting transfers between devices, send(): lax.ppermute(array, PLANE, [(i, i ^ mask) for i in range(plane_size())])  64.7 us
    dot_general x29, matrix products, mm(): lax.dot_general(a, b, ((dims[0], dims[1]), ((), ())), preferred_element_t...  59 us
    unnamed x336, local copies, waits for them, and re-layouts  42.6 us
    all_to_all x4, waiting for transfers between devices, gather_direct(): return lax.all_to_all(copies, 'row', split_axis=0, concat_axis=0)  34.8 us
    all_gather x2, waiting for transfers between devices, gather_weights(): attn = lax.all_gather(attn_pieces[layer], 'row', axis=0, tiled=True)  24.2 us
    all_to_all x4, starting transfers between devices, gather_direct(): return lax.all_to_all(copies, 'row', split_axis=0, concat_axis=0)  17.2 us
    another operation x13, other arithmetic  15 us
  transfers between devices with their start and end apart: 88, of which 59 were waited for; matrix products, arithmetic and copies ran while one was open for 30% of the time, Pallas kernels for 0%

profile of v3, /device:TPU:0, one launch (start us, length us, event | category | flops | bytes accessed | tf_op | source)
XLA Modules:
  0.0 647.8 jit_solution(11926431967646890735)
XLA Ops:
  14.4 4.9 all-to-all-start
  22.2 9.2 %all-gather.1 = f32[8,12,256]{2,1,0:T(8,128)S(1)} all-gather(f32[1,12,256]{2,1,0:T(8,128)S(1)} %maximum_bitcast_fusion.4), channel_id=2, replica_groups=mesh['section'=2,'row'=4,'col'=4] {'section','col'}, dimensions={0}, use_global_device_ids=true | all-gather | bytes 110592 | tf_op jit(solution)/shard_map/all_gather | solution.py:322
  32.6 12.1 %all-to-all-done = bf16[4,512,256]{2,1,0:T(8,128)(2,1)S(1)} async-done(((bf16[4,512,256]{2,1,0:T(8,128)(2,1)}), bf16[4,512,256]{2,1,0:T(8,128)(2,1)S(1)}, u32[]{:S(2)}, u32[]{:S(2)}) %all-to-all-start) | async-done | bytes 1048608 | tf_op jit(solution)/shard_map/all_to_all | solution.py:66
  46.3 3.4 all-to-all-start.1
  51.1 5.5 all-to-all-done.1
  64.5 4.7 collective-permute-done.2
  69.2 3.7 collective-permute-done.1
  81.8 10.3 %all-gather.8.cloned.1.call-done = bf16[1024,512]{0,1:T(8,128)(2,1)} async-done(((bf16[256,512]{0,1:T(8,128)(2,1)}), bf16[1024,512]{0,1:T(8,128)(2,1)}) %all-gather.8.cloned.1.call-update) | async-done | bytes 1048592 | tf_op jit(solution)/shard_map/all_gather | solution.py:315
  105.0 12.9 %collective-permute-done.13 = bf16[256,1024]{0,1:T(8,128)(2,1)S(1)} collective-permute-done((bf16[256,1024]{0,1:T(8,128)(2,1)S(1)}, bf16[256,1024]{0,1:T(8,128)(2,1)S(1)}, u32[]{:S(2)}, u32[]{:S(2)}) %collective-permute-start.13) | collective-permute-done | bytes 524320 | tf_op jit(solution)/shard_map/ppermute | solution.py:35
  125.3 5.8 collective-permute-done.6
  131.1 4.3 collective-permute-done.8
  141.5 5.6 collective-permute-done.11
  156.0 7.9 %all-gather.10.cloned.1.call-done = bf16[1024,1024]{0,1:T(8,128)(2,1)} async-done(((bf16[256,1024]{0,1:T(8,128)(2,1)}), bf16[1024,1024]{0,1:T(8,128)(2,1)}) %all-gather.10.cloned.1.call-update) | async-done | bytes 2097168 | tf_op jit(solution)/shard_map/all_gather | solution.py:316
  181.0 5.5 collective-permute-done.15
  186.6 5.9 collective-permute-done.17
  198.6 6.4 collective-permute-done.20
  210.9 4.2 all-to-all-start.3
  222.3 13.9 %all-gather.12.cloned.1.call-done = bf16[1024,512]{0,1:T(8,128)(2,1)} async-done(((bf16[256,512]{0,1:T(8,128)(2,1)}), bf16[1024,512]{0,1:T(8,128)(2,1)}) %all-gather.12.cloned.1.call-update) | async-done | bytes 1048592 | tf_op jit(solution)/shard_map/all_gather | solution.py:315
  251.8 3.4 all-to-all-start.4
  255.8 6.3 all-to-all-done.4
  277.3 5.5 collective-permute-done.23
  282.7 4.7 collective-permute-done.25
  292.1 6.7 %collective-permute-done.28 = bf16[2,64,1024]{2,1,0:T(8,128)(2,1)S(1)} collective-permute-done((bf16[2,64,1024]{2,1,0:T(8,128)(2,1)S(1)}, bf16[2,64,1024]{2,1,0:T(8,128)(2,1)S(1)}, u32[]{:S(2)}, u32[]{:S(2)}) %collective-permute-start.28) | collective-permute-done | bytes 262176 | tf_op jit(solution)/shard_map/ppermute | solution.py:35
  326.9 5.1 collective-permute-done.42
  337.3 5.5 collective-permute-done.33
  348.7 6.6 %collective-permute-done.45 = bf16[2,64,1024]{2,1,0:T(8,128)(2,1)S(1)} collective-permute-done((bf16[2,64,1024]{2,1,0:T(8,128)(2,1)S(1)}, bf16[2,64,1024]{2,1,0:T(8,128)(2,1)S(1)}, u32[]{:S(2)}, u32[]{:S(2)}) %collective-permute-start.45) | collective-permute-done | bytes 262176 | tf_op jit(solution)/shard_map/ppermute | solution.py:35
  355.3 3.6 collective-permute-done.44
  361.0 4.2 all-to-all-start.2
  369.1 5.8 all-to-all-done.2
  383.3 3.9 fusion.43
  391.0 4.7 multiply_convert_fusion.1
  420.1 4.7 collective-permute-done.50
  432.5 6.2 collective-permute-done.53
  466.4 3.4 all-to-all-start.7
  478.9 3.7 collective-permute-done.56
  482.6 6.3 collective-permute-done.58
  501.9 3.4 collective-permute-done.60
  507.6 4.3 all-to-all-start.8
  522.0 3.5 multiply_reduce_fusion
  543.8 12.4 %all-to-all-done.8 = bf16[4,528,256]{2,1,0:T(8,128)(2,1)} async-done(((bf16[4,528,256]{2,1,0:T(8,128)(2,1)}), bf16[4,528,256]{2,1,0:T(8,128)(2,1)}, u32[]{:S(2)}, u32[]{:S(2)}) %all-to-all-start.8) | async-done | bytes 1081376 | tf_op jit(solution)/shard_map/all_to_all | solution.py:66
  575.1 5.5 collective-permute-done.64
  580.7 4.2 collective-permute-done.66
  588.0 3.4 all-to-all-start.5
  594.7 4.4 all-to-all-done.5
  600.3 3.8 all-to-all-start.6
  606.3 3.5 collective-permute-done.69
  619.4 10.3 %all-to-all-done.6 = bf16[4,528,256]{2,1,0:T(8,128)(2,1)S(1)} async-done(((bf16[4,528,256]{2,1,0:T(8,128)(2,1)}), bf16[4,528,256]{2,1,0:T(8,128)(2,1)S(1)}, u32[]{:S(2)}, u32[]{:S(2)}) %all-to-all-start.6) | async-done | bytes 1081376 | tf_op jit(solution)/shard_map/all_to_all | solution.py:66
  632.1 6.2 collective-permute-done.67
  (760 shorter events, 349.6 us)
Async XLA Ops:
  10.3 52.2 %collective-permute-start.4 = (bf16[256,512]{0,1:T(8,128)(2,1)}, bf16[256,512]{0,1:T(8,128)(2,1)}, u32[]{:S(2)}, u32[]{:S(2)}) collective-permute-start(bf16[256,512]{0,1:T(8,128)(2,1)} %broadcast_select_fusion.12), channel_id=1, source_target_pairs={{0,16},{1,17},{2,18},{3,19},{16,0},{17,1},{18,2},{19,3},{4,20},{5,... | collective-permute-start | bytes 786440 | tf_op jit(solution)/shard_map/ppermute | solution.py:35
  14.4 30.3 %all-to-all-start = ((bf16[4,512,256]{2,1,0:T(8,128)(2,1)}), bf16[4,512,256]{2,1,0:T(8,128)(2,1)S(1)}, u32[]{:S(2)}, u32[]{:S(2)}) async-start(bf16[4,512,256]{2,1,0:T(8,128)(2,1)} %broadcast_in_dim.241), calls=%async_computation | async-start | bytes 2097152 | tf_op jit(solution)/shard_map/all_to_all | solution.py:66
  49.7 42.3 %all-gather.8.cloned.1.call-start = ((), (), s32[]{:S(2)}) async-start(), calls=%async_computation.13 | async-start | bytes 1310720 | tf_op jit(solution)/shard_map/all_gather | solution.py:315
  59.6 13.3 %collective-permute-start.1 = (bf16[2,64,1024]{2,1,0:T(8,128)(2,1)S(1)}, bf16[2,64,1024]{2,1,0:T(8,128)(2,1)S(1)}, u32[]{:S(2)}, u32[]{:S(2)}) collective-permute-start(bf16[2,64,1024]{2,1,0:T(8,128)(2,1)S(1)} %get-tuple-element.132), channel_id=1, source_target_pairs={{0,16},{1,17},{2,18},{3,19},{16,0},{17,1},{18,2},{19,3},{4,20},{5,... | collective-permute-start | bytes 786440 | tf_op jit(solution)/shard_map/ppermute | solution.py:35
  61.1 11.8 %collective-permute-start = (bf16[2,64,1024]{2,1,0:T(8,128)(2,1)S(1)}, bf16[2,64,1024]{2,1,0:T(8,128)(2,1)S(1)}, u32[]{:S(2)}, u32[]{:S(2)}) collective-permute-start(bf16[2,64,1024]{2,1,0:T(8,128)(2,1)S(1)} %get-tuple-element.132), channel_id=1, source_target_pairs={{0,2},{1,3},{2,0},{3,1},{16,18},{17,19},{18,16},{19,17},{4,6},{5,7... | collective-permute-start | bytes 786440 | tf_op jit(solution)/shard_map/ppermute | solution.py:35
  64.5 99.5 %all-gather.10.cloned.1.call-start = ((), (), s32[]{:S(2)}) async-start(), calls=%async_computation.14 | async-start | bytes 2621440 | tf_op jit(solution)/shard_map/all_gather | solution.py:316
  103.3 16.1 %collective-permute-start.5 = (bf16[2,256,1024]{2,1,0:T(8,128)(2,1)}, bf16[2,256,1024]{2,1,0:T(8,128)(2,1)}, u32[]{:S(2)}, u32[]{:S(2)}) collective-permute-start(bf16[2,256,1024]{2,1,0:T(8,128)(2,1)} %slice.1070), channel_id=1, source_target_pairs={{0,1},{1,0},{2,3},{3,2},{16,17},{17,16},{18,19},{19,18},{4,5},{5,4... | collective-permute-start | bytes 3145736 | tf_op jit(solution)/shard_map/ppermute | solution.py:35
  104.5 13.4 %collective-permute-start.13 = (bf16[256,1024]{0,1:T(8,128)(2,1)S(1)}, bf16[256,1024]{0,1:T(8,128)(2,1)S(1)}, u32[]{:S(2)}, u32[]{:S(2)}) collective-permute-start(bf16[256,1024]{0,1:T(8,128)(2,1)S(1)} %broadcast_select_fusion.4), channel_id=1, source_target_pairs={{0,16},{1,17},{2,18},{3,19},{16,0},{17,1},{18,2},{19,3},{4,20},{5,... | collective-permute-start | bytes 1572872 | tf_op jit(solution)/shard_map/ppermute | solution.py:35
  119.1 117.0 %all-gather.12.cloned.1.call-start = ((), (), s32[]{:S(2)}) async-start(), calls=%async_computation.15 | async-start | bytes 1310720 | tf_op jit(solution)/shard_map/all_gather | solution.py:315
  122.8 12.6 %collective-permute-start.8 = (bf16[2,64,1024]{2,1,0:T(8,128)(2,1)S(1)}, bf16[2,64,1024]{2,1,0:T(8,128)(2,1)S(1)}, u32[]{:S(2)}, u32[]{:S(2)}) collective-permute-start(bf16[2,64,1024]{2,1,0:T(8,128)(2,1)S(1)} %get-tuple-element.171), channel_id=1, source_target_pairs={{0,18},{1,19},{2,16},{3,17},{16,2},{17,3},{18,0},{19,1},{4,22},{5,... | collective-permute-start | bytes 786440 | tf_op jit(solution)/shard_map/ppermute | solution.py:35
  124.3 12.5 %collective-permute-start.7 = (bf16[2,64,1024]{2,1,0:T(8,128)(2,1)S(1)}, bf16[2,64,1024]{2,1,0:T(8,128)(2,1)S(1)}, u32[]{:S(2)}, u32[]{:S(2)}) collective-permute-start(bf16[2,64,1024]{2,1,0:T(8,128)(2,1)S(1)} %get-tuple-element.172), channel_id=1, source_target_pairs={{0,16},{1,17},{2,18},{3,19},{16,0},{17,1},{18,2},{19,3},{4,20},{5,... | collective-permute-start | bytes 786440 | tf_op jit(solution)/shard_map/ppermute | solution.py:35
  178.9 13.5 %collective-permute-start.17 = (bf16[2,64,1024]{2,1,0:T(8,128)(2,1)S(1)}, bf16[2,64,1024]{2,1,0:T(8,128)(2,1)S(1)}, u32[]{:S(2)}, u32[]{:S(2)}) collective-permute-start(bf16[2,64,1024]{2,1,0:T(8,128)(2,1)S(1)} %get-tuple-element.168), channel_id=1, source_target_pairs={{0,18},{1,19},{2,16},{3,17},{16,2},{17,3},{18,0},{19,1},{4,22},{5,... | collective-permute-start | bytes 786440 | tf_op jit(solution)/shard_map/ppermute | solution.py:35
  180.4 13.4 %collective-permute-start.16 = (bf16[2,64,1024]{2,1,0:T(8,128)(2,1)S(1)}, bf16[2,64,1024]{2,1,0:T(8,128)(2,1)S(1)}, u32[]{:S(2)}, u32[]{:S(2)}) collective-permute-start(bf16[2,64,1024]{2,1,0:T(8,128)(2,1)S(1)} %get-tuple-element.169), channel_id=1, source_target_pairs={{0,16},{1,17},{2,18},{3,19},{16,0},{17,1},{18,2},{19,3},{4,20},{5,... | collective-permute-start | bytes 786440 | tf_op jit(solution)/shard_map/ppermute | solution.py:35
  210.9 37.7 %all-to-all-start.3 = ((bf16[4,512,256]{2,1,0:T(8,128)(2,1)}), bf16[4,512,256]{2,1,0:T(8,128)(2,1)}, u32[]{:S(2)}, u32[]{:S(2)}) async-start(bf16[4,512,256]{2,1,0:T(8,128)(2,1)} %broadcast_in_dim.250), calls=%async_computation.3 | async-start | bytes 2097152 | tf_op jit(solution)/shard_map/all_to_all | solution.py:66
  248.5 17.2 %collective-permute-start.22 = (bf16[2,256,1024]{2,1,0:T(8,128)(2,1)S(1)}, bf16[2,256,1024]{2,1,0:T(8,128)(2,1)}, u32[]{:S(2)}, u32[]{:S(2)}) collective-permute-start(bf16[2,256,1024]{2,1,0:T(8,128)(2,1)S(1)} %slice.1068), channel_id=1, source_target_pairs={{0,1},{1,0},{2,3},{3,2},{16,17},{17,16},{18,19},{19,18},{4,5},{5,4... | collective-permute-start | bytes 3145736 | tf_op jit(solution)/shard_map/ppermute | solution.py:35
  255.3 50.4 %all-gather.14.cloned.1.call-start = ((), (), s32[]{:S(2)}) async-start(), calls=%async_computation.16 | async-start | bytes 2621440 | tf_op jit(solution)/shard_map/all_gather | solution.py:316
  262.8 13.5 %collective-permute-start.36 = (bf16[2,64,1024]{2,1,0:T(8,128)(2,1)S(1)}, bf16[2,64,1024]{2,1,0:T(8,128)(2,1)S(1)}, u32[]{:S(2)}, u32[]{:S(2)}) collective-permute-start(bf16[2,64,1024]{2,1,0:T(8,128)(2,1)S(1)} %bitcast.319), channel_id=1, source_target_pairs={{0,16},{1,17},{2,18},{3,19},{16,0},{17,1},{18,2},{19,3},{4,20},{5,... | collective-permute-start | bytes 786440 | tf_op jit(solution)/shard_map/ppermute | solution.py:35
  264.2 12.9 %collective-permute-start.35 = (bf16[2,64,1024]{2,1,0:T(8,128)(2,1)S(1)}, bf16[2,64,1024]{2,1,0:T(8,128)(2,1)S(1)}, u32[]{:S(2)}, u32[]{:S(2)}) collective-permute-start(bf16[2,64,1024]{2,1,0:T(8,128)(2,1)S(1)} %bitcast.320), channel_id=1, source_target_pairs={{0,2},{1,3},{2,0},{3,1},{16,18},{17,19},{18,16},{19,17},{4,6},{5,7... | collective-permute-start | bytes 786440 | tf_op jit(solution)/shard_map/ppermute | solution.py:35
  268.3 14.5 %collective-permute-start.23 = (bf16[2,64,1024]{2,1,0:T(8,128)(2,1)S(1)}, bf16[2,64,1024]{2,1,0:T(8,128)(2,1)S(1)}, u32[]{:S(2)}, u32[]{:S(2)}) collective-permute-start(bf16[2,64,1024]{2,1,0:T(8,128)(2,1)S(1)} %get-tuple-element.164), channel_id=1, source_target_pairs={{0,2},{1,3},{2,0},{3,1},{16,18},{17,19},{18,16},{19,17},{4,6},{5,7... | collective-permute-start | bytes 786440 | tf_op jit(solution)/shard_map/ppermute | solution.py:35
  269.0 18.4 %collective-permute-start.25 = (bf16[2,64,1024]{2,1,0:T(8,128)(2,1)S(1)}, bf16[2,64,1024]{2,1,0:T(8,128)(2,1)S(1)}, u32[]{:S(2)}, u32[]{:S(2)}) collective-permute-start(bf16[2,64,1024]{2,1,0:T(8,128)(2,1)S(1)} %get-tuple-element.165), channel_id=1, source_target_pairs={{0,18},{1,19},{2,16},{3,17},{16,2},{17,3},{18,0},{19,1},{4,22},{5,... | collective-permute-start | bytes 786440 | tf_op jit(solution)/shard_map/ppermute | solution.py:35
  272.4 15.0 %collective-permute-start.24 = (bf16[2,64,1024]{2,1,0:T(8,128)(2,1)S(1)}, bf16[2,64,1024]{2,1,0:T(8,128)(2,1)S(1)}, u32[]{:S(2)}, u32[]{:S(2)}) collective-permute-start(bf16[2,64,1024]{2,1,0:T(8,128)(2,1)S(1)} %get-tuple-element.166), channel_id=1, source_target_pairs={{0,16},{1,17},{2,18},{3,19},{16,0},{17,1},{18,2},{19,3},{4,20},{5,... | collective-permute-start | bytes 786440 | tf_op jit(solution)/shard_map/ppermute | solution.py:35
  277.2 24.9 %collective-permute-start.38 = (bf16[2,256,1024]{2,1,0:T(8,128)(2,1)S(1)}, bf16[2,256,1024]{2,1,0:T(8,128)(2,1)S(1)}, u32[]{:S(2)}, u32[]{:S(2)}) collective-permute-start(bf16[2,256,1024]{2,1,0:T(8,128)(2,1)S(1)} %pad_maximum_fusion.6), channel_id=1, source_target_pairs={{0,1},{1,0},{2,3},{3,2},{16,17},{17,16},{18,19},{19,18},{4,5},{5,4... | collective-permute-start | bytes 3145736 | tf_op jit(solution)/shard_map/ppermute | solution.py:35
  289.7 12.0 %collective-permute-start.27 = (bf16[2,64,1024]{2,1,0:T(8,128)(2,1)S(1)}, bf16[2,64,1024]{2,1,0:T(8,128)(2,1)S(1)}, u32[]{:S(2)}, u32[]{:S(2)}) collective-permute-start(bf16[2,64,1024]{2,1,0:T(8,128)(2,1)S(1)} %get-tuple-element.115), channel_id=1, source_target_pairs={{0,16},{1,17},{2,18},{3,19},{16,0},{17,1},{18,2},{19,3},{4,20},{5,... | collective-permute-start | bytes 786440 | tf_op jit(solution)/shard_map/ppermute | solution.py:35
  318.1 13.9 %collective-permute-start.42 = (bf16[2,64,1024]{2,1,0:T(8,128)(2,1)S(1)}, bf16[2,64,1024]{2,1,0:T(8,128)(2,1)S(1)}, u32[]{:S(2)}, u32[]{:S(2)}) collective-permute-start(bf16[2,64,1024]{2,1,0:T(8,128)(2,1)S(1)} %get-tuple-element.159), channel_id=1, source_target_pairs={{0,18},{1,19},{2,16},{3,17},{16,2},{17,3},{18,0},{19,1},{4,22},{5,... | collective-permute-start | bytes 786440 | tf_op jit(solution)/shard_map/ppermute | solution.py:35
  319.3 14.8 %collective-permute-start.41 = (bf16[2,64,1024]{2,1,0:T(8,128)(2,1)S(1)}, bf16[2,64,1024]{2,1,0:T(8,128)(2,1)S(1)}, u32[]{:S(2)}, u32[]{:S(2)}) collective-permute-start(bf16[2,64,1024]{2,1,0:T(8,128)(2,1)S(1)} %get-tuple-element.160), channel_id=1, source_target_pairs={{0,16},{1,17},{2,18},{3,19},{16,0},{17,1},{18,2},{19,3},{4,20},{5,... | collective-permute-start | bytes 786440 | tf_op jit(solution)/shard_map/ppermute | solution.py:35
  321.1 16.3 %collective-permute-start.31 = (bf16[2,64,1024]{2,1,0:T(8,128)(2,1)S(1)}, bf16[2,64,1024]{2,1,0:T(8,128)(2,1)S(1)}, u32[]{:S(2)}, u32[]{:S(2)}) collective-permute-start(bf16[2,64,1024]{2,1,0:T(8,128)(2,1)S(1)} %get-tuple-element.161), channel_id=1, source_target_pairs={{0,2},{1,3},{2,0},{3,1},{16,18},{17,19},{18,16},{19,17},{4,6},{5,7... | collective-permute-start | bytes 786440 | tf_op jit(solution)/shard_map/ppermute | solution.py:35
  322.3 20.6 %collective-permute-start.33 = (bf16[2,64,1024]{2,1,0:T(8,128)(2,1)S(1)}, bf16[2,64,1024]{2,1,0:T(8,128)(2,1)S(1)}, u32[]{:S(2)}, u32[]{:S(2)}) collective-permute-start(bf16[2,64,1024]{2,1,0:T(8,128)(2,1)S(1)} %get-tuple-element.162), channel_id=1, source_target_pairs={{0,18},{1,19},{2,16},{3,17},{16,2},{17,3},{18,0},{19,1},{4,22},{5,... | collective-permute-start | bytes 786440 | tf_op jit(solution)/shard_map/ppermute | solution.py:35
  326.0 18.2 %collective-permute-start.32 = (bf16[2,64,1024]{2,1,0:T(8,128)(2,1)S(1)}, bf16[2,64,1024]{2,1,0:T(8,128)(2,1)S(1)}, u32[]{:S(2)}, u32[]{:S(2)}) collective-permute-start(bf16[2,64,1024]{2,1,0:T(8,128)(2,1)S(1)} %get-tuple-element.163), channel_id=1, source_target_pairs={{0,16},{1,17},{2,18},{3,19},{16,0},{17,1},{18,2},{19,3},{4,20},{5,... | collective-permute-start | bytes 786440 | tf_op jit(solution)/shard_map/ppermute | solution.py:35
  346.8 12.2 %collective-permute-start.44 = (bf16[2,64,1024]{2,1,0:T(8,128)(2,1)S(1)}, bf16[2,64,1024]{2,1,0:T(8,128)(2,1)S(1)}, u32[]{:S(2)}, u32[]{:S(2)}) collective-permute-start(bf16[2,64,1024]{2,1,0:T(8,128)(2,1)S(1)} %get-tuple-element.103), channel_id=1, source_target_pairs={{0,16},{1,17},{2,18},{3,19},{16,0},{17,1},{18,2},{19,3},{4,20},{5,... | collective-permute-start | bytes 786440 | tf_op jit(solution)/shard_map/ppermute | solution.py:35
  360.1 15.3 %collective-permute-start.46 = (bf16[2,256,1024]{2,1,0:T(8,128)(2,1)}, bf16[2,256,1024]{2,1,0:T(8,128)(2,1)}, u32[]{:S(2)}, u32[]{:S(2)}) collective-permute-start(bf16[2,256,1024]{2,1,0:T(8,128)(2,1)} %pad_maximum_fusion.7), channel_id=1, source_target_pairs={{0,1},{1,0},{2,3},{3,2},{16,17},{17,16},{18,19},{19,18},{4,5},{5,4... | collective-permute-start | bytes 3145736 | tf_op jit(solution)/shard_map/ppermute | solution.py:35
  361.0 13.9 %all-to-all-start.2 = ((bf16[8,64,512]{2,1,0:T(8,128)(2,1)}), bf16[8,64,512]{2,1,0:T(8,128)(2,1)}, u32[]{:S(2)}, u32[]{:S(2)}) async-start(bf16[8,64,512]{2,1,0:T(8,128)(2,1)} %pad_maximum_fusion.18), calls=%async_computation.2 | async-start | bytes 1048576 | tf_op jit(solution)/shard_map/all_to_all | solution.py:390
  365.2 130.3 %all-gather.16.cloned.1.call-start = ((), (), s32[]{:S(2)}) async-start(), calls=%async_computation.17 | async-start | bytes 2621440 | tf_op jit(solution)/shard_map/all_gather | solution.py:391
  375.0 216.5 %reduce-scatter.11.cloned.1.call-start = ((), (), s32[]{:S(2)}) async-start(), calls=%async_computation.21 | async-start | bytes 2621440 | tf_op jit(solution)/shard_map/reduce_scatter | solution.py:419
  411.1 13.7 %collective-permute-start.50 = (bf16[2,64,1024]{2,1,0:T(8,128)(2,1)}, bf16[2,64,1024]{2,1,0:T(8,128)(2,1)}, u32[]{:S(2)}, u32[]{:S(2)}) collective-permute-start(bf16[2,64,1024]{2,1,0:T(8,128)(2,1)} %get-tuple-element.156), channel_id=1, source_target_pairs={{0,18},{1,19},{2,16},{3,17},{16,2},{17,3},{18,0},{19,1},{4,22},{5,... | collective-permute-start | bytes 786440 | tf_op jit(solution)/shard_map/ppermute | solution.py:35
  412.6 13.6 %collective-permute-start.49 = (bf16[2,64,1024]{2,1,0:T(8,128)(2,1)}, bf16[2,64,1024]{2,1,0:T(8,128)(2,1)}, u32[]{:S(2)}, u32[]{:S(2)}) collective-permute-start(bf16[2,64,1024]{2,1,0:T(8,128)(2,1)} %get-tuple-element.157), channel_id=1, source_target_pairs={{0,16},{1,17},{2,18},{3,19},{16,0},{17,1},{18,2},{19,3},{4,20},{5,... | collective-permute-start | bytes 786440 | tf_op jit(solution)/shard_map/ppermute | solution.py:35
  418.6 173.0 %reduce-scatter.9.cloned.1.call-start = ((), (), s32[]{:S(2)}) async-start(), calls=%async_computation.20 | async-start | bytes 2621440 | tf_op jit(solution)/shard_map/reduce_scatter | solution.py:419
  466.4 12.5 %all-to-all-start.7 = ((bf16[8,80,256]{2,1,0:T(8,128)(2,1)}), bf16[8,80,256]{2,1,0:T(8,128)(2,1)S(1)}, u32[]{:S(2)}, u32[]{:S(2)}) async-start(bf16[8,80,256]{2,1,0:T(8,128)(2,1)} %pad_maximum_fusion.20), calls=%async_computation.7 | async-start | bytes 655360 | tf_op jit(solution)/shard_map/all_to_all | solution.py:404
  469.8 134.3 %reduce-scatter.7.cloned.1.call-start = ((), (), s32[]{:S(2)}) async-start(), calls=%async_computation.19 | async-start | bytes 1310720 | tf_op jit(solution)/shard_map/reduce_scatter | solution.py:419
  475.0 13.8 %collective-permute-start.58 = (bf16[2,64,1024]{2,1,0:T(8,128)(2,1)}, bf16[2,64,1024]{2,1,0:T(8,128)(2,1)}, u32[]{:S(2)}, u32[]{:S(2)}) collective-permute-start(bf16[2,64,1024]{2,1,0:T(8,128)(2,1)} %get-tuple-element.153), channel_id=1, source_target_pairs={{0,18},{1,19},{2,16},{3,17},{16,2},{17,3},{18,0},{19,1},{4,22},{5,... | collective-permute-start | bytes 786440 | tf_op jit(solution)/shard_map/ppermute | solution.py:35
  476.5 13.7 %collective-permute-start.57 = (bf16[2,64,1024]{2,1,0:T(8,128)(2,1)}, bf16[2,64,1024]{2,1,0:T(8,128)(2,1)}, u32[]{:S(2)}, u32[]{:S(2)}) collective-permute-start(bf16[2,64,1024]{2,1,0:T(8,128)(2,1)} %get-tuple-element.154), channel_id=1, source_target_pairs={{0,16},{1,17},{2,18},{3,19},{16,0},{17,1},{18,2},{19,3},{4,20},{5,... | collective-permute-start | bytes 786440 | tf_op jit(solution)/shard_map/ppermute | solution.py:35
  499.2 13.0 %collective-permute-start.34 = (bf16[512,256]{1,0:T(8,128)(2,1)}, bf16[512,256]{1,0:T(8,128)(2,1)S(1)}, u32[]{:S(2)}, u32[]{:S(2)}) collective-permute-start(bf16[512,256]{1,0:T(8,128)(2,1)} %broadcast_select_fusion.15), channel_id=1, source_target_pairs={{0,16},{1,17},{2,18},{3,19},{16,0},{17,1},{18,2},{19,3},{4,20},{5,... | collective-permute-start | bytes 786440 | tf_op jit(solution)/shard_map/ppermute | solution.py:35
  507.6 48.6 %all-to-all-start.8 = ((bf16[4,528,256]{2,1,0:T(8,128)(2,1)}), bf16[4,528,256]{2,1,0:T(8,128)(2,1)}, u32[]{:S(2)}, u32[]{:S(2)}) async-start(bf16[4,528,256]{2,1,0:T(8,128)(2,1)} %broadcast_in_dim.253), calls=%async_computation.8 | async-start | bytes 2162688 | tf_op jit(solution)/shard_map/all_to_all | solution.py:66
  511.9 92.2 %reduce-scatter.5.cloned.1.call-start = ((), (), s32[]{:S(2)}) async-start(), calls=%async_computation.18 | async-start | bytes 1310720 | tf_op jit(solution)/shard_map/reduce_scatter | solution.py:419
  543.3 25.5 %collective-permute-start.63 = (bf16[2,256,1024]{2,1,0:T(8,128)(2,1)}, bf16[2,256,1024]{2,1,0:T(8,128)(2,1)}, u32[]{:S(2)}, u32[]{:S(2)}) collective-permute-start(bf16[2,256,1024]{2,1,0:T(8,128)(2,1)} %slice.1063), channel_id=1, source_target_pairs={{0,1},{1,0},{2,3},{3,2},{16,17},{17,16},{18,19},{19,18},{4,5},{5,4... | collective-permute-start | bytes 3145736 | tf_op jit(solution)/shard_map/ppermute | solution.py:35
  572.4 12.5 %collective-permute-start.66 = (bf16[2,64,1024]{2,1,0:T(8,128)(2,1)S(1)}, bf16[2,64,1024]{2,1,0:T(8,128)(2,1)S(1)}, u32[]{:S(2)}, u32[]{:S(2)}) collective-permute-start(bf16[2,64,1024]{2,1,0:T(8,128)(2,1)S(1)} %get-tuple-element.150), channel_id=1, source_target_pairs={{0,18},{1,19},{2,16},{3,17},{16,2},{17,3},{18,0},{19,1},{4,22},{5,... | collective-permute-start | bytes 786440 | tf_op jit(solution)/shard_map/ppermute | solution.py:35
  573.8 12.5 %collective-permute-start.65 = (bf16[2,64,1024]{2,1,0:T(8,128)(2,1)S(1)}, bf16[2,64,1024]{2,1,0:T(8,128)(2,1)S(1)}, u32[]{:S(2)}, u32[]{:S(2)}) collective-permute-start(bf16[2,64,1024]{2,1,0:T(8,128)(2,1)S(1)} %get-tuple-element.151), channel_id=1, source_target_pairs={{0,16},{1,17},{2,18},{3,19},{16,0},{17,1},{18,2},{19,3},{4,20},{5,... | collective-permute-start | bytes 786440 | tf_op jit(solution)/shard_map/ppermute | solution.py:35
  592.7 17.2 %collective-permute-start.69 = (bf16[256,1024]{0,1:T(8,128)(2,1)S(1)}, bf16[256,1024]{0,1:T(8,128)(2,1)S(1)}, u32[]{:S(2)}, u32[]{:S(2)}) collective-permute-start(bf16[256,1024]{0,1:T(8,128)(2,1)S(1)} %broadcast_select_fusion), channel_id=1, source_target_pairs={{0,16},{1,17},{2,18},{3,19},{16,0},{17,1},{18,2},{19,3},{4,20},{5,... | collective-permute-start | bytes 1572872 | tf_op jit(solution)/shard_map/ppermute | solution.py:35
  600.3 29.4 %all-to-all-start.6 = ((bf16[4,528,256]{2,1,0:T(8,128)(2,1)}), bf16[4,528,256]{2,1,0:T(8,128)(2,1)S(1)}, u32[]{:S(2)}, u32[]{:S(2)}) async-start(bf16[4,528,256]{2,1,0:T(8,128)(2,1)} %broadcast_in_dim.252), calls=%async_computation.6 | async-start | bytes 2162688 | tf_op jit(solution)/shard_map/all_to_all | solution.py:66
  (182 other events, 1391.5 us)
Sparse Core Ops, SparseCore 0:
  64.6 27.4 all-gather.7
  119.2 44.6 all-gather.9
  198.7 37.4 all-gather.11
  257.9 46.8 all-gather.13
  375.1 44.1 all-gather.15
  421.5 42.5 reduce-scatter.10
  466.5 43.1 reduce-scatter.8
  512.6 42.2 reduce-scatter.6
  568.9 25.0 reduce-scatter.4

commit v4 on v3

v4 whole, which is shorter than its diff:
```python
import functools

import jax
import jax.numpy as jnp
from jax import lax
from jax.experimental import pallas as pl
from jax.experimental.pallas import tpu as pltpu
from jax.sharding import PartitionSpec as P

HEAD_DIM = 64
epsilon = 1e-05
far_away = 1e34
F32 = jnp.float32
BF16 = jnp.bfloat16
PLANE = ("section", "col")
ROOM = 28


def mm(a, b, dims):
    return lax.dot_general(a, b, ((dims[0], dims[1]), ((), ())), preferred_element_type=F32)


def nn(a, b):
    return mm(a, b, ((1,), (0,)))


def nt(a, b):
    return mm(a, b, ((1,), (1,)))


def tn(a, b):
    return mm(a, b, ((0,), (0,)))


def plane_size():
    return lax.axis_size("section") * lax.axis_size("col")


def send(array, mask):
    return lax.ppermute(array, PLANE, [(i, i ^ mask) for i in range(plane_size())])


def far_masks():
    return list(range(2, plane_size(), 2))


def spread_order():
    near = [0] + far_masks()
    return near + [m ^ 1 for m in near]


def spread(own):
    near = [own] + [send(own, m) for m in far_masks()]
    return near + [send(n, 1) for n in near]


def together(*values):
    return lax.optimization_barrier(values)


def gather_direct(array):
    count = lax.axis_size("row")
    copies = jnp.broadcast_to(array[None], (count,) + array.shape)
    return lax.all_to_all(copies, "row", split_axis=0, concat_axis=0)


def owned_layout(lengths, deal, holder, rows_dev):
    starts = jnp.cumsum(lengths) - lengths
    first = deal == 2 * holder
    second = deal == 2 * holder + 1
    first_len = jnp.sum(jnp.where(first, lengths, 0))
    second_len = jnp.sum(jnp.where(second, lengths, 0))
    first_start = jnp.sum(jnp.where(first, starts, 0))
    second_start = jnp.sum(jnp.where(second, starts, 0))
    slots = jnp.arange(rows_dev, dtype=jnp.int32)
    in_first = slots < first_len
    in_second = jnp.logical_and(jnp.logical_not(in_first), slots < first_len + second_len)
    usable = jnp.logical_or(in_first, in_second)
    position = jnp.where(in_first, slots, slots - first_len)
    source = jnp.where(in_first, first_start + slots, second_start + position)
    source = jnp.where(usable, source, -1)
    segment = jnp.where(in_first, 0, jnp.where(in_second, 1, 2)).astype(jnp.int32)
    return source, usable, segment, position


def given_targets(lengths, deal, positions, rows_dev):
    starts = jnp.cumsum(lengths) - lengths
    before = deal[None, :] == (deal - 1)[:, None]
    partner_len = jnp.sum(jnp.where(before, lengths[None, :], 0), axis=1)
    offset = jnp.where(deal % 2 == 1, partner_len, 0)
    base = deal // 2 * rows_dev + offset - starts
    inside = jnp.logical_and(
        positions[:, None] >= starts[None, :], positions[:, None] < (starts + lengths)[None, :]
    )
    target = jnp.sum(jnp.where(inside, base[None, :] + positions[:, None], 0), axis=1)
    return jnp.where(jnp.any(inside, axis=1), target, -1)


def pick_rows(rows, wanted):
    onehot = (wanted[:, None] == jnp.arange(rows.shape[0], dtype=jnp.int32)[None, :]).astype(BF16)
    return nn(onehot, rows)


class Moves:
    def __init__(self):
        self.loads, self.stores, self.started = {}, {}, []

    def need(self, *refs):
        for ref in refs:
            if id(ref) in self.loads:
                self.loads.pop(id(ref)).wait()

    def put(self, *refs):
        for ref in refs:
            if id(ref) in self.stores:
                copy = self.stores.pop(id(ref))
                copy.start()
                self.started.append(copy)

    def finish(self):
        for copy in self.started:
            copy.wait()


def run(kernel, outs, *args, scalars=0, scratch=(), room=10, cost=0, load=(), store=()):
    vmem, hbm, smem = [pl.BlockSpec(memory_space=m) for m in (pltpu.VMEM, pltpu.HBM, pltpu.SMEM)]
    n_in, n_out = len(args), len(outs)
    load = [i % n_in for i in load]
    buffers = [(args[i].shape, args[i].dtype) for i in load] + [outs[i] for i in store]

    def body(*refs):
        refs = list(refs)
        ins, results, rest = refs[:n_in], refs[n_in : n_in + n_out], refs[n_in + n_out :]
        own, held = rest[: len(scratch)], rest[len(scratch) : len(scratch) + len(buffers)]
        moves = Moves()
        for i, place in enumerate(load):
            copy = pltpu.make_async_copy(ins[place], held[i], rest[-1].at[i])
            copy.start()
            moves.loads[id(held[i])] = copy
            ins[place] = held[i]
        for i, place in enumerate(store, len(load)):
            copy = pltpu.make_async_copy(held[i], results[place], rest[-1].at[i])
            moves.stores[id(held[i])] = copy
            results[place] = held[i]
        kernel(moves, *ins, *results, *own)
        moves.finish()

    shapes = [pltpu.VMEM(shape, kind) for shape, kind in [*scratch, *buffers]]
    call = pl.pallas_call(
        body,
        out_shape=[
            pltpu.HBM(shape, kind) if i in store else jax.ShapeDtypeStruct(shape, kind)
            for i, (shape, kind) in enumerate(outs)
        ],
        in_specs=[
            hbm if i in load else smem if i >= n_in - scalars else vmem for i in range(n_in)
        ],
        out_specs=[hbm if i in store else vmem for i in range(n_out)],
        scratch_shapes=shapes + [pltpu.SemaphoreType.DMA((len(buffers),))] * bool(buffers),
        cost_estimate=pl.CostEstimate(flops=cost, bytes_accessed=0, transcendentals=0),
        compiler_params=pltpu.CompilerParams(vmem_limit_bytes=room * 2**20),
    )
    args = [
        pltpu.with_memory_space_constraint(a, pltpu.HBM) if i in load else a
        for i, a in enumerate(args)
    ]
    return list(call(*args))


def collect(blocks, rows_ref):
    size = blocks[0].shape[0]
    for i, block in enumerate(blocks):
        rows_ref[i * size : (i + 1) * size, :] = block[...]


def tiles(total, most=256):
    size = min(total, most)
    return [slice(i, i + size) for i in range(0, total, size)]


def norm_stats(hidden):
    average = jnp.mean(hidden, axis=1, keepdims=True)
    square = jnp.mean(hidden * hidden, axis=1, keepdims=True)
    inverse = lax.rsqrt(square - average * average + epsilon)
    return (hidden - average) * inverse, inverse


def norm_kernel(moves, hidden, gain, shift, normed):
    centered, _ = norm_stats(hidden[...].astype(F32))
    normed[...] = (centered * gain[...] + shift[...]).astype(BF16)


def add_norm_kernel(count, moves, *refs):
    parts, (hidden, bias, gain, shift, middle, normed) = refs[:count], refs[count:]
    total = bias[...] + parts[1][...].astype(F32)
    for part in parts[2:]:
        total = total + part[...].astype(F32)
    moves.need(parts[0], hidden)
    total = total + parts[0][...] + hidden[...].astype(F32)
    middle[...] = total
    moves.put(middle)
    centered, _ = norm_stats(total)
    normed[...] = (centered * gain[...] + shift[...]).astype(BF16)


def end_norm_kernel(count, moves, *refs):
    parts, (hidden, bias, gain, shift, usable, result, normed) = refs[:count], refs[count:]
    total = bias[...] + parts[1][...].astype(F32)
    for part in parts[2:]:
        total = total + part[...].astype(F32)
    moves.need(parts[0], hidden)
    total = total + parts[0][...] + hidden[...]
    rounded = jnp.where(usable[...] > 0, total, 0.0).astype(BF16)
    result[...] = rounded
    moves.put(result)
    centered, _ = norm_stats(rounded.astype(F32))
    normed[...] = (centered * gain[...] + shift[...]).astype(BF16)


def norm_back_kernel(count, moves, *refs):
    parts, rest = refs[:count], refs[count:]
    hidden, gain, grad_out, grad_in, rounded, sums = rest
    grad = parts[1][...].astype(F32)
    for part in parts[2:]:
        grad = grad + part[...].astype(F32)
    moves.need(hidden, parts[0], grad_out)
    grad = grad + parts[0][...]
    centered, inverse = norm_stats(hidden[...].astype(F32))
    grad_cent = grad * gain[...]
    mean = jnp.mean(grad_cent, axis=1, keepdims=True)
    cross = jnp.mean(grad_cent * centered, axis=1, keepdims=True)
    total = grad_out[...].astype(F32) + inverse * (grad_cent - mean - centered * cross)
    low = total.astype(BF16)
    grad_in[...] = total
    moves.put(grad_in)
    rounded[...] = low
    sums[0:1, :] = jnp.sum(grad * centered, axis=0, keepdims=True)
    sums[1:2, :] = jnp.sum(grad, axis=0, keepdims=True)
    sums[2:3, :] = jnp.sum(low.astype(F32), axis=0, keepdims=True)


def fold_kernel(moves, near, came, kept, *outs):
    size = kept.shape[0]
    kept[...] = near[:size, :].astype(F32) + came[:size, :].astype(F32)
    moves.put(kept)
    for i, out in enumerate(outs):
        part = slice((i + 1) * size, (i + 2) * size)
        out[...] = (near[part, :].astype(F32) + came[part, :].astype(F32)).astype(BF16)


def put_partial(left, weight, near, far):
    half = near.shape[0]
    for part in tiles(weight.shape[0]):
        got = nt(left, weight[part, :]).astype(BF16)
        near[:, part] = got[:half]
        far[:, part] = got[half:]


def collect_micro(micro, blocks, rows_ref):
    size = blocks[0].shape[0] // micro
    for i, block in enumerate(blocks):
        for m in range(micro):
            start = (m * len(blocks) + i) * size
            rows_ref[start : start + size, :] = block[m * size : (m + 1) * size, :]


def put_partial_micro(micro, count, left, weight, near, far):
    size = near.shape[0] * 2 // (count * micro)
    for part in tiles(weight.shape[0]):
        got = nt(left, weight[part, :]).astype(BF16)
        for i in range(count):
            out = near if i < count // 2 else far
            for m in range(micro):
                start = (i % (count // 2) * micro + m) * size
                source = (m * count + i) * size
                out[start : start + size, part] = got[source : source + size]


def attn_forward_kernel(micro, count, moves, *refs):
    blocks, rest = refs[:count], refs[count:]
    (weight, bias_q, bias_v, seg_col, pos_col, seg_row, pos_row, slopes) = rest[:8]
    rows, qkv, soft, attended, near, far, distance = rest[8:]
    collect_micro(micro, blocks, rows)
    moves.put(rows)
    width = attended.shape[1]
    heads = width // HEAD_DIM
    tokens = rows.shape[0] // micro
    full = nn(rows[...], weight[:, : 3 * width])
    queries = (full[:, :width] + bias_q[...]).astype(BF16)
    key_rows = full[:, width : 2 * width].astype(BF16)
    value_rows = (full[:, 2 * width :] + bias_v[...]).astype(BF16)
    qkv[:, :width] = queries
    qkv[:, width : 2 * width] = key_rows
    qkv[:, 2 * width :] = value_rows
    moves.put(qkv)
    values_t = value_rows.astype(F32).T.astype(BF16)
    mixed = [[] for _ in range(heads)]
    for m in range(micro):
        own = slice(m * tokens, (m + 1) * tokens)
        seg_r, pos_r, seg_c, pos_c = seg_row[m], pos_row[m], seg_col[m], pos_col[m]
        allowed = jnp.logical_and(seg_c == seg_r, jnp.logical_and(seg_r < 2, pos_r >= pos_c))
        distance[...] = jnp.where(allowed, (pos_r - pos_c).astype(F32), far_away)
        for j in range(heads):
            lanes = slice(j * HEAD_DIM, (j + 1) * HEAD_DIM)
            for part in tiles(tokens, 128):
                asking = slice(own.start + part.start, own.start + part.stop)
                scores = nt(key_rows[own, lanes], queries[asking, lanes])
                scores = scores * HEAD_DIM ** (-0.5) - slopes[j] * distance[:, part]
                highest = jnp.max(scores, axis=0, keepdims=True)
                raised = jnp.exp(scores - highest)
                weights = raised * (1.0 / jnp.sum(raised, axis=0, keepdims=True))
                weights = weights.astype(BF16)
                soft[m * heads + j, :, part] = weights
                mixed[j].append(nn(values_t[lanes, own], weights))
    mixed = [jnp.concatenate(columns, axis=1) for columns in mixed]
    out = jnp.concatenate(mixed, axis=0).T.astype(BF16)
    attended[...] = out
    moves.put(soft, attended)
    put_partial_micro(micro, count, out, weight[:, 3 * width :], near, far)


def attn_backward_kernel(micro, count, moves, *refs):
    blocks, rest = refs[:count], refs[count:]
    weight, qkv, soft = rest[:3]
    rows, grad_qkv, sums, near, far, held = rest[3:]
    collect_micro(micro, blocks, rows)
    moves.put(rows)
    width = qkv.shape[1] // 3
    heads = width // HEAD_DIM
    tokens = rows.shape[0] // micro
    scale = HEAD_DIM ** (-0.5)
    grad_attended = nn(rows[...], weight[:, 3 * width :]).astype(BF16)
    moves.need(qkv, soft)
    keys_t = qkv[:, width : 2 * width].astype(F32).T.astype(BF16)
    grads_q = [[] for _ in range(heads)]
    for m in range(micro):
        own = slice(m * tokens, (m + 1) * tokens)
        for j in range(heads):
            lanes = slice(j * HEAD_DIM, (j + 1) * HEAD_DIM)
            key_lanes = slice(width + lanes.start, width + lanes.stop)
            value_lanes = slice(2 * width + lanes.start, 2 * width + lanes.stop)
            grad_head = grad_attended[own, lanes]
            for part in tiles(tokens, 128):
                grad_prob = nt(qkv[own, value_lanes], grad_head[part, :])
                weights = soft[m * heads + j, :, part].astype(F32)
                row_dot = jnp.sum(weights * grad_prob, axis=0, keepdims=True)
                held[:, part] = (weights * (grad_prob - row_dot)).astype(BF16)
            grad_score = held[...]
            grad_key = nn(grad_score, qkv[own, lanes]) * scale
            grad_qkv[own, key_lanes] = grad_key.astype(BF16)
            grad_qkv[own, value_lanes] = nn(soft[m * heads + j], grad_head).astype(BF16)
            grads_q[j].append(nn(keys_t[lanes, own], grad_score))
    grads_q = [jnp.concatenate(columns, axis=1) for columns in grads_q]
    grad_qkv[:, :width] = (jnp.concatenate(grads_q, axis=0).T * scale).astype(BF16)
    moves.put(grad_qkv)
    sums[...] = jnp.sum(grad_qkv[...].astype(F32), axis=0, keepdims=True)
    put_partial_micro(micro, count, grad_qkv[...], weight[:, : 3 * width], near, far)


def gelu_and_slope(u):
    root = (2.0 / 3.141592653589793) ** 0.5
    square = u * u
    tanh = jnp.tanh(u * (root + (root * 0.044715) * square))
    half = 0.5 + 0.5 * tanh
    inner = root + (3.0 * root * 0.044715) * square
    return u * half, half + (0.5 * u) * (1.0 - tanh * tanh) * inner


def ffn_forward_kernel(count, moves, *refs):
    blocks, (up_w, down_w, up_bias) = refs[:count], refs[count : count + 3]
    rows, activated, slope, near, far = refs[count + 3 :]
    collect(blocks, rows)
    moves.put(rows)
    for part in tiles(up_w.shape[1]):
        u = nn(rows[...], up_w[:, part]) + up_bias[:, part]
        act, grad = gelu_and_slope(u)
        activated[:, part] = act.astype(BF16)
        slope[:, part] = grad.astype(BF16)
    moves.put(activated, slope)
    put_partial(activated[...], down_w, near, far)


def ffn_turn_kernel(micro, count, moves, *refs):
    blocks, (grads, up_w, down_w, up_bias, order) = refs[:count], refs[count : count + 5]
    rows, grad_rows, activated, grad_upper, sums, near, far = refs[count + 5 :]
    collect(blocks, rows)
    size, width = blocks[0].shape[0] // micro, grads.shape[2]
    for i in range(count):
        start = pl.multiple_of(order[i] * size, size)
        for j in range(count):
            m, column = divmod(j, count // micro)
            row = (i * micro + m) * size
            grad_rows[row : row + size, column * width : (column + 1) * width] = grads[
                j, pl.ds(start, size), :
            ]
    moves.put(rows, grad_rows)
    for part in tiles(up_w.shape[1]):
        u = nn(rows[...], up_w[:, part]) + up_bias[:, part]
        act, slope = gelu_and_slope(u)
        activated[:, part] = act.astype(BF16)
        grad = (nn(grad_rows[...], down_w[:, part]) * slope).astype(BF16)
        grad_upper[:, part] = grad
        sums[:, part] = jnp.sum(grad.astype(F32), axis=0, keepdims=True)
    moves.put(activated, grad_upper)
    put_partial(grad_upper[...], up_w, near, far)


def down_kernel(micro, moves, activated, down_w, middle, bias, order, out):
    count, _, width = out.shape
    size = middle.shape[0] // micro
    for column in range(count // micro):
        lanes = slice(column * width, (column + 1) * width)
        got = nt(activated[...], down_w[lanes, :])
        for i in range(count):
            start = pl.multiple_of(order[i] * size, size)
            for m in range(micro):
                row = (i * micro + m) * size
                part = got[row : row + size]
                if i == 0:
                    part = part + middle[m * size : (m + 1) * size, lanes] + bias[:, lanes]
                out[m * (count // micro) + column, pl.ds(start, size), :] = part.astype(BF16)


def ffn_backward_kernel(count, moves, *refs):
    blocks, (up_w, down_w, slope) = refs[:count], refs[count : count + 3]
    rows, grad_upper, sums, near, far = refs[count + 3 :]
    collect(blocks, rows)
    moves.put(rows)
    moves.need(slope)
    for part in tiles(up_w.shape[1]):
        grad = (nn(rows[...], down_w[:, part]) * slope[:, part].astype(F32)).astype(BF16)
        grad_upper[:, part] = grad
        sums[:, part] = jnp.sum(grad.astype(F32), axis=0, keepdims=True)
    moves.put(grad_upper)
    put_partial(grad_upper[...], up_w, near, far)


def sum_up(near, far, later=()):
    half, model = near.shape
    masks = far_masks()
    size = half // (len(masks) + 1)
    came = send(far, 1)
    outs = [((size, model), F32)] + [((size, model), BF16)] * len(masks)
    kept, *others = run(fold_kernel, outs, near, came, store=(0,))
    if later:
        kept, *later = together(kept, *later)
    return [kept] + [send(o, m) for o, m in zip(others, masks)], later


def attn_forward(normed, layout, weights, small):
    _, seg_col, pos_col, seg_row, pos_row, slopes = layout
    weight = weights[0]
    micro = seg_col.shape[0]
    model, width = weight.shape[0], weight.shape[1] // 4
    blocks = spread(normed)
    count, size = len(blocks), normed.shape[0]
    tokens = count * size
    heads = width // HEAD_DIM
    rows, qkv, soft, attended, near, far = run(
        functools.partial(attn_forward_kernel, micro, count),
        [
            ((tokens, model), BF16),
            ((tokens, 3 * width), BF16),
            ((micro * heads, tokens // micro, tokens // micro), BF16),
            ((tokens, width), BF16),
            ((tokens // 2, model), BF16),
            ((tokens // 2, model), BF16),
        ],
        *blocks,
        weight,
        small["bias_q"],
        small["bias_v"],
        seg_col,
        pos_col,
        seg_row,
        pos_row,
        slopes,
        scalars=1,
        scratch=[((tokens // micro, tokens // micro), F32)],
        store=(0, 1, 2, 3),
        room=ROOM,
    )
    return sum_up(near, far)[0], (rows, qkv, soft, attended)


def ffn_forward(normed, weights, small):
    _, up_w, down_w = weights
    model, hidden = up_w.shape
    blocks = spread(normed)
    count, size = len(blocks), normed.shape[0]
    tokens = count * size
    rows, activated, slope, near, far = run(
        functools.partial(ffn_forward_kernel, count),
        [
            ((tokens, model), BF16),
            ((tokens, hidden), BF16),
            ((tokens, hidden), BF16),
            ((tokens // 2, model), BF16),
            ((tokens // 2, model), BF16),
        ],
        *blocks,
        up_w,
        down_w,
        small["up_bias"],
        room=ROOM,
        store=(0, 1, 2),
    )
    return sum_up(near, far)[0], (rows, activated, slope)


def ffn_turn(normed, middle, grads, order, micro, weights, small):
    _, up_w, down_w = weights
    model, hidden = up_w.shape
    blocks = spread(normed)
    count, size = len(blocks), normed.shape[0]
    tokens = count * size
    halves = [((tokens // 2, model), BF16), ((tokens // 2, model), BF16)]
    rows, grad_rows, activated, grad_upper, sums, near, far = run(
        functools.partial(ffn_turn_kernel, micro, count),
        [
            ((tokens, model), BF16),
            ((tokens, model), BF16),
            ((tokens, hidden), BF16),
            ((tokens, hidden), BF16),
            ((1, hidden), F32),
        ]
        + halves,
        *blocks,
        grads,
        up_w,
        down_w,
        small["up_bias"],
        order,
        scalars=1,
        room=ROOM,
        store=(0, 1, 2, 3),
    )
    grad_parts, factors = sum_up(near, far, (rows, grad_upper, grad_rows, activated))
    out = run(
        functools.partial(down_kernel, micro),
        [(grads.shape, BF16)],
        factors[3],
        down_w,
        middle,
        small["bias_down"],
        order,
        scalars=1,
        room=ROOM,
    )[0]
    return grad_parts, factors, sums, out


def ffn_backward(grad_down, weights, stored):
    _, up_w, down_w = weights
    model, hidden = up_w.shape
    rows_two, activated, slope = stored
    blocks = spread(grad_down)
    count, size = len(blocks), grad_down.shape[0]
    tokens = count * size
    rows, grad_upper, sums, near, far = run(
        functools.partial(ffn_backward_kernel, count),
        [
            ((tokens, model), BF16),
            ((tokens, hidden), BF16),
            ((1, hidden), F32),
            ((tokens // 2, model), BF16),
            ((tokens // 2, model), BF16),
        ],
        *blocks,
        up_w,
        down_w,
        slope,
        room=ROOM,
        load=(-1,),
        store=(0, 1),
    )
    return *sum_up(near, far, (rows_two, grad_upper, rows, activated)), sums


def attn_backward(grad_branch, micro, weights, stored):
    weight = weights[0]
    model, width = weight.shape[0], weight.shape[1] // 4
    rows_one, qkv, soft, attended = stored
    blocks = spread(grad_branch)
    count, size = len(blocks), grad_branch.shape[0]
    tokens = count * size
    rows, grad_qkv, sums, near, far = run(
        functools.partial(attn_backward_kernel, micro, count),
        [
            ((tokens, model), BF16),
            ((tokens, 3 * width), BF16),
            ((1, 3 * width), F32),
            ((tokens // 2, model), BF16),
            ((tokens // 2, model), BF16),
        ],
        *blocks,
        weight,
        qkv,
        soft,
        scratch=[((tokens // micro, tokens // micro), BF16)],
        load=(-1, -2),
        store=(0, 1),
        room=ROOM,
    )
    return *sum_up(near, far, (rows_one, grad_qkv, rows, attended)), sums


def norm_back(parts, hidden, gain, grad_out):
    shape = hidden.shape
    return run(
        functools.partial(norm_back_kernel, len(parts)),
        [(shape, F32), (shape, BF16), ((3, shape[1]), F32)],
        *parts,
        hidden,
        gain,
        grad_out,
        load=(0, len(parts), len(parts) + 2),
        store=(0,),
    )


def weight_term(factors):
    pairs = zip(factors[0::2], factors[1::2])
    return jnp.concatenate([tn(left, right).astype(BF16) for left, right in pairs], axis=1)


def on_device(
    inputs,
    cotangent,
    lengths,
    deal,
    query_key_value_weight,
    out_weight,
    up_weight,
    down_weight,
    norm_gain,
    norm_shift,
    proj_bias,
    up_bias,
):
    section = lax.axis_index("section")
    holder = lax.axis_index("row")
    column = lax.axis_index("col")
    cols_count = lax.axis_size("col")
    micro_count, rows_dev, width = inputs.shape
    model = width * cols_count
    count = plane_size()
    place = section * cols_count + column
    tokens = rows_dev // count
    block = query_key_value_weight.shape[1]
    half = width // 2
    heads_dev = half // HEAD_DIM
    hidden_half = up_weight.shape[2] // 2
    is_zero = section == 0

    def pick(zero, one):
        return jnp.where(is_zero, zero, one)

    def halves(array, axis):
        size = array.shape[axis] // 2
        return (
            lax.slice_in_dim(array, 0, size, axis=axis),
            lax.slice_in_dim(array, size, 2 * size, axis=axis),
        )

    attn_parts = [
        jnp.concatenate([q.reshape(block, 3 * half), o.T], axis=1)
        for q, o in zip(halves(query_key_value_weight[0], 2), halves(out_weight[0], 0))
    ]
    ffn_parts = [
        jnp.concatenate([u, d.T], axis=1)
        for u, d in zip(halves(up_weight[0], 1), halves(down_weight[0], 0))
    ]

    def both_layers(parts):
        kept, given = pick(parts[0], parts[1]), pick(parts[1], parts[0])
        came = send(given, cols_count)
        return pick(kept, came), pick(came, kept)

    def gather_weights(layer):
        attn = lax.all_gather(attn_pieces[layer], "row", axis=0, tiled=True)
        ffn = lax.all_gather(ffn_pieces[layer], "row", axis=0, tiled=True)
        return attn, ffn[:, :hidden_half], ffn[:, hidden_half:]

    mine_small = jnp.concatenate(
        [norm_gain[0], norm_shift[0], proj_bias[0], up_bias[0].reshape(-1, width)], axis=0
    )
    all_small = lax.all_gather(mine_small, PLANE, axis=0, tiled=False)
    all_small = all_small.reshape((2, cols_count) + mine_small.shape)

    def layer_small(layer):
        table = all_small[layer]
        whole = jnp.transpose(table[:, :8], (1, 0, 2)).reshape(8, model)
        own = lax.dynamic_index_in_dim(table, column, axis=0, keepdims=False)
        own_half = pick(own[:, :half], own[:, half:])
        hidden = own[8:].reshape(2, hidden_half)
        return {
            "gain": (whole[0:1], whole[1:2]),
            "shift": (whole[2:3], whole[3:4]),
            "bias_q": own_half[4:5],
            "bias_v": own_half[5:6],
            "bias_out": whole[6:7],
            "bias_down": whole[7:8],
            "up_bias": pick(hidden[0:1], hidden[1:2]),
        }

    source, usable, segment, position = jax.vmap(owned_layout, (0, 0, None, None))(
        lengths, deal, holder, rows_dev
    )
    source = pick(source[0], source[1])
    order = jnp.bitwise_xor(place, jnp.array(spread_order(), jnp.int32))

    def in_spread_order(values):
        values = values.reshape(micro_count, count, tokens)
        return jnp.take(values, order, axis=1).reshape(micro_count, rows_dev)

    own_usable = lax.dynamic_index_in_dim(
        usable.reshape(micro_count, count, tokens), place, axis=1, keepdims=False
    )
    head_ids = (
        column * (2 * heads_dev) + section * heads_dev + jnp.arange(heads_dev, dtype=jnp.int32)
    )
    slopes = jnp.exp2(-8.0 * (head_ids.astype(F32) + 1.0) / (model // HEAD_DIM))
    segment, position = in_spread_order(segment), in_spread_order(position)
    own_usable = own_usable.astype(jnp.int32).reshape(-1, 1)
    layout = (
        own_usable,
        segment[:, :, None],
        position[:, :, None],
        segment[:, None],
        position[:, None],
        slopes,
    )

    def deal_rows(portion):
        return pick_rows(portion.reshape(-1, width), source).astype(BF16)

    def to_tokens(owned):
        own = lax.all_to_all(
            owned.reshape(count, tokens, width), PLANE, split_axis=0, concat_axis=0
        )
        own = own.reshape(micro_count, cols_count, tokens, width)
        return jnp.transpose(own, (0, 2, 1, 3)).reshape(micro_count * tokens, model)

    portion = gather_direct(pick(inputs[0], inputs[1]))
    attn_pieces = both_layers(attn_parts)
    ffn_pieces = both_layers(ffn_parts)
    all_small, attn_first = together(all_small, attn_pieces[0])
    attn_pieces = (attn_first, attn_pieces[1])
    portion, all_small, *ffn_pieces = together(portion, all_small, *ffn_pieces)
    first_rows = to_tokens(deal_rows(portion))
    weights = [gather_weights(0), gather_weights(1)]
    smalls = [layer_small(0), layer_small(1)]

    def to_columns(own):
        parts = own.reshape(micro_count, tokens, cols_count, width)
        return jnp.transpose(parts, (0, 2, 1, 3)).reshape(count, tokens, width)

    shape = (micro_count * tokens, model)

    def middle_norm(parts, hidden, layer):
        small = smalls[layer]
        return run(
            functools.partial(add_norm_kernel, len(parts)),
            [(shape, F32), (shape, BF16)],
            *parts,
            hidden,
            small["bias_out"],
            small["gain"][1],
            small["shift"][1],
            load=(0, len(parts)),
            store=(0,),
        )

    def end_norm(parts, middle, layer):
        small, following = smalls[layer], smalls[min(layer + 1, 1)]
        return run(
            functools.partial(end_norm_kernel, len(parts)),
            [(shape, BF16), (shape, BF16)],
            *parts,
            middle,
            small["bias_down"],
            following["gain"][0],
            following["shift"][0],
            own_usable,
            load=(0, len(parts)),
            store=(0,),
        )

    small = smalls[0]
    normed = run(norm_kernel, [(shape, BF16)], first_rows, small["gain"][0], small["shift"][0])[0]
    parts, attn_zero = attn_forward(normed, layout, weights[0], small)
    parts[0], cotangent = together(parts[0], cotangent)
    given_grads = gather_direct(pick(cotangent[0], cotangent[1]))
    middle_zero, normed = middle_norm(parts, first_rows, 0)
    parts, ffn_zero = ffn_forward(normed, weights[0], small)
    middle_in, normed = end_norm(parts, middle_zero, 0)
    normed, given_grads = together(normed, given_grads)
    given_grads = lax.all_gather(deal_rows(given_grads), PLANE)
    parts, attn_one = attn_forward(normed, layout, weights[1], smalls[1])
    hidden_zero = to_columns(middle_in)
    hidden_zero = lax.all_to_all(hidden_zero, PLANE, split_axis=0, concat_axis=0)
    parts[0], hidden_zero = together(parts[0], hidden_zero)
    hidden_zero = lax.all_gather(hidden_zero.reshape(rows_dev, width), "row", tiled=True)
    middle_one, normed = middle_norm(parts, middle_in, 1)
    normed, given_grads = together(normed, given_grads)
    grad_parts, factors, up_sums, last_out = ffn_turn(
        normed, middle_one, given_grads, order, micro_count, weights[1], smalls[1]
    )
    last_out = lax.psum_scatter(last_out, PLANE, scatter_dimension=0)
    grad_parts[0], hidden_zero = together(grad_parts[0], hidden_zero)
    cotangent_rows = factors[2][: shape[0]]
    positions = holder * rows_dev + jnp.arange(rows_dev, dtype=jnp.int32)
    targets = given_targets(lengths[section], deal[section], positions, rows_dev)

    extra = 16

    def start_return(grad_in, a, b):
        sums = jnp.stack([a[0], b[0], a[1], b[1], b[2], b[3]]).reshape(-1, cols_count, width)
        sums = jnp.pad(jnp.transpose(sums, (1, 0, 2)), ((0, 0), (0, extra - 6), (0, 0)))
        sums = jnp.concatenate([sums.astype(BF16)] * micro_count, axis=0)
        rows = jnp.concatenate([to_columns(grad_in), sums], axis=1)
        return lax.all_to_all(rows, PLANE, split_axis=0, concat_axis=0)

    def gather_return(got, qkv_sums, up_sums):
        column_sums = [qkv_sums[:half], qkv_sums[2 * half :], up_sums[0]]
        sums = jnp.sum(got[:, tokens : tokens + 6].astype(F32), axis=0)
        sums = jnp.concatenate([sums, jnp.concatenate(column_sums).reshape(-1, width)], axis=0)
        sums = jnp.pad(sums, ((0, extra - sums.shape[0]), (0, 0)))
        rows = [got[:, :tokens].reshape(rows_dev, width), sums.astype(BF16)]
        return jnp.concatenate(rows, axis=0)

    def finish_return(all_rows):
        picked = pick_rows(all_rows[:, :rows_dev].reshape(-1, width), targets)
        return jnp.concatenate([picked, jnp.sum(all_rows[:, rows_dev:].astype(F32), axis=0)], axis=0)

    def reduce_rows(total):
        return lax.psum_scatter(total, "row", scatter_dimension=0, tiled=True)

    def ffn_back(grad_parts, grad, factors, layer, middle):
        mid, low, sums = norm_back(grad_parts, middle, smalls[layer]["gain"][1], grad)
        sums = [sums[0], sums[1], sums[2], jnp.sum(grad, axis=0, dtype=F32)]
        return mid, low, sums, weight_term(factors)

    def attn_back(mid, low, layer, hidden, stored):
        parts, factors, qkv_sums = attn_backward(low, micro_count, weights[layer], stored)
        _, low, sums = norm_back(parts, hidden, smalls[layer]["gain"][0], mid)
        return low, sums, qkv_sums[0], weight_term(factors)

    mid, low, sums_b, ffn_term_one = ffn_back(grad_parts, cotangent_rows, factors, 1, middle_one)
    ffn_term_one = reduce_rows(ffn_term_one)
    grad_one, sums_a, qkv_sums, attn_term_one = attn_back(mid, low, 1, middle_in, attn_one)
    attn_term_one = reduce_rows(attn_term_one)
    back_one = start_return(grad_one, sums_a, sums_b)
    late_sums = (qkv_sums, up_sums)
    grad_zero = jnp.where(own_usable > 0, grad_one, jnp.zeros_like(grad_one))
    grad_zero, last_out = together(grad_zero, last_out)
    grad_parts, factors, up_sums = ffn_backward(grad_zero, weights[0], ffn_zero)
    mid, low, sums_b, ffn_term_zero = ffn_back(grad_parts, grad_zero, factors, 0, middle_zero)
    low, ffn_term_one, back_one = together(low, ffn_term_one, back_one)
    ffn_term_zero = reduce_rows(ffn_term_zero)
    back_one = gather_return(back_one, *late_sums)
    parts, factors, qkv_sums = attn_backward(low, micro_count, weights[0], attn_zero)
    term = weight_term(factors)
    term = lax.all_to_all(
        term.reshape(-1, block, term.shape[1]), "row", split_axis=0, concat_axis=0
    )
    parts[0], term, attn_term_one, ffn_term_zero, last_out, back_one = together(
        parts[0], term, attn_term_one, ffn_term_zero, last_out, back_one
    )
    last_out = lax.all_gather(last_out, "row", tiled=True)
    back_one = lax.all_gather(back_one, "row")
    _, grad_in, sums_a = norm_back(parts, first_rows, smalls[0]["gain"][0], mid)
    back_zero = gather_return(start_return(grad_in, sums_a, sums_b), qkv_sums[0], up_sums)
    back_zero = gather_direct(back_zero)
    back_zero, back_one = finish_return(back_zero), finish_return(back_one)
    attn_term_zero = jnp.sum(term.astype(F32), axis=0).astype(BF16)
    hidden = [pick_rows(h, targets).astype(BF16) for h in (hidden_zero, last_out)]
    stays, comes = pick(hidden[0], hidden[1]), send(pick(hidden[1], hidden[0]), cols_count)
    hidden_out = jnp.stack([pick(stays, comes), pick(comes, stays)])

    def both_halves(zero, one):
        mine = pick(zero, one)
        other = send(pick(one, zero), cols_count)
        return pick(mine, other).astype(F32), pick(other, mine).astype(F32)

    attn_grad = jnp.stack(
        [g.reshape(block, 4, half) for g in both_halves(attn_term_zero, attn_term_one)], axis=2
    ).reshape(block, 4, width)
    ffn_grad = both_halves(ffn_term_zero, ffn_term_one)
    up_grad = jnp.concatenate([g[:, :hidden_half] for g in ffn_grad], axis=1)
    down_grad = jnp.concatenate([g[:, hidden_half:].T for g in ffn_grad], axis=0)

    stays = pick(back_zero, back_one)
    comes = send(pick(back_one, back_zero).astype(BF16), cols_count).astype(F32)
    kept, came = stays[:rows_dev], comes[:rows_dev]
    in_grad = jnp.stack([pick(kept, came), pick(came, kept)])
    sums = stays[rows_dev:]
    kept, came = sums[6:].reshape(-1), comes[rows_dev + 6 :].reshape(-1)
    first, second = pick(kept, came), pick(came, kept)
    bias_grad = jnp.stack(
        [
            jnp.concatenate([first[:half], second[:half]]),
            jnp.concatenate([first[half:width], second[half:width]]),
            sums[4],
            sums[5],
        ]
    )
    up_sums = jnp.concatenate(
        [first[width : width + hidden_half], second[width : width + hidden_half]]
    )
    return (
        hidden_out[None],
        in_grad[None],
        attn_grad[:, :3][None],
        attn_grad[:, 3].T[None],
        up_grad[None],
        down_grad[None],
        sums[0:2][None],
        sums[2:4][None],
        bias_grad[None],
        up_sums[None],
    )


def solution(mesh):
    placed = (
        P(None, "row", "col"),
        P(None, "row", "col"),
        P(),
        P(),
        P("section", "row", None, "col"),
        P("section", "col", "row"),
        P("section", "row", "col"),
        P("section", "col", "row"),
        P("section", None, "col"),
        P("section", None, "col"),
        P("section", None, "col"),
        P("section", "col"),
    )
    return jax.shard_map(
        on_device,
        mesh=mesh,
        in_specs=placed,
        out_specs=(
            P("section", None, "row", "col"),
            P("section", None, "row", "col"),
            P("section", "row", None, "col"),
            P("section", "col", "row"),
            P("section", "row", "col"),
            P("section", "col", "row"),
            P("section", None, "col"),
            P("section", None, "col"),
            P("section", None, "col"),
            P("section", "col"),
        ),
        check_vma=False,
    )
```

time: 658 us -> 559 us (0.85)
  Pallas kernels: 0 us -> 88.4 us
  local copies, waits for them, and re-layouts: 97.8 us -> 38.2 us
  matrix products: 83.4 us -> 27.9 us
  other arithmetic: 69.3 us -> 26.5 us
  waiting for transfers between devices: 270 us -> 240 us
  blocking collectives: 9.2 us -> 18.5 us
    pallas_call x0 -> x23, Pallas kernels: none -> 88.4 us  [run(): return list(call(*args))]
    dot_general x29 -> x14, matrix products: 59 us -> 27.9 us  [mm(): lax.dot_general(a, b, ((dims[0], dims[1]), ((), ())), preferred_element_t...]
    all_to_all x4 -> x3, waiting for transfers between devices: 34.8 us -> 8.93 us  [gather_direct(): return lax.all_to_all(copies, 'row', split_axis=0, concat_axis=0)]
    unnamed x336 -> x154, local copies, waits for them, and re-layouts: 42.6 us -> 17.1 us
    dot_general x12 -> x0, matrix products: 24.4 us -> none  [the longest x2 6.43 us: attend_backward(): jnp.einsum('mqhe,mkhe->mhqk', grad_mixed, value_rows, preferred_element_t...]
    all_gather x2, waiting for transfers between devices: 24.2 us -> 0.03 us  [gather_weights(): attn = lax.all_gather(attn_pieces[layer], 'row', axis=0, tiled=True)]
    concatenate x16 -> x0, local copies, waits for them, and re-layouts: 19.1 us -> none  [the longest x8 10.7 us: spread(): return jnp.concatenate([near, send(near, 1)], axis=1)]
    all_to_all x5, waiting for transfers between devices: 22 us -> 40.5 us  [the longest x1 27.7 us: on_device(): lax.all_to_all(term.reshape(-1, block, term.shape[1]), 'row', split_axis=...]
  transfers between devices with their start and end apart: 88 -> 103, of which waited for: 59 -> 53; matrix products, arithmetic and copies ran while one was open for 30% -> 13% of each run, Pallas kernels for 0% -> 16%
where the time goes in v4:
time: 559 us; the launch traced here: 554 us
  waiting for transfers between devices  240 us (43%)
  starting transfers between devices  97.6 us (17%)
  Pallas kernels  88.4 us (16%)
  local copies, waits for them, and re-layouts  38.2 us (7%)
  matrix products  27.9 us (5%)
  other arithmetic  26.5 us (5%)
  blocking collectives  18.5 us (3%)
  between operations  16.6 us (3%)
    ppermute x83, waiting for transfers between devices, send(): lax.ppermute(array, PLANE, [(i, i ^ mask) for i in range(plane_size())])  167 us
    pallas_call x23, Pallas kernels, run(): return list(call(*args))  88.4 us
    ppermute x83, starting transfers between devices, send(): lax.ppermute(array, PLANE, [(i, i ^ mask) for i in range(plane_size())])  63 us
    dot_general x14, matrix products, mm(): lax.dot_general(a, b, ((dims[0], dims[1]), ((), ())), preferred_element_t...  27.9 us
    all_to_all x1, waiting for transfers between devices, on_device(): lax.all_to_all(term.reshape(-1, block, term.shape[1]), 'row', split_axis=...  27.7 us
    all_gather x1, blocking collectives, on_device(): all_small = lax.all_gather(mine_small, PLANE, axis=0, tiled=False)  18.5 us
    unnamed x154, local copies, waits for them, and re-layouts  17.1 us
    all_to_all x3, starting transfers between devices, gather_direct(): return lax.all_to_all(copies, 'row', split_axis=0, concat_axis=0)  14.7 us
  transfers between devices with their start and end apart: 103, of which 53 were waited for; matrix products, arithmetic and copies ran while one was open for 13% of the time, Pallas kernels for 16%

profile of v4, /device:TPU:0, one launch (start us, length us, event | category | flops | bytes accessed | tf_op | source)
XLA Modules:
  0.0 553.6 jit_solution(13818363581809100631)
XLA Ops:
  9.3 6.3 %all-to-all-start = ((bf16[4,512,256]{2,1,0:T(8,128)(2,1)}), bf16[4,512,256]{2,1,0:T(8,128)(2,1)S(1)}, u32[]{:S(2)}, u32[]{:S(2)}) async-start(bf16[4,512,256]{2,1,0:T(8,128)(2,1)} %broadcast_in_dim.160), calls=%async_computation | async-start | bytes 2097152 | tf_op jit(solution)/shard_map/all_to_all | solution.py:64
  22.4 18.5 %all-gather.3 = f32[8,12,256]{2,1,0:T(8,128)S(1)} all-gather(f32[1,12,256]{2,1,0:T(8,128)S(1)} %maximum_bitcast_fusion.4), channel_id=2, replica_groups=mesh['section'=2,'row'=4,'col'=4] {'section','col'}, dimensions={0}, use_global_device_ids=true | all-gather | bytes 110592 | tf_op jit(solution)/shard_map/all_gather | solution.py:688
  48.3 3.4 all-to-all-start.1
  53.2 5.4 all-to-all-done.1
  63.9 4.4 collective-permute-done.2.refs_1_
  68.4 4.9 collective-permute-done.3.refs_2_
  76.4 9.5 %shard_map.205 = (bf16[1024,1024]{1,0:T(8,128)(2,1)}, bf16[1024,384]{1,0:T(8,128)(2,1)}, bf16[4,512,512]{2,1,0:T(8,128)(2,1)}, bf16[1024,128]{1,0:T(8,128)(2,1)}...) custom-call(bf16[128,1024]{1,0:T(8,128)(2,1)S(1)} %shard_map.204.refs_0_, ...), custom_call_target="tpu_custom_call" | custom-call | tf_op jit(solution)/shard_map/pallas_call | solution.py:167
  93.1 5.6 %collective-permute-done.10.refs_1_ = bf16[128,1024]{1,0:T(8,128)(2,1)S(1)} collective-permute-done((bf16[128,1024]{1,0:T(8,128)(2,1)S(1)}, bf16[128,1024]{1,0:T(8,128)(2,1)S(1)}, u32[]{:S(2)}, u32[]{:S(2)}) %collective-permute-start.10) | collective-permute-done | bytes 262176 | tf_op jit(solution)/shard_map/ppermute | solution.py:40
  98.8 5.3 collective-permute-done.11.refs_2_
  111.4 4.9 all-to-all-start.2
  121.8 7.5 %shard_map.208 = (bf16[1024,1024]{1,0:T(8,128)(2,1)}, bf16[1024,512]{1,0:T(8,128)(2,1)}, bf16[1024,512]{1,0:T(8,128)(2,1)}, bf16[512,1024]{1,0:T(8,128)(2,1)S(1)}, bf16[512,1024]{1,0:T(8,128)(2,1)}) custom-call(bf16[128,1024]{1,0:T(8,128)(2,1)S(1)} %get-tuple-element.152.refs_0_, bf16[128,1024]{1,0:T(8,128)(2,1)} %collective-permute-done.13.refs_1_, ...), custom_call_target="tpu_custom_call" | custom-call | tf_op jit(solution)/shard_map/pallas_call | solution.py:167
  137.5 4.2 collective-permute-start.21
  144.6 4.4 collective-permute-done.21.refs_1_
  149.7 4.1 collective-permute-done.22.refs_2_
  166.7 7.4 %collective-permute-done.24.refs_1_ = bf16[128,1024]{1,0:T(8,128)(2,1)} collective-permute-done((bf16[128,1024]{1,0:T(8,128)(2,1)S(1)}, bf16[128,1024]{1,0:T(8,128)(2,1)}, u32[]{:S(2)}, u32[]{:S(2)}) %collective-permute-start.24) | collective-permute-done | bytes 262176 | tf_op jit(solution)/shard_map/ppermute | solution.py:40
  182.3 10.0 %shard_map.211 = (bf16[1024,1024]{1,0:T(8,128)(2,1)}, bf16[1024,384]{1,0:T(8,128)(2,1)}, bf16[4,512,512]{2,1,0:T(8,128)(2,1)}, bf16[1024,128]{1,0:T(8,128)(2,1)}...) custom-call(bf16[128,1024]{1,0:T(8,128)(2,1)S(1)} %get-tuple-element.163.refs_0_, ...), custom_call_target="tpu_custom_call" | custom-call | tf_op jit(solution)/shard_map/pallas_call | solution.py:167
  203.7 4.0 all-to-all-start.3
  207.9 7.3 %all-to-all-done.3 = bf16[8,64,256]{2,1,0:T(8,128)(2,1)} async-done(((bf16[8,64,256]{2,1,0:T(8,128)(2,1)}), bf16[8,64,256]{2,1,0:T(8,128)(2,1)}, u32[]{:S(2)}, u32[]{:S(2)}) %all-to-all-start.3) | async-done | bytes 262176 | tf_op jit(solution)/shard_map/all_to_all | solution.py:802
  222.2 4.9 collective-permute-done.35.refs_1_
  227.1 4.8 collective-permute-done.36.refs_2_
  232.4 8.2 %all-gather.19.cloned.1.call-done = bf16[1024,1024]{1,0:T(8,128)(2,1)} async-done(((bf16[256,1024]{1,0:T(8,128)(2,1)}), bf16[1024,1024]{1,0:T(8,128)(2,1)}) %all-gather.19.cloned.1.call-update) | async-done | bytes 2097168 | tf_op jit(solution)/shard_map/all_gather | solution.py:682
  242.8 6.3 %shard_map.214 = (bf16[1024,1024]{1,0:T(8,128)(2,1)}, bf16[1024,1024]{1,0:T(8,128)(2,1)}, bf16[1024,512]{1,0:T(8,128)(2,1)}, bf16[1024,512]{1,0:T(8,128)(2,1)}, ...) custom-call(bf16[128,1024]{1,0:T(8,128)(2,1)S(1)} %get-tuple-element.174.refs_0_, ...), custom_call_target="tpu_custom_call" | custom-call | tf_op jit(solution)/shard_map/pallas_call | solution.py:167
  272.5 6.1 %collective-permute-done.44.refs_2_ = bf16[128,1024]{1,0:T(8,128)(2,1)} collective-permute-done((bf16[128,1024]{1,0:T(8,128)(2,1)}, bf16[128,1024]{1,0:T(8,128)(2,1)}, u32[]{:S(2)}, u32[]{:S(2)}) %collective-permute-start.44) | collective-permute-done | bytes 262176 | tf_op jit(solution)/shard_map/ppermute | solution.py:40
  278.6 3.7 shard_map.216
  285.9 5.8 %collective-permute-done.46.refs_1_ = bf16[128,1024]{1,0:T(8,128)(2,1)S(1)} collective-permute-done((bf16[128,1024]{1,0:T(8,128)(2,1)S(1)}, bf16[128,1024]{1,0:T(8,128)(2,1)S(1)}, u32[]{:S(2)}, u32[]{:S(2)}) %collective-permute-start.46) | collective-permute-done | bytes 262176 | tf_op jit(solution)/shard_map/ppermute | solution.py:40
  291.7 6.9 %collective-permute-done.47.refs_2_ = bf16[128,1024]{1,0:T(8,128)(2,1)S(1)} collective-permute-done((bf16[128,1024]{1,0:T(8,128)(2,1)S(1)}, bf16[128,1024]{1,0:T(8,128)(2,1)S(1)}, u32[]{:S(2)}, u32[]{:S(2)}) %collective-permute-start.47) | collective-permute-done | bytes 262176 | tf_op jit(solution)/shard_map/ppermute | solution.py:40
  300.5 9.2 %shard_map.217 = (bf16[1024,1024]{1,0:T(8,128)(2,1)}, bf16[1024,384]{1,0:T(8,128)(2,1)}, f32[1,384]{1,0:T(1,128)S(1)}, bf16[512,1024]{1,0:T(8,128)(2,1)S(1)}, bf16[512,1024]{1,0:T(8,128)(2,1)}) custom-call(bf16[128,1024]{1,0:T(8,128)(2,1)S(1)} %get-tuple-element.193.refs_0_, bf16[128,1024]{1,0:T(8,128)(2,1)S(1)} %collective-permute-done.46.refs_1_, ...), custom_call_target="tpu_custom_call" | custom-call | tf_op jit(solution)/shard_map/pallas_call | solution.py:167
  324.8 5.2 collective-permute-done.55.refs_2_
  338.8 3.3 collective-permute-done.57.refs_1_
  342.1 5.2 collective-permute-done.58.refs_2_
  349.3 7.1 %shard_map.221 = (bf16[1024,1024]{1,0:T(8,128)(2,1)}, bf16[1024,512]{1,0:T(8,128)(2,1)}, f32[1,512]{1,0:T(1,128)S(1)}, bf16[512,1024]{1,0:T(8,128)(2,1)S(1)}, bf16[512,1024]{1,0:T(8,128)(2,1)}) custom-call(bf16[128,1024]{1,0:T(8,128)(2,1)S(1)} %broadcast_select_fusion.6.refs_0_.refs_6_, bf16[128,1024]{1,0:T(8,128)(2,1)S(1)} %collective-permute-done.57.refs_1_, ...), custom_call_target="tpu_custom_call" | custom-call | tf_op jit(solution)/shard_map/pallas_call | solution.py:167
  358.8 3.4 all-to-all-start.4
  373.3 5.6 %collective-permute-done.65.refs_1_ = bf16[128,1024]{1,0:T(8,128)(2,1)S(1)} collective-permute-done((bf16[128,1024]{1,0:T(8,128)(2,1)S(1)}, bf16[128,1024]{1,0:T(8,128)(2,1)S(1)}, u32[]{:S(2)}, u32[]{:S(2)}) %collective-permute-start.65) | collective-permute-done | bytes 262176 | tf_op jit(solution)/shard_map/ppermute | solution.py:40
  379.0 6.4 %collective-permute-done.66.refs_2_ = bf16[128,1024]{1,0:T(8,128)(2,1)S(1)} collective-permute-done((bf16[128,1024]{1,0:T(8,128)(2,1)S(1)}, bf16[128,1024]{1,0:T(8,128)(2,1)S(1)}, u32[]{:S(2)}, u32[]{:S(2)}) %collective-permute-start.66) | collective-permute-done | bytes 262176 | tf_op jit(solution)/shard_map/ppermute | solution.py:40
  391.6 5.8 %collective-permute-done.68.refs_1_ = bf16[128,1024]{1,0:T(8,128)(2,1)S(1)} collective-permute-done((bf16[128,1024]{1,0:T(8,128)(2,1)S(1)}, bf16[128,1024]{1,0:T(8,128)(2,1)S(1)}, u32[]{:S(2)}, u32[]{:S(2)}) %collective-permute-start.68) | collective-permute-done | bytes 262176 | tf_op jit(solution)/shard_map/ppermute | solution.py:40
  397.3 4.8 collective-permute-done.69.refs_2_
  404.1 9.1 %shard_map.224 = (bf16[1024,1024]{1,0:T(8,128)(2,1)}, bf16[1024,384]{1,0:T(8,128)(2,1)}, f32[1,384]{1,0:T(1,128)S(1)}, bf16[512,1024]{1,0:T(8,128)(2,1)S(1)}, bf16[512,1024]{1,0:T(8,128)(2,1)}) custom-call(bf16[128,1024]{1,0:T(8,128)(2,1)S(1)} %get-tuple-element.228.refs_0_, bf16[128,1024]{1,0:T(8,128)(2,1)S(1)} %collective-permute-done.68.refs_1_, ...), custom_call_target="tpu_custom_call" | custom-call | tf_op jit(solution)/shard_map/pallas_call | solution.py:167
  421.1 3.5 all-to-all-start.5
  426.2 27.7 %all-to-all-done.5 = bf16[4,256,512]{1,2,0:T(8,128)(2,1)S(1)} async-done(((bf16[4,256,512]{1,2,0:T(8,128)(2,1)}), bf16[4,256,512]{1,2,0:T(8,128)(2,1)S(1)}, u32[]{:S(2)}, u32[]{:S(2)}) %all-to-all-start.5) | async-done | bytes 1048608 | tf_op jit(solution)/shard_map/all_to_all | solution.py:865
  460.9 5.6 %collective-permute-done.77.refs_1_ = bf16[128,1024]{1,0:T(8,128)(2,1)S(1)} collective-permute-done((bf16[128,1024]{1,0:T(8,128)(2,1)S(1)}, bf16[128,1024]{1,0:T(8,128)(2,1)S(1)}, u32[]{:S(2)}, u32[]{:S(2)}) %collective-permute-start.77) | collective-permute-done | bytes 262176 | tf_op jit(solution)/shard_map/ppermute | solution.py:40
  466.5 6.0 %collective-permute-done.78.refs_2_ = bf16[128,1024]{1,0:T(8,128)(2,1)S(1)} collective-permute-done((bf16[128,1024]{1,0:T(8,128)(2,1)S(1)}, bf16[128,1024]{1,0:T(8,128)(2,1)S(1)}, u32[]{:S(2)}, u32[]{:S(2)}) %collective-permute-start.78) | collective-permute-done | bytes 262176 | tf_op jit(solution)/shard_map/ppermute | solution.py:40
  476.2 3.4 all-to-all-start.6
  483.2 9.3 %collective-permute-done.81 = bf16[256,512]{1,0:T(8,128)(2,1)S(1)} collective-permute-done((bf16[256,512]{1,0:T(8,128)(2,1)S(1)}, bf16[256,512]{1,0:T(8,128)(2,1)S(1)}, u32[]{:S(2)}, u32[]{:S(2)}) %collective-permute-start.81) | collective-permute-done | bytes 262176 | tf_op jit(solution)/shard_map/ppermute | solution.py:40
  496.2 3.5 all-to-all-start.7
  499.7 3.6 collective-permute-done.82
  509.6 12.1 %all-gather.27.cloned.1.call-done = bf16[2112,256]{1,0:T(8,128)(2,1)} async-done(((bf16[528,256]{1,0:T(8,128)(2,1)}), bf16[2112,256]{1,0:T(8,128)(2,1)}) %all-gather.27.cloned.1.call-update) | async-done | bytes 1081360 | tf_op jit(solution)/shard_map/all_gather | solution.py:872
  525.5 8.9 %all-to-all-done.7 = bf16[4,528,256]{2,1,0:T(8,128)(2,1)S(1)} async-done(((bf16[4,528,256]{2,1,0:T(8,128)(2,1)}), bf16[4,528,256]{2,1,0:T(8,128)(2,1)S(1)}, u32[]{:S(2)}, u32[]{:S(2)}) %all-to-all-start.7) | async-done | bytes 1081376 | tf_op jit(solution)/shard_map/all_to_all | solution.py:64
  537.7 6.1 %collective-permute-done.80 = bf16[528,256]{1,0:T(8,128)(2,1)S(1)} collective-permute-done((bf16[528,256]{1,0:T(8,128)(2,1)S(1)}, bf16[528,256]{1,0:T(8,128)(2,1)S(1)}, u32[]{:S(2)}, u32[]{:S(2)}) %collective-permute-start.80) | collective-permute-done | bytes 270368 | tf_op jit(solution)/shard_map/ppermute | solution.py:40
  (517 shorter events, 218.4 us)
Async XLA Ops:
  9.3 37.4 %all-to-all-start = ((bf16[4,512,256]{2,1,0:T(8,128)(2,1)}), bf16[4,512,256]{2,1,0:T(8,128)(2,1)S(1)}, u32[]{:S(2)}, u32[]{:S(2)}) async-start(bf16[4,512,256]{2,1,0:T(8,128)(2,1)} %broadcast_in_dim.160), calls=%async_computation | async-start | bytes 2097152 | tf_op jit(solution)/shard_map/all_to_all | solution.py:64
  15.7 58.1 %all-gather.13.cloned.1.call-start = ((), (), s32[]{:S(2)}) async-start(), calls=%async_computation.12 | async-start | bytes 1310720 | tf_op jit(solution)/shard_map/all_gather | solution.py:681
  17.3 23.8 %collective-permute-start = (bf16[256,512]{1,0:T(8,128)(2,1)}, bf16[256,512]{1,0:T(8,128)(2,1)}, u32[]{:S(2)}, u32[]{:S(2)}) collective-permute-start(bf16[256,512]{1,0:T(8,128)(2,1)} %broadcast_select_fusion.13), channel_id=1, source_target_pairs={{0,16},{1,17},{2,18},{3,19},{16,0},{17,1},{18,2},{19,3},{4,20},{5,... | collective-permute-start | bytes 786440 | tf_op jit(solution)/shard_map/ppermute | solution.py:40
  20.4 24.0 %collective-permute-start.1 = (bf16[256,1024]{1,0:T(8,128)(2,1)S(1)}, bf16[256,1024]{1,0:T(8,128)(2,1)}, u32[]{:S(2)}, u32[]{:S(2)}) collective-permute-start(bf16[256,1024]{1,0:T(8,128)(2,1)S(1)} %broadcast_select_fusion.4), channel_id=1, source_target_pairs={{0,16},{1,17},{2,18},{3,19},{16,0},{17,1},{18,2},{19,3},{4,20},{5,... | collective-permute-start | bytes 1572872 | tf_op jit(solution)/shard_map/ppermute | solution.py:40
  51.7 68.2 %all-gather.15.cloned.1.call-start = ((), (), s32[]{:S(2)}) async-start(), calls=%async_computation.13 | async-start | bytes 2621440 | tf_op jit(solution)/shard_map/all_gather | solution.py:682
  59.7 13.6 %collective-permute-start.3 = (bf16[128,1024]{1,0:T(8,128)(2,1)S(1)}, bf16[128,1024]{1,0:T(8,128)(2,1)S(1)}, u32[]{:S(2)}, u32[]{:S(2)}) collective-permute-start(bf16[128,1024]{1,0:T(8,128)(2,1)S(1)} %shard_map.204.refs_0_), channel_id=1, source_target_pairs={{0,16},{1,17},{2,18},{3,19},{16,0},{17,1},{18,2},{19,3},{4,20},{5,... | collective-permute-start | bytes 786440 | tf_op jit(solution)/shard_map/ppermute | solution.py:40
  60.2 13.0 %collective-permute-start.4 = (bf16[128,1024]{1,0:T(8,128)(2,1)S(1)}, bf16[128,1024]{1,0:T(8,128)(2,1)S(1)}, u32[]{:S(2)}, u32[]{:S(2)}) collective-permute-start(bf16[128,1024]{1,0:T(8,128)(2,1)S(1)} %shard_map.204.refs_0_), channel_id=1, source_target_pairs={{0,18},{1,19},{2,16},{3,17},{16,2},{17,3},{18,0},{19,1},{4,22},{5,... | collective-permute-start | bytes 786440 | tf_op jit(solution)/shard_map/ppermute | solution.py:40
  90.3 13.7 %collective-permute-start.11 = (bf16[128,1024]{1,0:T(8,128)(2,1)S(1)}, bf16[128,1024]{1,0:T(8,128)(2,1)S(1)}, u32[]{:S(2)}, u32[]{:S(2)}) collective-permute-start(bf16[128,1024]{1,0:T(8,128)(2,1)S(1)} %get-tuple-element.150), channel_id=1, source_target_pairs={{0,16},{1,17},{2,18},{3,19},{16,0},{17,1},{18,2},{19,3},{4,20},{5,... | collective-permute-start | bytes 786440 | tf_op jit(solution)/shard_map/ppermute | solution.py:40
  91.0 13.1 %collective-permute-start.12 = (bf16[128,1024]{1,0:T(8,128)(2,1)S(1)}, bf16[128,1024]{1,0:T(8,128)(2,1)S(1)}, u32[]{:S(2)}, u32[]{:S(2)}) collective-permute-start(bf16[128,1024]{1,0:T(8,128)(2,1)S(1)} %get-tuple-element.151), channel_id=1, source_target_pairs={{0,18},{1,19},{2,16},{3,17},{16,2},{17,3},{18,0},{19,1},{4,22},{5,... | collective-permute-start | bytes 786440 | tf_op jit(solution)/shard_map/ppermute | solution.py:40
  111.4 48.3 %all-to-all-start.2 = ((bf16[4,512,256]{2,1,0:T(8,128)(2,1)}), bf16[4,512,256]{2,1,0:T(8,128)(2,1)}, u32[]{:S(2)}, u32[]{:S(2)}) async-start(bf16[4,512,256]{2,1,0:T(8,128)(2,1)} %broadcast_in_dim.165), calls=%async_computation.2 | async-start | bytes 2097152 | tf_op jit(solution)/shard_map/all_to_all | solution.py:64
  116.3 62.9 %all-gather.17.cloned.1.call-start = ((), (), s32[]{:S(2)}) async-start(), calls=%async_computation.14 | async-start | bytes 1310720 | tf_op jit(solution)/shard_map/all_gather | solution.py:681
  130.7 87.2 %all-gather.25.cloned.1.call-start = ((), (), s32[]{:S(2)}) async-start(), calls=%async_computation.22 | async-start | bytes 2359296 | tf_op jit(solution)/shard_map/all_gather | solution.py:799
  141.9 13.7 %collective-permute-start.23 = (bf16[128,1024]{1,0:T(8,128)(2,1)}, bf16[128,1024]{1,0:T(8,128)(2,1)}, u32[]{:S(2)}, u32[]{:S(2)}) collective-permute-start(bf16[128,1024]{1,0:T(8,128)(2,1)} %get-tuple-element.159), channel_id=1, source_target_pairs={{0,18},{1,19},{2,16},{3,17},{16,2},{17,3},{18,0},{19,1},{4,22},{5,... | collective-permute-start | bytes 786440 | tf_op jit(solution)/shard_map/ppermute | solution.py:40
  162.6 78.0 %all-gather.19.cloned.1.call-start = ((), (), s32[]{:S(2)}) async-start(), calls=%async_computation.15 | async-start | bytes 2621440 | tf_op jit(solution)/shard_map/all_gather | solution.py:682
  163.7 13.6 %collective-permute-start.25 = (bf16[128,1024]{1,0:T(8,128)(2,1)S(1)}, bf16[128,1024]{1,0:T(8,128)(2,1)}, u32[]{:S(2)}, u32[]{:S(2)}) collective-permute-start(bf16[128,1024]{1,0:T(8,128)(2,1)S(1)} %get-tuple-element.163.refs_0_), channel_id=1, source_target_pairs={{0,16},{1,17},{2,18},{3,19},{16,0},{17,1},{18,2},{19,3},{4,20},{5,... | collective-permute-start | bytes 786440 | tf_op jit(solution)/shard_map/ppermute | solution.py:40
  165.5 13.7 %collective-permute-start.26 = (bf16[128,1024]{1,0:T(8,128)(2,1)S(1)}, bf16[128,1024]{1,0:T(8,128)(2,1)}, u32[]{:S(2)}, u32[]{:S(2)}) collective-permute-start(bf16[128,1024]{1,0:T(8,128)(2,1)S(1)} %get-tuple-element.163.refs_0_), channel_id=1, source_target_pairs={{0,18},{1,19},{2,16},{3,17},{16,2},{17,3},{18,0},{19,1},{4,22},{5,... | collective-permute-start | bytes 786440 | tf_op jit(solution)/shard_map/ppermute | solution.py:40
  166.7 12.5 %collective-permute-start.27 = (bf16[128,1024]{1,0:T(8,128)(2,1)S(1)}, bf16[128,1024]{1,0:T(8,128)(2,1)}, u32[]{:S(2)}, u32[]{:S(2)}) collective-permute-start(bf16[128,1024]{1,0:T(8,128)(2,1)S(1)} %get-tuple-element.163.refs_0_), channel_id=1, source_target_pairs={{0,1},{1,0},{2,3},{3,2},{16,17},{17,16},{18,19},{19,18},{4,5},{5,4... | collective-permute-start | bytes 786440 | tf_op jit(solution)/shard_map/ppermute | solution.py:40
  196.6 19.2 %collective-permute-start.32 = (bf16[128,1024]{1,0:T(8,128)(2,1)}, bf16[128,1024]{1,0:T(8,128)(2,1)S(1)}, u32[]{:S(2)}, u32[]{:S(2)}) collective-permute-start(bf16[128,1024]{1,0:T(8,128)(2,1)} %get-tuple-element.169), channel_id=1, source_target_pairs={{0,2},{1,3},{2,0},{3,1},{16,18},{17,19},{18,16},{19,17},{4,6},{5,7... | collective-permute-start | bytes 786440 | tf_op jit(solution)/shard_map/ppermute | solution.py:40
  198.5 17.3 %collective-permute-start.33 = (bf16[128,1024]{1,0:T(8,128)(2,1)S(1)}, bf16[128,1024]{1,0:T(8,128)(2,1)S(1)}, u32[]{:S(2)}, u32[]{:S(2)}) collective-permute-start(bf16[128,1024]{1,0:T(8,128)(2,1)S(1)} %get-tuple-element.170), channel_id=1, source_target_pairs={{0,16},{1,17},{2,18},{3,19},{16,0},{17,1},{18,2},{19,3},{4,20},{5,... | collective-permute-start | bytes 786440 | tf_op jit(solution)/shard_map/ppermute | solution.py:40
  198.7 17.1 %collective-permute-start.34 = (bf16[128,1024]{1,0:T(8,128)(2,1)S(1)}, bf16[128,1024]{1,0:T(8,128)(2,1)S(1)}, u32[]{:S(2)}, u32[]{:S(2)}) collective-permute-start(bf16[128,1024]{1,0:T(8,128)(2,1)S(1)} %get-tuple-element.171), channel_id=1, source_target_pairs={{0,18},{1,19},{2,16},{3,17},{16,2},{17,3},{18,0},{19,1},{4,22},{5,... | collective-permute-start | bytes 786440 | tf_op jit(solution)/shard_map/ppermute | solution.py:40
  207.8 61.0 %all-gather.21.cloned.1.call-start = ((), (), s32[]{:S(2)}) async-start(), calls=%async_computation.16 | async-start | bytes 1310720 | tf_op jit(solution)/shard_map/all_gather | solution.py:804
  215.2 117.6 %reduce-scatter.5.cloned.1.call-start = ((), (), s32[]{:S(2)}) async-start(), calls=%async_computation.17 | async-start | bytes 2359296 | tf_op jit(solution)/shard_map/reduce_scatter | solution.py:810
  218.4 13.5 %collective-permute-start.36 = (bf16[128,1024]{1,0:T(8,128)(2,1)S(1)}, bf16[128,1024]{1,0:T(8,128)(2,1)S(1)}, u32[]{:S(2)}, u32[]{:S(2)}) collective-permute-start(bf16[128,1024]{1,0:T(8,128)(2,1)S(1)} %get-tuple-element.174.refs_0_), channel_id=1, source_target_pairs={{0,16},{1,17},{2,18},{3,19},{16,0},{17,1},{18,2},{19,3},{4,20},{5,... | collective-permute-start | bytes 786440 | tf_op jit(solution)/shard_map/ppermute | solution.py:40
  222.2 20.3 %collective-permute-start.38 = (bf16[128,1024]{1,0:T(8,128)(2,1)S(1)}, bf16[128,1024]{1,0:T(8,128)(2,1)S(1)}, u32[]{:S(2)}, u32[]{:S(2)}) collective-permute-start(bf16[128,1024]{1,0:T(8,128)(2,1)S(1)} %get-tuple-element.174.refs_0_), channel_id=1, source_target_pairs={{0,1},{1,0},{2,3},{3,2},{16,17},{17,16},{18,19},{19,18},{4,5},{5,4... | collective-permute-start | bytes 786440 | tf_op jit(solution)/shard_map/ppermute | solution.py:40
  227.1 15.4 %collective-permute-start.39 = (bf16[128,1024]{1,0:T(8,128)(2,1)S(1)}, bf16[128,1024]{1,0:T(8,128)(2,1)}, u32[]{:S(2)}, u32[]{:S(2)}) collective-permute-start(bf16[128,1024]{1,0:T(8,128)(2,1)S(1)} %collective-permute-done.35.refs_1_), channel_id=1, source_target_pairs={{0,1},{1,0},{2,3},{3,2},{16,17},{17,16},{18,19},{19,18},{4,5},{5,4... | collective-permute-start | bytes 786440 | tf_op jit(solution)/shard_map/ppermute | solution.py:40
  256.8 131.2 %reduce-scatter.7.cloned.1.call-start = ((), (), s32[]{:S(2)}) async-start(), calls=%async_computation.18 | async-start | bytes 2621440 | tf_op jit(solution)/shard_map/reduce_scatter | solution.py:838
  262.9 163.3 %reduce-scatter.9.cloned.1.call-start = ((), (), s32[]{:S(2)}) async-start(), calls=%async_computation.19 | async-start | bytes 1310720 | tf_op jit(solution)/shard_map/reduce_scatter | solution.py:838
  264.6 14.0 %collective-permute-start.44 = (bf16[128,1024]{1,0:T(8,128)(2,1)}, bf16[128,1024]{1,0:T(8,128)(2,1)}, u32[]{:S(2)}, u32[]{:S(2)}) collective-permute-start(bf16[128,1024]{1,0:T(8,128)(2,1)} %copy-done.20), channel_id=1, source_target_pairs={{0,16},{1,17},{2,18},{3,19},{16,0},{17,1},{18,2},{19,3},{4,20},{5,... | collective-permute-start | bytes 786440 | tf_op jit(solution)/shard_map/ppermute | solution.py:40
  266.1 12.6 %collective-permute-start.45 = (bf16[128,1024]{1,0:T(8,128)(2,1)}, bf16[128,1024]{1,0:T(8,128)(2,1)}, u32[]{:S(2)}, u32[]{:S(2)}) collective-permute-start(bf16[128,1024]{1,0:T(8,128)(2,1)} %copy-done.19), channel_id=1, source_target_pairs={{0,18},{1,19},{2,16},{3,17},{16,2},{17,3},{18,0},{19,1},{4,22},{5,... | collective-permute-start | bytes 786440 | tf_op jit(solution)/shard_map/ppermute | solution.py:40
  283.6 15.0 %collective-permute-start.47 = (bf16[128,1024]{1,0:T(8,128)(2,1)S(1)}, bf16[128,1024]{1,0:T(8,128)(2,1)S(1)}, u32[]{:S(2)}, u32[]{:S(2)}) collective-permute-start(bf16[128,1024]{1,0:T(8,128)(2,1)S(1)} %get-tuple-element.193.refs_0_), channel_id=1, source_target_pairs={{0,16},{1,17},{2,18},{3,19},{16,0},{17,1},{18,2},{19,3},{4,20},{5,... | collective-permute-start | bytes 786440 | tf_op jit(solution)/shard_map/ppermute | solution.py:40
  284.4 14.1 %collective-permute-start.48 = (bf16[128,1024]{1,0:T(8,128)(2,1)S(1)}, bf16[128,1024]{1,0:T(8,128)(2,1)S(1)}, u32[]{:S(2)}, u32[]{:S(2)}) collective-permute-start(bf16[128,1024]{1,0:T(8,128)(2,1)S(1)} %get-tuple-element.193.refs_0_), channel_id=1, source_target_pairs={{0,18},{1,19},{2,16},{3,17},{16,2},{17,3},{18,0},{19,1},{4,22},{5,... | collective-permute-start | bytes 786440 | tf_op jit(solution)/shard_map/ppermute | solution.py:40
  285.9 13.2 %collective-permute-start.49 = (bf16[128,1024]{1,0:T(8,128)(2,1)S(1)}, bf16[128,1024]{1,0:T(8,128)(2,1)S(1)}, u32[]{:S(2)}, u32[]{:S(2)}) collective-permute-start(bf16[128,1024]{1,0:T(8,128)(2,1)S(1)} %get-tuple-element.193.refs_0_), channel_id=1, source_target_pairs={{0,1},{1,0},{2,3},{3,2},{16,17},{17,16},{18,19},{19,18},{4,5},{5,4... | collective-permute-start | bytes 786440 | tf_op jit(solution)/shard_map/ppermute | solution.py:40
  315.7 14.3 %collective-permute-start.55 = (bf16[128,1024]{1,0:T(8,128)(2,1)S(1)}, bf16[128,1024]{1,0:T(8,128)(2,1)S(1)}, u32[]{:S(2)}, u32[]{:S(2)}) collective-permute-start(bf16[128,1024]{1,0:T(8,128)(2,1)S(1)} %get-tuple-element.205), channel_id=1, source_target_pairs={{0,16},{1,17},{2,18},{3,19},{16,0},{17,1},{18,2},{19,3},{4,20},{5,... | collective-permute-start | bytes 786440 | tf_op jit(solution)/shard_map/ppermute | solution.py:40
  334.3 13.0 %collective-permute-start.58 = (bf16[128,1024]{1,0:T(8,128)(2,1)S(1)}, bf16[128,1024]{1,0:T(8,128)(2,1)S(1)}, u32[]{:S(2)}, u32[]{:S(2)}) collective-permute-start(bf16[128,1024]{1,0:T(8,128)(2,1)S(1)} %broadcast_select_fusion.6.refs_0_.refs_6_), channel_id=1, source_target_pairs={{0,16},{1,17},{2,18},{3,19},{16,0},{17,1},{18,2},{19,3},{4,20},{5,... | collective-permute-start | bytes 786440 | tf_op jit(solution)/shard_map/ppermute | solution.py:40
  334.9 12.3 %collective-permute-start.59 = (bf16[128,1024]{1,0:T(8,128)(2,1)S(1)}, bf16[128,1024]{1,0:T(8,128)(2,1)S(1)}, u32[]{:S(2)}, u32[]{:S(2)}) collective-permute-start(bf16[128,1024]{1,0:T(8,128)(2,1)S(1)} %broadcast_select_fusion.6.refs_0_.refs_6_), channel_id=1, source_target_pairs={{0,18},{1,19},{2,16},{3,17},{16,2},{17,3},{18,0},{19,1},{4,22},{5,... | collective-permute-start | bytes 786440 | tf_op jit(solution)/shard_map/ppermute | solution.py:40
  358.8 29.1 %all-to-all-start.4 = ((bf16[8,80,256]{2,1,0:T(8,128)(2,1)}), bf16[8,80,256]{2,1,0:T(8,128)(2,1)S(1)}, u32[]{:S(2)}, u32[]{:S(2)}) async-start(bf16[8,80,256]{2,1,0:T(8,128)(2,1)} %maximum_maximum_fusion), calls=%async_computation.6 | async-start | bytes 655360 | tf_op jit(solution)/shard_map/all_to_all | solution.py:823
  362.3 91.6 %reduce-scatter.11.cloned.1.call-start = ((), (), s32[]{:S(2)}) async-start(), calls=%async_computation.20 | async-start | bytes 2621440 | tf_op jit(solution)/shard_map/reduce_scatter | solution.py:838
  371.7 13.7 %collective-permute-start.66 = (bf16[128,1024]{1,0:T(8,128)(2,1)S(1)}, bf16[128,1024]{1,0:T(8,128)(2,1)S(1)}, u32[]{:S(2)}, u32[]{:S(2)}) collective-permute-start(bf16[128,1024]{1,0:T(8,128)(2,1)S(1)} %get-tuple-element.221), channel_id=1, source_target_pairs={{0,16},{1,17},{2,18},{3,19},{16,0},{17,1},{18,2},{19,3},{4,20},{5,... | collective-permute-start | bytes 786440 | tf_op jit(solution)/shard_map/ppermute | solution.py:40
  389.3 12.9 %collective-permute-start.69 = (bf16[128,1024]{1,0:T(8,128)(2,1)S(1)}, bf16[128,1024]{1,0:T(8,128)(2,1)S(1)}, u32[]{:S(2)}, u32[]{:S(2)}) collective-permute-start(bf16[128,1024]{1,0:T(8,128)(2,1)S(1)} %get-tuple-element.228.refs_0_), channel_id=1, source_target_pairs={{0,16},{1,17},{2,18},{3,19},{16,0},{17,1},{18,2},{19,3},{4,20},{5,... | collective-permute-start | bytes 786440 | tf_op jit(solution)/shard_map/ppermute | solution.py:40
  421.1 32.8 %all-to-all-start.5 = ((bf16[4,256,512]{1,2,0:T(8,128)(2,1)}), bf16[4,256,512]{1,2,0:T(8,128)(2,1)S(1)}, u32[]{:S(2)}, u32[]{:S(2)}) async-start(bf16[4,256,512]{1,2,0:T(8,128)(2,1)} %bitcast.244), calls=%async_computation.7 | async-start | bytes 2097152 | tf_op jit(solution)/shard_map/all_to_all | solution.py:865
  424.6 82.5 %all-gather.23.cloned.1.call-start = ((), (), s32[]{:S(2)}) async-start(), calls=%async_computation.21 | async-start | bytes 1310720 | tf_op jit(solution)/shard_map/all_gather | solution.py:871
  458.8 13.7 %collective-permute-start.78 = (bf16[128,1024]{1,0:T(8,128)(2,1)S(1)}, bf16[128,1024]{1,0:T(8,128)(2,1)S(1)}, u32[]{:S(2)}, u32[]{:S(2)}) collective-permute-start(bf16[128,1024]{1,0:T(8,128)(2,1)S(1)} %get-tuple-element.258), channel_id=1, source_target_pairs={{0,16},{1,17},{2,18},{3,19},{16,0},{17,1},{18,2},{19,3},{4,20},{5,... | collective-permute-start | bytes 786440 | tf_op jit(solution)/shard_map/ppermute | solution.py:40
  476.2 18.8 %all-to-all-start.6 = ((bf16[8,80,256]{2,1,0:T(8,128)(2,1)}), bf16[8,80,256]{2,1,0:T(8,128)(2,1)S(1)}, u32[]{:S(2)}, u32[]{:S(2)}) async-start(bf16[8,80,256]{2,1,0:T(8,128)(2,1)} %maximum_maximum_fusion.1), calls=%async_computation.10 | async-start | bytes 655360 | tf_op jit(solution)/shard_map/all_to_all | solution.py:823
  479.7 42.0 %all-gather.27.cloned.1.call-start = ((), (), s32[]{:S(2)}) async-start(), calls=%async_computation.23 | async-start | bytes 1351680 | tf_op jit(solution)/shard_map/all_gather | solution.py:872
  480.2 12.2 %collective-permute-start.81 = (bf16[256,512]{1,0:T(8,128)(2,1)S(1)}, bf16[256,512]{1,0:T(8,128)(2,1)S(1)}, u32[]{:S(2)}, u32[]{:S(2)}) collective-permute-start(bf16[256,512]{1,0:T(8,128)(2,1)S(1)} %broadcast_select_fusion.9), channel_id=1, source_target_pairs={{0,16},{1,17},{2,18},{3,19},{16,0},{17,1},{18,2},{19,3},{4,20},{5,... | collective-permute-start | bytes 786440 | tf_op jit(solution)/shard_map/ppermute | solution.py:40
  483.0 20.3 %collective-permute-start.82 = (bf16[256,1024]{1,0:T(8,128)(2,1)}, bf16[256,1024]{1,0:T(8,128)(2,1)}, u32[]{:S(2)}, u32[]{:S(2)}) collective-permute-start(bf16[256,1024]{1,0:T(8,128)(2,1)} %broadcast_select_fusion), channel_id=1, source_target_pairs={{0,16},{1,17},{2,18},{3,19},{16,0},{17,1},{18,2},{19,3},{4,20},{5,... | collective-permute-start | bytes 1572872 | tf_op jit(solution)/shard_map/ppermute | solution.py:40
  496.2 38.3 %all-to-all-start.7 = ((bf16[4,528,256]{2,1,0:T(8,128)(2,1)}), bf16[4,528,256]{2,1,0:T(8,128)(2,1)S(1)}, u32[]{:S(2)}, u32[]{:S(2)}) async-start(bf16[4,528,256]{2,1,0:T(8,128)(2,1)} %broadcast_in_dim.169), calls=%async_computation.11 | async-start | bytes 2162688 | tf_op jit(solution)/shard_map/all_to_all | solution.py:64
  509.2 15.4 %collective-permute-start.76 = (bf16[512,256]{1,0:T(8,128)(2,1)S(1)}, bf16[512,256]{1,0:T(8,128)(2,1)S(1)}, u32[]{:S(2)}, u32[]{:S(2)}) collective-permute-start(bf16[512,256]{1,0:T(8,128)(2,1)S(1)} %get-tuple-element.428), channel_id=1, source_target_pairs={{0,16},{1,17},{2,18},{3,19},{16,0},{17,1},{18,2},{19,3},{4,20},{5,... | collective-permute-start | bytes 786440 | tf_op jit(solution)/shard_map/ppermute | solution.py:40
  (118 other events, 908.0 us)
Sparse Core Ops, SparseCore 0:
  43.1 28.2 all-gather.12
  73.5 46.1 all-gather.14
  130.8 28.6 all-gather.16
  162.7 29.4 all-gather.24
  193.6 46.9 all-gather.18
  242.0 26.6 all-gather.20
  272.0 40.7 reduce-scatter.4
  315.2 43.8 reduce-scatter.6
  361.4 26.4 reduce-scatter.8
  390.2 44.3 reduce-scatter.10
  454.1 26.9 all-gather.22
  483.3 38.3 all-gather.26

commit v5 on v4

v5 whole, which is shorter than its diff:
```python
import functools

import jax
import jax.numpy as jnp
from jax import lax
from jax.experimental import pallas as pl
from jax.experimental.pallas import tpu as pltpu
from jax.sharding import PartitionSpec as P

HEAD_DIM = 64
epsilon = 1e-05
far_away = 1e34
F32 = jnp.float32
BF16 = jnp.bfloat16
PLANE = ("section", "col")
ROOM = 28
PIECES = 4
BLOCK_COST = 9200000000
TERM_COST = 5000000000
NORM_COST = 2500000000


def mm(a, b, dims):
    return lax.dot_general(a, b, ((dims[0], dims[1]), ((), ())), preferred_element_type=F32)


def nn(a, b):
    return mm(a, b, ((1,), (0,)))


def nt(a, b):
    return mm(a, b, ((1,), (1,)))


def tn(a, b):
    return mm(a, b, ((0,), (0,)))


def plane_size():
    return lax.axis_size("section") * lax.axis_size("col")


def send(array, mask):
    return lax.ppermute(array, PLANE, [(i, i ^ mask) for i in range(plane_size())])


def far_masks():
    return list(range(2, plane_size(), 2))


def spread(own):
    return [own] + [send(own, m) for m in far_masks()]


def sum_up(kept, sends, later=()):
    if later:
        kept, *later = together(kept, *later)
    return [kept] + [send(o, m) for o, m in zip(sends, far_masks())], later


def together(*values):
    return lax.optimization_barrier(values)


def gather_direct(array):
    count = lax.axis_size("row")
    copies = jnp.broadcast_to(array[None], (count,) + array.shape)
    return lax.all_to_all(copies, "row", split_axis=0, concat_axis=0)


def owned_layout(lengths, deal, holder, rows_dev):
    starts = jnp.cumsum(lengths) - lengths
    first = deal == 2 * holder
    second = deal == 2 * holder + 1
    first_len = jnp.sum(jnp.where(first, lengths, 0))
    second_len = jnp.sum(jnp.where(second, lengths, 0))
    first_start = jnp.sum(jnp.where(first, starts, 0))
    second_start = jnp.sum(jnp.where(second, starts, 0))
    slots = jnp.arange(rows_dev, dtype=jnp.int32)
    in_first = slots < first_len
    in_second = jnp.logical_and(jnp.logical_not(in_first), slots < first_len + second_len)
    usable = jnp.logical_or(in_first, in_second)
    position = jnp.where(in_first, slots, slots - first_len)
    source = jnp.where(in_first, first_start + slots, second_start + position)
    source = jnp.where(usable, source, -1)
    segment = jnp.where(in_first, 0, jnp.where(in_second, 1, 2)).astype(jnp.int32)
    return source, usable, segment, position


def given_targets(lengths, deal, positions, rows_dev):
    starts = jnp.cumsum(lengths) - lengths
    before = deal[None, :] == (deal - 1)[:, None]
    partner_len = jnp.sum(jnp.where(before, lengths[None, :], 0), axis=1)
    offset = jnp.where(deal % 2 == 1, partner_len, 0)
    base = deal // 2 * rows_dev + offset - starts
    inside = jnp.logical_and(
        positions[:, None] >= starts[None, :], positions[:, None] < (starts + lengths)[None, :]
    )
    target = jnp.sum(jnp.where(inside, base[None, :] + positions[:, None], 0), axis=1)
    return jnp.where(jnp.any(inside, axis=1), target, -1)


def pick_rows(rows, wanted):
    onehot = (wanted[:, None] == jnp.arange(rows.shape[0], dtype=jnp.int32)[None, :]).astype(BF16)
    return nn(onehot, rows)


class Moves:
    def __init__(self):
        self.loads, self.stores, self.started = {}, {}, []

    def need(self, *refs):
        for ref in refs:
            if id(ref) in self.loads:
                self.loads.pop(id(ref)).wait()

    def put(self, *refs):
        for ref in refs:
            if id(ref) in self.stores:
                copy = self.stores.pop(id(ref))
                copy.start()
                self.started.append(copy)

    def finish(self):
        for copy in self.started:
            copy.wait()


def run(kernel, outs, *args, scalars=0, scratch=(), room=10, cost=0, load=(), store=()):
    vmem, hbm, smem = [pl.BlockSpec(memory_space=m) for m in (pltpu.VMEM, pltpu.HBM, pltpu.SMEM)]
    n_in, n_out = len(args), len(outs)
    load = [i % n_in for i in load]
    buffers = [(args[i].shape, args[i].dtype) for i in load] + [outs[i] for i in store]

    def body(*refs):
        refs = list(refs)
        ins, results, rest = refs[:n_in], refs[n_in : n_in + n_out], refs[n_in + n_out :]
        own, held = rest[: len(scratch)], rest[len(scratch) : len(scratch) + len(buffers)]
        moves = Moves()
        for i, place in enumerate(load):
            copy = pltpu.make_async_copy(ins[place], held[i], rest[-1].at[i])
            copy.start()
            moves.loads[id(held[i])] = copy
            ins[place] = held[i]
        for i, place in enumerate(store, len(load)):
            copy = pltpu.make_async_copy(held[i], results[place], rest[-1].at[i])
            moves.stores[id(held[i])] = copy
            results[place] = held[i]
        kernel(moves, *ins, *results, *own)
        moves.finish()

    shapes = [pltpu.VMEM(shape, kind) for shape, kind in [*scratch, *buffers]]
    call = pl.pallas_call(
        body,
        out_shape=[
            pltpu.HBM(shape, kind) if i in store else jax.ShapeDtypeStruct(shape, kind)
            for i, (shape, kind) in enumerate(outs)
        ],
        in_specs=[
            hbm if i in load else smem if i >= n_in - scalars else vmem for i in range(n_in)
        ],
        out_specs=[hbm if i in store else vmem for i in range(n_out)],
        scratch_shapes=shapes + [pltpu.SemaphoreType.DMA((len(buffers),))] * bool(buffers),
        cost_estimate=pl.CostEstimate(flops=cost, bytes_accessed=0, transcendentals=0),
        compiler_params=pltpu.CompilerParams(vmem_limit_bytes=room * 2**20),
    )
    args = [
        pltpu.with_memory_space_constraint(a, pltpu.HBM) if i in load else a
        for i, a in enumerate(args)
    ]
    return list(call(*args))


def collect(blocks, rows_ref):
    size = blocks[0].shape[0]
    for i, block in enumerate(blocks):
        rows_ref[i * size : (i + 1) * size, :] = block[...]


def tiles(total, most=256):
    size = min(total, most)
    return [slice(i, i + size) for i in range(0, total, size)]


def norm_stats(hidden):
    average = jnp.mean(hidden, axis=1, keepdims=True)
    square = jnp.mean(hidden * hidden, axis=1, keepdims=True)
    inverse = lax.rsqrt(square - average * average + epsilon)
    return (hidden - average) * inverse, inverse


def norm_kernel(moves, hidden, gain, shift, normed):
    centered, _ = norm_stats(hidden[...].astype(F32))
    normed[...] = (centered * gain[...] + shift[...]).astype(BF16)


def add_norm_kernel(count, moves, *refs):
    parts, (hidden, bias, gain, shift, middle, normed) = refs[:count], refs[count:]
    total = bias[...] + parts[1][...].astype(F32)
    for part in parts[2:]:
        total = total + part[...].astype(F32)
    moves.need(parts[0], hidden)
    total = total + parts[0][...] + hidden[...].astype(F32)
    middle[...] = total
    moves.put(middle)
    centered, _ = norm_stats(total)
    normed[...] = (centered * gain[...] + shift[...]).astype(BF16)


def end_norm_kernel(count, moves, *refs):
    parts, (hidden, bias, gain, shift, usable, result, normed) = refs[:count], refs[count:]
    total = bias[...] + parts[1][...].astype(F32)
    for part in parts[2:]:
        total = total + part[...].astype(F32)
    moves.need(parts[0], hidden)
    total = total + parts[0][...] + hidden[...]
    rounded = jnp.where(usable[...] > 0, total, 0.0).astype(BF16)
    result[...] = rounded
    moves.put(result)
    centered, _ = norm_stats(rounded.astype(F32))
    normed[...] = (centered * gain[...] + shift[...]).astype(BF16)


def norm_back_kernel(count, moves, *refs):
    parts, rest = refs[:count], refs[count:]
    hidden, gain, grad_out, grad_in, rounded, sums = rest
    grad = parts[1][...].astype(F32)
    for part in parts[2:]:
        grad = grad + part[...].astype(F32)
    moves.need(hidden, parts[0], grad_out)
    grad = grad + parts[0][...]
    centered, inverse = norm_stats(hidden[...].astype(F32))
    grad_cent = grad * gain[...]
    mean = jnp.mean(grad_cent, axis=1, keepdims=True)
    cross = jnp.mean(grad_cent * centered, axis=1, keepdims=True)
    total = grad_out[...].astype(F32) + inverse * (grad_cent - mean - centered * cross)
    low = total.astype(BF16)
    grad_in[...] = total
    moves.put(grad_in)
    rounded[...] = low
    sums[0:1, :] = jnp.sum(grad * centered, axis=0, keepdims=True)
    sums[1:2, :] = jnp.sum(grad, axis=0, keepdims=True)
    sums[2:3, :] = jnp.sum(low.astype(F32), axis=0, keepdims=True)


class Slices:
    def __init__(self, refs):
        self.mine, *self.other = refs
        self.rows = self.mine.shape[0] // PIECES

    def times(self, left, k, columns):
        if k == 0:
            return nn(left[...], self.mine[:, columns])
        total = 0.0
        for i, piece in enumerate(self.other):
            total = total + nn(left[:, i * self.rows : (i + 1) * self.rows], piece[:, columns])
        return total

    def back(self, lefts, part, columns):
        piece = self.other[part.start // self.rows]
        inside = slice(part.start % self.rows, part.start % self.rows + part.stop - part.start)
        return nt(lefts[0], self.mine[part, columns]) + nt(lefts[1], piece[inside, columns])


def put_partial(lefts, weights, columns, kept, sends):
    size = kept.shape[0]
    for part in tiles(weights.mine.shape[0], min(256, weights.rows)):
        got = weights.back(lefts, part, columns)
        kept[:, part] = got[:size]
        for i, out in enumerate(sends):
            out[:, part] = got[(i + 1) * size : (i + 2) * size].astype(BF16)


def attn_forward_kernel(count, moves, *refs):
    blocks, rest = refs[:count], refs[count:]
    weights, rest = Slices(rest[: PIECES + 1]), rest[PIECES + 1 :]
    biases, seg_col, pos_col, seg_row, pos_row, slopes = rest[:6]
    rows, qkv, soft, attended, kept, *sends, distance = rest[6:]
    collect(blocks, rows)
    moves.put(rows)
    width = weights.mine.shape[1] // 4
    heads = width // HEAD_DIM
    tokens = rows.shape[0]
    seg_r, pos_r, seg_c, pos_c = seg_row[...], pos_row[...], seg_col[...], pos_col[...]
    allowed = jnp.logical_and(seg_c == seg_r, jnp.logical_and(seg_r < 2, pos_r >= pos_c))
    distance[...] = jnp.where(allowed, (pos_r - pos_c).astype(F32), far_away)
    lefts = []
    for k in range(2):
        base = 3 * width * k
        full = weights.times(rows, k, slice(0, 3 * width))
        queries = (full[:, :width] + biases[2 * k : 2 * k + 1, :]).astype(BF16)
        key_rows = full[:, width : 2 * width].astype(BF16)
        value_rows = (full[:, 2 * width :] + biases[2 * k + 1 : 2 * k + 2, :]).astype(BF16)
        qkv[:, base : base + width] = queries
        qkv[:, base + width : base + 2 * width] = key_rows
        qkv[:, base + 2 * width : base + 3 * width] = value_rows
        values_t = value_rows.astype(F32).T.astype(BF16)
        mixed = []
        for j in range(heads):
            lanes = slice(j * HEAD_DIM, (j + 1) * HEAD_DIM)
            columns = []
            for part in tiles(tokens, 128):
                scores = nt(key_rows[:, lanes], queries[part, lanes])
                slope = slopes[k * heads + j]
                scores = scores * HEAD_DIM ** (-0.5) - slope * distance[:, part]
                highest = jnp.max(scores, axis=0, keepdims=True)
                raised = jnp.exp(scores - highest)
                weights_t = raised * (1.0 / jnp.sum(raised, axis=0, keepdims=True))
                weights_t = weights_t.astype(BF16)
                soft[k * heads + j, :, part] = weights_t
                columns.append(nn(values_t[lanes, :], weights_t))
            mixed.append(jnp.concatenate(columns, axis=1))
        out = jnp.concatenate(mixed, axis=0).T.astype(BF16)
        attended[:, k * width : (k + 1) * width] = out
        lefts.append(out)
    moves.put(qkv, soft, attended)
    put_partial(lefts, weights, slice(3 * width, 4 * width), kept, sends)
    moves.put(kept)


def attn_backward_kernel(count, moves, *refs):
    blocks, rest = refs[:count], refs[count:]
    weights, rest = Slices(rest[: PIECES + 1]), rest[PIECES + 1 :]
    qkv, soft, rows, grad_qkv, sums, kept, *sends, held = rest
    collect(blocks, rows)
    moves.put(rows)
    width = weights.mine.shape[1] // 4
    heads = width // HEAD_DIM
    tokens = rows.shape[0]
    scale = HEAD_DIM ** (-0.5)
    outs = slice(3 * width, 4 * width)
    grads_attended = [weights.times(rows, k, outs).astype(BF16) for k in range(2)]
    moves.need(qkv, soft)
    for k in range(2):
        base = 3 * width * k
        keys_t = qkv[:, base + width : base + 2 * width].astype(F32).T.astype(BF16)
        grads_q = []
        for j in range(heads):
            lanes = slice(j * HEAD_DIM, (j + 1) * HEAD_DIM)
            query_lanes, key_lanes, value_lanes = [
                slice(base + n * width + lanes.start, base + n * width + lanes.stop)
                for n in range(3)
            ]
            grad_head = grads_attended[k][:, lanes]
            for part in tiles(tokens, 128):
                grad_prob = nt(qkv[:, value_lanes], grad_head[part, :])
                weights_t = soft[k * heads + j, :, part].astype(F32)
                row_dot = jnp.sum(weights_t * grad_prob, axis=0, keepdims=True)
                held[:, part] = (weights_t * (grad_prob - row_dot)).astype(BF16)
            grad_score = held[...]
            grad_key = nn(grad_score, qkv[:, query_lanes]) * scale
            grad_qkv[:, key_lanes] = grad_key.astype(BF16)
            grad_qkv[:, value_lanes] = nn(soft[k * heads + j], grad_head).astype(BF16)
            grads_q.append(nn(keys_t[lanes, :], grad_score))
        grad_query = jnp.concatenate(grads_q, axis=0).T * scale
        grad_qkv[:, base : base + width] = grad_query.astype(BF16)
    moves.put(grad_qkv)
    sums[...] = jnp.sum(grad_qkv[...].astype(F32), axis=0, keepdims=True)
    lefts = [grad_qkv[:, : 3 * width], grad_qkv[:, 3 * width :]]
    put_partial(lefts, weights, slice(0, 3 * width), kept, sends)
    moves.put(kept)


def gelu_and_slope(u):
    root = (2.0 / 3.141592653589793) ** 0.5
    square = u * u
    tanh = jnp.tanh(u * (root + (root * 0.044715) * square))
    half = 0.5 + 0.5 * tanh
    inner = root + (3.0 * root * 0.044715) * square
    return u * half, half + (0.5 * u) * (1.0 - tanh * tanh) * inner


def ffn_slices(weights):
    hidden = weights.mine.shape[1] // 2
    for k in range(2):
        for part in tiles(hidden):
            down = slice(hidden + part.start, hidden + part.stop)
            yield k, part, down, slice(k * hidden + part.start, k * hidden + part.stop)


def put_down(activated, weights, kept, sends):
    hidden = weights.mine.shape[1] // 2
    lefts = [activated[:, :hidden], activated[:, hidden:]]
    put_partial(lefts, weights, slice(hidden, 2 * hidden), kept, sends)


def put_up(grad_upper, weights, kept, sends):
    hidden = weights.mine.shape[1] // 2
    lefts = [grad_upper[:, :hidden], grad_upper[:, hidden:]]
    put_partial(lefts, weights, slice(0, hidden), kept, sends)


def ffn_forward_kernel(count, moves, *refs):
    blocks, rest = refs[:count], refs[count:]
    weights, rest = Slices(rest[: PIECES + 1]), rest[PIECES + 1 :]
    up_bias, rows, activated, slope, kept, *sends = rest
    collect(blocks, rows)
    moves.put(rows)
    for k, up, _, units in ffn_slices(weights):
        u = weights.times(rows, k, up) + up_bias[:, units]
        act, grad = gelu_and_slope(u)
        activated[:, units] = act.astype(BF16)
        slope[:, units] = grad.astype(BF16)
    moves.put(activated, slope)
    put_down(activated, weights, kept, sends)
    moves.put(kept)


def ffn_turn_kernel(count, moves, *refs):
    blocks, rest = refs[:count], refs[count:]
    grads, weights, rest = rest[0], Slices(rest[1 : PIECES + 2]), rest[PIECES + 2 :]
    up_bias, order, rows, grad_rows, activated, grad_upper, sums, kept, *sends = rest
    collect(blocks, rows)
    size, width = blocks[0].shape[0], grads.shape[2]
    columns = rows.shape[1] // width
    for i in range(count):
        start = pl.multiple_of(order[i] * size, size)
        for j in range(columns):
            grad_rows[i * size : (i + 1) * size, j * width : (j + 1) * width] = grads[
                j, pl.ds(start, size), :
            ]
    moves.put(rows, grad_rows)
    for k, up, down, units in ffn_slices(weights):
        u = weights.times(rows, k, up) + up_bias[:, units]
        act, slope = gelu_and_slope(u)
        activated[:, units] = act.astype(BF16)
        grad = (weights.times(grad_rows, k, down) * slope).astype(BF16)
        grad_upper[:, units] = grad
        sums[:, units] = jnp.sum(grad.astype(F32), axis=0, keepdims=True)
    moves.put(activated, grad_upper)
    put_up(grad_upper, weights, kept, sends)
    moves.put(kept)


def down_kernel(moves, activated, *refs):
    weights, (kept, *sends) = Slices(refs[: PIECES + 1]), refs[PIECES + 1 :]
    put_down(activated, weights, kept, sends)
    moves.put(kept)


def output_kernel(count, moves, *refs):
    parts, (hidden, bias, result) = refs[:count], refs[count:]
    total = bias[...] + parts[1][...].astype(F32)
    for part in parts[2:]:
        total = total + part[...].astype(F32)
    moves.need(parts[0], hidden)
    result[...] = (total + parts[0][...] + hidden[...]).astype(BF16)


def ffn_backward_kernel(count, moves, *refs):
    blocks, rest = refs[:count], refs[count:]
    weights, rest = Slices(rest[: PIECES + 1]), rest[PIECES + 1 :]
    slope, rows, grad_upper, sums, kept, *sends = rest
    collect(blocks, rows)
    moves.put(rows)
    moves.need(slope)
    for k, _, down, units in ffn_slices(weights):
        grad = weights.times(rows, k, down) * slope[:, units].astype(F32)
        grad = grad.astype(BF16)
        grad_upper[:, units] = grad
        sums[:, units] = jnp.sum(grad.astype(F32), axis=0, keepdims=True)
    moves.put(grad_upper)
    put_up(grad_upper, weights, kept, sends)
    moves.put(kept)


def by_blocks(kernel, own, outs, operands, **settings):
    blocks = spread(own)
    count = len(blocks)
    shape = own.shape
    partial = [(shape, F32)] + [(shape, BF16)] * (count - 1)
    store = settings.pop("store", ()) + (len(outs),)
    beside = settings.pop("beside", ())
    got = run(
        functools.partial(kernel, count),
        outs + partial,
        *blocks,
        *operands,
        room=ROOM,
        cost=BLOCK_COST,
        store=store,
        **settings,
    )
    kept, *beside = together(got[len(outs)], *beside)
    return got[: len(outs)], kept, got[len(outs) + 1 :], beside


def attn_forward(normed, layout, weights, small, beside=()):
    size, model = normed.shape
    tokens, width = size * (plane_size() // 2), weights[0].shape[1] // 4
    results, kept, sends, beside = by_blocks(
        attn_forward_kernel,
        normed,
        [
            ((tokens, model), BF16),
            ((tokens, 6 * width), BF16),
            ((2 * width // HEAD_DIM, tokens, tokens), BF16),
            ((tokens, 2 * width), BF16),
        ],
        [*weights, small["attn_bias"], *layout],
        scalars=1,
        scratch=[((tokens, tokens), F32)],
        store=(0, 1, 2, 3),
        beside=beside,
    )
    return sum_up(kept, sends)[0], results, beside


def ffn_forward(normed, weights, small, beside=()):
    size, model = normed.shape
    tokens, hidden = size * (plane_size() // 2), weights[0].shape[1]
    results, kept, sends, beside = by_blocks(
        ffn_forward_kernel,
        normed,
        [((tokens, model), BF16), ((tokens, hidden), BF16), ((tokens, hidden), BF16)],
        [*weights, small["up_bias"]],
        store=(0, 1, 2),
        beside=beside,
    )
    return sum_up(kept, sends)[0], results, beside


def ffn_turn(normed, grads, order, weights, small):
    size, model = normed.shape
    tokens, hidden = size * (plane_size() // 2), weights[0].shape[1]
    (rows, grad_rows, activated, grad_upper, sums), kept, sends, _ = by_blocks(
        ffn_turn_kernel,
        normed,
        [
            ((tokens, model), BF16),
            ((tokens, model), BF16),
            ((tokens, hidden), BF16),
            ((tokens, hidden), BF16),
            ((1, hidden), F32),
        ],
        [grads, *weights, small["up_bias"], order],
        scalars=1,
        store=(0, 1, 2, 3),
    )
    grad_parts, factors = sum_up(kept, sends, (rows, grad_upper, grad_rows, activated))
    kept, *sends = run(
        down_kernel,
        [(a.shape, a.dtype) for a in [kept] + sends],
        factors[3],
        *weights,
        room=ROOM,
        store=(0,),
    )
    return grad_parts, factors, sums, (kept, sends)


def ffn_backward(grad_down, weights, stored, beside=()):
    size, model = grad_down.shape
    tokens, hidden = size * (plane_size() // 2), weights[0].shape[1]
    rows_two, activated, slope = stored
    (rows, grad_upper, sums), kept, sends, beside = by_blocks(
        ffn_backward_kernel,
        grad_down,
        [((tokens, model), BF16), ((tokens, hidden), BF16), ((1, hidden), F32)],
        [*weights, slope],
        load=(-1,),
        store=(0, 1),
        beside=beside,
    )
    return *sum_up(kept, sends, (rows_two, grad_upper, rows, activated)), sums, beside


def attn_backward(grad_branch, weights, stored, beside=()):
    size, model = grad_branch.shape
    tokens, width = size * (plane_size() // 2), weights[0].shape[1] // 4
    rows_one, qkv, soft, attended = stored
    (rows, grad_qkv, sums), kept, sends, beside = by_blocks(
        attn_backward_kernel,
        grad_branch,
        [((tokens, model), BF16), ((tokens, 6 * width), BF16), ((1, 6 * width), F32)],
        [*weights, qkv, soft],
        scratch=[((tokens, tokens), BF16)],
        load=(-1, -2),
        store=(0, 1),
        beside=beside,
    )
    return *sum_up(kept, sends, (rows_one, grad_qkv, rows, attended)), sums, beside


def norm_back(parts, hidden, gain, grad_out, work=()):
    shape = hidden.shape
    hidden, *work = together(hidden, *work)
    got = run(
        functools.partial(norm_back_kernel, len(parts)),
        [(shape, F32), (shape, BF16), ((3, shape[1]), F32)],
        *parts,
        hidden,
        gain,
        grad_out,
        load=(0, len(parts), len(parts) + 2),
        store=(0,),
        cost=NORM_COST,
    )
    return *got, work


def weight_kernel(moves, first, first_grad, second, second_grad, mine, *other):
    ends = first_grad.shape[1] // 2, second_grad.shape[1] // 2
    size = mine.shape[0] // PIECES

    def put(k, part, value, columns):
        if k == 0:
            mine[part, columns] = value
        else:
            inside = slice(part.start % size, part.start % size + part.stop - part.start)
            other[part.start // size][inside, columns] = value

    for k in (1, 0):
        moves.need(first, first_grad)
        for part in tiles(first.shape[1], min(256, size)):
            grad = first_grad[:, k * ends[0] : (k + 1) * ends[0]]
            put(k, part, tn(first[:, part], grad).astype(BF16), slice(0, ends[0]))
        moves.need(second, second_grad)
        for part in tiles(second.shape[1], min(256, size)):
            grad = second_grad[:, k * ends[1] : (k + 1) * ends[1]]
            put(k, part, tn(second[:, part], grad).astype(BF16), slice(ends[0], ends[0] + ends[1]))


def weight_terms(factors):
    columns = (factors[1].shape[1] + factors[3].shape[1]) // 2
    rows = factors[0].shape[1]
    return run(
        weight_kernel,
        [((rows, columns), BF16)] + [((rows // PIECES, columns), BF16)] * PIECES,
        *factors,
        room=ROOM,
        cost=TERM_COST,
        load=(0, 1, 2, 3),
    )


def both_cores(mine, *other):
    came = jnp.concatenate([send(piece, 1) for piece in other], axis=0)
    return (mine.astype(F32) + came.astype(F32)).astype(BF16)


def on_device(
    inputs,
    cotangent,
    lengths,
    deal,
    query_key_value_weight,
    out_weight,
    up_weight,
    down_weight,
    norm_gain,
    norm_shift,
    proj_bias,
    up_bias,
):
    section = lax.axis_index("section")
    holder = lax.axis_index("row")
    column = lax.axis_index("col")
    cols_count = lax.axis_size("col")
    micro_count, rows_dev, width = inputs.shape
    model = width * cols_count
    count = plane_size()
    place = section * cols_count + column
    chips = count // 2
    tokens = rows_dev // chips
    core, chip = place % 2, place // 2
    block = query_key_value_weight.shape[1]
    half = width // 2
    heads_dev = half // HEAD_DIM
    hidden_half = up_weight.shape[2] // 2
    is_zero = section == 0

    def pick(zero, one):
        return jnp.where(is_zero, zero, one)

    def halves(array, axis):
        size = array.shape[axis] // 2
        return (
            lax.slice_in_dim(array, 0, size, axis=axis),
            lax.slice_in_dim(array, size, 2 * size, axis=axis),
        )

    attn_parts = [
        jnp.concatenate([q.reshape(block, 3 * half), o.T], axis=1)
        for q, o in zip(halves(query_key_value_weight[0], 2), halves(out_weight[0], 0))
    ]
    ffn_parts = [
        jnp.concatenate([u, d.T], axis=1)
        for u, d in zip(halves(up_weight[0], 1), halves(down_weight[0], 0))
    ]

    def both_layers(parts):
        kept, given = pick(parts[0], parts[1]), pick(parts[1], parts[0])
        came = send(given, cols_count)
        return pick(kept, came), pick(came, kept)

    def gather_slice(piece):
        return lax.all_gather(piece, "row", axis=0, tiled=True)

    def both_slices(mine):
        size = mine.shape[0] // PIECES
        return mine, *[send(mine[i * size : (i + 1) * size], 1) for i in range(PIECES)]

    mine_small = jnp.concatenate(
        [norm_gain[0], norm_shift[0], proj_bias[0], up_bias[0].reshape(-1, width)], axis=0
    )
    all_small = lax.all_gather(mine_small, PLANE, axis=0, tiled=False)
    all_small = all_small.reshape((2, cols_count) + mine_small.shape)

    def layer_small(layer):
        table = all_small[layer]
        whole = jnp.transpose(table[:, :8], (1, 0, 2)).reshape(8, model)
        slices = []
        for index in (column, jnp.bitwise_xor(column, 1)):
            own = lax.dynamic_index_in_dim(table, index, axis=0, keepdims=False)
            hidden = own[8:].reshape(2, hidden_half)
            slices.append((pick(own[:, :half], own[:, half:]), pick(hidden[0:1], hidden[1:2])))
        return {
            "gain": (whole[0:1], whole[1:2]),
            "shift": (whole[2:3], whole[3:4]),
            "attn_bias": jnp.concatenate([own[4:6] for own, _ in slices], axis=0),
            "bias_out": whole[6:7],
            "bias_down": whole[7:8],
            "up_bias": jnp.concatenate([hidden for _, hidden in slices], axis=1),
        }

    source = owned_layout(lengths[section], deal[section], holder, rows_dev)[0]
    _, usable, segment, position = owned_layout(lengths[core], deal[core], holder, rows_dev)
    order = jnp.bitwise_xor(chip, jnp.arange(chips, dtype=jnp.int32))

    def in_spread_order(values):
        return values.reshape(chips, tokens)[order].reshape(rows_dev)

    own_usable = lax.dynamic_index_in_dim(
        usable.astype(jnp.int32).reshape(chips, tokens, 1), chip, axis=0, keepdims=False
    )
    head_ids = [
        index * (2 * heads_dev) + section * heads_dev + jnp.arange(heads_dev, dtype=jnp.int32)
        for index in (column, jnp.bitwise_xor(column, 1))
    ]
    head_ids = jnp.concatenate(head_ids)
    slopes = jnp.exp2(-8.0 * (head_ids.astype(F32) + 1.0) / (model // HEAD_DIM))
    segment, position = in_spread_order(segment), in_spread_order(position)
    layout = (segment[:, None], position[:, None], segment[None], position[None], slopes)

    pairs = cols_count // 2
    trades = [(a, b) for a in range(2) for b in range(pairs)]

    def trade(array, a, b, to_worker=False):
        where = [(s, x, c) for s in range(2) for x in range(pairs) for c in range(2)]
        flat = lambda s, x, c: (s * pairs + x) * 2 + c
        ways = [(flat(s, x, c), flat(c, x ^ b, s ^ a)) for s, x, c in where]
        if to_worker:
            ways = [(to, come) for come, to in ways]
        return lax.ppermute(array, PLANE, ways)

    def at(array, index):
        return lax.dynamic_index_in_dim(array, index, axis=0, keepdims=False)

    def in_order(blocks, first, second):
        table = jnp.stack(blocks)
        return [at(table, (i ^ first) * pairs + (x ^ second)) for i in range(2) for x in range(pairs)]

    mine_x = column // 2

    def to_workers(rows):
        blocks = [trade(at(rows, (core ^ a) * pairs + (mine_x ^ b)), a, b, True) for a, b in trades]
        return by_column(blocks)

    def all_to_workers(rows):
        return [trade(rows, a, b, True) for a, b in trades]

    def by_column(blocks):
        table = jnp.stack(blocks)
        return jnp.stack(
            [at(table, ((c % 2) ^ section) * pairs + ((c // 2) ^ mine_x)) for c in range(cols_count)]
        )

    def to_dealers(rows):
        blocks = [trade(at(rows, (mine_x ^ b) * 2 + (section ^ a)), a, b) for a, b in trades]
        return jnp.stack(in_order(blocks, core, mine_x))

    def deal_rows(portion):
        return pick_rows(portion.reshape(-1, width), source).astype(BF16)

    def to_tokens(owned):
        own = to_workers(owned.reshape(chips, tokens, width))
        return jnp.transpose(own, (1, 0, 2)).reshape(tokens, model)

    portion = gather_direct(pick(inputs[0], inputs[1]))
    attn_pieces = both_layers(attn_parts)
    ffn_pieces = both_layers(ffn_parts)
    all_small, attn_first = together(all_small, attn_pieces[0])
    attn_pieces = (attn_first, attn_pieces[1])
    portion, all_small, *ffn_pieces = together(portion, all_small, *ffn_pieces)
    first_rows = to_tokens(deal_rows(portion))
    attn_w = [gather_slice(piece) for piece in attn_pieces]
    ffn_w = [gather_slice(piece) for piece in ffn_pieces]
    smalls = [layer_small(0), layer_small(1)]

    def to_columns(own):
        return jnp.transpose(own.reshape(tokens, cols_count, width), (1, 0, 2))

    shape = (tokens, model)

    def middle_norm(parts, hidden, layer, work=()):
        small = smalls[layer]
        hidden, *work = together(hidden, *work)
        got = run(
            functools.partial(add_norm_kernel, len(parts)),
            [(shape, F32), (shape, BF16)],
            *parts,
            hidden,
            small["bias_out"],
            small["gain"][1],
            small["shift"][1],
            load=(0, len(parts)),
            store=(0,),
            cost=NORM_COST,
        )
        return *got, work

    def end_norm(parts, middle, layer, work=()):
        small, following = smalls[layer], smalls[min(layer + 1, 1)]
        middle, *work = together(middle, *work)
        got = run(
            functools.partial(end_norm_kernel, len(parts)),
            [(shape, BF16), (shape, BF16)],
            *parts,
            middle,
            small["bias_down"],
            following["gain"][0],
            following["shift"][0],
            own_usable,
            load=(0, len(parts)),
            store=(0,),
            cost=NORM_COST,
        )
        return *got, work

    small = smalls[0]
    normed = run(norm_kernel, [(shape, BF16)], first_rows, small["gain"][0], small["shift"][0])[0]
    attn_w[0] = both_slices(attn_w[0])
    parts, attn_zero, (cotangent,) = attn_forward(
        normed, layout, attn_w[0], small, (cotangent,)
    )
    given_grads = gather_direct(pick(cotangent[0], cotangent[1]))
    middle_zero, normed, (ffn_w[0],) = middle_norm(parts, first_rows, 0, (ffn_w[0],))
    ffn_w[0] = both_slices(ffn_w[0])
    parts, ffn_zero, _ = ffn_forward(normed, ffn_w[0], small)
    middle_in, normed, (given_grads, attn_w[1]) = end_norm(
        parts, middle_zero, 0, (given_grads, attn_w[1])
    )
    attn_w[1] = both_slices(attn_w[1])
    given_grads = deal_rows(given_grads)
    given_grads = all_to_workers(given_grads)
    parts, attn_one, given_grads = attn_forward(
        normed, layout, attn_w[1], smalls[1], given_grads
    )
    given_grads = by_column(given_grads)
    middle_one, normed, _ = middle_norm(parts, middle_in, 1)
    ffn_w[1] = both_slices(ffn_w[1])
    grad_parts, factors, up_sums, last_out = ffn_turn(
        normed, given_grads, order, ffn_w[1], smalls[1]
    )
    cotangent_rows = factors[2][:tokens]
    positions = holder * rows_dev + jnp.arange(rows_dev, dtype=jnp.int32)
    targets = given_targets(lengths[section], deal[section], positions, rows_dev)

    extra = 16

    def start_return(grad_in, a, b, *others):
        sums = jnp.stack([a[0], b[0], a[1], b[1], b[2], b[3]]).reshape(-1, cols_count, width)
        sums = jnp.transpose(sums, (1, 0, 2)).astype(BF16)
        sums = jnp.pad(sums, ((0, 0), (0, extra - 6), (0, len(others) * width)))
        rows = jnp.concatenate([to_columns(rows) for rows in (grad_in,) + others], axis=2)
        got = to_dealers(jnp.concatenate([rows, sums], axis=1))
        sums = jnp.sum(got[:, tokens : tokens + 6, :width].astype(F32), axis=0)
        return got[:, :tokens].reshape(rows_dev, -1), sums

    def with_sums(rows, sums, qkv_sums, up_sums):
        sums_by_core = []
        for k in range(2):
            qkv = qkv_sums[0, 3 * half * k : 3 * half * (k + 1)]
            up = up_sums[0, hidden_half * k : hidden_half * (k + 1)]
            sums_by_core.append(jnp.concatenate([qkv[:half], qkv[2 * half :], up]))
        columns = sums_by_core[0] + send(sums_by_core[1], 1)
        sums = jnp.concatenate([sums, columns.reshape(-1, width)], axis=0)
        sums = jnp.pad(sums, ((0, extra - sums.shape[0]), (0, rows.shape[1] - width)))
        return jnp.concatenate([rows, sums.astype(BF16)], axis=0)

    def finish_return(held):
        picked = pick_rows(held[:, :rows_dev].reshape(-1, held.shape[2]), targets)
        return picked.astype(BF16), jnp.sum(held[:, rows_dev:, :width].astype(F32), axis=0)

    def reduce_rows(total):
        return lax.psum_scatter(total, "row", scatter_dimension=0, tiled=True)

    terms = weight_terms(factors)
    down_sum = jnp.sum(cotangent_rows, axis=0, dtype=F32)
    mid, low, sums_b, terms = norm_back(
        grad_parts, middle_one, smalls[1]["gain"][1], cotangent_rows, terms
    )
    sums_b = [*sums_b, down_sum]
    mid, *terms = together(mid, *terms)
    ffn_term_one = reduce_rows(both_cores(*terms))
    output_parts = sum_up(*last_out)[0]
    parts, factors, qkv_sums, output_parts = attn_backward(low, attn_w[1], attn_one, output_parts)
    terms = weight_terms(factors)
    _, grad_one, sums_a, terms = norm_back(parts, middle_in, smalls[1]["gain"][0], mid, terms)
    grad_one, *terms = together(grad_one, *terms)
    attn_term_one = reduce_rows(both_cores(*terms))
    last_out = run(
        functools.partial(output_kernel, len(output_parts)),
        [(shape, BF16)],
        *output_parts,
        middle_one,
        smalls[1]["bias_down"],
        load=(0, len(output_parts)),
    )[0]
    late = start_return(grad_one, sums_a, sums_b, last_out, middle_in)
    late_sums = (qkv_sums, up_sums)
    grad_zero = jnp.where(own_usable > 0, grad_one, jnp.zeros_like(grad_one))
    down_sum = jnp.sum(grad_zero, axis=0, dtype=F32)
    grad_parts, factors, up_sums, late = ffn_backward(grad_zero, ffn_w[0], ffn_zero, late)
    terms = weight_terms(factors)
    mid, low, sums_b, (ffn_term_one, *terms) = norm_back(
        grad_parts, middle_zero, smalls[0]["gain"][1], grad_zero, (ffn_term_one, *terms)
    )
    sums_b = [*sums_b, down_sum]
    late = lax.all_gather(with_sums(*late, *late_sums), "row")
    mid, *terms = together(mid, *terms)
    ffn_term_zero = reduce_rows(both_cores(*terms))
    parts, factors, qkv_sums, _ = attn_backward(low, attn_w[0], attn_zero)
    terms = weight_terms(factors)
    _, grad_in, sums_a, (attn_term_one, *terms) = norm_back(
        parts, first_rows, smalls[0]["gain"][0], mid, (attn_term_one, *terms)
    )
    attn_term_zero = both_cores(*terms)
    back_zero = with_sums(*start_return(grad_in, sums_a, sums_b), qkv_sums, up_sums)
    back_zero = gather_direct(back_zero)
    late, sums_one = finish_return(late)
    ffn_term_zero, attn_term_zero, late = together(ffn_term_zero, attn_term_zero, late)
    attn_term_zero = reduce_rows(attn_term_zero)
    back_zero, ffn_term_zero, late = together(back_zero, ffn_term_zero, late)
    back_zero, sums_zero = finish_return(back_zero)
    back_one = late[:, :width]
    hidden = late[:, 2 * width :], late[:, width : 2 * width]
    stays, comes = pick(hidden[0], hidden[1]), send(pick(hidden[1], hidden[0]), cols_count)
    hidden_out = jnp.stack([pick(stays, comes), pick(comes, stays)])

    def both_halves(zero, one):
        mine = pick(zero, one)
        other = send(pick(one, zero), cols_count)
        return pick(mine, other).astype(F32), pick(other, mine).astype(F32)

    attn_grad = jnp.stack(
        [g.reshape(block, 4, half) for g in both_halves(attn_term_zero, attn_term_one)], axis=2
    ).reshape(block, 4, width)
    ffn_grad = both_halves(ffn_term_zero, ffn_term_one)
    up_grad = jnp.concatenate([g[:, :hidden_half] for g in ffn_grad], axis=1)
    down_grad = jnp.concatenate([g[:, hidden_half:].T for g in ffn_grad], axis=0)

    given = pick(back_one, back_zero)
    given = jnp.concatenate([given, pick(sums_one, sums_zero).astype(BF16)], axis=0)
    comes = send(given, cols_count).astype(F32)
    stays, came = pick(back_zero, back_one).astype(F32), comes[:rows_dev]
    in_grad = jnp.stack([pick(stays, came), pick(came, stays)])
    sums = pick(sums_zero, sums_one)
    sums = jnp.concatenate([sums[:6] + comes[rows_dev : rows_dev + 6], sums[6:]], axis=0)
    kept, came = sums[6:].reshape(-1), comes[rows_dev + 6 :].reshape(-1)
    first, second = pick(kept, came), pick(came, kept)
    bias_grad = jnp.stack(
        [
            jnp.concatenate([first[:half], second[:half]]),
            jnp.concatenate([first[half:width], second[half:width]]),
            sums[4],
            sums[5],
        ]
    )
    up_sums = jnp.concatenate(
        [first[width : width + hidden_half], second[width : width + hidden_half]]
    )
    return (
        hidden_out[None],
        in_grad[None],
        attn_grad[:, :3][None],
        attn_grad[:, 3].T[None],
        up_grad[None],
        down_grad[None],
        sums[0:2][None],
        sums[2:4][None],
        bias_grad[None],
        up_sums[None],
    )


def solution(mesh):
    placed = (
        P(None, "row", "col"),
        P(None, "row", "col"),
        P(),
        P(),
        P("section", "row", None, "col"),
        P("section", "col", "row"),
        P("section", "row", "col"),
        P("section", "col", "row"),
        P("section", None, "col"),
        P("section", None, "col"),
        P("section", None, "col"),
        P("section", "col"),
    )
    return jax.shard_map(
        on_device,
        mesh=mesh,
        in_specs=placed,
        out_specs=(
            P("section", None, "row", "col"),
            P("section", None, "row", "col"),
            P("section", "row", None, "col"),
            P("section", "col", "row"),
            P("section", "row", "col"),
            P("section", "col", "row"),
            P("section", None, "col"),
            P("section", None, "col"),
            P("section", None, "col"),
            P("section", "col"),
        ),
        check_vma=False,
    )
```

time: 559 us -> 531 us (0.950)
  matrix products: 27.9 us -> 5.77 us
  waiting for transfers between devices: 240 us -> 227 us
  blocking collectives: 18.5 us -> 9.2 us
  starting transfers between devices: 97.6 us -> 104 us
    reduce_scatter x3 -> x4, waiting for transfers between devices: 0.02 us -> 41.4 us  [reduce_rows(): return lax.psum_scatter(total, 'row', scatter_dimension=0, tiled=True)]
    all_to_all x5 -> x0, waiting for transfers between devices: 40.5 us -> none  [the longest x1 27.7 us: on_device(): lax.all_to_all(term.reshape(-1, block, term.shape[1]), 'row', split_axis=...]
    dot_general x14 -> x4, matrix products: 27.9 us -> 5.77 us  [mm(): lax.dot_general(a, b, ((dims[0], dims[1]), ((), ())), preferred_element_t...]
    all_to_all x5 -> x0, starting transfers between devices: 17.8 us -> none  [the longest x2 6.86 us: start_return(): return lax.all_to_all(rows, PLANE, split_axis=0, concat_axis=0)]
    ppermute x0 -> x16, starting transfers between devices: none -> 17.2 us  [trade(): return lax.ppermute(array, PLANE, ways)]
    ppermute x83 -> x85, waiting for transfers between devices: 167 us -> 151 us  [send(): lax.ppermute(array, PLANE, [(i, i ^ mask) for i in range(plane_size())])]
    convert_element_type x2 -> x7, other arithmetic: 0.11 us -> 12.3 us  [the longest x4 10.1 us: both_cores(): return (mine.astype(F32) + came.astype(F32)).astype(BF16)]
    ppermute x83 -> x85, starting transfers between devices: 63 us -> 73.4 us  [send(): lax.ppermute(array, PLANE, [(i, i ^ mask) for i in range(plane_size())])]
  transfers between devices with their start and end apart: 103 -> 113, of which waited for: 53 -> 56; matrix products, arithmetic and copies ran while one was open for 13% -> 10% of each run, Pallas kernels for 16% -> 16%
where the time goes in v5:
time: 531 us; the launch traced here: 526 us
  waiting for transfers between devices  227 us (43%)
  starting transfers between devices  104 us (20%)
  Pallas kernels  93 us (18%)
  local copies, waits for them, and re-layouts  36.6 us (7%)
  other arithmetic  30.6 us (6%)
  between operations  18.8 us (4%)
  blocking collectives  9.2 us (2%)
  matrix products  5.77 us (1%)
    ppermute x85, waiting for transfers between devices, send(): lax.ppermute(array, PLANE, [(i, i ^ mask) for i in range(plane_size())])  151 us
    pallas_call x21, Pallas kernels, run(): return list(call(*args))  93 us
    ppermute x85, starting transfers between devices, send(): lax.ppermute(array, PLANE, [(i, i ^ mask) for i in range(plane_size())])  73.4 us
    reduce_scatter x4, waiting for transfers between devices, reduce_rows(): return lax.psum_scatter(total, 'row', scatter_dimension=0, tiled=True)  41.4 us
    ppermute x16, starting transfers between devices, trade(): return lax.ppermute(array, PLANE, ways)  17.2 us
    unnamed x175, local copies, waits for them, and re-layouts  17.1 us
    all_gather x4, waiting for transfers between devices, gather_slice(): return lax.all_gather(piece, 'row', axis=0, tiled=True)  15 us
    all_to_all x3, starting transfers between devices, gather_direct(): return lax.all_to_all(copies, 'row', split_axis=0, concat_axis=0)  12.8 us
  transfers between devices with their start and end apart: 113, of which 56 were waited for; matrix products, arithmetic and copies ran while one was open for 10% of the time, Pallas kernels for 16%

profile of v5, /device:TPU:0, one launch (start us, length us, event | category | flops | bytes accessed | tf_op | source)
XLA Modules:
  0.0 525.6 jit_solution(13536614920683308555)
XLA Ops:
  10.0 3.0 collective-permute-start
  14.2 5.0 all-to-all-start
  20.4 9.2 %all-gather.2 = f32[8,12,256]{2,1,0:T(8,128)S(1)} all-gather(f32[1,12,256]{2,1,0:T(8,128)S(1)} %maximum_bitcast_fusion.5), channel_id=2, replica_groups=mesh['section'=2,'row'=4,'col'=4] {'section','col'}, dimensions={0}, use_global_device_ids=true | all-gather | bytes 110592 | tf_op jit(solution)/shard_map/all_gather | solution.py:707
  31.8 13.6 %collective-permute-done.1 = bf16[256,1024]{1,0:T(8,128)(2,1)S(1)} collective-permute-done((bf16[256,1024]{1,0:T(8,128)(2,1)S(1)}, bf16[256,1024]{1,0:T(8,128)(2,1)S(1)}, u32[]{:S(2)}, u32[]{:S(2)}) %collective-permute-start.1) | collective-permute-done | bytes 524320 | tf_op jit(solution)/shard_map/ppermute | solution.py:44
  46.6 6.0 %all-to-all-done = bf16[4,512,256]{2,1,0:T(8,128)(2,1)S(1)} async-done(((bf16[4,512,256]{2,1,0:T(8,128)(2,1)}), bf16[4,512,256]{2,1,0:T(8,128)(2,1)S(1)}, u32[]{:S(2)}, u32[]{:S(2)}) %all-to-all-start) | async-done | bytes 1048608 | tf_op jit(solution)/shard_map/all_to_all | solution.py:68
  77.0 4.7 collective-permute-done.8.refs_3_
  81.7 4.8 collective-permute-done.7.refs_2_
  88.0 9.5 %shard_map.196 = (bf16[512,1024]{1,0:T(8,128)(2,1)}, bf16[512,768]{1,0:T(8,128)(2,1)}, bf16[4,512,512]{2,1,0:T(8,128)(2,1)}, bf16[512,256]{1,0:T(8,128)(2,1)}, f...) custom-call(bf16[128,1024]{1,0:T(8,128)(2,1)S(1)} %shard_map.195.ref, ...), custom_call_target="tpu_custom_call" | custom-call | flops 9200000000 | tf_op jit(solution)/shard_map/pallas_call | solution.py:171
  98.7 4.3 all-to-all-start.1
  107.4 7.2 %all-gather.11.cloned.1.call-done.refs_4_ = bf16[1024,1024]{1,0:T(8,128)(2,1)} async-done(((bf16[256,1024]{1,0:T(8,128)(2,1)}), bf16[1024,1024]{1,0:T(8,128)(2,1)}) %all-gather.11.cloned.1.call-update) | async-done | bytes 2097168 | tf_op jit(solution)/shard_map/all_gather | solution.py:698
  115.3 3.4 collective-permute-done.14.refs_2_
  129.5 3.5 collective-permute-done.18.refs_3_
  133.6 4.8 collective-permute-done.17.refs_2_
  139.7 7.8 %all-gather.13.cloned.1.call-done.refs_4_ = bf16[1024,512]{1,0:T(8,128)(2,1)} async-done(((bf16[256,512]{1,0:T(8,128)(2,1)}), bf16[1024,512]{1,0:T(8,128)(2,1)}) %all-gather.13.cloned.1.call-update) | async-done | bytes 1048592 | tf_op jit(solution)/shard_map/all_gather | solution.py:698
  149.6 5.8 %shard_map.198 = (bf16[512,1024]{1,0:T(8,128)(2,1)}, bf16[512,1024]{1,0:T(8,128)(2,1)}, bf16[512,1024]{1,0:T(8,128)(2,1)}, f32[128,1024]{1,0:T(8,128)}, bf16[128...) custom-call(bf16[128,1024]{1,0:T(8,128)(2,1)S(1)} %get-tuple-element.210.refs_0_, ...), custom_call_target="tpu_custom_call" | custom-call | flops 9200000000 | tf_op jit(solution)/shard_map/pallas_call | solution.py:171
  159.6 5.0 collective-permute-done.23.refs_1_
  164.6 5.8 %collective-permute-done.24.refs_2_ = bf16[128,1024]{1,0:T(8,128)(2,1)S(1)} collective-permute-done((bf16[128,1024]{1,0:T(8,128)(2,1)S(1)}, bf16[128,1024]{1,0:T(8,128)(2,1)S(1)}, u32[]{:S(2)}, u32[]{:S(2)}) %collective-permute-start.24) | collective-permute-done | bytes 262176 | tf_op jit(solution)/shard_map/ppermute | solution.py:44
  184.0 4.4 collective-permute-done.27.refs_2_
  189.4 9.5 %shard_map.200 = (bf16[512,1024]{1,0:T(8,128)(2,1)}, bf16[512,768]{1,0:T(8,128)(2,1)}, bf16[4,512,512]{2,1,0:T(8,128)(2,1)}, bf16[512,256]{1,0:T(8,128)(2,1)}, f...) custom-call(bf16[128,1024]{1,0:T(8,128)(2,1)S(1)} %get-tuple-element, ...), custom_call_target="tpu_custom_call" | custom-call | flops 9200000000 | tf_op jit(solution)/shard_map/pallas_call | solution.py:171
  208.3 7.2 %collective-permute-done.38.refs_2_ = bf16[128,1024]{1,0:T(8,128)(2,1)S(1)} collective-permute-done((bf16[128,1024]{1,0:T(8,128)(2,1)S(1)}, bf16[128,1024]{1,0:T(8,128)(2,1)S(1)}, u32[]{:S(2)}, u32[]{:S(2)}) %collective-permute-start.38) | collective-permute-done | bytes 262176 | tf_op jit(solution)/shard_map/ppermute | solution.py:44
  221.6 6.3 %collective-permute-done.42.refs_3_ = bf16[128,1024]{1,0:T(8,128)(2,1)S(1)} collective-permute-done((bf16[128,1024]{1,0:T(8,128)(2,1)S(1)}, bf16[128,1024]{1,0:T(8,128)(2,1)S(1)}, u32[]{:S(2)}, u32[]{:S(2)}) %collective-permute-start.42) | collective-permute-done | bytes 262176 | tf_op jit(solution)/shard_map/ppermute | solution.py:44
  227.9 4.4 collective-permute-done.41.refs_2_
  232.3 6.5 %shard_map.202 = (bf16[512,1024]{1,0:T(8,128)(2,1)}, bf16[512,1024]{1,0:T(8,128)(2,1)}, bf16[512,1024]{1,0:T(8,128)(2,1)}, bf16[512,1024]{1,0:T(8,128)(2,1)}, f3...) custom-call(bf16[128,1024]{1,0:T(8,128)(2,1)S(1)} %get-tuple-element, ...), custom_call_target="tpu_custom_call" | custom-call | flops 9200000000 | tf_op jit(solution)/shard_map/pallas_call | solution.py:171
  242.4 4.3 shard_map.203
  248.4 5.4 %collective-permute-done.48.refs_2_ = bf16[128,1024]{1,0:T(8,128)(2,1)S(1)} collective-permute-done((bf16[128,1024]{1,0:T(8,128)(2,1)S(1)}, bf16[128,1024]{1,0:T(8,128)(2,1)S(1)}, u32[]{:S(2)}, u32[]{:S(2)}) %collective-permute-start.48) | collective-permute-done | bytes 262176 | tf_op jit(solution)/shard_map/ppermute | solution.py:44
  278.4 7.7 %shard_map.205 = (bf16[512,1024]{1,0:T(8,128)(2,1)}, bf16[512,768]{1,0:T(8,128)(2,1)}, f32[1,768]{1,0:T(1,128)S(1)}, f32[128,1024]{1,0:T(8,128)}, bf16[128,1024]...) custom-call(bf16[128,1024]{1,0:T(8,128)(2,1)S(1)} %copy-done.35, ...), custom_call_target="tpu_custom_call" | custom-call | flops 9200000000 | tf_op jit(solution)/shard_map/pallas_call | solution.py:171
  286.1 3.4 collective-permute-done.55.refs_3_
  293.2 3.6 shard_map.207
  298.8 5.3 %collective-permute-done.57.refs_2_ = bf16[128,1024]{1,0:T(8,128)(2,1)S(1)} collective-permute-done((bf16[128,1024]{1,0:T(8,128)(2,1)S(1)}, bf16[128,1024]{1,0:T(8,128)(2,1)S(1)}, u32[]{:S(2)}, u32[]{:S(2)}) %collective-permute-start.57) | collective-permute-done | bytes 262176 | tf_op jit(solution)/shard_map/ppermute | solution.py:44
  321.7 4.4 collective-permute-start.60
  330.1 5.1 collective-permute-done.61.refs_3_
  335.2 4.4 collective-permute-done.60.refs_2_
  339.6 7.3 %shard_map.209 = (bf16[512,1024]{1,0:T(8,128)(2,1)}, bf16[512,1024]{1,0:T(8,128)(2,1)}, f32[1,1024]{1,0:T(1,128)S(1)}, f32[128,1024]{1,0:T(8,128)}, bf16[128,102...) custom-call(bf16[128,1024]{1,0:T(8,128)(2,1)S(1)} %get-tuple-element.467.refs_0_.refs_6_, ...), custom_call_target="tpu_custom_call" | custom-call | flops 9200000000 | tf_op jit(solution)/shard_map/pallas_call | solution.py:171
  351.9 4.4 shard_map.211
  357.9 4.0 collective-permute-done.67.refs_2_
  363.5 3.7 shard_map.212
  371.9 3.9 add_convert_fusion
  378.8 4.7 collective-permute-done.74.refs_2_
  383.6 8.7 %shard_map.213 = (bf16[512,1024]{1,0:T(8,128)(2,1)}, bf16[512,768]{1,0:T(8,128)(2,1)}, f32[1,768]{1,0:T(1,128)S(1)}, f32[128,1024]{1,0:T(8,128)}, bf16[128,1024]...) custom-call(bf16[128,1024]{1,0:T(8,128)(2,1)S(1)} %copy-done.37, ...), custom_call_target="tpu_custom_call" | custom-call | flops 9200000000 | tf_op jit(solution)/shard_map/pallas_call | solution.py:171
  396.0 3.5 shard_map.214
  401.6 5.9 %collective-permute-done.77.refs_2_ = bf16[128,1024]{1,0:T(8,128)(2,1)} collective-permute-done((bf16[128,1024]{1,0:T(8,128)(2,1)S(1)}, bf16[128,1024]{1,0:T(8,128)(2,1)}, u32[]{:S(2)}, u32[]{:S(2)}) %collective-permute-start.77) | collective-permute-done | bytes 262176 | tf_op jit(solution)/shard_map/ppermute | solution.py:44
  407.5 3.6 shard_map.215
  421.0 3.5 all-to-all-start.2
  433.8 39.6 %reduce-scatter.9.cloned.1.call-done = bf16[256,1024]{1,0:T(8,128)(2,1)} async-done(((bf16[1024,1024]{1,0:T(8,128)(2,1)}), bf16[256,1024]{1,0:T(8,128)(2,1)}) %reduce-scatter.9.cloned.1.call-update) | async-done | bytes 524304 | tf_op jit(solution)/shard_map/reduce_scatter | solution.py:897
  473.4 3.4 all-to-all-done.2
  481.0 6.1 %collective-permute-done.97 = bf16[512,256]{1,0:T(8,128)(2,1)S(1)} collective-permute-done((bf16[512,256]{1,0:T(8,128)(2,1)S(1)}, bf16[512,256]{1,0:T(8,128)(2,1)S(1)}, u32[]{:S(2)}, u32[]{:S(2)}) %collective-permute-start.97) | collective-permute-done | bytes 262176 | tf_op jit(solution)/shard_map/ppermute | solution.py:44
  489.9 8.4 %collective-permute-done.100 = bf16[256,1024]{1,0:T(8,128)(2,1)S(1)} collective-permute-done((bf16[256,1024]{1,0:T(8,128)(2,1)S(1)}, bf16[256,1024]{1,0:T(8,128)(2,1)S(1)}, u32[]{:S(2)}, u32[]{:S(2)}) %collective-permute-start.100) | collective-permute-done | bytes 524320 | tf_op jit(solution)/shard_map/ppermute | solution.py:44
  511.8 4.5 collective-permute-done.99
  (554 shorter events, 206.4 us)
Async XLA Ops:
  10.0 19.6 %collective-permute-start = (bf16[256,512]{1,0:T(8,128)(2,1)S(1)}, bf16[256,512]{1,0:T(8,128)(2,1)S(1)}, u32[]{:S(2)}, u32[]{:S(2)}) collective-permute-start(bf16[256,512]{1,0:T(8,128)(2,1)S(1)} %broadcast_select_fusion.13), channel_id=1, source_target_pairs={{0,16},{1,17},{2,18},{3,19},{16,0},{17,1},{18,2},{19,3},{4,20},{5,... | collective-permute-start | bytes 786440 | tf_op jit(solution)/shard_map/ppermute | solution.py:44
  14.2 38.5 %all-to-all-start = ((bf16[4,512,256]{2,1,0:T(8,128)(2,1)}), bf16[4,512,256]{2,1,0:T(8,128)(2,1)S(1)}, u32[]{:S(2)}, u32[]{:S(2)}) async-start(bf16[4,512,256]{2,1,0:T(8,128)(2,1)} %broadcast_in_dim.130), calls=%async_computation | async-start | bytes 2097152 | tf_op jit(solution)/shard_map/all_to_all | solution.py:68
  19.2 55.9 %all-gather.9.cloned.1.call-start = ((), (), s32[]{:S(2)}) async-start(), calls=%async_computation.7 | async-start | bytes 1310720 | tf_op jit(solution)/shard_map/all_gather | solution.py:698
  30.5 84.1 %all-gather.11.cloned.1.call-start = ((), (), s32[]{:S(2)}) async-start(), calls=%async_computation.8 | async-start | bytes 2621440 | tf_op jit(solution)/shard_map/all_gather | solution.py:698
  31.2 14.2 %collective-permute-start.1 = (bf16[256,1024]{1,0:T(8,128)(2,1)S(1)}, bf16[256,1024]{1,0:T(8,128)(2,1)S(1)}, u32[]{:S(2)}, u32[]{:S(2)}) collective-permute-start(bf16[256,1024]{1,0:T(8,128)(2,1)S(1)} %broadcast_select_fusion.4), channel_id=1, source_target_pairs={{0,16},{1,17},{2,18},{3,19},{16,0},{17,1},{18,2},{19,3},{4,20},{5,... | collective-permute-start | bytes 1572872 | tf_op jit(solution)/shard_map/ppermute | solution.py:44
  52.6 94.9 %all-gather.13.cloned.1.call-start = ((), (), s32[]{:S(2)}) async-start(), calls=%async_computation.9 | async-start | bytes 1310720 | tf_op jit(solution)/shard_map/all_gather | solution.py:698
  98.7 48.8 %all-to-all-start.1 = ((bf16[4,512,256]{2,1,0:T(8,128)(2,1)}), bf16[4,512,256]{2,1,0:T(8,128)(2,1)}, u32[]{:S(2)}, u32[]{:S(2)}) async-start(bf16[4,512,256]{2,1,0:T(8,128)(2,1)} %broadcast_in_dim.135), calls=%async_computation.1 | async-start | bytes 2097152 | tf_op jit(solution)/shard_map/all_to_all | solution.py:68
  103.0 100.2 %all-gather.15.cloned.1.call-start = ((), (), s32[]{:S(2)}) async-start(), calls=%async_computation.10 | async-start | bytes 2621440 | tf_op jit(solution)/shard_map/all_gather | solution.py:698
  103.6 252.8 %reduce-scatter.5.cloned.1.call-start = ((), (), s32[]{:S(2)}) async-start(), calls=%async_computation.11 | async-start | bytes 2621440 | tf_op jit(solution)/shard_map/reduce_scatter | solution.py:897
  105.0 13.7 %collective-permute-start.14 = (bf16[128,1024]{1,0:T(8,128)(2,1)S(1)}, bf16[128,1024]{1,0:T(8,128)(2,1)S(1)}, u32[]{:S(2)}, u32[]{:S(2)}) collective-permute-start(bf16[128,1024]{1,0:T(8,128)(2,1)S(1)} %get-tuple-element.206), channel_id=1, source_target_pairs={{0,16},{1,17},{2,18},{3,19},{16,0},{17,1},{18,2},{19,3},{4,20},{5,... | collective-permute-start | bytes 786440 | tf_op jit(solution)/shard_map/ppermute | solution.py:44
  105.6 13.8 %collective-permute-start.15 = (bf16[128,1024]{1,0:T(8,128)(2,1)S(1)}, bf16[128,1024]{1,0:T(8,128)(2,1)S(1)}, u32[]{:S(2)}, u32[]{:S(2)}) collective-permute-start(bf16[128,1024]{1,0:T(8,128)(2,1)S(1)} %get-tuple-element.207), channel_id=1, source_target_pairs={{0,18},{1,19},{2,16},{3,17},{16,2},{17,3},{18,0},{19,1},{4,22},{5,... | collective-permute-start | bytes 786440 | tf_op jit(solution)/shard_map/ppermute | solution.py:44
  128.9 18.7 %collective-permute-start.22 = (bf16[256,1024]{1,0:T(8,128)(2,1)}, bf16[256,1024]{1,0:T(8,128)(2,1)}, u32[]{:S(2)}, u32[]{:S(2)}) collective-permute-start(bf16[256,1024]{1,0:T(8,128)(2,1)} %get-tuple-element.472), channel_id=1, source_target_pairs={{0,1},{1,0},{2,3},{3,2},{16,17},{17,16},{18,19},{19,18},{4,5},{5,4... | collective-permute-start | bytes 1572872 | tf_op jit(solution)/shard_map/ppermute | solution.py:44
  128.9 18.7 %collective-permute-start.21 = (bf16[256,1024]{1,0:T(8,128)(2,1)}, bf16[256,1024]{1,0:T(8,128)(2,1)}, u32[]{:S(2)}, u32[]{:S(2)}) collective-permute-start(bf16[256,1024]{1,0:T(8,128)(2,1)} %get-tuple-element.473), channel_id=1, source_target_pairs={{0,1},{1,0},{2,3},{3,2},{16,17},{17,16},{18,19},{19,18},{4,5},{5,4... | collective-permute-start | bytes 1572872 | tf_op jit(solution)/shard_map/ppermute | solution.py:44
  129.5 18.2 %collective-permute-start.20 = (bf16[256,1024]{1,0:T(8,128)(2,1)}, bf16[256,1024]{1,0:T(8,128)(2,1)}, u32[]{:S(2)}, u32[]{:S(2)}) collective-permute-start(bf16[256,1024]{1,0:T(8,128)(2,1)} %get-tuple-element.474), channel_id=1, source_target_pairs={{0,1},{1,0},{2,3},{3,2},{16,17},{17,16},{18,19},{19,18},{4,5},{5,4... | collective-permute-start | bytes 1572872 | tf_op jit(solution)/shard_map/ppermute | solution.py:44
  133.6 14.0 %collective-permute-start.19 = (bf16[256,1024]{1,0:T(8,128)(2,1)}, bf16[256,1024]{1,0:T(8,128)(2,1)}, u32[]{:S(2)}, u32[]{:S(2)}) collective-permute-start(bf16[256,1024]{1,0:T(8,128)(2,1)} %get-tuple-element.475), channel_id=1, source_target_pairs={{0,1},{1,0},{2,3},{3,2},{16,17},{17,16},{18,19},{19,18},{4,5},{5,4... | collective-permute-start | bytes 1572872 | tf_op jit(solution)/shard_map/ppermute | solution.py:44
  156.9 13.6 %collective-permute-start.24 = (bf16[128,1024]{1,0:T(8,128)(2,1)S(1)}, bf16[128,1024]{1,0:T(8,128)(2,1)S(1)}, u32[]{:S(2)}, u32[]{:S(2)}) collective-permute-start(bf16[128,1024]{1,0:T(8,128)(2,1)S(1)} %get-tuple-element.214), channel_id=1, source_target_pairs={{0,16},{1,17},{2,18},{3,19},{16,0},{17,1},{18,2},{19,3},{4,20},{5,... | collective-permute-start | bytes 786440 | tf_op jit(solution)/shard_map/ppermute | solution.py:44
  159.0 15.2 %collective-permute-start.32 = (bf16[256,512]{1,0:T(8,128)(2,1)S(1)}, bf16[256,512]{1,0:T(8,128)(2,1)S(1)}, u32[]{:S(2)}, u32[]{:S(2)}) collective-permute-start(bf16[256,512]{1,0:T(8,128)(2,1)S(1)} %get-tuple-element.494), channel_id=1, source_target_pairs={{0,1},{1,0},{2,3},{3,2},{16,17},{17,16},{18,19},{19,18},{4,5},{5,4... | collective-permute-start | bytes 786440 | tf_op jit(solution)/shard_map/ppermute | solution.py:44
  159.1 16.2 %collective-permute-start.31 = (bf16[256,512]{1,0:T(8,128)(2,1)S(1)}, bf16[256,512]{1,0:T(8,128)(2,1)S(1)}, u32[]{:S(2)}, u32[]{:S(2)}) collective-permute-start(bf16[256,512]{1,0:T(8,128)(2,1)S(1)} %get-tuple-element.495), channel_id=1, source_target_pairs={{0,1},{1,0},{2,3},{3,2},{16,17},{17,16},{18,19},{19,18},{4,5},{5,4... | collective-permute-start | bytes 786440 | tf_op jit(solution)/shard_map/ppermute | solution.py:44
  164.6 13.6 %collective-permute-start.30 = (bf16[256,512]{1,0:T(8,128)(2,1)S(1)}, bf16[256,512]{1,0:T(8,128)(2,1)S(1)}, u32[]{:S(2)}, u32[]{:S(2)}) collective-permute-start(bf16[256,512]{1,0:T(8,128)(2,1)S(1)} %get-tuple-element.496), channel_id=1, source_target_pairs={{0,1},{1,0},{2,3},{3,2},{16,17},{17,16},{18,19},{19,18},{4,5},{5,4... | collective-permute-start | bytes 786440 | tf_op jit(solution)/shard_map/ppermute | solution.py:44
  174.2 14.2 %collective-permute-start.27 = (bf16[128,1024]{1,0:T(8,128)(2,1)S(1)}, bf16[128,1024]{1,0:T(8,128)(2,1)S(1)}, u32[]{:S(2)}, u32[]{:S(2)}) collective-permute-start(bf16[128,1024]{1,0:T(8,128)(2,1)S(1)} %get-tuple-element.219.refs_0_), channel_id=1, source_target_pairs={{0,16},{1,17},{2,18},{3,19},{16,0},{17,1},{18,2},{19,3},{4,20},{5,... | collective-permute-start | bytes 786440 | tf_op jit(solution)/shard_map/ppermute | solution.py:44
  175.3 14.1 %collective-permute-start.26 = (bf16[128,1024]{1,0:T(8,128)(2,1)S(1)}, bf16[128,1024]{1,0:T(8,128)(2,1)S(1)}, u32[]{:S(2)}, u32[]{:S(2)}) collective-permute-start(bf16[128,1024]{1,0:T(8,128)(2,1)S(1)} %get-tuple-element.219.refs_0_), channel_id=1, source_target_pairs={{0,2},{1,3},{2,0},{3,1},{16,18},{17,19},{18,16},{19,17},{4,6},{5,7... | collective-permute-start | bytes 786440 | tf_op jit(solution)/shard_map/ppermute | solution.py:44
  178.3 22.1 %collective-permute-start.36 = (bf16[512,256]{1,0:T(8,128)(2,1)S(1)}, bf16[512,256]{1,0:T(8,128)(2,1)S(1)}, u32[]{:S(2)}, u32[]{:S(2)}) collective-permute-start(bf16[512,256]{1,0:T(8,128)(2,1)S(1)} %fusion.11), channel_id=1, source_target_pairs={{3,0},{19,1},{1,2},{17,3},{2,16},{18,17},{0,18},{16,19},{7,4},{23,... | collective-permute-start | bytes 786440 | tf_op jit(solution)/shard_map/ppermute | solution.py:755
  179.9 25.0 %collective-permute-start.35 = (bf16[512,256]{1,0:T(8,128)(2,1)S(1)}, bf16[512,256]{1,0:T(8,128)(2,1)S(1)}, u32[]{:S(2)}, u32[]{:S(2)}) collective-permute-start(bf16[512,256]{1,0:T(8,128)(2,1)S(1)} %fusion.11), channel_id=1, source_target_pairs={{1,0},{17,1},{3,2},{19,3},{0,16},{16,17},{2,18},{18,19},{5,4},{21,... | collective-permute-start | bytes 786440 | tf_op jit(solution)/shard_map/ppermute | solution.py:755
  182.7 22.3 %collective-permute-start.34 = (bf16[512,256]{1,0:T(8,128)(2,1)S(1)}, bf16[512,256]{1,0:T(8,128)(2,1)S(1)}, u32[]{:S(2)}, u32[]{:S(2)}) collective-permute-start(bf16[512,256]{1,0:T(8,128)(2,1)S(1)} %fusion.11), channel_id=1, source_target_pairs={{2,0},{18,1},{0,2},{16,3},{3,16},{19,17},{1,18},{17,19},{6,4},{22,... | collective-permute-start | bytes 786440 | tf_op jit(solution)/shard_map/ppermute | solution.py:755
  188.3 17.1 %collective-permute-start.33 = (bf16[512,256]{1,0:T(8,128)(2,1)S(1)}, bf16[512,256]{1,0:T(8,128)(2,1)S(1)}, u32[]{:S(2)}, u32[]{:S(2)}) collective-permute-start(bf16[512,256]{1,0:T(8,128)(2,1)S(1)} %fusion.11), channel_id=1, source_target_pairs={{0,0},{16,1},{2,2},{18,3},{1,16},{17,17},{3,18},{19,19},{4,4},{20,... | collective-permute-start | bytes 786440 | tf_op jit(solution)/shard_map/ppermute | solution.py:755
  200.3 15.2 %collective-permute-start.38 = (bf16[128,1024]{1,0:T(8,128)(2,1)S(1)}, bf16[128,1024]{1,0:T(8,128)(2,1)S(1)}, u32[]{:S(2)}, u32[]{:S(2)}) collective-permute-start(bf16[128,1024]{1,0:T(8,128)(2,1)S(1)} %get-tuple-element.225), channel_id=1, source_target_pairs={{0,16},{1,17},{2,18},{3,19},{16,0},{17,1},{18,2},{19,3},{4,20},{5,... | collective-permute-start | bytes 786440 | tf_op jit(solution)/shard_map/ppermute | solution.py:44
  205.0 14.9 %collective-permute-start.45 = (bf16[256,1024]{1,0:T(8,128)(2,1)S(1)}, bf16[256,1024]{1,0:T(8,128)(2,1)S(1)}, u32[]{:S(2)}, u32[]{:S(2)}) collective-permute-start(bf16[256,1024]{1,0:T(8,128)(2,1)S(1)} %get-tuple-element.469), channel_id=1, source_target_pairs={{0,1},{1,0},{2,3},{3,2},{16,17},{17,16},{18,19},{19,18},{4,5},{5,4... | collective-permute-start | bytes 1572872 | tf_op jit(solution)/shard_map/ppermute | solution.py:44
  207.7 13.8 %collective-permute-start.44 = (bf16[256,1024]{1,0:T(8,128)(2,1)S(1)}, bf16[256,1024]{1,0:T(8,128)(2,1)S(1)}, u32[]{:S(2)}, u32[]{:S(2)}) collective-permute-start(bf16[256,1024]{1,0:T(8,128)(2,1)S(1)} %get-tuple-element.470), channel_id=1, source_target_pairs={{0,1},{1,0},{2,3},{3,2},{16,17},{17,16},{18,19},{19,18},{4,5},{5,4... | collective-permute-start | bytes 1572872 | tf_op jit(solution)/shard_map/ppermute | solution.py:44
  217.9 14.4 %collective-permute-start.41 = (bf16[128,1024]{1,0:T(8,128)(2,1)S(1)}, bf16[128,1024]{1,0:T(8,128)(2,1)S(1)}, u32[]{:S(2)}, u32[]{:S(2)}) collective-permute-start(bf16[128,1024]{1,0:T(8,128)(2,1)S(1)} %get-tuple-element.228.refs_0_), channel_id=1, source_target_pairs={{0,16},{1,17},{2,18},{3,19},{16,0},{17,1},{18,2},{19,3},{4,20},{5,... | collective-permute-start | bytes 786440 | tf_op jit(solution)/shard_map/ppermute | solution.py:44
  240.3 13.5 %collective-permute-start.48 = (bf16[128,1024]{1,0:T(8,128)(2,1)S(1)}, bf16[128,1024]{1,0:T(8,128)(2,1)S(1)}, u32[]{:S(2)}, u32[]{:S(2)}) collective-permute-start(bf16[128,1024]{1,0:T(8,128)(2,1)S(1)} %get-tuple-element.241), channel_id=1, source_target_pairs={{0,16},{1,17},{2,18},{3,19},{16,0},{17,1},{18,2},{19,3},{4,20},{5,... | collective-permute-start | bytes 786440 | tf_op jit(solution)/shard_map/ppermute | solution.py:44
  263.0 136.5 %reduce-scatter.7.cloned.1.call-start = ((), (), s32[]{:S(2)}) async-start(), calls=%async_computation.12 | async-start | bytes 1310720 | tf_op jit(solution)/shard_map/reduce_scatter | solution.py:897
  264.4 13.9 %collective-permute-start.51 = (bf16[128,1024]{1,0:T(8,128)(2,1)}, bf16[128,1024]{1,0:T(8,128)(2,1)S(1)}, u32[]{:S(2)}, u32[]{:S(2)}) collective-permute-start(bf16[128,1024]{1,0:T(8,128)(2,1)} %copy-done.34), channel_id=1, source_target_pairs={{0,16},{1,17},{2,18},{3,19},{16,0},{17,1},{18,2},{19,3},{4,20},{5,... | collective-permute-start | bytes 786440 | tf_op jit(solution)/shard_map/ppermute | solution.py:44
  274.8 14.7 %collective-permute-start.55 = (bf16[128,1024]{1,0:T(8,128)(2,1)S(1)}, bf16[128,1024]{1,0:T(8,128)(2,1)S(1)}, u32[]{:S(2)}, u32[]{:S(2)}) collective-permute-start(bf16[128,1024]{1,0:T(8,128)(2,1)S(1)} %get-tuple-element.261), channel_id=1, source_target_pairs={{0,18},{1,19},{2,16},{3,17},{16,2},{17,3},{18,0},{19,1},{4,22},{5,... | collective-permute-start | bytes 786440 | tf_op jit(solution)/shard_map/ppermute | solution.py:44
  289.5 21.3 %collective-permute-start.96 = (f32[768]{0:T(1024)S(1)}, f32[768]{0:T(1024)S(1)}, u32[]{:S(2)}, u32[]{:S(2)}) collective-permute-start(f32[768]{0:T(1024)S(1)} %pad_maximum_fusion.17), channel_id=1, source_target_pairs={{0,1},{1,0},{2,3},{3,2},{16,17},{17,16},{18,19},{19,18},{4,5},{5,4... | collective-permute-start | bytes 9224 | tf_op jit(solution)/shard_map/ppermute | solution.py:44
  290.1 14.0 %collective-permute-start.57 = (bf16[128,1024]{1,0:T(8,128)(2,1)S(1)}, bf16[128,1024]{1,0:T(8,128)(2,1)S(1)}, u32[]{:S(2)}, u32[]{:S(2)}) collective-permute-start(bf16[128,1024]{1,0:T(8,128)(2,1)S(1)} %get-tuple-element.269), channel_id=1, source_target_pairs={{0,16},{1,17},{2,18},{3,19},{16,0},{17,1},{18,2},{19,3},{4,20},{5,... | collective-permute-start | bytes 786440 | tf_op jit(solution)/shard_map/ppermute | solution.py:44
  313.5 115.5 %all-gather.17.cloned.1.call-start = ((), (), s32[]{:S(2)}) async-start(), calls=%async_computation.15 | async-start | bytes 4055040 | tf_op jit(solution)/shard_map/all_gather | solution.py:931
  319.0 16.2 %collective-permute-start.61 = (bf16[128,1024]{1,0:T(8,128)(2,1)S(1)}, bf16[128,1024]{1,0:T(8,128)(2,1)S(1)}, u32[]{:S(2)}, u32[]{:S(2)}) collective-permute-start(bf16[128,1024]{1,0:T(8,128)(2,1)S(1)} %get-tuple-element.467.refs_0_.refs_6_), channel_id=1, source_target_pairs={{0,18},{1,19},{2,16},{3,17},{16,2},{17,3},{18,0},{19,1},{4,22},{5,... | collective-permute-start | bytes 786440 | tf_op jit(solution)/shard_map/ppermute | solution.py:44
  321.7 17.9 %collective-permute-start.60 = (bf16[128,1024]{1,0:T(8,128)(2,1)S(1)}, bf16[128,1024]{1,0:T(8,128)(2,1)S(1)}, u32[]{:S(2)}, u32[]{:S(2)}) collective-permute-start(bf16[128,1024]{1,0:T(8,128)(2,1)S(1)} %get-tuple-element.467.refs_0_.refs_6_), channel_id=1, source_target_pairs={{0,16},{1,17},{2,18},{3,19},{16,0},{17,1},{18,2},{19,3},{4,20},{5,... | collective-permute-start | bytes 786440 | tf_op jit(solution)/shard_map/ppermute | solution.py:44
  326.1 13.5 %collective-permute-start.59 = (bf16[128,1024]{1,0:T(8,128)(2,1)S(1)}, bf16[128,1024]{1,0:T(8,128)(2,1)S(1)}, u32[]{:S(2)}, u32[]{:S(2)}) collective-permute-start(bf16[128,1024]{1,0:T(8,128)(2,1)S(1)} %get-tuple-element.467.refs_0_.refs_6_), channel_id=1, source_target_pairs={{0,2},{1,3},{2,0},{3,1},{16,18},{17,19},{18,16},{19,17},{4,6},{5,7... | collective-permute-start | bytes 786440 | tf_op jit(solution)/shard_map/ppermute | solution.py:44
  347.9 125.5 %reduce-scatter.9.cloned.1.call-start = ((), (), s32[]{:S(2)}) async-start(), calls=%async_computation.13 | async-start | bytes 2621440 | tf_op jit(solution)/shard_map/reduce_scatter | solution.py:897
  350.1 13.4 %collective-permute-start.68 = (bf16[128,1024]{1,0:T(8,128)(2,1)}, bf16[128,1024]{1,0:T(8,128)(2,1)}, u32[]{:S(2)}, u32[]{:S(2)}) collective-permute-start(bf16[128,1024]{1,0:T(8,128)(2,1)} %get-tuple-element.311), channel_id=1, source_target_pairs={{0,18},{1,19},{2,16},{3,17},{16,2},{17,3},{18,0},{19,1},{4,22},{5,... | collective-permute-start | bytes 786440 | tf_op jit(solution)/shard_map/ppermute | solution.py:44
  370.2 13.4 %collective-permute-start.74 = (bf16[128,1024]{1,0:T(8,128)(2,1)}, bf16[128,1024]{1,0:T(8,128)(2,1)}, u32[]{:S(2)}, u32[]{:S(2)}) collective-permute-start(bf16[128,1024]{1,0:T(8,128)(2,1)} %copy-done.36), channel_id=1, source_target_pairs={{0,16},{1,17},{2,18},{3,19},{16,0},{17,1},{18,2},{19,3},{4,20},{5,... | collective-permute-start | bytes 786440 | tf_op jit(solution)/shard_map/ppermute | solution.py:44
  392.3 24.2 %collective-permute-start.87 = (f32[768]{0:T(1024)S(1)}, f32[768]{0:T(1024)S(1)}, u32[]{:S(2)}, u32[]{:S(2)}) collective-permute-start(f32[768]{0:T(1024)S(1)} %pad_maximum_fusion.16), channel_id=1, source_target_pairs={{0,1},{1,0},{2,3},{3,2},{16,17},{17,16},{18,19},{19,18},{4,5},{5,4... | collective-permute-start | bytes 9224 | tf_op jit(solution)/shard_map/ppermute | solution.py:44
  393.4 14.1 %collective-permute-start.77 = (bf16[128,1024]{1,0:T(8,128)(2,1)S(1)}, bf16[128,1024]{1,0:T(8,128)(2,1)}, u32[]{:S(2)}, u32[]{:S(2)}) collective-permute-start(bf16[128,1024]{1,0:T(8,128)(2,1)S(1)} %get-tuple-element.337), channel_id=1, source_target_pairs={{0,16},{1,17},{2,18},{3,19},{16,0},{17,1},{18,2},{19,3},{4,20},{5,... | collective-permute-start | bytes 786440 | tf_op jit(solution)/shard_map/ppermute | solution.py:44
  421.0 55.7 %all-to-all-start.2 = ((bf16[4,528,256]{2,1,0:T(8,128)(2,1)}), bf16[4,528,256]{2,1,0:T(8,128)(2,1)S(1)}, u32[]{:S(2)}, u32[]{:S(2)}) async-start(bf16[4,528,256]{2,1,0:T(8,128)(2,1)} %broadcast_in_dim.137), calls=%async_computation.4 | async-start | bytes 2162688 | tf_op jit(solution)/shard_map/all_to_all | solution.py:68
  424.5 83.0 %reduce-scatter.11.cloned.1.call-start = ((), (), s32[]{:S(2)}) async-start(), calls=%async_computation.14 | async-start | bytes 1310720 | tf_op jit(solution)/shard_map/reduce_scatter | solution.py:897
  479.1 19.2 %collective-permute-start.100 = (bf16[256,1024]{1,0:T(8,128)(2,1)S(1)}, bf16[256,1024]{1,0:T(8,128)(2,1)S(1)}, u32[]{:S(2)}, u32[]{:S(2)}) collective-permute-start(bf16[256,1024]{1,0:T(8,128)(2,1)S(1)} %broadcast_select_fusion), channel_id=1, source_target_pairs={{0,16},{1,17},{2,18},{3,19},{16,0},{17,1},{18,2},{19,3},{4,20},{5,... | collective-permute-start | bytes 1572872 | tf_op jit(solution)/shard_map/ppermute | solution.py:44
  487.9 15.5 %collective-permute-start.98 = (bf16[528,256]{1,0:T(8,128)(2,1)}, bf16[528,256]{1,0:T(8,128)(2,1)}, u32[]{:S(2)}, u32[]{:S(2)}) collective-permute-start(bf16[528,256]{1,0:T(8,128)(2,1)} %pad_maximum_fusion.10), channel_id=1, source_target_pairs={{0,16},{1,17},{2,18},{3,19},{16,0},{17,1},{18,2},{19,3},{4,20},{5,... | collective-permute-start | bytes 811016 | tf_op jit(solution)/shard_map/ppermute | solution.py:44
  (138 other events, 1179.8 us)
Sparse Core Ops, SparseCore 0:
  30.7 31.1 all-gather.8
  64.0 50.5 all-gather.10
  116.8 30.6 all-gather.12
  148.9 44.6 all-gather.14
  263.2 41.8 reduce-scatter.4
  313.6 25.3 reduce-scatter.6
  348.0 63.3 all-gather.16
  413.7 59.6 reduce-scatter.8
  478.0 29.5 reduce-scatter.10

commit v6 on v5

--- a/solution.py
+++ b/solution.py
@@ -776,9 +776,21 @@
             [at(table, ((c % 2) ^ section) * pairs + ((c // 2) ^ mine_x)) for c in range(cols_count)]
         )
 
+    def to_dealers_at_once(rows):
+        blocks = jnp.broadcast_to(rows[None], (2,) + rows.shape)
+        chosen = jnp.arange(2, dtype=jnp.int32)[:, None, None, None] == core
+        blocks = jnp.where(chosen, blocks, jnp.zeros_like(blocks)).reshape((count,) + rows.shape[1:])
+        got = lax.all_to_all(blocks, PLANE, split_axis=0, concat_axis=0)
+        return lax.dynamic_index_in_dim(
+            got.reshape((chips, 2) + rows.shape[1:]), section, axis=1, keepdims=False
+        )
+
     def to_dealers(rows):
-        blocks = [trade(at(rows, (mine_x ^ b) * 2 + (section ^ a)), a, b) for a, b in trades]
+        blocks = [trade(block, a, b) for block, a, b in dealt(rows)]
         return jnp.stack(in_order(blocks, core, mine_x))
+
+    def dealt(rows):
+        return [(at(rows, (mine_x ^ b) * 2 + (section ^ a)), a, b) for a, b in trades]
 
     def deal_rows(portion):
         return pick_rows(portion.reshape(-1, width), source).astype(BF16)
@@ -841,8 +853,8 @@
     small = smalls[0]
     normed = run(norm_kernel, [(shape, BF16)], first_rows, small["gain"][0], small["shift"][0])[0]
     attn_w[0] = both_slices(attn_w[0])
-    parts, attn_zero, (cotangent,) = attn_forward(
-        normed, layout, attn_w[0], small, (cotangent,)
+    parts, attn_zero, _ = attn_forward(
+        normed, layout, attn_w[0], small
     )
     given_grads = gather_direct(pick(cotangent[0], cotangent[1]))
     middle_zero, normed, (ffn_w[0],) = middle_norm(parts, first_rows, 0, (ffn_w[0],))
@@ -854,9 +866,11 @@
     attn_w[1] = both_slices(attn_w[1])
     given_grads = deal_rows(given_grads)
     given_grads = all_to_workers(given_grads)
-    parts, attn_one, given_grads = attn_forward(
-        normed, layout, attn_w[1], smalls[1], given_grads
-    )
+    hidden_zero = to_dealers_at_once(to_columns(middle_in))
+    parts, attn_one, (hidden_zero, *given_grads) = attn_forward(
+        normed, layout, attn_w[1], smalls[1], (hidden_zero, *given_grads)
+    )
+    hidden_zero = lax.all_gather(hidden_zero.reshape(rows_dev, width), "row", tiled=True)
     given_grads = by_column(given_grads)
     middle_one, normed, _ = middle_norm(parts, middle_in, 1)
     ffn_w[1] = both_slices(ffn_w[1])
@@ -902,7 +916,7 @@
         grad_parts, middle_one, smalls[1]["gain"][1], cotangent_rows, terms
     )
     sums_b = [*sums_b, down_sum]
-    mid, *terms = together(mid, *terms)
+    mid, hidden_zero, *terms = together(mid, hidden_zero, *terms)
     ffn_term_one = reduce_rows(both_cores(*terms))
     output_parts = sum_up(*last_out)[0]
     parts, factors, qkv_sums, output_parts = attn_backward(low, attn_w[1], attn_one, output_parts)
@@ -918,7 +932,7 @@
         smalls[1]["bias_down"],
         load=(0, len(output_parts)),
     )[0]
-    late = start_return(grad_one, sums_a, sums_b, last_out, middle_in)
+    late = start_return(grad_one, sums_a, sums_b, last_out)
     late_sums = (qkv_sums, up_sums)
     grad_zero = jnp.where(own_usable > 0, grad_one, jnp.zeros_like(grad_one))
     down_sum = jnp.sum(grad_zero, axis=0, dtype=F32)
@@ -945,7 +959,7 @@
     back_zero, ffn_term_zero, late = together(back_zero, ffn_term_zero, late)
     back_zero, sums_zero = finish_return(back_zero)
     back_one = late[:, :width]
-    hidden = late[:, 2 * width :], late[:, width : 2 * width]
+    hidden = pick_rows(hidden_zero, targets).astype(BF16), late[:, width:]
     stays, comes = pick(hidden[0], hidden[1]), send(pick(hidden[1], hidden[0]), cols_count)
     hidden_out = jnp.stack([pick(stays, comes), pick(comes, stays)])
 

time: 531 us -> 523 us (0.985)
  waiting for transfers between devices: 227 us -> 191 us
  local copies, waits for them, and re-layouts: 36.6 us -> 49.2 us
  starting transfers between devices: 104 us -> 110 us
    reduce_scatter x4, waiting for transfers between devices: 41.4 us -> 14.4 us  [reduce_rows(): return lax.psum_scatter(total, 'row', scatter_dimension=0, tiled=True)]
    ppermute x85, waiting for transfers between devices: 151 us -> 135 us  [send(): lax.ppermute(array, PLANE, [(i, i ^ mask) for i in range(plane_size())])]
    all_to_all x3, waiting for transfers between devices: 9.34 us -> 19.8 us  [gather_direct(): return lax.all_to_all(copies, 'row', split_axis=0, concat_axis=0)]
    unnamed x175 -> x207, local copies, waits for them, and re-layouts: 17.1 us -> 23 us
  transfers between devices with their start and end apart: 113 -> 115, of which waited for: 56 -> 47; matrix products, arithmetic and copies ran while one was open for 10% -> 12% of each run, Pallas kernels for 16% -> 18%
where the time goes in v6:
time: 523 us; the launch traced here: 517 us
  waiting for transfers between devices  191 us (37%)
  starting transfers between devices  110 us (21%)
  Pallas kernels  94.3 us (18%)
  local copies, waits for them, and re-layouts  49.2 us (9%)
  other arithmetic  34.9 us (7%)
  between operations  19.5 us (4%)
  blocking collectives  9.2 us (2%)
  matrix products  8.82 us (2%)
    ppermute x85, waiting for transfers between devices, send(): lax.ppermute(array, PLANE, [(i, i ^ mask) for i in range(plane_size())])  135 us
    pallas_call x21, Pallas kernels, run(): return list(call(*args))  94.3 us
    ppermute x85, starting transfers between devices, send(): lax.ppermute(array, PLANE, [(i, i ^ mask) for i in range(plane_size())])  71.1 us
    unnamed x207, local copies, waits for them, and re-layouts  23 us
    ppermute x16, starting transfers between devices, trade(): return lax.ppermute(array, PLANE, ways)  20.3 us
    all_to_all x3, waiting for transfers between devices, gather_direct(): return lax.all_to_all(copies, 'row', split_axis=0, concat_axis=0)  19.8 us
    reduce_scatter x4, waiting for transfers between devices, reduce_rows(): return lax.psum_scatter(total, 'row', scatter_dimension=0, tiled=True)  14.4 us
    all_gather x4, waiting for transfers between devices, gather_slice(): return lax.all_gather(piece, 'row', axis=0, tiled=True)  13.9 us
  transfers between devices with their start and end apart: 115, of which 47 were waited for; matrix products, arithmetic and copies ran while one was open for 12% of the time, Pallas kernels for 18%

profile of v6, /device:TPU:0, one launch (start us, length us, event | category | flops | bytes accessed | tf_op | source)
XLA Modules:
  0.0 516.7 jit_solution(16705816942146059725)
XLA Ops:
  14.8 5.0 all-to-all-start
  21.1 9.2 %all-gather.2 = f32[8,12,256]{2,1,0:T(8,128)S(1)} all-gather(f32[1,12,256]{2,1,0:T(8,128)S(1)} %maximum_bitcast_fusion.5), channel_id=2, replica_groups=mesh['section'=2,'row'=4,'col'=4] {'section','col'}, dimensions={0}, use_global_device_ids=true | all-gather | bytes 110592 | tf_op jit(solution)/shard_map/all_gather | solution.py:707
  32.4 13.6 %collective-permute-done.1 = bf16[256,1024]{1,0:T(8,128)(2,1)S(1)} collective-permute-done((bf16[256,1024]{1,0:T(8,128)(2,1)S(1)}, bf16[256,1024]{1,0:T(8,128)(2,1)S(1)}, u32[]{:S(2)}, u32[]{:S(2)}) %collective-permute-start.1) | collective-permute-done | bytes 524320 | tf_op jit(solution)/shard_map/ppermute | solution.py:44
  47.3 5.9 %all-to-all-done = bf16[4,512,256]{2,1,0:T(8,128)(2,1)S(1)} async-done(((bf16[4,512,256]{2,1,0:T(8,128)(2,1)}), bf16[4,512,256]{2,1,0:T(8,128)(2,1)S(1)}, u32[]{:S(2)}, u32[]{:S(2)}) %all-to-all-start) | async-done | bytes 1048608 | tf_op jit(solution)/shard_map/all_to_all | solution.py:68
  54.4 4.3 all-to-all-start.1
  83.2 4.6 collective-permute-done.8.refs_3_
  87.8 4.8 collective-permute-done.7.refs_2_
  94.1 9.5 %shard_map.196 = (bf16[512,1024]{1,0:T(8,128)(2,1)}, bf16[512,768]{1,0:T(8,128)(2,1)}, bf16[4,512,512]{2,1,0:T(8,128)(2,1)}, bf16[512,256]{1,0:T(8,128)(2,1)}, f...) custom-call(bf16[128,1024]{1,0:T(8,128)(2,1)S(1)} %shard_map.195.ref, ...), custom_call_target="tpu_custom_call" | custom-call | flops 9200000000 | tf_op jit(solution)/shard_map/pallas_call | solution.py:171
  108.7 10.1 %all-gather.12.cloned.1.call-done.refs_4_ = bf16[1024,1024]{1,0:T(8,128)(2,1)} async-done(((bf16[256,1024]{1,0:T(8,128)(2,1)}), bf16[1024,1024]{1,0:T(8,128)(2,1)}) %all-gather.12.cloned.1.call-update) | async-done | bytes 2097168 | tf_op jit(solution)/shard_map/all_gather | solution.py:698
  131.8 4.4 collective-permute-done.18.refs_3_
  137.5 4.2 collective-permute-done.17.refs_2_
  143.4 3.8 all-gather.14.cloned.1.call-done.refs_4_
  147.2 3.9 collective-permute-done.16.refs_1_
  153.0 5.8 %shard_map.198 = (bf16[512,1024]{1,0:T(8,128)(2,1)}, bf16[512,1024]{1,0:T(8,128)(2,1)}, bf16[512,1024]{1,0:T(8,128)(2,1)}, f32[128,1024]{1,0:T(8,128)}, bf16[128...) custom-call(bf16[128,1024]{1,0:T(8,128)(2,1)} %get-tuple-element.209.refs_0_, ...), custom_call_target="tpu_custom_call" | custom-call | flops 9200000000 | tf_op jit(solution)/shard_map/pallas_call | solution.py:171
  164.7 3.4 collective-permute-done.23.refs_1_
  184.4 4.1 all-to-all-start.2
  193.1 3.6 collective-permute-start.33
  197.6 10.4 %shard_map.200 = (bf16[512,1024]{1,0:T(8,128)(2,1)}, bf16[512,768]{1,0:T(8,128)(2,1)}, bf16[4,512,512]{2,1,0:T(8,128)(2,1)}, bf16[512,256]{1,0:T(8,128)(2,1)}, f...) custom-call(bf16[128,1024]{1,0:T(8,128)(2,1)S(1)} %get-tuple-element., ...), custom_call_target="tpu_custom_call" | custom-call | flops 9200000000 | tf_op jit(solution)/shard_map/pallas_call | solution.py:171
  218.3 5.6 %collective-permute-done.38.refs_2_ = bf16[128,1024]{1,0:T(8,128)(2,1)S(1)} collective-permute-done((bf16[128,1024]{1,0:T(8,128)(2,1)}, bf16[128,1024]{1,0:T(8,128)(2,1)S(1)}, u32[]{:S(2)}, u32[]{:S(2)}) %collective-permute-start.38) | collective-permute-done | bytes 262176 | tf_op jit(solution)/shard_map/ppermute | solution.py:44
  231.1 6.3 %collective-permute-done.42.refs_3_ = bf16[128,1024]{1,0:T(8,128)(2,1)S(1)} collective-permute-done((bf16[128,1024]{1,0:T(8,128)(2,1)S(1)}, bf16[128,1024]{1,0:T(8,128)(2,1)S(1)}, u32[]{:S(2)}, u32[]{:S(2)}) %collective-permute-start.42) | collective-permute-done | bytes 262176 | tf_op jit(solution)/shard_map/ppermute | solution.py:44
  237.4 4.3 collective-permute-done.41.refs_2_
  241.8 6.6 %shard_map.202 = (bf16[512,1024]{1,0:T(8,128)(2,1)}, bf16[512,1024]{1,0:T(8,128)(2,1)}, bf16[512,1024]{1,0:T(8,128)(2,1)}, bf16[512,1024]{1,0:T(8,128)(2,1)}, f3...) custom-call(bf16[128,1024]{1,0:T(8,128)(2,1)S(1)} %get-tuple-element, ...), custom_call_target="tpu_custom_call" | custom-call | flops 9200000000 | tf_op jit(solution)/shard_map/pallas_call | solution.py:171
  251.9 4.2 shard_map.203
  260.2 3.3 collective-permute-done.48.refs_2_
  270.9 3.6 add_convert_fusion.1
  290.1 7.7 %shard_map.205 = (bf16[512,1024]{1,0:T(8,128)(2,1)}, bf16[512,768]{1,0:T(8,128)(2,1)}, f32[1,768]{1,0:T(1,128)S(1)}, f32[128,1024]{1,0:T(8,128)}, bf16[128,1024]...) custom-call(bf16[128,1024]{1,0:T(8,128)(2,1)S(1)} %copy-done.40, ...), custom_call_target="tpu_custom_call" | custom-call | flops 9200000000 | tf_op jit(solution)/shard_map/pallas_call | solution.py:171
  297.8 3.4 collective-permute-done.55.refs_3_
  304.9 3.5 shard_map.207
  310.5 5.2 %collective-permute-done.57.refs_2_ = bf16[128,1024]{1,0:T(8,128)(2,1)S(1)} collective-permute-done((bf16[128,1024]{1,0:T(8,128)(2,1)S(1)}, bf16[128,1024]{1,0:T(8,128)(2,1)S(1)}, u32[]{:S(2)}, u32[]{:S(2)}) %collective-permute-start.57) | collective-permute-done | bytes 262176 | tf_op jit(solution)/shard_map/ppermute | solution.py:44
  337.5 6.6 %collective-permute-done.61.refs_3_ = bf16[128,1024]{1,0:T(8,128)(2,1)S(1)} collective-permute-done((bf16[128,1024]{1,0:T(8,128)(2,1)S(1)}, bf16[128,1024]{1,0:T(8,128)(2,1)S(1)}, u32[]{:S(2)}, u32[]{:S(2)}) %collective-permute-start.61) | collective-permute-done | bytes 262176 | tf_op jit(solution)/shard_map/ppermute | solution.py:44
  344.1 4.4 collective-permute-done.60.refs_2_
  348.6 7.3 %shard_map.209 = (bf16[512,1024]{1,0:T(8,128)(2,1)}, bf16[512,1024]{1,0:T(8,128)(2,1)}, f32[1,1024]{1,0:T(1,128)S(1)}, f32[128,1024]{1,0:T(8,128)}, bf16[128,102...) custom-call(bf16[128,1024]{1,0:T(8,128)(2,1)S(1)} %get-tuple-element.465.refs_0_.refs_6_, ...), custom_call_target="tpu_custom_call" | custom-call | flops 9200000000 | tf_op jit(solution)/shard_map/pallas_call | solution.py:171
  360.5 4.2 shard_map.211
  366.5 6.1 %collective-permute-done.67.refs_2_ = bf16[128,1024]{1,0:T(8,128)(2,1)} collective-permute-done((bf16[128,1024]{1,0:T(8,128)(2,1)}, bf16[128,1024]{1,0:T(8,128)(2,1)}, u32[]{:S(2)}, u32[]{:S(2)}) %collective-permute-start.67) | collective-permute-done | bytes 262176 | tf_op jit(solution)/shard_map/ppermute | solution.py:44
  372.7 3.7 shard_map.212
  381.7 3.6 add_convert_fusion
  388.6 4.6 collective-permute-done.74.refs_2_
  393.3 8.7 %shard_map.213 = (bf16[512,1024]{1,0:T(8,128)(2,1)}, bf16[512,768]{1,0:T(8,128)(2,1)}, f32[1,768]{1,0:T(1,128)S(1)}, f32[128,1024]{1,0:T(8,128)}, bf16[128,1024]...) custom-call(bf16[128,1024]{1,0:T(8,128)(2,1)S(1)} %copy-done.43, ...), custom_call_target="tpu_custom_call" | custom-call | flops 9200000000 | tf_op jit(solution)/shard_map/pallas_call | solution.py:171
  405.6 3.6 shard_map.214
  411.4 5.3 %collective-permute-done.78.refs_3_ = bf16[128,1024]{1,0:T(8,128)(2,1)} collective-permute-done((bf16[128,1024]{1,0:T(8,128)(2,1)S(1)}, bf16[128,1024]{1,0:T(8,128)(2,1)}, u32[]{:S(2)}, u32[]{:S(2)}) %collective-permute-start.78) | collective-permute-done | bytes 262176 | tf_op jit(solution)/shard_map/ppermute | solution.py:44
  416.7 3.5 shard_map.215
  421.1 3.5 collective-permute-start.86
  430.2 3.5 all-to-all-start.3
  441.6 14.3 %reduce-scatter.9.cloned.1.call-done = bf16[256,1024]{1,0:T(8,128)(2,1)} async-done(((bf16[1024,1024]{1,0:T(8,128)(2,1)}), bf16[256,1024]{1,0:T(8,128)(2,1)}) %reduce-scatter.9.cloned.1.call-update) | async-done | bytes 524304 | tf_op jit(solution)/shard_map/reduce_scatter | solution.py:911
  455.9 13.8 %all-to-all-done.3 = bf16[4,528,256]{2,1,0:T(8,128)(2,1)S(1)} async-done(((bf16[4,528,256]{2,1,0:T(8,128)(2,1)}), bf16[4,528,256]{2,1,0:T(8,128)(2,1)S(1)}, u32[]{:S(2)}, u32[]{:S(2)}) %all-to-all-start.3) | async-done | bytes 1081376 | tf_op jit(solution)/shard_map/all_to_all | solution.py:68
  475.2 6.1 %collective-permute-done.97 = bf16[512,256]{1,0:T(8,128)(2,1)S(1)} collective-permute-done((bf16[512,256]{1,0:T(8,128)(2,1)S(1)}, bf16[512,256]{1,0:T(8,128)(2,1)S(1)}, u32[]{:S(2)}, u32[]{:S(2)}) %collective-permute-start.97) | collective-permute-done | bytes 262176 | tf_op jit(solution)/shard_map/ppermute | solution.py:44
  483.9 8.7 %collective-permute-done.100 = bf16[256,1024]{1,0:T(8,128)(2,1)S(1)} collective-permute-done((bf16[256,1024]{1,0:T(8,128)(2,1)S(1)}, bf16[256,1024]{1,0:T(8,128)(2,1)S(1)}, u32[]{:S(2)}, u32[]{:S(2)}) %collective-permute-start.100) | collective-permute-done | bytes 524320 | tf_op jit(solution)/shard_map/ppermute | solution.py:44
  503.0 3.8 collective-permute-done.99
  (597 shorter events, 217.4 us)
Async XLA Ops:
  10.7 19.6 %collective-permute-start = (bf16[256,512]{1,0:T(8,128)(2,1)}, bf16[256,512]{1,0:T(8,128)(2,1)S(1)}, u32[]{:S(2)}, u32[]{:S(2)}) collective-permute-start(bf16[256,512]{1,0:T(8,128)(2,1)} %broadcast_select_fusion.13), channel_id=1, source_target_pairs={{0,16},{1,17},{2,18},{3,19},{16,0},{17,1},{18,2},{19,3},{4,20},{5,... | collective-permute-start | bytes 786440 | tf_op jit(solution)/shard_map/ppermute | solution.py:44
  14.8 38.4 %all-to-all-start = ((bf16[4,512,256]{2,1,0:T(8,128)(2,1)}), bf16[4,512,256]{2,1,0:T(8,128)(2,1)S(1)}, u32[]{:S(2)}, u32[]{:S(2)}) async-start(bf16[4,512,256]{2,1,0:T(8,128)(2,1)} %broadcast_in_dim.155), calls=%async_computation | async-start | bytes 2097152 | tf_op jit(solution)/shard_map/all_to_all | solution.py:68
  19.8 61.4 %all-gather.10.cloned.1.call-start = ((), (), s32[]{:S(2)}) async-start(), calls=%async_computation.8 | async-start | bytes 1310720 | tf_op jit(solution)/shard_map/all_gather | solution.py:698
  31.2 87.5 %all-gather.12.cloned.1.call-start = ((), (), s32[]{:S(2)}) async-start(), calls=%async_computation.9 | async-start | bytes 2621440 | tf_op jit(solution)/shard_map/all_gather | solution.py:698
  31.8 14.2 %collective-permute-start.1 = (bf16[256,1024]{1,0:T(8,128)(2,1)S(1)}, bf16[256,1024]{1,0:T(8,128)(2,1)S(1)}, u32[]{:S(2)}, u32[]{:S(2)}) collective-permute-start(bf16[256,1024]{1,0:T(8,128)(2,1)S(1)} %broadcast_select_fusion.4), channel_id=1, source_target_pairs={{0,16},{1,17},{2,18},{3,19},{16,0},{17,1},{18,2},{19,3},{4,20},{5,... | collective-permute-start | bytes 1572872 | tf_op jit(solution)/shard_map/ppermute | solution.py:44
  54.4 89.0 %all-to-all-start.1 = ((bf16[4,512,256]{2,1,0:T(8,128)(2,1)}), bf16[4,512,256]{2,1,0:T(8,128)(2,1)}, u32[]{:S(2)}, u32[]{:S(2)}) async-start(bf16[4,512,256]{2,1,0:T(8,128)(2,1)} %broadcast_in_dim.160), calls=%async_computation.1 | async-start | bytes 2097152 | tf_op jit(solution)/shard_map/all_to_all | solution.py:68
  58.7 88.5 %all-gather.14.cloned.1.call-start = ((), (), s32[]{:S(2)}) async-start(), calls=%async_computation.10 | async-start | bytes 1310720 | tf_op jit(solution)/shard_map/all_gather | solution.py:698
  69.5 140.9 %all-gather.16.cloned.1.call-start = ((), (), s32[]{:S(2)}) async-start(), calls=%async_computation.11 | async-start | bytes 2621440 | tf_op jit(solution)/shard_map/all_gather | solution.py:698
  103.7 15.1 %collective-permute-start.13 = (bf16[128,1024]{1,0:T(8,128)(2,1)S(1)}, bf16[128,1024]{1,0:T(8,128)(2,1)S(1)}, u32[]{:S(2)}, u32[]{:S(2)}) collective-permute-start(bf16[128,1024]{1,0:T(8,128)(2,1)S(1)} %get-tuple-element.204), channel_id=1, source_target_pairs={{0,2},{1,3},{2,0},{3,1},{16,18},{17,19},{18,16},{19,17},{4,6},{5,7... | collective-permute-start | bytes 786440 | tf_op jit(solution)/shard_map/ppermute | solution.py:44
  104.9 14.5 %collective-permute-start.14 = (bf16[128,1024]{1,0:T(8,128)(2,1)S(1)}, bf16[128,1024]{1,0:T(8,128)(2,1)S(1)}, u32[]{:S(2)}, u32[]{:S(2)}) collective-permute-start(bf16[128,1024]{1,0:T(8,128)(2,1)S(1)} %get-tuple-element.205), channel_id=1, source_target_pairs={{0,16},{1,17},{2,18},{3,19},{16,0},{17,1},{18,2},{19,3},{4,20},{5,... | collective-permute-start | bytes 786440 | tf_op jit(solution)/shard_map/ppermute | solution.py:44
  105.5 14.7 %collective-permute-start.15 = (bf16[128,1024]{1,0:T(8,128)(2,1)S(1)}, bf16[128,1024]{1,0:T(8,128)(2,1)S(1)}, u32[]{:S(2)}, u32[]{:S(2)}) collective-permute-start(bf16[128,1024]{1,0:T(8,128)(2,1)S(1)} %get-tuple-element.206), channel_id=1, source_target_pairs={{0,18},{1,19},{2,16},{3,17},{16,2},{17,3},{18,0},{19,1},{4,22},{5,... | collective-permute-start | bytes 786440 | tf_op jit(solution)/shard_map/ppermute | solution.py:44
  131.3 19.8 %collective-permute-start.22 = (bf16[256,1024]{1,0:T(8,128)(2,1)}, bf16[256,1024]{1,0:T(8,128)(2,1)}, u32[]{:S(2)}, u32[]{:S(2)}) collective-permute-start(bf16[256,1024]{1,0:T(8,128)(2,1)} %get-tuple-element.472), channel_id=1, source_target_pairs={{0,1},{1,0},{2,3},{3,2},{16,17},{17,16},{18,19},{19,18},{4,5},{5,4... | collective-permute-start | bytes 1572872 | tf_op jit(solution)/shard_map/ppermute | solution.py:44
  131.3 19.8 %collective-permute-start.21 = (bf16[256,1024]{1,0:T(8,128)(2,1)}, bf16[256,1024]{1,0:T(8,128)(2,1)}, u32[]{:S(2)}, u32[]{:S(2)}) collective-permute-start(bf16[256,1024]{1,0:T(8,128)(2,1)} %get-tuple-element.473), channel_id=1, source_target_pairs={{0,1},{1,0},{2,3},{3,2},{16,17},{17,16},{18,19},{19,18},{4,5},{5,4... | collective-permute-start | bytes 1572872 | tf_op jit(solution)/shard_map/ppermute | solution.py:44
  131.8 19.3 %collective-permute-start.20 = (bf16[256,1024]{1,0:T(8,128)(2,1)}, bf16[256,1024]{1,0:T(8,128)(2,1)}, u32[]{:S(2)}, u32[]{:S(2)}) collective-permute-start(bf16[256,1024]{1,0:T(8,128)(2,1)} %get-tuple-element.474), channel_id=1, source_target_pairs={{0,1},{1,0},{2,3},{3,2},{16,17},{17,16},{18,19},{19,18},{4,5},{5,4... | collective-permute-start | bytes 1572872 | tf_op jit(solution)/shard_map/ppermute | solution.py:44
  136.9 14.2 %collective-permute-start.19 = (bf16[256,1024]{1,0:T(8,128)(2,1)}, bf16[256,1024]{1,0:T(8,128)(2,1)}, u32[]{:S(2)}, u32[]{:S(2)}) collective-permute-start(bf16[256,1024]{1,0:T(8,128)(2,1)} %get-tuple-element.475), channel_id=1, source_target_pairs={{0,1},{1,0},{2,3},{3,2},{16,17},{17,16},{18,19},{19,18},{4,5},{5,4... | collective-permute-start | bytes 1572872 | tf_op jit(solution)/shard_map/ppermute | solution.py:44
  163.2 14.1 %collective-permute-start.31 = (bf16[256,512]{1,0:T(8,128)(2,1)S(1)}, bf16[256,512]{1,0:T(8,128)(2,1)S(1)}, u32[]{:S(2)}, u32[]{:S(2)}) collective-permute-start(bf16[256,512]{1,0:T(8,128)(2,1)S(1)} %get-tuple-element.495), channel_id=1, source_target_pairs={{0,1},{1,0},{2,3},{3,2},{16,17},{17,16},{18,19},{19,18},{4,5},{5,4... | collective-permute-start | bytes 786440 | tf_op jit(solution)/shard_map/ppermute | solution.py:44
  168.1 20.5 %collective-permute-start.30 = (bf16[256,512]{1,0:T(8,128)(2,1)}, bf16[256,512]{1,0:T(8,128)(2,1)S(1)}, u32[]{:S(2)}, u32[]{:S(2)}) collective-permute-start(bf16[256,512]{1,0:T(8,128)(2,1)} %get-tuple-element.496), channel_id=1, source_target_pairs={{0,1},{1,0},{2,3},{3,2},{16,17},{17,16},{18,19},{19,18},{4,5},{5,4... | collective-permute-start | bytes 786440 | tf_op jit(solution)/shard_map/ppermute | solution.py:44
  171.3 20.1 %collective-permute-start.29 = (bf16[256,512]{1,0:T(8,128)(2,1)}, bf16[256,512]{1,0:T(8,128)(2,1)S(1)}, u32[]{:S(2)}, u32[]{:S(2)}) collective-permute-start(bf16[256,512]{1,0:T(8,128)(2,1)} %get-tuple-element.497), channel_id=1, source_target_pairs={{0,1},{1,0},{2,3},{3,2},{16,17},{17,16},{18,19},{19,18},{4,5},{5,4... | collective-permute-start | bytes 786440 | tf_op jit(solution)/shard_map/ppermute | solution.py:44
  174.2 17.7 %collective-permute-start.28 = (bf16[128,1024]{1,0:T(8,128)(2,1)S(1)}, bf16[128,1024]{1,0:T(8,128)(2,1)S(1)}, u32[]{:S(2)}, u32[]{:S(2)}) collective-permute-start(bf16[128,1024]{1,0:T(8,128)(2,1)S(1)} %get-tuple-element.217.refs_0_), channel_id=1, source_target_pairs={{0,18},{1,19},{2,16},{3,17},{16,2},{17,3},{18,0},{19,1},{4,22},{5,... | collective-permute-start | bytes 786440 | tf_op jit(solution)/shard_map/ppermute | solution.py:44
  176.0 17.1 %collective-permute-start.27 = (bf16[128,1024]{1,0:T(8,128)(2,1)S(1)}, bf16[128,1024]{1,0:T(8,128)(2,1)}, u32[]{:S(2)}, u32[]{:S(2)}) collective-permute-start(bf16[128,1024]{1,0:T(8,128)(2,1)S(1)} %get-tuple-element.217.refs_0_), channel_id=1, source_target_pairs={{0,16},{1,17},{2,18},{3,19},{16,0},{17,1},{18,2},{19,3},{4,20},{5,... | collective-permute-start | bytes 786440 | tf_op jit(solution)/shard_map/ppermute | solution.py:44
  177.3 19.3 %collective-permute-start.26 = (bf16[128,1024]{1,0:T(8,128)(2,1)S(1)}, bf16[128,1024]{1,0:T(8,128)(2,1)}, u32[]{:S(2)}, u32[]{:S(2)}) collective-permute-start(bf16[128,1024]{1,0:T(8,128)(2,1)S(1)} %get-tuple-element.217.refs_0_), channel_id=1, source_target_pairs={{0,2},{1,3},{2,0},{3,1},{16,18},{17,19},{18,16},{19,17},{4,6},{5,7... | collective-permute-start | bytes 786440 | tf_op jit(solution)/shard_map/ppermute | solution.py:44
  184.4 31.5 %all-to-all-start.2 = ((bf16[8,128,256]{2,1,0:T(8,128)(2,1)}), bf16[8,128,256]{2,1,0:T(8,128)(2,1)}, u32[]{:S(2)}, u32[]{:S(2)}) async-start(bf16[8,128,256]{2,1,0:T(8,128)(2,1)} %bitcast_select_fusion), calls=%async_computation.2 | async-start | bytes 1048576 | tf_op jit(solution)/shard_map/all_to_all | solution.py:783
  188.6 78.2 %all-gather.18.cloned.1.call-start = ((), (), s32[]{:S(2)}) async-start(), calls=%async_computation.12 | async-start | bytes 1310720 | tf_op jit(solution)/shard_map/all_gather | solution.py:873
  188.7 21.0 %collective-permute-start.36 = (bf16[512,256]{1,0:T(8,128)(2,1)}, bf16[512,256]{1,0:T(8,128)(2,1)S(1)}, u32[]{:S(2)}, u32[]{:S(2)}) collective-permute-start(bf16[512,256]{1,0:T(8,128)(2,1)} %fusion.14), channel_id=1, source_target_pairs={{3,0},{19,1},{1,2},{17,3},{2,16},{18,17},{0,18},{16,19},{7,4},{23,... | collective-permute-start | bytes 786440 | tf_op jit(solution)/shard_map/ppermute | solution.py:755
  191.5 21.9 %collective-permute-start.35 = (bf16[512,256]{1,0:T(8,128)(2,1)}, bf16[512,256]{1,0:T(8,128)(2,1)}, u32[]{:S(2)}, u32[]{:S(2)}) collective-permute-start(bf16[512,256]{1,0:T(8,128)(2,1)} %fusion.14), channel_id=1, source_target_pairs={{1,0},{17,1},{3,2},{19,3},{0,16},{16,17},{2,18},{18,19},{5,4},{21,... | collective-permute-start | bytes 786440 | tf_op jit(solution)/shard_map/ppermute | solution.py:755
  192.5 20.9 %collective-permute-start.34 = (bf16[512,256]{1,0:T(8,128)(2,1)}, bf16[512,256]{1,0:T(8,128)(2,1)}, u32[]{:S(2)}, u32[]{:S(2)}) collective-permute-start(bf16[512,256]{1,0:T(8,128)(2,1)} %fusion.14), channel_id=1, source_target_pairs={{2,0},{18,1},{0,2},{16,3},{3,16},{19,17},{1,18},{17,19},{6,4},{22,... | collective-permute-start | bytes 786440 | tf_op jit(solution)/shard_map/ppermute | solution.py:755
  193.1 20.9 %collective-permute-start.33 = (bf16[512,256]{1,0:T(8,128)(2,1)}, bf16[512,256]{1,0:T(8,128)(2,1)}, u32[]{:S(2)}, u32[]{:S(2)}) collective-permute-start(bf16[512,256]{1,0:T(8,128)(2,1)} %fusion.14), channel_id=1, source_target_pairs={{0,0},{16,1},{2,2},{18,3},{1,16},{17,17},{3,18},{19,19},{4,4},{20,... | collective-permute-start | bytes 786440 | tf_op jit(solution)/shard_map/ppermute | solution.py:755
  210.4 13.5 %collective-permute-start.38 = (bf16[128,1024]{1,0:T(8,128)(2,1)}, bf16[128,1024]{1,0:T(8,128)(2,1)S(1)}, u32[]{:S(2)}, u32[]{:S(2)}) collective-permute-start(bf16[128,1024]{1,0:T(8,128)(2,1)} %get-tuple-element.224), channel_id=1, source_target_pairs={{0,16},{1,17},{2,18},{3,19},{16,0},{17,1},{18,2},{19,3},{4,20},{5,... | collective-permute-start | bytes 786440 | tf_op jit(solution)/shard_map/ppermute | solution.py:44
  213.4 14.1 %collective-permute-start.46 = (bf16[256,1024]{1,0:T(8,128)(2,1)}, bf16[256,1024]{1,0:T(8,128)(2,1)S(1)}, u32[]{:S(2)}, u32[]{:S(2)}) collective-permute-start(bf16[256,1024]{1,0:T(8,128)(2,1)} %get-tuple-element.468), channel_id=1, source_target_pairs={{0,1},{1,0},{2,3},{3,2},{16,17},{17,16},{18,19},{19,18},{4,5},{5,4... | collective-permute-start | bytes 1572872 | tf_op jit(solution)/shard_map/ppermute | solution.py:44
  213.4 15.9 %collective-permute-start.45 = (bf16[256,1024]{1,0:T(8,128)(2,1)}, bf16[256,1024]{1,0:T(8,128)(2,1)S(1)}, u32[]{:S(2)}, u32[]{:S(2)}) collective-permute-start(bf16[256,1024]{1,0:T(8,128)(2,1)} %get-tuple-element.469), channel_id=1, source_target_pairs={{0,1},{1,0},{2,3},{3,2},{16,17},{17,16},{18,19},{19,18},{4,5},{5,4... | collective-permute-start | bytes 1572872 | tf_op jit(solution)/shard_map/ppermute | solution.py:44
  217.7 147.1 %reduce-scatter.5.cloned.1.call-start = ((), (), s32[]{:S(2)}) async-start(), calls=%async_computation.13 | async-start | bytes 2621440 | tf_op jit(solution)/shard_map/reduce_scatter | solution.py:911
  227.4 14.3 %collective-permute-start.41 = (bf16[128,1024]{1,0:T(8,128)(2,1)S(1)}, bf16[128,1024]{1,0:T(8,128)(2,1)S(1)}, u32[]{:S(2)}, u32[]{:S(2)}) collective-permute-start(bf16[128,1024]{1,0:T(8,128)(2,1)S(1)} %get-tuple-element.226.refs_0_), channel_id=1, source_target_pairs={{0,16},{1,17},{2,18},{3,19},{16,0},{17,1},{18,2},{19,3},{4,20},{5,... | collective-permute-start | bytes 786440 | tf_op jit(solution)/shard_map/ppermute | solution.py:44
  249.8 13.7 %collective-permute-start.48 = (bf16[128,1024]{1,0:T(8,128)(2,1)S(1)}, bf16[128,1024]{1,0:T(8,128)(2,1)S(1)}, u32[]{:S(2)}, u32[]{:S(2)}) collective-permute-start(bf16[128,1024]{1,0:T(8,128)(2,1)S(1)} %get-tuple-element.239), channel_id=1, source_target_pairs={{0,16},{1,17},{2,18},{3,19},{16,0},{17,1},{18,2},{19,3},{4,20},{5,... | collective-permute-start | bytes 786440 | tf_op jit(solution)/shard_map/ppermute | solution.py:44
  274.6 134.6 %reduce-scatter.7.cloned.1.call-start = ((), (), s32[]{:S(2)}) async-start(), calls=%async_computation.14 | async-start | bytes 1310720 | tf_op jit(solution)/shard_map/reduce_scatter | solution.py:911
  276.0 14.0 %collective-permute-start.51 = (bf16[128,1024]{1,0:T(8,128)(2,1)}, bf16[128,1024]{1,0:T(8,128)(2,1)S(1)}, u32[]{:S(2)}, u32[]{:S(2)}) collective-permute-start(bf16[128,1024]{1,0:T(8,128)(2,1)} %copy-done.39), channel_id=1, source_target_pairs={{0,16},{1,17},{2,18},{3,19},{16,0},{17,1},{18,2},{19,3},{4,20},{5,... | collective-permute-start | bytes 786440 | tf_op jit(solution)/shard_map/ppermute | solution.py:44
  286.4 14.8 %collective-permute-start.55 = (bf16[128,1024]{1,0:T(8,128)(2,1)S(1)}, bf16[128,1024]{1,0:T(8,128)(2,1)S(1)}, u32[]{:S(2)}, u32[]{:S(2)}) collective-permute-start(bf16[128,1024]{1,0:T(8,128)(2,1)S(1)} %get-tuple-element.267), channel_id=1, source_target_pairs={{0,18},{1,19},{2,16},{3,17},{16,2},{17,3},{18,0},{19,1},{4,22},{5,... | collective-permute-start | bytes 786440 | tf_op jit(solution)/shard_map/ppermute | solution.py:44
  301.2 20.9 %collective-permute-start.96 = (f32[768]{0:T(1024)S(1)}, f32[768]{0:T(1024)S(1)}, u32[]{:S(2)}, u32[]{:S(2)}) collective-permute-start(f32[768]{0:T(1024)S(1)} %pad_maximum_fusion.17), channel_id=1, source_target_pairs={{0,1},{1,0},{2,3},{3,2},{16,17},{17,16},{18,19},{19,18},{4,5},{5,4... | collective-permute-start | bytes 9224 | tf_op jit(solution)/shard_map/ppermute | solution.py:44
  301.7 14.0 %collective-permute-start.57 = (bf16[128,1024]{1,0:T(8,128)(2,1)S(1)}, bf16[128,1024]{1,0:T(8,128)(2,1)S(1)}, u32[]{:S(2)}, u32[]{:S(2)}) collective-permute-start(bf16[128,1024]{1,0:T(8,128)(2,1)S(1)} %get-tuple-element.275), channel_id=1, source_target_pairs={{0,16},{1,17},{2,18},{3,19},{16,0},{17,1},{18,2},{19,3},{4,20},{5,... | collective-permute-start | bytes 786440 | tf_op jit(solution)/shard_map/ppermute | solution.py:44
  325.5 108.5 %all-gather.20.cloned.1.call-start = ((), (), s32[]{:S(2)}) async-start(), calls=%async_computation.17 | async-start | bytes 2703360 | tf_op jit(solution)/shard_map/all_gather | solution.py:945
  333.7 14.8 %collective-permute-start.60 = (bf16[128,1024]{1,0:T(8,128)(2,1)S(1)}, bf16[128,1024]{1,0:T(8,128)(2,1)S(1)}, u32[]{:S(2)}, u32[]{:S(2)}) collective-permute-start(bf16[128,1024]{1,0:T(8,128)(2,1)S(1)} %get-tuple-element.465.refs_0_.refs_6_), channel_id=1, source_target_pairs={{0,16},{1,17},{2,18},{3,19},{16,0},{17,1},{18,2},{19,3},{4,20},{5,... | collective-permute-start | bytes 786440 | tf_op jit(solution)/shard_map/ppermute | solution.py:44
  356.7 99.2 %reduce-scatter.9.cloned.1.call-start = ((), (), s32[]{:S(2)}) async-start(), calls=%async_computation.15 | async-start | bytes 2621440 | tf_op jit(solution)/shard_map/reduce_scatter | solution.py:911
  358.7 14.0 %collective-permute-start.67 = (bf16[128,1024]{1,0:T(8,128)(2,1)}, bf16[128,1024]{1,0:T(8,128)(2,1)}, u32[]{:S(2)}, u32[]{:S(2)}) collective-permute-start(bf16[128,1024]{1,0:T(8,128)(2,1)} %get-tuple-element.310), channel_id=1, source_target_pairs={{0,16},{1,17},{2,18},{3,19},{16,0},{17,1},{18,2},{19,3},{4,20},{5,... | collective-permute-start | bytes 786440 | tf_op jit(solution)/shard_map/ppermute | solution.py:44
  379.4 13.9 %collective-permute-start.74 = (bf16[128,1024]{1,0:T(8,128)(2,1)}, bf16[128,1024]{1,0:T(8,128)(2,1)}, u32[]{:S(2)}, u32[]{:S(2)}) collective-permute-start(bf16[128,1024]{1,0:T(8,128)(2,1)} %copy-done.42), channel_id=1, source_target_pairs={{0,16},{1,17},{2,18},{3,19},{16,0},{17,1},{18,2},{19,3},{4,20},{5,... | collective-permute-start | bytes 786440 | tf_op jit(solution)/shard_map/ppermute | solution.py:44
  402.0 23.7 %collective-permute-start.87 = (f32[768]{0:T(1024)S(1)}, f32[768]{0:T(1024)S(1)}, u32[]{:S(2)}, u32[]{:S(2)}) collective-permute-start(f32[768]{0:T(1024)S(1)} %pad_maximum_fusion.16), channel_id=1, source_target_pairs={{0,1},{1,0},{2,3},{3,2},{16,17},{17,16},{18,19},{19,18},{4,5},{5,4... | collective-permute-start | bytes 9224 | tf_op jit(solution)/shard_map/ppermute | solution.py:44
  430.2 39.5 %all-to-all-start.3 = ((bf16[4,528,256]{2,1,0:T(8,128)(2,1)}), bf16[4,528,256]{2,1,0:T(8,128)(2,1)S(1)}, u32[]{:S(2)}, u32[]{:S(2)}) async-start(bf16[4,528,256]{2,1,0:T(8,128)(2,1)} %broadcast_in_dim.169), calls=%async_computation.5 | async-start | bytes 2162688 | tf_op jit(solution)/shard_map/all_to_all | solution.py:68
  433.8 65.2 %reduce-scatter.11.cloned.1.call-start = ((), (), s32[]{:S(2)}) async-start(), calls=%async_computation.16 | async-start | bytes 1310720 | tf_op jit(solution)/shard_map/reduce_scatter | solution.py:911
  473.7 18.8 %collective-permute-start.100 = (bf16[256,1024]{1,0:T(8,128)(2,1)S(1)}, bf16[256,1024]{1,0:T(8,128)(2,1)S(1)}, u32[]{:S(2)}, u32[]{:S(2)}) collective-permute-start(bf16[256,1024]{1,0:T(8,128)(2,1)S(1)} %broadcast_select_fusion), channel_id=1, source_target_pairs={{0,16},{1,17},{2,18},{3,19},{16,0},{17,1},{18,2},{19,3},{4,20},{5,... | collective-permute-start | bytes 1572872 | tf_op jit(solution)/shard_map/ppermute | solution.py:44
  481.4 16.1 %collective-permute-start.98 = (bf16[528,256]{1,0:T(8,128)(2,1)S(1)}, bf16[528,256]{1,0:T(8,128)(2,1)S(1)}, u32[]{:S(2)}, u32[]{:S(2)}) collective-permute-start(bf16[528,256]{1,0:T(8,128)(2,1)S(1)} %pad_maximum_fusion.10), channel_id=1, source_target_pairs={{0,16},{1,17},{2,18},{3,19},{16,0},{17,1},{18,2},{19,3},{4,20},{5,... | collective-permute-start | bytes 811016 | tf_op jit(solution)/shard_map/ppermute | solution.py:44
  (156 other events, 1304.9 us)
Sparse Core Ops, SparseCore 0:
  31.3 40.6 all-gather.9
  74.2 44.5 all-gather.11
  120.9 26.2 all-gather.13
  148.6 45.3 all-gather.15
  217.8 26.4 all-gather.17
  274.7 42.0 reduce-scatter.4
  325.7 25.8 reduce-scatter.6
  356.8 46.0 all-gather.19
  405.2 50.6 reduce-scatter.8
  470.0 26.1 reduce-scatter.10

commit v7 on v6

--- a/solution.py
+++ b/solution.py
@@ -860,9 +860,7 @@
     middle_zero, normed, (ffn_w[0],) = middle_norm(parts, first_rows, 0, (ffn_w[0],))
     ffn_w[0] = both_slices(ffn_w[0])
     parts, ffn_zero, _ = ffn_forward(normed, ffn_w[0], small)
-    middle_in, normed, (given_grads, attn_w[1]) = end_norm(
-        parts, middle_zero, 0, (given_grads, attn_w[1])
-    )
+    middle_in, normed, (given_grads,) = end_norm(parts, middle_zero, 0, (given_grads,))
     attn_w[1] = both_slices(attn_w[1])
     given_grads = deal_rows(given_grads)
     given_grads = all_to_workers(given_grads)

time: 523 us -> 509 us (0.973)
  local copies, waits for them, and re-layouts: 49.2 us -> 36.6 us
  waiting for transfers between devices: 191 us -> 197 us
    unnamed x207 -> x165, local copies, waits for them, and re-layouts: 23 us -> 13.1 us
    ppermute x85, waiting for transfers between devices: 135 us -> 141 us  [send(): lax.ppermute(array, PLANE, [(i, i ^ mask) for i in range(plane_size())])]
  transfers between devices with their start and end apart: 115 -> 115, of which waited for: 47 -> 46; matrix products, arithmetic and copies ran while one was open for 12% -> 11% of each run, Pallas kernels for 18% -> 18%
where the time goes in v7:
time: 509 us; the launch traced here: 503 us
  waiting for transfers between devices  197 us (39%)
  starting transfers between devices  109 us (21%)
  Pallas kernels  91.7 us (18%)
  local copies, waits for them, and re-layouts  36.6 us (7%)
  other arithmetic  31.3 us (6%)
  between operations  19.3 us (4%)
  blocking collectives  9.2 us (2%)
  matrix products  8.79 us (2%)
    ppermute x85, waiting for transfers between devices, send(): lax.ppermute(array, PLANE, [(i, i ^ mask) for i in range(plane_size())])  141 us
    pallas_call x21, Pallas kernels, run(): return list(call(*args))  91.7 us
    ppermute x85, starting transfers between devices, send(): lax.ppermute(array, PLANE, [(i, i ^ mask) for i in range(plane_size())])  70.8 us
    ppermute x16, starting transfers between devices, trade(): return lax.ppermute(array, PLANE, ways)  20.3 us
    all_to_all x3, waiting for transfers between devices, gather_direct(): return lax.all_to_all(copies, 'row', split_axis=0, concat_axis=0)  19.8 us
    reduce_scatter x4, waiting for transfers between devices, reduce_rows(): return lax.psum_scatter(total, 'row', scatter_dimension=0, tiled=True)  14.7 us
    all_to_all x3, starting transfers between devices, gather_direct(): return lax.all_to_all(copies, 'row', split_axis=0, concat_axis=0)  13.2 us
    unnamed x165, local copies, waits for them, and re-layouts  13.1 us
  transfers between devices with their start and end apart: 115, of which 46 were waited for; matrix products, arithmetic and copies ran while one was open for 11% of the time, Pallas kernels for 18%

profile of v7, /device:TPU:0, one launch (start us, length us, event | category | flops | bytes accessed | tf_op | source)
XLA Modules:
  0.0 503.2 jit_solution(3443221856393147440)
XLA Ops:
  10.0 3.0 collective-permute-start
  14.2 5.0 all-to-all-start
  20.4 9.2 %all-gather.2 = f32[8,12,256]{2,1,0:T(8,128)S(1)} all-gather(f32[1,12,256]{2,1,0:T(8,128)S(1)} %maximum_bitcast_fusion.5), channel_id=2, replica_groups=mesh['section'=2,'row'=4,'col'=4] {'section','col'}, dimensions={0}, use_global_device_ids=true | all-gather | bytes 110592 | tf_op jit(solution)/shard_map/all_gather | solution.py:707
  31.8 13.6 %collective-permute-done.1 = bf16[256,1024]{1,0:T(8,128)(2,1)S(1)} collective-permute-done((bf16[256,1024]{1,0:T(8,128)(2,1)S(1)}, bf16[256,1024]{1,0:T(8,128)(2,1)S(1)}, u32[]{:S(2)}, u32[]{:S(2)}) %collective-permute-start.1) | collective-permute-done | bytes 524320 | tf_op jit(solution)/shard_map/ppermute | solution.py:44
  46.6 6.0 %all-to-all-done = bf16[4,512,256]{2,1,0:T(8,128)(2,1)S(1)} async-done(((bf16[4,512,256]{2,1,0:T(8,128)(2,1)}), bf16[4,512,256]{2,1,0:T(8,128)(2,1)S(1)}, u32[]{:S(2)}, u32[]{:S(2)}) %all-to-all-start) | async-done | bytes 1048608 | tf_op jit(solution)/shard_map/all_to_all | solution.py:68
  53.8 4.3 all-to-all-start.1
  81.6 4.5 collective-permute-done.8.refs_3_
  86.1 4.8 collective-permute-done.7.refs_2_
  92.4 10.2 %shard_map.196 = (bf16[512,1024]{1,0:T(8,128)(2,1)}, bf16[512,768]{1,0:T(8,128)(2,1)}, bf16[4,512,512]{2,1,0:T(8,128)(2,1)}, bf16[512,256]{1,0:T(8,128)(2,1)}, f...) custom-call(bf16[128,1024]{1,0:T(8,128)(2,1)S(1)} %shard_map.195.ref, ...), custom_call_target="tpu_custom_call" | custom-call | flops 9200000000 | tf_op jit(solution)/shard_map/pallas_call | solution.py:171
  106.2 12.1 %all-gather.12.cloned.1.call-done.refs_4_ = bf16[1024,1024]{1,0:T(8,128)(2,1)} async-done(((bf16[256,1024]{1,0:T(8,128)(2,1)}), bf16[1024,1024]{1,0:T(8,128)(2,1)}) %all-gather.12.cloned.1.call-update) | async-done | bytes 2097168 | tf_op jit(solution)/shard_map/all_gather | solution.py:698
  124.4 5.5 %collective-permute-done.18.refs_3_ = bf16[128,1024]{1,0:T(8,128)(2,1)S(1)} collective-permute-done((bf16[128,1024]{1,0:T(8,128)(2,1)S(1)}, bf16[128,1024]{1,0:T(8,128)(2,1)S(1)}, u32[]{:S(2)}, u32[]{:S(2)}) %collective-permute-start.18) | collective-permute-done | bytes 262176 | tf_op jit(solution)/shard_map/ppermute | solution.py:44
  129.9 5.5 %collective-permute-done.17.refs_2_ = bf16[128,1024]{1,0:T(8,128)(2,1)S(1)} collective-permute-done((bf16[128,1024]{1,0:T(8,128)(2,1)S(1)}, bf16[128,1024]{1,0:T(8,128)(2,1)S(1)}, u32[]{:S(2)}, u32[]{:S(2)}) %collective-permute-start.17) | collective-permute-done | bytes 262176 | tf_op jit(solution)/shard_map/ppermute | solution.py:44
  136.1 7.6 %collective-permute-done.16.refs_1_ = bf16[128,1024]{1,0:T(8,128)(2,1)S(1)} collective-permute-done((bf16[128,1024]{1,0:T(8,128)(2,1)S(1)}, bf16[128,1024]{1,0:T(8,128)(2,1)S(1)}, u32[]{:S(2)}, u32[]{:S(2)}) %collective-permute-start.16) | collective-permute-done | bytes 262176 | tf_op jit(solution)/shard_map/ppermute | solution.py:44
  143.8 4.6 shard_map.198
  157.8 4.1 collective-permute-done.24.refs_2_
  174.7 4.1 all-to-all-start.2
  182.7 3.6 collective-permute-start.33
  186.3 10.5 %shard_map.200 = (bf16[512,1024]{1,0:T(8,128)(2,1)}, bf16[512,768]{1,0:T(8,128)(2,1)}, bf16[4,512,512]{2,1,0:T(8,128)(2,1)}, bf16[512,256]{1,0:T(8,128)(2,1)}, f...) custom-call(bf16[128,1024]{1,0:T(8,128)(2,1)S(1)} %get-tuple-element., ...), custom_call_target="tpu_custom_call" | custom-call | flops 9200000000 | tf_op jit(solution)/shard_map/pallas_call | solution.py:171
  207.2 6.0 %collective-permute-done.38.refs_2_ = bf16[128,1024]{1,0:T(8,128)(2,1)S(1)} collective-permute-done((bf16[128,1024]{1,0:T(8,128)(2,1)}, bf16[128,1024]{1,0:T(8,128)(2,1)S(1)}, u32[]{:S(2)}, u32[]{:S(2)}) %collective-permute-start.38) | collective-permute-done | bytes 262176 | tf_op jit(solution)/shard_map/ppermute | solution.py:44
  220.3 6.3 %collective-permute-done.42.refs_3_ = bf16[128,1024]{1,0:T(8,128)(2,1)S(1)} collective-permute-done((bf16[128,1024]{1,0:T(8,128)(2,1)S(1)}, bf16[128,1024]{1,0:T(8,128)(2,1)S(1)}, u32[]{:S(2)}, u32[]{:S(2)}) %collective-permute-start.42) | collective-permute-done | bytes 262176 | tf_op jit(solution)/shard_map/ppermute | solution.py:44
  226.6 4.4 collective-permute-done.41.refs_2_
  231.0 6.5 %shard_map.202 = (bf16[512,1024]{1,0:T(8,128)(2,1)}, bf16[512,1024]{1,0:T(8,128)(2,1)}, bf16[512,1024]{1,0:T(8,128)(2,1)}, bf16[512,1024]{1,0:T(8,128)(2,1)}, f3...) custom-call(bf16[128,1024]{1,0:T(8,128)(2,1)S(1)} %get-tuple-element, ...), custom_call_target="tpu_custom_call" | custom-call | flops 9200000000 | tf_op jit(solution)/shard_map/pallas_call | solution.py:171
  241.1 4.2 shard_map.203
  249.3 3.3 collective-permute-done.48.refs_2_
  260.0 3.9 add_convert_fusion.1
  279.6 7.7 %shard_map.205 = (bf16[512,1024]{1,0:T(8,128)(2,1)}, bf16[512,768]{1,0:T(8,128)(2,1)}, f32[1,768]{1,0:T(1,128)S(1)}, f32[128,1024]{1,0:T(8,128)}, bf16[128,1024]...) custom-call(bf16[128,1024]{1,0:T(8,128)(2,1)S(1)} %copy-done.46, ...), custom_call_target="tpu_custom_call" | custom-call | flops 9200000000 | tf_op jit(solution)/shard_map/pallas_call | solution.py:171
  287.3 3.4 collective-permute-done.55.refs_3_
  294.3 3.6 shard_map.207
  300.0 5.3 %collective-permute-done.57.refs_2_ = bf16[128,1024]{1,0:T(8,128)(2,1)S(1)} collective-permute-done((bf16[128,1024]{1,0:T(8,128)(2,1)S(1)}, bf16[128,1024]{1,0:T(8,128)(2,1)S(1)}, u32[]{:S(2)}, u32[]{:S(2)}) %collective-permute-start.57) | collective-permute-done | bytes 262176 | tf_op jit(solution)/shard_map/ppermute | solution.py:44
  325.1 6.6 %collective-permute-done.61.refs_3_ = bf16[128,1024]{1,0:T(8,128)(2,1)S(1)} collective-permute-done((bf16[128,1024]{1,0:T(8,128)(2,1)S(1)}, bf16[128,1024]{1,0:T(8,128)(2,1)S(1)}, u32[]{:S(2)}, u32[]{:S(2)}) %collective-permute-start.61) | collective-permute-done | bytes 262176 | tf_op jit(solution)/shard_map/ppermute | solution.py:44
  331.7 4.4 collective-permute-done.60.refs_2_
  336.2 5.7 %shard_map.209 = (bf16[512,1024]{1,0:T(8,128)(2,1)}, bf16[512,1024]{1,0:T(8,128)(2,1)}, f32[1,1024]{1,0:T(1,128)S(1)}, f32[128,1024]{1,0:T(8,128)}, bf16[128,102...) custom-call(bf16[128,1024]{1,0:T(8,128)(2,1)S(1)} %get-tuple-element.463.refs_0_.refs_6_, ...), custom_call_target="tpu_custom_call" | custom-call | flops 9200000000 | tf_op jit(solution)/shard_map/pallas_call | solution.py:171
  346.9 4.2 shard_map.211
  352.8 6.1 %collective-permute-done.67.refs_2_ = bf16[128,1024]{1,0:T(8,128)(2,1)} collective-permute-done((bf16[128,1024]{1,0:T(8,128)(2,1)}, bf16[128,1024]{1,0:T(8,128)(2,1)}, u32[]{:S(2)}, u32[]{:S(2)}) %collective-permute-start.67) | collective-permute-done | bytes 262176 | tf_op jit(solution)/shard_map/ppermute | solution.py:44
  359.0 3.7 shard_map.212
  368.0 3.9 add_convert_fusion
  374.9 4.6 collective-permute-done.74.refs_2_
  379.6 8.7 %shard_map.213 = (bf16[512,1024]{1,0:T(8,128)(2,1)}, bf16[512,768]{1,0:T(8,128)(2,1)}, f32[1,768]{1,0:T(1,128)S(1)}, f32[128,1024]{1,0:T(8,128)}, bf16[128,1024]...) custom-call(bf16[128,1024]{1,0:T(8,128)(2,1)S(1)} %copy-done.50, ...), custom_call_target="tpu_custom_call" | custom-call | flops 9200000000 | tf_op jit(solution)/shard_map/pallas_call | solution.py:171
  392.0 3.5 shard_map.214
  397.9 5.2 %collective-permute-done.78.refs_3_ = bf16[128,1024]{1,0:T(8,128)(2,1)} collective-permute-done((bf16[128,1024]{1,0:T(8,128)(2,1)S(1)}, bf16[128,1024]{1,0:T(8,128)(2,1)}, u32[]{:S(2)}, u32[]{:S(2)}) %collective-permute-start.78) | collective-permute-done | bytes 262176 | tf_op jit(solution)/shard_map/ppermute | solution.py:44
  403.0 3.7 shard_map.215
  407.8 3.3 collective-permute-start.86
  416.8 3.9 all-to-all-start.3
  428.0 14.7 %reduce-scatter.9.cloned.1.call-done = bf16[256,1024]{1,0:T(8,128)(2,1)} async-done(((bf16[1024,1024]{1,0:T(8,128)(2,1)}), bf16[256,1024]{1,0:T(8,128)(2,1)}) %reduce-scatter.9.cloned.1.call-update) | async-done | bytes 524304 | tf_op jit(solution)/shard_map/reduce_scatter | solution.py:909
  442.7 13.8 %all-to-all-done.3 = bf16[4,528,256]{2,1,0:T(8,128)(2,1)S(1)} async-done(((bf16[4,528,256]{2,1,0:T(8,128)(2,1)}), bf16[4,528,256]{2,1,0:T(8,128)(2,1)S(1)}, u32[]{:S(2)}, u32[]{:S(2)}) %all-to-all-start.3) | async-done | bytes 1081376 | tf_op jit(solution)/shard_map/all_to_all | solution.py:68
  462.0 6.1 %collective-permute-done.97 = bf16[512,256]{1,0:T(8,128)(2,1)S(1)} collective-permute-done((bf16[512,256]{1,0:T(8,128)(2,1)S(1)}, bf16[512,256]{1,0:T(8,128)(2,1)S(1)}, u32[]{:S(2)}, u32[]{:S(2)}) %collective-permute-start.97) | collective-permute-done | bytes 262176 | tf_op jit(solution)/shard_map/ppermute | solution.py:44
  470.7 8.7 %collective-permute-done.100 = bf16[256,1024]{1,0:T(8,128)(2,1)S(1)} collective-permute-done((bf16[256,1024]{1,0:T(8,128)(2,1)S(1)}, bf16[256,1024]{1,0:T(8,128)(2,1)S(1)}, u32[]{:S(2)}, u32[]{:S(2)}) %collective-permute-start.100) | collective-permute-done | bytes 524320 | tf_op jit(solution)/shard_map/ppermute | solution.py:44
  489.8 3.8 collective-permute-done.99
  (555 shorter events, 196.6 us)
Async XLA Ops:
  10.0 19.6 %collective-permute-start = (bf16[256,512]{1,0:T(8,128)(2,1)S(1)}, bf16[256,512]{1,0:T(8,128)(2,1)S(1)}, u32[]{:S(2)}, u32[]{:S(2)}) collective-permute-start(bf16[256,512]{1,0:T(8,128)(2,1)S(1)} %broadcast_select_fusion.13), channel_id=1, source_target_pairs={{0,16},{1,17},{2,18},{3,19},{16,0},{17,1},{18,2},{19,3},{4,20},{5,... | collective-permute-start | bytes 786440 | tf_op jit(solution)/shard_map/ppermute | solution.py:44
  14.2 38.5 %all-to-all-start = ((bf16[4,512,256]{2,1,0:T(8,128)(2,1)}), bf16[4,512,256]{2,1,0:T(8,128)(2,1)S(1)}, u32[]{:S(2)}, u32[]{:S(2)}) async-start(bf16[4,512,256]{2,1,0:T(8,128)(2,1)} %broadcast_in_dim.155), calls=%async_computation | async-start | bytes 2097152 | tf_op jit(solution)/shard_map/all_to_all | solution.py:68
  19.2 60.4 %all-gather.10.cloned.1.call-start = ((), (), s32[]{:S(2)}) async-start(), calls=%async_computation.8 | async-start | bytes 1310720 | tf_op jit(solution)/shard_map/all_gather | solution.py:698
  30.5 87.8 %all-gather.12.cloned.1.call-start = ((), (), s32[]{:S(2)}) async-start(), calls=%async_computation.9 | async-start | bytes 2621440 | tf_op jit(solution)/shard_map/all_gather | solution.py:698
  31.1 14.2 %collective-permute-start.1 = (bf16[256,1024]{1,0:T(8,128)(2,1)S(1)}, bf16[256,1024]{1,0:T(8,128)(2,1)S(1)}, u32[]{:S(2)}, u32[]{:S(2)}) collective-permute-start(bf16[256,1024]{1,0:T(8,128)(2,1)S(1)} %broadcast_select_fusion.4), channel_id=1, source_target_pairs={{0,16},{1,17},{2,18},{3,19},{16,0},{17,1},{18,2},{19,3},{4,20},{5,... | collective-permute-start | bytes 1572872 | tf_op jit(solution)/shard_map/ppermute | solution.py:44
  53.8 101.0 %all-to-all-start.1 = ((bf16[4,512,256]{2,1,0:T(8,128)(2,1)}), bf16[4,512,256]{2,1,0:T(8,128)(2,1)}, u32[]{:S(2)}, u32[]{:S(2)}) async-start(bf16[4,512,256]{2,1,0:T(8,128)(2,1)} %broadcast_in_dim.160), calls=%async_computation.1 | async-start | bytes 2097152 | tf_op jit(solution)/shard_map/all_to_all | solution.py:68
  58.0 94.0 %all-gather.14.cloned.1.call-start = ((), (), s32[]{:S(2)}) async-start(), calls=%async_computation.10 | async-start | bytes 1310720 | tf_op jit(solution)/shard_map/all_gather | solution.py:698
  67.7 132.0 %all-gather.16.cloned.1.call-start = ((), (), s32[]{:S(2)}) async-start(), calls=%async_computation.11 | async-start | bytes 2621440 | tf_op jit(solution)/shard_map/all_gather | solution.py:698
  102.6 15.7 %collective-permute-start.13 = (bf16[128,1024]{1,0:T(8,128)(2,1)}, bf16[128,1024]{1,0:T(8,128)(2,1)S(1)}, u32[]{:S(2)}, u32[]{:S(2)}) collective-permute-start(bf16[128,1024]{1,0:T(8,128)(2,1)} %get-tuple-element.203), channel_id=1, source_target_pairs={{0,2},{1,3},{2,0},{3,1},{16,18},{17,19},{18,16},{19,17},{4,6},{5,7... | collective-permute-start | bytes 786440 | tf_op jit(solution)/shard_map/ppermute | solution.py:44
  103.8 14.5 %collective-permute-start.14 = (bf16[128,1024]{1,0:T(8,128)(2,1)S(1)}, bf16[128,1024]{1,0:T(8,128)(2,1)S(1)}, u32[]{:S(2)}, u32[]{:S(2)}) collective-permute-start(bf16[128,1024]{1,0:T(8,128)(2,1)S(1)} %get-tuple-element.204), channel_id=1, source_target_pairs={{0,16},{1,17},{2,18},{3,19},{16,0},{17,1},{18,2},{19,3},{4,20},{5,... | collective-permute-start | bytes 786440 | tf_op jit(solution)/shard_map/ppermute | solution.py:44
  104.4 13.9 %collective-permute-start.15 = (bf16[128,1024]{1,0:T(8,128)(2,1)S(1)}, bf16[128,1024]{1,0:T(8,128)(2,1)S(1)}, u32[]{:S(2)}, u32[]{:S(2)}) collective-permute-start(bf16[128,1024]{1,0:T(8,128)(2,1)S(1)} %get-tuple-element.205), channel_id=1, source_target_pairs={{0,18},{1,19},{2,16},{3,17},{16,2},{17,3},{18,0},{19,1},{4,22},{5,... | collective-permute-start | bytes 786440 | tf_op jit(solution)/shard_map/ppermute | solution.py:44
  123.8 20.0 %collective-permute-start.22 = (bf16[256,1024]{1,0:T(8,128)(2,1)S(1)}, bf16[256,1024]{1,0:T(8,128)(2,1)S(1)}, u32[]{:S(2)}, u32[]{:S(2)}) collective-permute-start(bf16[256,1024]{1,0:T(8,128)(2,1)S(1)} %get-tuple-element.470), channel_id=1, source_target_pairs={{0,1},{1,0},{2,3},{3,2},{16,17},{17,16},{18,19},{19,18},{4,5},{5,4... | collective-permute-start | bytes 1572872 | tf_op jit(solution)/shard_map/ppermute | solution.py:44
  123.9 19.9 %collective-permute-start.21 = (bf16[256,1024]{1,0:T(8,128)(2,1)S(1)}, bf16[256,1024]{1,0:T(8,128)(2,1)S(1)}, u32[]{:S(2)}, u32[]{:S(2)}) collective-permute-start(bf16[256,1024]{1,0:T(8,128)(2,1)S(1)} %get-tuple-element.471), channel_id=1, source_target_pairs={{0,1},{1,0},{2,3},{3,2},{16,17},{17,16},{18,19},{19,18},{4,5},{5,4... | collective-permute-start | bytes 1572872 | tf_op jit(solution)/shard_map/ppermute | solution.py:44
  124.4 19.4 %collective-permute-start.20 = (bf16[256,1024]{1,0:T(8,128)(2,1)S(1)}, bf16[256,1024]{1,0:T(8,128)(2,1)S(1)}, u32[]{:S(2)}, u32[]{:S(2)}) collective-permute-start(bf16[256,1024]{1,0:T(8,128)(2,1)S(1)} %get-tuple-element.472), channel_id=1, source_target_pairs={{0,1},{1,0},{2,3},{3,2},{16,17},{17,16},{18,19},{19,18},{4,5},{5,4... | collective-permute-start | bytes 1572872 | tf_op jit(solution)/shard_map/ppermute | solution.py:44
  129.9 13.9 %collective-permute-start.19 = (bf16[256,1024]{1,0:T(8,128)(2,1)S(1)}, bf16[256,1024]{1,0:T(8,128)(2,1)S(1)}, u32[]{:S(2)}, u32[]{:S(2)}) collective-permute-start(bf16[256,1024]{1,0:T(8,128)(2,1)S(1)} %get-tuple-element.473), channel_id=1, source_target_pairs={{0,1},{1,0},{2,3},{3,2},{16,17},{17,16},{18,19},{19,18},{4,5},{5,4... | collective-permute-start | bytes 1572872 | tf_op jit(solution)/shard_map/ppermute | solution.py:44
  154.3 13.5 %collective-permute-start.31 = (bf16[256,512]{1,0:T(8,128)(2,1)}, bf16[256,512]{1,0:T(8,128)(2,1)S(1)}, u32[]{:S(2)}, u32[]{:S(2)}) collective-permute-start(bf16[256,512]{1,0:T(8,128)(2,1)} %get-tuple-element.493), channel_id=1, source_target_pairs={{0,1},{1,0},{2,3},{3,2},{16,17},{17,16},{18,19},{19,18},{4,5},{5,4... | collective-permute-start | bytes 786440 | tf_op jit(solution)/shard_map/ppermute | solution.py:44
  157.8 21.1 %collective-permute-start.30 = (bf16[256,512]{1,0:T(8,128)(2,1)}, bf16[256,512]{1,0:T(8,128)(2,1)S(1)}, u32[]{:S(2)}, u32[]{:S(2)}) collective-permute-start(bf16[256,512]{1,0:T(8,128)(2,1)} %get-tuple-element.494), channel_id=1, source_target_pairs={{0,1},{1,0},{2,3},{3,2},{16,17},{17,16},{18,19},{19,18},{4,5},{5,4... | collective-permute-start | bytes 786440 | tf_op jit(solution)/shard_map/ppermute | solution.py:44
  161.9 19.9 %collective-permute-start.29 = (bf16[256,512]{1,0:T(8,128)(2,1)}, bf16[256,512]{1,0:T(8,128)(2,1)S(1)}, u32[]{:S(2)}, u32[]{:S(2)}) collective-permute-start(bf16[256,512]{1,0:T(8,128)(2,1)} %get-tuple-element.495), channel_id=1, source_target_pairs={{0,1},{1,0},{2,3},{3,2},{16,17},{17,16},{18,19},{19,18},{4,5},{5,4... | collective-permute-start | bytes 786440 | tf_op jit(solution)/shard_map/ppermute | solution.py:44
  164.5 17.6 %collective-permute-start.28 = (bf16[128,1024]{1,0:T(8,128)(2,1)S(1)}, bf16[128,1024]{1,0:T(8,128)(2,1)S(1)}, u32[]{:S(2)}, u32[]{:S(2)}) collective-permute-start(bf16[128,1024]{1,0:T(8,128)(2,1)S(1)} %get-tuple-element.216.refs_0_), channel_id=1, source_target_pairs={{0,18},{1,19},{2,16},{3,17},{16,2},{17,3},{18,0},{19,1},{4,22},{5,... | collective-permute-start | bytes 786440 | tf_op jit(solution)/shard_map/ppermute | solution.py:44
  166.1 16.5 %collective-permute-start.27 = (bf16[128,1024]{1,0:T(8,128)(2,1)S(1)}, bf16[128,1024]{1,0:T(8,128)(2,1)}, u32[]{:S(2)}, u32[]{:S(2)}) collective-permute-start(bf16[128,1024]{1,0:T(8,128)(2,1)S(1)} %get-tuple-element.216.refs_0_), channel_id=1, source_target_pairs={{0,16},{1,17},{2,18},{3,19},{16,0},{17,1},{18,2},{19,3},{4,20},{5,... | collective-permute-start | bytes 786440 | tf_op jit(solution)/shard_map/ppermute | solution.py:44
  167.7 18.5 %collective-permute-start.26 = (bf16[128,1024]{1,0:T(8,128)(2,1)S(1)}, bf16[128,1024]{1,0:T(8,128)(2,1)}, u32[]{:S(2)}, u32[]{:S(2)}) collective-permute-start(bf16[128,1024]{1,0:T(8,128)(2,1)S(1)} %get-tuple-element.216.refs_0_), channel_id=1, source_target_pairs={{0,2},{1,3},{2,0},{3,1},{16,18},{17,19},{18,16},{19,17},{4,6},{5,7... | collective-permute-start | bytes 786440 | tf_op jit(solution)/shard_map/ppermute | solution.py:44
  174.7 30.5 %all-to-all-start.2 = ((bf16[8,128,256]{2,1,0:T(8,128)(2,1)}), bf16[8,128,256]{2,1,0:T(8,128)(2,1)}, u32[]{:S(2)}, u32[]{:S(2)}) async-start(bf16[8,128,256]{2,1,0:T(8,128)(2,1)} %bitcast_select_fusion), calls=%async_computation.2 | async-start | bytes 1048576 | tf_op jit(solution)/shard_map/all_to_all | solution.py:783
  178.9 77.0 %all-gather.18.cloned.1.call-start = ((), (), s32[]{:S(2)}) async-start(), calls=%async_computation.12 | async-start | bytes 1310720 | tf_op jit(solution)/shard_map/all_gather | solution.py:871
  178.9 20.0 %collective-permute-start.36 = (bf16[512,256]{1,0:T(8,128)(2,1)}, bf16[512,256]{1,0:T(8,128)(2,1)S(1)}, u32[]{:S(2)}, u32[]{:S(2)}) collective-permute-start(bf16[512,256]{1,0:T(8,128)(2,1)} %fusion.14), channel_id=1, source_target_pairs={{3,0},{19,1},{1,2},{17,3},{2,16},{18,17},{0,18},{16,19},{7,4},{23,... | collective-permute-start | bytes 786440 | tf_op jit(solution)/shard_map/ppermute | solution.py:755
  181.8 20.9 %collective-permute-start.35 = (bf16[512,256]{1,0:T(8,128)(2,1)}, bf16[512,256]{1,0:T(8,128)(2,1)}, u32[]{:S(2)}, u32[]{:S(2)}) collective-permute-start(bf16[512,256]{1,0:T(8,128)(2,1)} %fusion.14), channel_id=1, source_target_pairs={{1,0},{17,1},{3,2},{19,3},{0,16},{16,17},{2,18},{18,19},{5,4},{21,... | collective-permute-start | bytes 786440 | tf_op jit(solution)/shard_map/ppermute | solution.py:755
  182.1 20.6 %collective-permute-start.34 = (bf16[512,256]{1,0:T(8,128)(2,1)}, bf16[512,256]{1,0:T(8,128)(2,1)}, u32[]{:S(2)}, u32[]{:S(2)}) collective-permute-start(bf16[512,256]{1,0:T(8,128)(2,1)} %fusion.14), channel_id=1, source_target_pairs={{2,0},{18,1},{0,2},{16,3},{3,16},{19,17},{1,18},{17,19},{6,4},{22,... | collective-permute-start | bytes 786440 | tf_op jit(solution)/shard_map/ppermute | solution.py:755
  182.7 20.5 %collective-permute-start.33 = (bf16[512,256]{1,0:T(8,128)(2,1)}, bf16[512,256]{1,0:T(8,128)(2,1)}, u32[]{:S(2)}, u32[]{:S(2)}) collective-permute-start(bf16[512,256]{1,0:T(8,128)(2,1)} %fusion.14), channel_id=1, source_target_pairs={{0,0},{16,1},{2,2},{18,3},{1,16},{17,17},{3,18},{19,19},{4,4},{20,... | collective-permute-start | bytes 786440 | tf_op jit(solution)/shard_map/ppermute | solution.py:755
  199.7 13.5 %collective-permute-start.38 = (bf16[128,1024]{1,0:T(8,128)(2,1)}, bf16[128,1024]{1,0:T(8,128)(2,1)S(1)}, u32[]{:S(2)}, u32[]{:S(2)}) collective-permute-start(bf16[128,1024]{1,0:T(8,128)(2,1)} %get-tuple-element.222), channel_id=1, source_target_pairs={{0,16},{1,17},{2,18},{3,19},{16,0},{17,1},{18,2},{19,3},{4,20},{5,... | collective-permute-start | bytes 786440 | tf_op jit(solution)/shard_map/ppermute | solution.py:44
  202.7 13.9 %collective-permute-start.46 = (bf16[256,1024]{1,0:T(8,128)(2,1)}, bf16[256,1024]{1,0:T(8,128)(2,1)S(1)}, u32[]{:S(2)}, u32[]{:S(2)}) collective-permute-start(bf16[256,1024]{1,0:T(8,128)(2,1)} %get-tuple-element.466), channel_id=1, source_target_pairs={{0,1},{1,0},{2,3},{3,2},{16,17},{17,16},{18,19},{19,18},{4,5},{5,4... | collective-permute-start | bytes 1572872 | tf_op jit(solution)/shard_map/ppermute | solution.py:44
  202.7 15.9 %collective-permute-start.45 = (bf16[256,1024]{1,0:T(8,128)(2,1)}, bf16[256,1024]{1,0:T(8,128)(2,1)S(1)}, u32[]{:S(2)}, u32[]{:S(2)}) collective-permute-start(bf16[256,1024]{1,0:T(8,128)(2,1)} %get-tuple-element.467), channel_id=1, source_target_pairs={{0,1},{1,0},{2,3},{3,2},{16,17},{17,16},{18,19},{19,18},{4,5},{5,4... | collective-permute-start | bytes 1572872 | tf_op jit(solution)/shard_map/ppermute | solution.py:44
  206.9 144.2 %reduce-scatter.5.cloned.1.call-start = ((), (), s32[]{:S(2)}) async-start(), calls=%async_computation.13 | async-start | bytes 2621440 | tf_op jit(solution)/shard_map/reduce_scatter | solution.py:909
  216.6 14.4 %collective-permute-start.41 = (bf16[128,1024]{1,0:T(8,128)(2,1)S(1)}, bf16[128,1024]{1,0:T(8,128)(2,1)S(1)}, u32[]{:S(2)}, u32[]{:S(2)}) collective-permute-start(bf16[128,1024]{1,0:T(8,128)(2,1)S(1)} %get-tuple-element.224.refs_0_), channel_id=1, source_target_pairs={{0,16},{1,17},{2,18},{3,19},{16,0},{17,1},{18,2},{19,3},{4,20},{5,... | collective-permute-start | bytes 786440 | tf_op jit(solution)/shard_map/ppermute | solution.py:44
  239.0 13.7 %collective-permute-start.48 = (bf16[128,1024]{1,0:T(8,128)(2,1)S(1)}, bf16[128,1024]{1,0:T(8,128)(2,1)S(1)}, u32[]{:S(2)}, u32[]{:S(2)}) collective-permute-start(bf16[128,1024]{1,0:T(8,128)(2,1)S(1)} %get-tuple-element.237), channel_id=1, source_target_pairs={{0,16},{1,17},{2,18},{3,19},{16,0},{17,1},{18,2},{19,3},{4,20},{5,... | collective-permute-start | bytes 786440 | tf_op jit(solution)/shard_map/ppermute | solution.py:44
  264.0 131.5 %reduce-scatter.7.cloned.1.call-start = ((), (), s32[]{:S(2)}) async-start(), calls=%async_computation.14 | async-start | bytes 1310720 | tf_op jit(solution)/shard_map/reduce_scatter | solution.py:909
  265.5 14.0 %collective-permute-start.51 = (bf16[128,1024]{1,0:T(8,128)(2,1)}, bf16[128,1024]{1,0:T(8,128)(2,1)S(1)}, u32[]{:S(2)}, u32[]{:S(2)}) collective-permute-start(bf16[128,1024]{1,0:T(8,128)(2,1)} %copy-done.45), channel_id=1, source_target_pairs={{0,16},{1,17},{2,18},{3,19},{16,0},{17,1},{18,2},{19,3},{4,20},{5,... | collective-permute-start | bytes 786440 | tf_op jit(solution)/shard_map/ppermute | solution.py:44
  276.0 14.7 %collective-permute-start.55 = (bf16[128,1024]{1,0:T(8,128)(2,1)S(1)}, bf16[128,1024]{1,0:T(8,128)(2,1)S(1)}, u32[]{:S(2)}, u32[]{:S(2)}) collective-permute-start(bf16[128,1024]{1,0:T(8,128)(2,1)S(1)} %get-tuple-element.265), channel_id=1, source_target_pairs={{0,18},{1,19},{2,16},{3,17},{16,2},{17,3},{18,0},{19,1},{4,22},{5,... | collective-permute-start | bytes 786440 | tf_op jit(solution)/shard_map/ppermute | solution.py:44
  290.7 19.6 %collective-permute-start.96 = (f32[768]{0:T(1024)S(1)}, f32[768]{0:T(1024)S(1)}, u32[]{:S(2)}, u32[]{:S(2)}) collective-permute-start(f32[768]{0:T(1024)S(1)} %pad_maximum_fusion.17), channel_id=1, source_target_pairs={{0,1},{1,0},{2,3},{3,2},{16,17},{17,16},{18,19},{19,18},{4,5},{5,4... | collective-permute-start | bytes 9224 | tf_op jit(solution)/shard_map/ppermute | solution.py:44
  291.2 14.0 %collective-permute-start.57 = (bf16[128,1024]{1,0:T(8,128)(2,1)S(1)}, bf16[128,1024]{1,0:T(8,128)(2,1)S(1)}, u32[]{:S(2)}, u32[]{:S(2)}) collective-permute-start(bf16[128,1024]{1,0:T(8,128)(2,1)S(1)} %get-tuple-element.273), channel_id=1, source_target_pairs={{0,16},{1,17},{2,18},{3,19},{16,0},{17,1},{18,2},{19,3},{4,20},{5,... | collective-permute-start | bytes 786440 | tf_op jit(solution)/shard_map/ppermute | solution.py:44
  313.1 107.8 %all-gather.20.cloned.1.call-start = ((), (), s32[]{:S(2)}) async-start(), calls=%async_computation.17 | async-start | bytes 2703360 | tf_op jit(solution)/shard_map/all_gather | solution.py:943
  321.4 14.8 %collective-permute-start.60 = (bf16[128,1024]{1,0:T(8,128)(2,1)S(1)}, bf16[128,1024]{1,0:T(8,128)(2,1)S(1)}, u32[]{:S(2)}, u32[]{:S(2)}) collective-permute-start(bf16[128,1024]{1,0:T(8,128)(2,1)S(1)} %get-tuple-element.463.refs_0_.refs_6_), channel_id=1, source_target_pairs={{0,16},{1,17},{2,18},{3,19},{16,0},{17,1},{18,2},{19,3},{4,20},{5,... | collective-permute-start | bytes 786440 | tf_op jit(solution)/shard_map/ppermute | solution.py:44
  342.8 99.8 %reduce-scatter.9.cloned.1.call-start = ((), (), s32[]{:S(2)}) async-start(), calls=%async_computation.15 | async-start | bytes 2621440 | tf_op jit(solution)/shard_map/reduce_scatter | solution.py:909
  345.0 14.0 %collective-permute-start.67 = (bf16[128,1024]{1,0:T(8,128)(2,1)}, bf16[128,1024]{1,0:T(8,128)(2,1)}, u32[]{:S(2)}, u32[]{:S(2)}) collective-permute-start(bf16[128,1024]{1,0:T(8,128)(2,1)} %get-tuple-element.308), channel_id=1, source_target_pairs={{0,16},{1,17},{2,18},{3,19},{16,0},{17,1},{18,2},{19,3},{4,20},{5,... | collective-permute-start | bytes 786440 | tf_op jit(solution)/shard_map/ppermute | solution.py:44
  365.8 13.8 %collective-permute-start.74 = (bf16[128,1024]{1,0:T(8,128)(2,1)}, bf16[128,1024]{1,0:T(8,128)(2,1)}, u32[]{:S(2)}, u32[]{:S(2)}) collective-permute-start(bf16[128,1024]{1,0:T(8,128)(2,1)} %copy-done.49), channel_id=1, source_target_pairs={{0,16},{1,17},{2,18},{3,19},{16,0},{17,1},{18,2},{19,3},{4,20},{5,... | collective-permute-start | bytes 786440 | tf_op jit(solution)/shard_map/ppermute | solution.py:44
  388.3 23.9 %collective-permute-start.87 = (f32[768]{0:T(1024)S(1)}, f32[768]{0:T(1024)S(1)}, u32[]{:S(2)}, u32[]{:S(2)}) collective-permute-start(f32[768]{0:T(1024)S(1)} %pad_maximum_fusion.16), channel_id=1, source_target_pairs={{0,1},{1,0},{2,3},{3,2},{16,17},{17,16},{18,19},{19,18},{4,5},{5,4... | collective-permute-start | bytes 9224 | tf_op jit(solution)/shard_map/ppermute | solution.py:44
  416.8 39.8 %all-to-all-start.3 = ((bf16[4,528,256]{2,1,0:T(8,128)(2,1)}), bf16[4,528,256]{2,1,0:T(8,128)(2,1)S(1)}, u32[]{:S(2)}, u32[]{:S(2)}) async-start(bf16[4,528,256]{2,1,0:T(8,128)(2,1)} %broadcast_in_dim.169), calls=%async_computation.5 | async-start | bytes 2162688 | tf_op jit(solution)/shard_map/all_to_all | solution.py:68
  420.7 65.0 %reduce-scatter.11.cloned.1.call-start = ((), (), s32[]{:S(2)}) async-start(), calls=%async_computation.16 | async-start | bytes 1310720 | tf_op jit(solution)/shard_map/reduce_scatter | solution.py:909
  460.5 18.9 %collective-permute-start.100 = (bf16[256,1024]{1,0:T(8,128)(2,1)S(1)}, bf16[256,1024]{1,0:T(8,128)(2,1)S(1)}, u32[]{:S(2)}, u32[]{:S(2)}) collective-permute-start(bf16[256,1024]{1,0:T(8,128)(2,1)S(1)} %broadcast_select_fusion), channel_id=1, source_target_pairs={{0,16},{1,17},{2,18},{3,19},{16,0},{17,1},{18,2},{19,3},{4,20},{5,... | collective-permute-start | bytes 1572872 | tf_op jit(solution)/shard_map/ppermute | solution.py:44
  468.3 16.0 %collective-permute-start.98 = (bf16[528,256]{1,0:T(8,128)(2,1)S(1)}, bf16[528,256]{1,0:T(8,128)(2,1)S(1)}, u32[]{:S(2)}, u32[]{:S(2)}) collective-permute-start(bf16[528,256]{1,0:T(8,128)(2,1)S(1)} %pad_maximum_fusion.10), channel_id=1, source_target_pairs={{0,16},{1,17},{2,18},{3,19},{16,0},{17,1},{18,2},{19,3},{4,20},{5,... | collective-permute-start | bytes 811016 | tf_op jit(solution)/shard_map/ppermute | solution.py:44
  (135 other events, 1177.1 us)
Sparse Core Ops, SparseCore 0:
  30.7 40.7 all-gather.9
  73.6 44.6 all-gather.11
  120.5 26.0 all-gather.13
  148.0 45.3 all-gather.15
  207.0 27.1 all-gather.17
  264.1 42.8 reduce-scatter.4
  313.3 26.6 reduce-scatter.6
  343.0 46.6 all-gather.19
  391.9 50.7 reduce-scatter.8
  456.8 26.1 reduce-scatter.10

commit v8 on v7

--- a/solution.py
+++ b/solution.py
@@ -859,10 +859,12 @@
     given_grads = gather_direct(pick(cotangent[0], cotangent[1]))
     middle_zero, normed, (ffn_w[0],) = middle_norm(parts, first_rows, 0, (ffn_w[0],))
     ffn_w[0] = both_slices(ffn_w[0])
-    parts, ffn_zero, _ = ffn_forward(normed, ffn_w[0], small)
+    parts, ffn_zero, (given_grads, attn_w[1]) = ffn_forward(
+        normed, ffn_w[0], small, (given_grads, attn_w[1])
+    )
+    given_grads = deal_rows(given_grads)
+    attn_w[1] = both_slices(attn_w[1])
     middle_in, normed, (given_grads,) = end_norm(parts, middle_zero, 0, (given_grads,))
-    attn_w[1] = both_slices(attn_w[1])
-    given_grads = deal_rows(given_grads)
     given_grads = all_to_workers(given_grads)
     hidden_zero = to_dealers_at_once(to_columns(middle_in))
     parts, attn_one, (hidden_zero, *given_grads) = attn_forward(

time: 509 us -> 509 us (level)
  transfers between devices with their start and end apart: 115 -> 115, of which waited for: 46 -> 45; matrix products, arithmetic and copies ran while one was open for 11% -> 12% of each run, Pallas kernels for 18% -> 18%
where the time goes in v8:
time: 509 us; the launch traced here: 503 us
  waiting for transfers between devices  192 us (38%)
  starting transfers between devices  110 us (22%)
  Pallas kernels  92 us (18%)
  local copies, waits for them, and re-layouts  39.8 us (8%)
  other arithmetic  31.3 us (6%)
  between operations  19.4 us (4%)
  blocking collectives  9.2 us (2%)
  matrix products  9.06 us (2%)
    ppermute x85, waiting for transfers between devices, send(): lax.ppermute(array, PLANE, [(i, i ^ mask) for i in range(plane_size())])  137 us
    pallas_call x21, Pallas kernels, run(): return list(call(*args))  92 us
    ppermute x85, starting transfers between devices, send(): lax.ppermute(array, PLANE, [(i, i ^ mask) for i in range(plane_size())])  71.6 us
    all_to_all x3, waiting for transfers between devices, gather_direct(): return lax.all_to_all(copies, 'row', split_axis=0, concat_axis=0)  20 us
    ppermute x16, starting transfers between devices, trade(): return lax.ppermute(array, PLANE, ways)  19.3 us
    unnamed x165, local copies, waits for them, and re-layouts  16.5 us
    all_to_all x3, starting transfers between devices, gather_direct(): return lax.all_to_all(copies, 'row', split_axis=0, concat_axis=0)  14.2 us
    reduce_scatter x4, waiting for transfers between devices, reduce_rows(): return lax.psum_scatter(total, 'row', scatter_dimension=0, tiled=True)  13.8 us
  transfers between devices with their start and end apart: 115, of which 45 were waited for; matrix products, arithmetic and copies ran while one was open for 12% of the time, Pallas kernels for 18%

profile of v8, /device:TPU:0, one launch (start us, length us, event | category | flops | bytes accessed | tf_op | source)
XLA Modules:
  0.0 503.0 jit_solution(4987379666649764532)
XLA Ops:
  10.0 3.0 collective-permute-start
  14.2 5.0 all-to-all-start
  20.4 9.2 %all-gather.2 = f32[8,12,256]{2,1,0:T(8,128)S(1)} all-gather(f32[1,12,256]{2,1,0:T(8,128)S(1)} %maximum_bitcast_fusion.5), channel_id=2, replica_groups=mesh['section'=2,'row'=4,'col'=4] {'section','col'}, dimensions={0}, use_global_device_ids=true | all-gather | bytes 110592 | tf_op jit(solution)/shard_map/all_gather | solution.py:707
  31.8 13.6 %collective-permute-done.1 = bf16[256,1024]{1,0:T(8,128)(2,1)S(1)} collective-permute-done((bf16[256,1024]{1,0:T(8,128)(2,1)S(1)}, bf16[256,1024]{1,0:T(8,128)(2,1)S(1)}, u32[]{:S(2)}, u32[]{:S(2)}) %collective-permute-start.1) | collective-permute-done | bytes 524320 | tf_op jit(solution)/shard_map/ppermute | solution.py:44
  46.6 6.0 %all-to-all-done = bf16[4,512,256]{2,1,0:T(8,128)(2,1)S(1)} async-done(((bf16[4,512,256]{2,1,0:T(8,128)(2,1)}), bf16[4,512,256]{2,1,0:T(8,128)(2,1)S(1)}, u32[]{:S(2)}, u32[]{:S(2)}) %all-to-all-start) | async-done | bytes 1048608 | tf_op jit(solution)/shard_map/all_to_all | solution.py:68
  53.9 4.2 all-to-all-start.1
  81.6 4.5 collective-permute-done.8.refs_3_
  86.1 4.8 collective-permute-done.7.refs_2_
  92.4 10.2 %shard_map.196 = (bf16[512,1024]{1,0:T(8,128)(2,1)}, bf16[512,768]{1,0:T(8,128)(2,1)}, bf16[4,512,512]{2,1,0:T(8,128)(2,1)}, bf16[512,256]{1,0:T(8,128)(2,1)}, f...) custom-call(bf16[128,1024]{1,0:T(8,128)(2,1)S(1)} %shard_map.195.ref, ...), custom_call_target="tpu_custom_call" | custom-call | flops 9200000000 | tf_op jit(solution)/shard_map/pallas_call | solution.py:171
  106.2 12.1 %all-gather.12.cloned.1.call-done.refs_4_ = bf16[1024,1024]{1,0:T(8,128)(2,1)} async-done(((bf16[256,1024]{1,0:T(8,128)(2,1)}), bf16[1024,1024]{1,0:T(8,128)(2,1)}) %all-gather.12.cloned.1.call-update) | async-done | bytes 2097168 | tf_op jit(solution)/shard_map/all_gather | solution.py:698
  124.4 5.5 %collective-permute-done.18.refs_3_ = bf16[128,1024]{1,0:T(8,128)(2,1)S(1)} collective-permute-done((bf16[128,1024]{1,0:T(8,128)(2,1)S(1)}, bf16[128,1024]{1,0:T(8,128)(2,1)S(1)}, u32[]{:S(2)}, u32[]{:S(2)}) %collective-permute-start.18) | collective-permute-done | bytes 262176 | tf_op jit(solution)/shard_map/ppermute | solution.py:44
  129.9 5.5 %collective-permute-done.17.refs_2_ = bf16[128,1024]{1,0:T(8,128)(2,1)S(1)} collective-permute-done((bf16[128,1024]{1,0:T(8,128)(2,1)S(1)}, bf16[128,1024]{1,0:T(8,128)(2,1)S(1)}, u32[]{:S(2)}, u32[]{:S(2)}) %collective-permute-start.17) | collective-permute-done | bytes 262176 | tf_op jit(solution)/shard_map/ppermute | solution.py:44
  136.2 7.6 %collective-permute-done.16.refs_1_ = bf16[128,1024]{1,0:T(8,128)(2,1)S(1)} collective-permute-done((bf16[128,1024]{1,0:T(8,128)(2,1)S(1)}, bf16[128,1024]{1,0:T(8,128)(2,1)S(1)}, u32[]{:S(2)}, u32[]{:S(2)}) %collective-permute-start.16) | collective-permute-done | bytes 262176 | tf_op jit(solution)/shard_map/ppermute | solution.py:44
  143.8 4.6 shard_map.198
  157.0 3.1 fusion.14
  160.1 4.0 collective-permute-done.24.refs_2_
  173.6 4.1 all-to-all-start.2
  181.7 3.6 collective-permute-start.33
  185.3 10.5 %shard_map.200 = (bf16[512,1024]{1,0:T(8,128)(2,1)}, bf16[512,768]{1,0:T(8,128)(2,1)}, bf16[4,512,512]{2,1,0:T(8,128)(2,1)}, bf16[512,256]{1,0:T(8,128)(2,1)}, f...) custom-call(bf16[128,1024]{1,0:T(8,128)(2,1)S(1)} %get-tuple-element., ...), custom_call_target="tpu_custom_call" | custom-call | flops 9200000000 | tf_op jit(solution)/shard_map/pallas_call | solution.py:171
  206.5 5.5 %collective-permute-done.38.refs_2_ = bf16[128,1024]{1,0:T(8,128)(2,1)S(1)} collective-permute-done((bf16[128,1024]{1,0:T(8,128)(2,1)}, bf16[128,1024]{1,0:T(8,128)(2,1)S(1)}, u32[]{:S(2)}, u32[]{:S(2)}) %collective-permute-start.38) | collective-permute-done | bytes 262176 | tf_op jit(solution)/shard_map/ppermute | solution.py:44
  219.2 6.3 %collective-permute-done.42.refs_3_ = bf16[128,1024]{1,0:T(8,128)(2,1)S(1)} collective-permute-done((bf16[128,1024]{1,0:T(8,128)(2,1)S(1)}, bf16[128,1024]{1,0:T(8,128)(2,1)S(1)}, u32[]{:S(2)}, u32[]{:S(2)}) %collective-permute-start.42) | collective-permute-done | bytes 262176 | tf_op jit(solution)/shard_map/ppermute | solution.py:44
  225.4 4.4 collective-permute-done.41.refs_2_
  230.5 6.5 %shard_map.202 = (bf16[512,1024]{1,0:T(8,128)(2,1)}, bf16[512,1024]{1,0:T(8,128)(2,1)}, bf16[512,1024]{1,0:T(8,128)(2,1)}, bf16[512,1024]{1,0:T(8,128)(2,1)}, f3...) custom-call(bf16[128,1024]{1,0:T(8,128)(2,1)S(1)} %get-tuple-element, ...), custom_call_target="tpu_custom_call" | custom-call | flops 9200000000 | tf_op jit(solution)/shard_map/pallas_call | solution.py:171
  240.6 4.2 shard_map.203
  259.0 3.9 add_convert_fusion.1
  278.4 7.7 %shard_map.205 = (bf16[512,1024]{1,0:T(8,128)(2,1)}, bf16[512,768]{1,0:T(8,128)(2,1)}, f32[1,768]{1,0:T(1,128)S(1)}, f32[128,1024]{1,0:T(8,128)}, bf16[128,1024]...) custom-call(bf16[128,1024]{1,0:T(8,128)(2,1)S(1)} %copy-done.46, ...), custom_call_target="tpu_custom_call" | custom-call | flops 9200000000 | tf_op jit(solution)/shard_map/pallas_call | solution.py:171
  286.2 3.4 collective-permute-done.55.refs_3_
  293.2 3.5 shard_map.207
  298.8 5.9 %collective-permute-done.57.refs_2_ = bf16[128,1024]{1,0:T(8,128)(2,1)S(1)} collective-permute-done((bf16[128,1024]{1,0:T(8,128)(2,1)S(1)}, bf16[128,1024]{1,0:T(8,128)(2,1)S(1)}, u32[]{:S(2)}, u32[]{:S(2)}) %collective-permute-start.57) | collective-permute-done | bytes 262176 | tf_op jit(solution)/shard_map/ppermute | solution.py:44
  324.4 6.0 %collective-permute-done.61.refs_3_ = bf16[128,1024]{1,0:T(8,128)(2,1)S(1)} collective-permute-done((bf16[128,1024]{1,0:T(8,128)(2,1)S(1)}, bf16[128,1024]{1,0:T(8,128)(2,1)S(1)}, u32[]{:S(2)}, u32[]{:S(2)}) %collective-permute-start.61) | collective-permute-done | bytes 262176 | tf_op jit(solution)/shard_map/ppermute | solution.py:44
  330.4 5.2 %collective-permute-done.60.refs_2_ = bf16[128,1024]{1,0:T(8,128)(2,1)S(1)} collective-permute-done((bf16[128,1024]{1,0:T(8,128)(2,1)S(1)}, bf16[128,1024]{1,0:T(8,128)(2,1)S(1)}, u32[]{:S(2)}, u32[]{:S(2)}) %collective-permute-start.60) | collective-permute-done | bytes 262176 | tf_op jit(solution)/shard_map/ppermute | solution.py:44
  335.7 5.7 %shard_map.209 = (bf16[512,1024]{1,0:T(8,128)(2,1)}, bf16[512,1024]{1,0:T(8,128)(2,1)}, f32[1,1024]{1,0:T(1,128)S(1)}, f32[128,1024]{1,0:T(8,128)}, bf16[128,102...) custom-call(bf16[128,1024]{1,0:T(8,128)(2,1)S(1)} %get-tuple-element.469.refs_0_.refs_6_, ...), custom_call_target="tpu_custom_call" | custom-call | flops 9200000000 | tf_op jit(solution)/shard_map/pallas_call | solution.py:171
  346.1 4.2 shard_map.211
  352.6 3.7 collective-permute-done.67.refs_2_
  358.5 3.6 shard_map.212
  367.1 3.9 add_convert_fusion
  373.4 4.8 collective-permute-done.74.refs_2_
  378.3 9.4 %shard_map.213 = (bf16[512,1024]{1,0:T(8,128)(2,1)}, bf16[512,768]{1,0:T(8,128)(2,1)}, f32[1,768]{1,0:T(1,128)S(1)}, f32[128,1024]{1,0:T(8,128)}, bf16[128,1024]...) custom-call(bf16[128,1024]{1,0:T(8,128)(2,1)S(1)} %get-tuple-element.331.refs_0_, ...), custom_call_target="tpu_custom_call" | custom-call | flops 9200000000 | tf_op jit(solution)/shard_map/pallas_call | solution.py:171
  391.4 3.5 shard_map.214
  397.8 5.3 %collective-permute-done.78.refs_3_ = bf16[128,1024]{1,0:T(8,128)(2,1)} collective-permute-done((bf16[128,1024]{1,0:T(8,128)(2,1)S(1)}, bf16[128,1024]{1,0:T(8,128)(2,1)}, u32[]{:S(2)}, u32[]{:S(2)}) %collective-permute-start.78) | collective-permute-done | bytes 262176 | tf_op jit(solution)/shard_map/ppermute | solution.py:44
  403.1 3.5 shard_map.215
  407.7 3.1 collective-permute-start.86
  416.4 5.0 all-to-all-start.3
  428.5 13.7 %reduce-scatter.9.cloned.1.call-done = bf16[256,1024]{1,0:T(8,128)(2,1)} async-done(((bf16[1024,1024]{1,0:T(8,128)(2,1)}), bf16[256,1024]{1,0:T(8,128)(2,1)}) %reduce-scatter.9.cloned.1.call-update) | async-done | bytes 524304 | tf_op jit(solution)/shard_map/reduce_scatter | solution.py:911
  442.2 14.0 %all-to-all-done.3 = bf16[4,528,256]{2,1,0:T(8,128)(2,1)S(1)} async-done(((bf16[4,528,256]{2,1,0:T(8,128)(2,1)}), bf16[4,528,256]{2,1,0:T(8,128)(2,1)S(1)}, u32[]{:S(2)}, u32[]{:S(2)}) %all-to-all-start.3) | async-done | bytes 1081376 | tf_op jit(solution)/shard_map/all_to_all | solution.py:68
  461.6 6.2 %collective-permute-done.97 = bf16[512,256]{1,0:T(8,128)(2,1)S(1)} collective-permute-done((bf16[512,256]{1,0:T(8,128)(2,1)S(1)}, bf16[512,256]{1,0:T(8,128)(2,1)S(1)}, u32[]{:S(2)}, u32[]{:S(2)}) %collective-permute-start.97) | collective-permute-done | bytes 262176 | tf_op jit(solution)/shard_map/ppermute | solution.py:44
  470.3 8.7 %collective-permute-done.100 = bf16[256,1024]{1,0:T(8,128)(2,1)S(1)} collective-permute-done((bf16[256,1024]{1,0:T(8,128)(2,1)S(1)}, bf16[256,1024]{1,0:T(8,128)(2,1)S(1)}, u32[]{:S(2)}, u32[]{:S(2)}) %collective-permute-start.100) | collective-permute-done | bytes 524320 | tf_op jit(solution)/shard_map/ppermute | solution.py:44
  489.4 3.7 collective-permute-done.99
  (555 shorter events, 197.9 us)
Async XLA Ops:
  10.0 19.6 %collective-permute-start = (bf16[256,512]{1,0:T(8,128)(2,1)S(1)}, bf16[256,512]{1,0:T(8,128)(2,1)S(1)}, u32[]{:S(2)}, u32[]{:S(2)}) collective-permute-start(bf16[256,512]{1,0:T(8,128)(2,1)S(1)} %broadcast_select_fusion.13), channel_id=1, source_target_pairs={{0,16},{1,17},{2,18},{3,19},{16,0},{17,1},{18,2},{19,3},{4,20},{5,... | collective-permute-start | bytes 786440 | tf_op jit(solution)/shard_map/ppermute | solution.py:44
  14.2 38.5 %all-to-all-start = ((bf16[4,512,256]{2,1,0:T(8,128)(2,1)}), bf16[4,512,256]{2,1,0:T(8,128)(2,1)S(1)}, u32[]{:S(2)}, u32[]{:S(2)}) async-start(bf16[4,512,256]{2,1,0:T(8,128)(2,1)} %broadcast_in_dim.155), calls=%async_computation | async-start | bytes 2097152 | tf_op jit(solution)/shard_map/all_to_all | solution.py:68
  19.2 60.4 %all-gather.10.cloned.1.call-start = ((), (), s32[]{:S(2)}) async-start(), calls=%async_computation.8 | async-start | bytes 1310720 | tf_op jit(solution)/shard_map/all_gather | solution.py:698
  30.5 87.8 %all-gather.12.cloned.1.call-start = ((), (), s32[]{:S(2)}) async-start(), calls=%async_computation.9 | async-start | bytes 2621440 | tf_op jit(solution)/shard_map/all_gather | solution.py:698
  31.1 14.2 %collective-permute-start.1 = (bf16[256,1024]{1,0:T(8,128)(2,1)S(1)}, bf16[256,1024]{1,0:T(8,128)(2,1)S(1)}, u32[]{:S(2)}, u32[]{:S(2)}) collective-permute-start(bf16[256,1024]{1,0:T(8,128)(2,1)S(1)} %broadcast_select_fusion.4), channel_id=1, source_target_pairs={{0,16},{1,17},{2,18},{3,19},{16,0},{17,1},{18,2},{19,3},{4,20},{5,... | collective-permute-start | bytes 1572872 | tf_op jit(solution)/shard_map/ppermute | solution.py:44
  53.9 97.0 %all-to-all-start.1 = ((bf16[4,512,256]{2,1,0:T(8,128)(2,1)}), bf16[4,512,256]{2,1,0:T(8,128)(2,1)}, u32[]{:S(2)}, u32[]{:S(2)}) async-start(bf16[4,512,256]{2,1,0:T(8,128)(2,1)} %broadcast_in_dim.160), calls=%async_computation.1 | async-start | bytes 2097152 | tf_op jit(solution)/shard_map/all_to_all | solution.py:68
  58.1 92.7 %all-gather.14.cloned.1.call-start = ((), (), s32[]{:S(2)}) async-start(), calls=%async_computation.10 | async-start | bytes 1310720 | tf_op jit(solution)/shard_map/all_gather | solution.py:698
  67.8 130.7 %all-gather.16.cloned.1.call-start = ((), (), s32[]{:S(2)}) async-start(), calls=%async_computation.11 | async-start | bytes 2621440 | tf_op jit(solution)/shard_map/all_gather | solution.py:698
  102.6 15.7 %collective-permute-start.13 = (bf16[128,1024]{1,0:T(8,128)(2,1)}, bf16[128,1024]{1,0:T(8,128)(2,1)S(1)}, u32[]{:S(2)}, u32[]{:S(2)}) collective-permute-start(bf16[128,1024]{1,0:T(8,128)(2,1)} %get-tuple-element.206), channel_id=1, source_target_pairs={{0,2},{1,3},{2,0},{3,1},{16,18},{17,19},{18,16},{19,17},{4,6},{5,7... | collective-permute-start | bytes 786440 | tf_op jit(solution)/shard_map/ppermute | solution.py:44
  103.8 14.5 %collective-permute-start.14 = (bf16[128,1024]{1,0:T(8,128)(2,1)S(1)}, bf16[128,1024]{1,0:T(8,128)(2,1)S(1)}, u32[]{:S(2)}, u32[]{:S(2)}) collective-permute-start(bf16[128,1024]{1,0:T(8,128)(2,1)S(1)} %get-tuple-element.207), channel_id=1, source_target_pairs={{0,16},{1,17},{2,18},{3,19},{16,0},{17,1},{18,2},{19,3},{4,20},{5,... | collective-permute-start | bytes 786440 | tf_op jit(solution)/shard_map/ppermute | solution.py:44
  104.4 13.9 %collective-permute-start.15 = (bf16[128,1024]{1,0:T(8,128)(2,1)S(1)}, bf16[128,1024]{1,0:T(8,128)(2,1)S(1)}, u32[]{:S(2)}, u32[]{:S(2)}) collective-permute-start(bf16[128,1024]{1,0:T(8,128)(2,1)S(1)} %get-tuple-element.208), channel_id=1, source_target_pairs={{0,18},{1,19},{2,16},{3,17},{16,2},{17,3},{18,0},{19,1},{4,22},{5,... | collective-permute-start | bytes 786440 | tf_op jit(solution)/shard_map/ppermute | solution.py:44
  122.1 13.3 %collective-permute-start.17 = (bf16[128,1024]{1,0:T(8,128)(2,1)S(1)}, bf16[128,1024]{1,0:T(8,128)(2,1)S(1)}, u32[]{:S(2)}, u32[]{:S(2)}) collective-permute-start(bf16[128,1024]{1,0:T(8,128)(2,1)S(1)} %get-tuple-element.211.refs_0_), channel_id=1, source_target_pairs={{0,16},{1,17},{2,18},{3,19},{16,0},{17,1},{18,2},{19,3},{4,20},{5,... | collective-permute-start | bytes 786440 | tf_op jit(solution)/shard_map/ppermute | solution.py:44
  123.8 20.0 %collective-permute-start.22 = (bf16[256,1024]{1,0:T(8,128)(2,1)S(1)}, bf16[256,1024]{1,0:T(8,128)(2,1)S(1)}, u32[]{:S(2)}, u32[]{:S(2)}) collective-permute-start(bf16[256,1024]{1,0:T(8,128)(2,1)S(1)} %get-tuple-element.476), channel_id=1, source_target_pairs={{0,1},{1,0},{2,3},{3,2},{16,17},{17,16},{18,19},{19,18},{4,5},{5,4... | collective-permute-start | bytes 1572872 | tf_op jit(solution)/shard_map/ppermute | solution.py:44
  123.9 19.9 %collective-permute-start.21 = (bf16[256,1024]{1,0:T(8,128)(2,1)S(1)}, bf16[256,1024]{1,0:T(8,128)(2,1)S(1)}, u32[]{:S(2)}, u32[]{:S(2)}) collective-permute-start(bf16[256,1024]{1,0:T(8,128)(2,1)S(1)} %get-tuple-element.477), channel_id=1, source_target_pairs={{0,1},{1,0},{2,3},{3,2},{16,17},{17,16},{18,19},{19,18},{4,5},{5,4... | collective-permute-start | bytes 1572872 | tf_op jit(solution)/shard_map/ppermute | solution.py:44
  124.4 19.4 %collective-permute-start.20 = (bf16[256,1024]{1,0:T(8,128)(2,1)S(1)}, bf16[256,1024]{1,0:T(8,128)(2,1)S(1)}, u32[]{:S(2)}, u32[]{:S(2)}) collective-permute-start(bf16[256,1024]{1,0:T(8,128)(2,1)S(1)} %get-tuple-element.478), channel_id=1, source_target_pairs={{0,1},{1,0},{2,3},{3,2},{16,17},{17,16},{18,19},{19,18},{4,5},{5,4... | collective-permute-start | bytes 1572872 | tf_op jit(solution)/shard_map/ppermute | solution.py:44
  129.9 13.9 %collective-permute-start.19 = (bf16[256,1024]{1,0:T(8,128)(2,1)S(1)}, bf16[256,1024]{1,0:T(8,128)(2,1)S(1)}, u32[]{:S(2)}, u32[]{:S(2)}) collective-permute-start(bf16[256,1024]{1,0:T(8,128)(2,1)S(1)} %get-tuple-element.479), channel_id=1, source_target_pairs={{0,1},{1,0},{2,3},{3,2},{16,17},{17,16},{18,19},{19,18},{4,5},{5,4... | collective-permute-start | bytes 1572872 | tf_op jit(solution)/shard_map/ppermute | solution.py:44
  160.1 17.7 %collective-permute-start.30 = (bf16[256,512]{1,0:T(8,128)(2,1)}, bf16[256,512]{1,0:T(8,128)(2,1)S(1)}, u32[]{:S(2)}, u32[]{:S(2)}) collective-permute-start(bf16[256,512]{1,0:T(8,128)(2,1)} %get-tuple-element.500), channel_id=1, source_target_pairs={{0,1},{1,0},{2,3},{3,2},{16,17},{17,16},{18,19},{19,18},{4,5},{5,4... | collective-permute-start | bytes 786440 | tf_op jit(solution)/shard_map/ppermute | solution.py:44
  164.1 16.5 %collective-permute-start.29 = (bf16[256,512]{1,0:T(8,128)(2,1)}, bf16[256,512]{1,0:T(8,128)(2,1)S(1)}, u32[]{:S(2)}, u32[]{:S(2)}) collective-permute-start(bf16[256,512]{1,0:T(8,128)(2,1)} %get-tuple-element.501), channel_id=1, source_target_pairs={{0,1},{1,0},{2,3},{3,2},{16,17},{17,16},{18,19},{19,18},{4,5},{5,4... | collective-permute-start | bytes 786440 | tf_op jit(solution)/shard_map/ppermute | solution.py:44
  166.2 14.7 %collective-permute-start.28 = (bf16[128,1024]{1,0:T(8,128)(2,1)S(1)}, bf16[128,1024]{1,0:T(8,128)(2,1)S(1)}, u32[]{:S(2)}, u32[]{:S(2)}) collective-permute-start(bf16[128,1024]{1,0:T(8,128)(2,1)S(1)} %get-tuple-element.221.refs_0_), channel_id=1, source_target_pairs={{0,18},{1,19},{2,16},{3,17},{16,2},{17,3},{18,0},{19,1},{4,22},{5,... | collective-permute-start | bytes 786440 | tf_op jit(solution)/shard_map/ppermute | solution.py:44
  167.8 13.9 %collective-permute-start.27 = (bf16[128,1024]{1,0:T(8,128)(2,1)S(1)}, bf16[128,1024]{1,0:T(8,128)(2,1)}, u32[]{:S(2)}, u32[]{:S(2)}) collective-permute-start(bf16[128,1024]{1,0:T(8,128)(2,1)S(1)} %get-tuple-element.221.refs_0_), channel_id=1, source_target_pairs={{0,16},{1,17},{2,18},{3,19},{16,0},{17,1},{18,2},{19,3},{4,20},{5,... | collective-permute-start | bytes 786440 | tf_op jit(solution)/shard_map/ppermute | solution.py:44
  169.4 15.9 %collective-permute-start.26 = (bf16[128,1024]{1,0:T(8,128)(2,1)S(1)}, bf16[128,1024]{1,0:T(8,128)(2,1)}, u32[]{:S(2)}, u32[]{:S(2)}) collective-permute-start(bf16[128,1024]{1,0:T(8,128)(2,1)S(1)} %get-tuple-element.221.refs_0_), channel_id=1, source_target_pairs={{0,2},{1,3},{2,0},{3,1},{16,18},{17,19},{18,16},{19,17},{4,6},{5,7... | collective-permute-start | bytes 786440 | tf_op jit(solution)/shard_map/ppermute | solution.py:44
  173.6 30.6 %all-to-all-start.2 = ((bf16[8,128,256]{2,1,0:T(8,128)(2,1)}), bf16[8,128,256]{2,1,0:T(8,128)(2,1)}, u32[]{:S(2)}, u32[]{:S(2)}) async-start(bf16[8,128,256]{2,1,0:T(8,128)(2,1)} %bitcast_select_fusion), calls=%async_computation.2 | async-start | bytes 1048576 | tf_op jit(solution)/shard_map/all_to_all | solution.py:783
  177.7 77.1 %all-gather.18.cloned.1.call-start = ((), (), s32[]{:S(2)}) async-start(), calls=%async_computation.12 | async-start | bytes 1310720 | tf_op jit(solution)/shard_map/all_gather | solution.py:873
  177.8 20.0 %collective-permute-start.36 = (bf16[512,256]{1,0:T(8,128)(2,1)}, bf16[512,256]{1,0:T(8,128)(2,1)S(1)}, u32[]{:S(2)}, u32[]{:S(2)}) collective-permute-start(bf16[512,256]{1,0:T(8,128)(2,1)} %fusion.14), channel_id=1, source_target_pairs={{3,0},{19,1},{1,2},{17,3},{2,16},{18,17},{0,18},{16,19},{7,4},{23,... | collective-permute-start | bytes 786440 | tf_op jit(solution)/shard_map/ppermute | solution.py:755
  180.7 20.8 %collective-permute-start.35 = (bf16[512,256]{1,0:T(8,128)(2,1)}, bf16[512,256]{1,0:T(8,128)(2,1)}, u32[]{:S(2)}, u32[]{:S(2)}) collective-permute-start(bf16[512,256]{1,0:T(8,128)(2,1)} %fusion.14), channel_id=1, source_target_pairs={{1,0},{17,1},{3,2},{19,3},{0,16},{16,17},{2,18},{18,19},{5,4},{21,... | collective-permute-start | bytes 786440 | tf_op jit(solution)/shard_map/ppermute | solution.py:755
  181.0 20.9 %collective-permute-start.34 = (bf16[512,256]{1,0:T(8,128)(2,1)}, bf16[512,256]{1,0:T(8,128)(2,1)}, u32[]{:S(2)}, u32[]{:S(2)}) collective-permute-start(bf16[512,256]{1,0:T(8,128)(2,1)} %fusion.14), channel_id=1, source_target_pairs={{2,0},{18,1},{0,2},{16,3},{3,16},{19,17},{1,18},{17,19},{6,4},{22,... | collective-permute-start | bytes 786440 | tf_op jit(solution)/shard_map/ppermute | solution.py:755
  181.7 20.3 %collective-permute-start.33 = (bf16[512,256]{1,0:T(8,128)(2,1)}, bf16[512,256]{1,0:T(8,128)(2,1)}, u32[]{:S(2)}, u32[]{:S(2)}) collective-permute-start(bf16[512,256]{1,0:T(8,128)(2,1)} %fusion.14), channel_id=1, source_target_pairs={{0,0},{16,1},{2,2},{18,3},{1,16},{17,17},{3,18},{19,19},{4,4},{20,... | collective-permute-start | bytes 786440 | tf_op jit(solution)/shard_map/ppermute | solution.py:755
  198.5 13.5 %collective-permute-start.38 = (bf16[128,1024]{1,0:T(8,128)(2,1)}, bf16[128,1024]{1,0:T(8,128)(2,1)S(1)}, u32[]{:S(2)}, u32[]{:S(2)}) collective-permute-start(bf16[128,1024]{1,0:T(8,128)(2,1)} %get-tuple-element.228), channel_id=1, source_target_pairs={{0,16},{1,17},{2,18},{3,19},{16,0},{17,1},{18,2},{19,3},{4,20},{5,... | collective-permute-start | bytes 786440 | tf_op jit(solution)/shard_map/ppermute | solution.py:44
  201.5 13.9 %collective-permute-start.46 = (bf16[256,1024]{1,0:T(8,128)(2,1)}, bf16[256,1024]{1,0:T(8,128)(2,1)S(1)}, u32[]{:S(2)}, u32[]{:S(2)}) collective-permute-start(bf16[256,1024]{1,0:T(8,128)(2,1)} %get-tuple-element.472), channel_id=1, source_target_pairs={{0,1},{1,0},{2,3},{3,2},{16,17},{17,16},{18,19},{19,18},{4,5},{5,4... | collective-permute-start | bytes 1572872 | tf_op jit(solution)/shard_map/ppermute | solution.py:44
  201.8 15.6 %collective-permute-start.45 = (bf16[256,1024]{1,0:T(8,128)(2,1)}, bf16[256,1024]{1,0:T(8,128)(2,1)S(1)}, u32[]{:S(2)}, u32[]{:S(2)}) collective-permute-start(bf16[256,1024]{1,0:T(8,128)(2,1)} %get-tuple-element.473), channel_id=1, source_target_pairs={{0,1},{1,0},{2,3},{3,2},{16,17},{17,16},{18,19},{19,18},{4,5},{5,4... | collective-permute-start | bytes 1572872 | tf_op jit(solution)/shard_map/ppermute | solution.py:44
  205.9 144.4 %reduce-scatter.5.cloned.1.call-start = ((), (), s32[]{:S(2)}) async-start(), calls=%async_computation.13 | async-start | bytes 2621440 | tf_op jit(solution)/shard_map/reduce_scatter | solution.py:911
  215.4 14.4 %collective-permute-start.41 = (bf16[128,1024]{1,0:T(8,128)(2,1)S(1)}, bf16[128,1024]{1,0:T(8,128)(2,1)S(1)}, u32[]{:S(2)}, u32[]{:S(2)}) collective-permute-start(bf16[128,1024]{1,0:T(8,128)(2,1)S(1)} %get-tuple-element.230.refs_0_), channel_id=1, source_target_pairs={{0,16},{1,17},{2,18},{3,19},{16,0},{17,1},{18,2},{19,3},{4,20},{5,... | collective-permute-start | bytes 786440 | tf_op jit(solution)/shard_map/ppermute | solution.py:44
  237.8 13.7 %collective-permute-start.48 = (bf16[128,1024]{1,0:T(8,128)(2,1)S(1)}, bf16[128,1024]{1,0:T(8,128)(2,1)S(1)}, u32[]{:S(2)}, u32[]{:S(2)}) collective-permute-start(bf16[128,1024]{1,0:T(8,128)(2,1)S(1)} %get-tuple-element.243), channel_id=1, source_target_pairs={{0,16},{1,17},{2,18},{3,19},{16,0},{17,1},{18,2},{19,3},{4,20},{5,... | collective-permute-start | bytes 786440 | tf_op jit(solution)/shard_map/ppermute | solution.py:44
  262.9 132.0 %reduce-scatter.7.cloned.1.call-start = ((), (), s32[]{:S(2)}) async-start(), calls=%async_computation.14 | async-start | bytes 1310720 | tf_op jit(solution)/shard_map/reduce_scatter | solution.py:911
  264.5 13.9 %collective-permute-start.51 = (bf16[128,1024]{1,0:T(8,128)(2,1)}, bf16[128,1024]{1,0:T(8,128)(2,1)S(1)}, u32[]{:S(2)}, u32[]{:S(2)}) collective-permute-start(bf16[128,1024]{1,0:T(8,128)(2,1)} %copy-done.45), channel_id=1, source_target_pairs={{0,16},{1,17},{2,18},{3,19},{16,0},{17,1},{18,2},{19,3},{4,20},{5,... | collective-permute-start | bytes 786440 | tf_op jit(solution)/shard_map/ppermute | solution.py:44
  274.9 14.6 %collective-permute-start.55 = (bf16[128,1024]{1,0:T(8,128)(2,1)S(1)}, bf16[128,1024]{1,0:T(8,128)(2,1)S(1)}, u32[]{:S(2)}, u32[]{:S(2)}) collective-permute-start(bf16[128,1024]{1,0:T(8,128)(2,1)S(1)} %get-tuple-element.271), channel_id=1, source_target_pairs={{0,18},{1,19},{2,16},{3,17},{16,2},{17,3},{18,0},{19,1},{4,22},{5,... | collective-permute-start | bytes 786440 | tf_op jit(solution)/shard_map/ppermute | solution.py:44
  289.6 20.3 %collective-permute-start.96 = (f32[768]{0:T(1024)S(1)}, f32[768]{0:T(1024)S(1)}, u32[]{:S(2)}, u32[]{:S(2)}) collective-permute-start(f32[768]{0:T(1024)S(1)} %pad_maximum_fusion.17), channel_id=1, source_target_pairs={{0,1},{1,0},{2,3},{3,2},{16,17},{17,16},{18,19},{19,18},{4,5},{5,4... | collective-permute-start | bytes 9224 | tf_op jit(solution)/shard_map/ppermute | solution.py:44
  290.7 14.0 %collective-permute-start.57 = (bf16[128,1024]{1,0:T(8,128)(2,1)S(1)}, bf16[128,1024]{1,0:T(8,128)(2,1)S(1)}, u32[]{:S(2)}, u32[]{:S(2)}) collective-permute-start(bf16[128,1024]{1,0:T(8,128)(2,1)S(1)} %get-tuple-element.279), channel_id=1, source_target_pairs={{0,16},{1,17},{2,18},{3,19},{16,0},{17,1},{18,2},{19,3},{4,20},{5,... | collective-permute-start | bytes 786440 | tf_op jit(solution)/shard_map/ppermute | solution.py:44
  312.7 108.9 %all-gather.20.cloned.1.call-start = ((), (), s32[]{:S(2)}) async-start(), calls=%async_computation.17 | async-start | bytes 2703360 | tf_op jit(solution)/shard_map/all_gather | solution.py:945
  320.2 15.4 %collective-permute-start.60 = (bf16[128,1024]{1,0:T(8,128)(2,1)S(1)}, bf16[128,1024]{1,0:T(8,128)(2,1)S(1)}, u32[]{:S(2)}, u32[]{:S(2)}) collective-permute-start(bf16[128,1024]{1,0:T(8,128)(2,1)S(1)} %get-tuple-element.469.refs_0_.refs_6_), channel_id=1, source_target_pairs={{0,16},{1,17},{2,18},{3,19},{16,0},{17,1},{18,2},{19,3},{4,20},{5,... | collective-permute-start | bytes 786440 | tf_op jit(solution)/shard_map/ppermute | solution.py:44
  321.8 13.9 %collective-permute-start.59 = (bf16[128,1024]{1,0:T(8,128)(2,1)S(1)}, bf16[128,1024]{1,0:T(8,128)(2,1)S(1)}, u32[]{:S(2)}, u32[]{:S(2)}) collective-permute-start(bf16[128,1024]{1,0:T(8,128)(2,1)S(1)} %get-tuple-element.469.refs_0_.refs_6_), channel_id=1, source_target_pairs={{0,2},{1,3},{2,0},{3,1},{16,18},{17,19},{18,16},{19,17},{4,6},{5,7... | collective-permute-start | bytes 786440 | tf_op jit(solution)/shard_map/ppermute | solution.py:44
  342.3 99.9 %reduce-scatter.9.cloned.1.call-start = ((), (), s32[]{:S(2)}) async-start(), calls=%async_computation.15 | async-start | bytes 2621440 | tf_op jit(solution)/shard_map/reduce_scatter | solution.py:911
  365.0 13.2 %collective-permute-start.74 = (bf16[128,1024]{1,0:T(8,128)(2,1)S(1)}, bf16[128,1024]{1,0:T(8,128)(2,1)}, u32[]{:S(2)}, u32[]{:S(2)}) collective-permute-start(bf16[128,1024]{1,0:T(8,128)(2,1)S(1)} %get-tuple-element.331.refs_0_), channel_id=1, source_target_pairs={{0,16},{1,17},{2,18},{3,19},{16,0},{17,1},{18,2},{19,3},{4,20},{5,... | collective-permute-start | bytes 786440 | tf_op jit(solution)/shard_map/ppermute | solution.py:44
  387.7 24.0 %collective-permute-start.87 = (f32[768]{0:T(1024)S(1)}, f32[768]{0:T(1024)S(1)}, u32[]{:S(2)}, u32[]{:S(2)}) collective-permute-start(f32[768]{0:T(1024)S(1)} %pad_maximum_fusion.16), channel_id=1, source_target_pairs={{0,1},{1,0},{2,3},{3,2},{16,17},{17,16},{18,19},{19,18},{4,5},{5,4... | collective-permute-start | bytes 9224 | tf_op jit(solution)/shard_map/ppermute | solution.py:44
  416.4 39.8 %all-to-all-start.3 = ((bf16[4,528,256]{2,1,0:T(8,128)(2,1)}), bf16[4,528,256]{2,1,0:T(8,128)(2,1)S(1)}, u32[]{:S(2)}, u32[]{:S(2)}) async-start(bf16[4,528,256]{2,1,0:T(8,128)(2,1)} %broadcast_in_dim.169), calls=%async_computation.5 | async-start | bytes 2162688 | tf_op jit(solution)/shard_map/all_to_all | solution.py:68
  421.4 63.7 %reduce-scatter.11.cloned.1.call-start = ((), (), s32[]{:S(2)}) async-start(), calls=%async_computation.16 | async-start | bytes 1310720 | tf_op jit(solution)/shard_map/reduce_scatter | solution.py:911
  460.2 18.9 %collective-permute-start.100 = (bf16[256,1024]{1,0:T(8,128)(2,1)S(1)}, bf16[256,1024]{1,0:T(8,128)(2,1)S(1)}, u32[]{:S(2)}, u32[]{:S(2)}) collective-permute-start(bf16[256,1024]{1,0:T(8,128)(2,1)S(1)} %broadcast_select_fusion), channel_id=1, source_target_pairs={{0,16},{1,17},{2,18},{3,19},{16,0},{17,1},{18,2},{19,3},{4,20},{5,... | collective-permute-start | bytes 1572872 | tf_op jit(solution)/shard_map/ppermute | solution.py:44
  468.0 15.7 %collective-permute-start.98 = (bf16[528,256]{1,0:T(8,128)(2,1)S(1)}, bf16[528,256]{1,0:T(8,128)(2,1)S(1)}, u32[]{:S(2)}, u32[]{:S(2)}) collective-permute-start(bf16[528,256]{1,0:T(8,128)(2,1)S(1)} %pad_maximum_fusion.10), channel_id=1, source_target_pairs={{0,16},{1,17},{2,18},{3,19},{16,0},{17,1},{18,2},{19,3},{4,20},{5,... | collective-permute-start | bytes 811016 | tf_op jit(solution)/shard_map/ppermute | solution.py:44
  (135 other events, 1173.3 us)
Sparse Core Ops, SparseCore 0:
  30.7 40.7 all-gather.9
  73.6 44.6 all-gather.11
  120.5 26.0 all-gather.13
  148.0 45.3 all-gather.15
  206.0 27.2 all-gather.17
  263.0 43.1 reduce-scatter.4
  312.8 26.9 reduce-scatter.6
  342.4 46.9 all-gather.19
  391.7 50.5 reduce-scatter.8
  456.5 26.1 reduce-scatter.10
